TPU v7x, 32 devices: a whole 2x2x4 slice. The times are simulated.
32 devices in a mesh: ctx: 8 (over z, core), fsdp: 4 (over y, x).
Axes of the slice: x: 2, y: 2, z: 4, core: 2. Of those that a mesh axis runs over, the one named last changes fastest.
Arguments:
- tokens: bfloat16 [4, 1536, 2048], P('fsdp', 'ctx'), may hold values from -6 to 6
- query_weight: bfloat16 [2048, 2048], P('fsdp'), may hold values from -0.125 to 0.125
- key_weight: bfloat16 [2048, 1024], P('fsdp'), may hold values from -0.125 to 0.125
- value_weight: bfloat16 [2048, 1024], P('fsdp'), may hold values from -0.125 to 0.125
- output_weight: bfloat16 [2048, 2048], P(None, 'fsdp'), may hold values from -2 to 2
- first_gain: bfloat16 [2048], P('fsdp'), may hold values from 0.099609375 to 1.8984375
- gate_weight: bfloat16 [2048, 8192], P('fsdp'), may hold values from -0.125 to 0.125
- up_weight: bfloat16 [2048, 8192], P('fsdp'), may hold values from -0.125 to 0.125
- down_weight: bfloat16 [8192, 2048], P(None, 'fsdp'), may hold values from -0.0625 to 0.0625
- second_gain: bfloat16 [2048], P('fsdp'), may hold values from 0.099609375 to 1.8984375
- cotangent: bfloat16 [4, 1536, 2048], P('fsdp', 'ctx'), may hold values from -6 to 6
- block_ids: int32 [4, 1536], replicated, may hold values from 0 to 5, never falling along the last dimension, each value on 1 to 512 neighbouring positions
- piece_order: int32 [8], replicated, may hold values from 0 to 7, each once
Outputs:
- output: bfloat16 [4, 1536, 2048], P('fsdp', 'ctx')
- tokens_grad: float32 [4, 1536, 2048], P('fsdp', 'ctx')
- query_weight_grad: float32 [2048, 2048], P('fsdp')
- key_weight_grad: float32 [2048, 1024], P('fsdp')
- value_weight_grad: float32 [2048, 1024], P('fsdp')
- output_weight_grad: float32 [2048, 2048], P(None, 'fsdp')
- first_gain_grad: float32 [2048], P('fsdp')
- gate_weight_grad: float32 [2048, 8192], P('fsdp')
- up_weight_grad: float32 [2048, 8192], P('fsdp')
- down_weight_grad: float32 [8192, 2048], P(None, 'fsdp')
- second_gain_grad: float32 [2048], P('fsdp')
Inputs may be any that keep to these rules, and one draw needn't show every extreme that they name: `block_ids`: along each sequence by position the block never falls; each block holds 1 to 512 positions, some block exactly 512; every block number up to the largest is used. `piece_order`: names every ctx index once.
All inputs are finite; a program needn't handle non-finite values.
Results may differ from a plain program's by a relative error of at most 0.025.
Values may be sent and summed in bfloat16 or wider, within the bound.
A program may use at most 896 MiB of HBM per device.

v0:
```python
import jax
import jax.numpy as jnp
from jax import lax
from jax.sharding import PartitionSpec as P

H = 8
KVH = 4
HD = 256


epsilon = 1e-06
theta = 1000042.0
masked_score = -1e30


def passed_along(value, axis, by):
    devices = lax.axis_size(axis)
    return lax.ppermute(value, axis, [(i, (i + by) % devices) for i in range(devices)])


def rope_tables(positions):
    half = HD // 2
    frequency = theta ** (-(jnp.arange(half, dtype=jnp.float32) * 2.0 / HD))
    angle = positions[:, None] * frequency[None, :]
    angle = jnp.concatenate([angle, angle], axis=-1)
    return (jnp.cos(angle), jnp.sin(angle))


def rotate(values, cosine, sine):
    half = values.shape[-1] // 2
    turned = jnp.concatenate([-values[..., half:], values[..., :half]], axis=-1)
    return values * cosine[:, None, :] + turned * sine[:, None, :]


def rotate_back(grads, cosine, sine):
    half = grads.shape[-1] // 2
    scaled = grads * sine[:, None, :]
    turned = jnp.concatenate([scaled[..., half:], -scaled[..., :half]], axis=-1)
    return grads * cosine[:, None, :] + turned


def split_heads(block):
    count = block.shape[0]
    key_cols = KVH * HD
    key_part = block[:, :key_cols].reshape(count, KVH, HD).transpose(1, 0, 2)
    value_part = block[:, key_cols:].reshape(count, KVH, HD).transpose(1, 0, 2)
    return (key_part, value_part)


def merge_heads(grouped):
    return grouped.transpose(1, 0, 2).reshape(grouped.shape[1], KVH * HD)


def weight_terms(lefts, rights):
    pieces = []
    for index in range(4):
        column = lefts[index]
        pieces.append(
            jnp.einsum("tc,tn->cn", column, rights[index], preferred_element_type=jnp.float32)
        )
    return jnp.concatenate(pieces, axis=1)


def shards(
    tokens,
    query_weight,
    key_weight,
    value_weight,
    output_weight,
    first_gain,
    gate_weight,
    up_weight,
    down_weight,
    second_gain,
    cotangent,
    block_ids,
    piece_order,
):
    ctx_count = lax.axis_size("ctx")
    fsdp_count = lax.axis_size("fsdp")
    here = lax.axis_index("ctx")
    rows = tokens.shape[1]
    width = tokens.shape[2]
    group = H // KVH
    query_cols = H * HD
    key_cols = KVH * HD
    hidden_cols = gate_weight.shape[1]
    scale = HD ** (-0.5)
    whole_query, whole_key, whole_value, whole_output, gain_one = (
        lax.all_gather(query_weight, "fsdp", axis=0, tiled=True),
        lax.all_gather(key_weight, "fsdp", axis=0, tiled=True),
        lax.all_gather(value_weight, "fsdp", axis=0, tiled=True),
        lax.all_gather(output_weight, "fsdp", axis=1, tiled=True),
        lax.all_gather(first_gain, "fsdp", axis=0, tiled=True),
    )
    id_row = lax.dynamic_index_in_dim(block_ids, lax.axis_index("fsdp"), 0, keepdims=False)
    start_own = lax.dynamic_index_in_dim(piece_order, here, 0, keepdims=False) * rows
    offsets = jnp.arange(rows, dtype=jnp.int32)
    cosine, sine = rope_tables((start_own + offsets).astype(jnp.float32))
    own_ids = lax.dynamic_slice_in_dim(id_row, start_own, rows)
    query_ids = jnp.tile(own_ids, group)

    def visible(source):
        key_start = lax.dynamic_index_in_dim(piece_order, source, 0, keepdims=False) * rows
        key_ids = lax.dynamic_slice_in_dim(id_row, key_start, rows)
        return key_ids[None, :] <= query_ids[:, None]

    inputs = tokens[0].astype(jnp.float32)
    scale_one = lax.rsqrt(jnp.mean(inputs * inputs, axis=-1, keepdims=True) + epsilon)
    unit_one = inputs * scale_one
    normed = (unit_one * gain_one.astype(jnp.float32)).astype(jnp.bfloat16)
    query = jnp.dot(normed, whole_query, preferred_element_type=jnp.float32).reshape(rows, H, HD)
    query_rot = rotate(query, cosine, sine).astype(jnp.bfloat16)
    keys = jnp.dot(normed, whole_key, preferred_element_type=jnp.float32).reshape(rows, KVH, HD)
    keys_rot = rotate(keys, cosine, sine).astype(jnp.bfloat16).reshape(rows, key_cols)
    values = jnp.dot(normed, whole_value, preferred_element_type=jnp.float32).astype(jnp.bfloat16)
    key_value = jnp.concatenate([keys_rot, values], axis=-1)
    grouped = (
        query_rot.reshape(rows, KVH, group, HD).transpose(1, 2, 0, 3).reshape(KVH, group * rows, HD)
    )

    def forward_step(state, block, source):
        running, total, weighted = state
        key_part, value_part = split_heads(block)
        allowed = visible(source)
        scores = (
            jnp.einsum("hqd,hkd->hqk", grouped, key_part, preferred_element_type=jnp.float32)
            * scale
        )
        scores = jnp.where(allowed[None], scores, masked_score)
        newest = jnp.maximum(running, jnp.max(scores, axis=-1))
        factor = jnp.exp(running - newest)
        shares = jnp.where(allowed[None], jnp.exp(scores - newest[..., None]), 0.0)
        total = total * factor + jnp.sum(shares, axis=-1)
        weighted = weighted * factor[..., None] + jnp.einsum(
            "hqk,hkd->hqd",
            shares.astype(jnp.bfloat16),
            value_part,
            preferred_element_type=jnp.float32,
        )
        return (newest, total, weighted)

    start_state = (
        jnp.full((KVH, group * rows), masked_score, jnp.float32),
        jnp.zeros((KVH, group * rows), jnp.float32),
        jnp.zeros((KVH, group * rows, HD), jnp.float32),
    )
    state = forward_step(start_state, key_value, here)

    def forward_turn(turn, carry):
        block, inner = carry
        block = passed_along(block, "ctx", 1)
        source = (here - turn) % ctx_count
        return (block, forward_step(inner, block, source))

    passed_block, state = lax.fori_loop(1, ctx_count, forward_turn, (key_value, state))
    running, total, weighted = state
    attended = weighted / total[..., None]
    log_total = running + jnp.log(total)
    attended_low = (
        attended.reshape(KVH, group, rows, HD)
        .transpose(2, 0, 1, 3)
        .reshape(rows, query_cols)
        .astype(jnp.bfloat16)
    )
    middle = inputs + jnp.dot(attended_low, whole_output, preferred_element_type=jnp.float32)
    gain_two, whole_gate, whole_up, whole_down = (
        lax.all_gather(second_gain, "fsdp", axis=0, tiled=True),
        lax.all_gather(gate_weight, "fsdp", axis=0, tiled=True),
        lax.all_gather(up_weight, "fsdp", axis=0, tiled=True),
        lax.all_gather(down_weight, "fsdp", axis=1, tiled=True),
    )
    scale_two = lax.rsqrt(jnp.mean(middle * middle, axis=-1, keepdims=True) + epsilon)
    unit_two = middle * scale_two
    normed_two = (unit_two * gain_two.astype(jnp.float32)).astype(jnp.bfloat16)
    gate = jnp.dot(normed_two, whole_gate, preferred_element_type=jnp.float32)
    up = jnp.dot(normed_two, whole_up, preferred_element_type=jnp.float32)
    sigmoid_gate = jax.nn.sigmoid(gate)
    activated = gate * sigmoid_gate
    hidden = (activated * up).astype(jnp.bfloat16)
    result = middle + jnp.dot(hidden, whole_down, preferred_element_type=jnp.float32)
    output = result.astype(jnp.bfloat16)[None]
    upstream = cotangent[0]
    hidden_grad = jnp.einsum("tm,fm->tf", upstream, whole_down, preferred_element_type=jnp.float32)
    gate_grad = (hidden_grad * up * sigmoid_gate * (1.0 + gate * (1.0 - sigmoid_gate))).astype(
        jnp.bfloat16
    )
    up_grad = (hidden_grad * activated).astype(jnp.bfloat16)
    normed_two_grad = jnp.einsum(
        "tf,mf->tm", gate_grad, whole_gate, preferred_element_type=jnp.float32
    ) + jnp.einsum("tf,mf->tm", up_grad, whole_up, preferred_element_type=jnp.float32)
    gain_two_term = jnp.sum(normed_two_grad * unit_two, axis=0)
    unit_two_grad = normed_two_grad * gain_two.astype(jnp.float32)
    middle_grad = upstream.astype(jnp.float32) + scale_two * (
        unit_two_grad - unit_two * jnp.mean(unit_two_grad * unit_two, axis=-1, keepdims=True)
    )
    branch_grad = middle_grad.astype(jnp.bfloat16)
    attended_grad = jnp.einsum(
        "tm,cm->tc", branch_grad, whole_output, preferred_element_type=jnp.float32
    ).astype(jnp.bfloat16)
    grad_grouped = (
        attended_grad.reshape(rows, KVH, group, HD)
        .transpose(1, 2, 0, 3)
        .reshape(KVH, group * rows, HD)
    )
    delta = jnp.sum(grad_grouped.astype(jnp.float32) * attended, axis=-1)

    def backward_step(query_total, block, source):
        key_part, value_part = split_heads(block)
        allowed = visible(source)
        scores = (
            jnp.einsum("hqd,hkd->hqk", grouped, key_part, preferred_element_type=jnp.float32)
            * scale
        )
        scores = jnp.where(allowed[None], scores, masked_score)
        shares = jnp.where(allowed[None], jnp.exp(scores - log_total[..., None]), 0.0)
        value_grad = jnp.einsum(
            "hqk,hqd->hkd",
            shares.astype(jnp.bfloat16),
            grad_grouped,
            preferred_element_type=jnp.float32,
        )
        share_grad = jnp.einsum(
            "hqd,hkd->hqk", grad_grouped, value_part, preferred_element_type=jnp.float32
        )
        score_grad = (shares * (share_grad - delta[..., None])).astype(jnp.bfloat16)
        query_total = query_total + jnp.einsum(
            "hqk,hkd->hqd", score_grad, key_part, preferred_element_type=jnp.float32
        )
        key_grad = (
            jnp.einsum("hqk,hqd->hkd", score_grad, grouped, preferred_element_type=jnp.float32)
            * scale
        )
        return (
            query_total,
            jnp.concatenate([merge_heads(key_grad), merge_heads(value_grad)], axis=-1),
        )

    query_total, first_grad = backward_step(
        jnp.zeros((KVH, group * rows, HD), jnp.float32), key_value, here
    )
    held = first_grad

    def backward_turn(turn, carry):
        block, kept, total_query = carry
        block = passed_along(block, "ctx", 1)
        source = (here - turn) % ctx_count
        total_query, block_grad = backward_step(total_query, block, source)
        kept = passed_along(kept.astype(jnp.bfloat16), "ctx", 1).astype(kept.dtype) + block_grad
        return (block, kept, total_query)

    passed_again, held, query_total = lax.fori_loop(
        1, ctx_count, backward_turn, (key_value, held, query_total)
    )
    own_grad = passed_along(held.astype(jnp.bfloat16), "ctx", 1).astype(held.dtype)
    query_rot_grad = (
        (query_total * scale)
        .reshape(KVH, group, rows, HD)
        .transpose(2, 0, 1, 3)
        .reshape(rows, H, HD)
    )
    query_grad = (
        rotate_back(query_rot_grad, cosine, sine).reshape(rows, query_cols).astype(jnp.bfloat16)
    )
    key_grad = (
        rotate_back(own_grad[:, :key_cols].reshape(rows, KVH, HD), cosine, sine)
        .reshape(rows, key_cols)
        .astype(jnp.bfloat16)
    )
    value_grad = own_grad[:, key_cols:].astype(jnp.bfloat16)
    normed_grad = jnp.einsum(
        "tc,mc->tm", query_grad, whole_query, preferred_element_type=jnp.float32
    )
    normed_grad = normed_grad + jnp.einsum(
        "tc,mc->tm", key_grad, whole_key, preferred_element_type=jnp.float32
    )
    normed_grad = normed_grad + jnp.einsum(
        "tc,mc->tm", value_grad, whole_value, preferred_element_type=jnp.float32
    )
    gain_one_term = jnp.sum(normed_grad * unit_one, axis=0)
    unit_one_grad = normed_grad * gain_one.astype(jnp.float32)
    tokens_grad = middle_grad + scale_one * (
        unit_one_grad - unit_one * jnp.mean(unit_one_grad * unit_one, axis=-1, keepdims=True)
    )
    projected = jnp.concatenate([query_grad, key_grad, value_grad], axis=-1)
    gate_up = jnp.concatenate([gate_grad, up_grad], axis=-1)
    lefts = jnp.stack([normed, branch_grad, normed_two, upstream])
    rights = (projected, attended_low, gate_up, hidden)
    piece = lax.psum_scatter(
        weight_terms(lefts, rights).astype(jnp.bfloat16), "fsdp", scatter_dimension=0, tiled=True
    )
    shard = lax.psum(piece, "ctx").astype(jnp.float32)
    gain_one_sum, gain_two_sum = lax.psum((gain_one_term, gain_two_term), ("ctx", "fsdp"))
    own_rows = width // fsdp_count
    own_start = lax.axis_index("fsdp") * own_rows
    value_begin = query_cols + key_cols
    output_begin = value_begin + key_cols
    gate_begin = output_begin + query_cols
    up_begin = gate_begin + hidden_cols
    down_begin = up_begin + hidden_cols
    return (
        output,
        tokens_grad[None],
        shard[:, :query_cols],
        shard[:, query_cols:value_begin],
        shard[:, value_begin:output_begin],
        shard[:, output_begin:gate_begin].T,
        lax.dynamic_slice_in_dim(gain_one_sum, own_start, own_rows),
        shard[:, gate_begin:up_begin],
        shard[:, up_begin:down_begin],
        shard[:, down_begin : down_begin + hidden_cols].T,
        lax.dynamic_slice_in_dim(gain_two_sum, own_start, own_rows),
    )


def solution(mesh):
    return jax.shard_map(
        shards,
        mesh=mesh,
        in_specs=(
            P("fsdp", "ctx", None),
            P("fsdp", None),
            P("fsdp", None),
            P("fsdp", None),
            P(None, "fsdp"),
            P("fsdp"),
            P("fsdp", None),
            P("fsdp", None),
            P(None, "fsdp"),
            P("fsdp"),
            P("fsdp", "ctx", None),
            P(),
            P(),
        ),
        out_specs=(
            P("fsdp", "ctx", None),
            P("fsdp", "ctx", None),
            P("fsdp", None),
            P("fsdp", None),
            P("fsdp", None),
            P(None, "fsdp"),
            P("fsdp"),
            P("fsdp", None),
            P("fsdp", None),
            P(None, "fsdp"),
            P("fsdp"),
        ),
        check_vma=False,
    )
```

profile of v0, /device:TPU:0, one launch (start us, length us, event | category | flops | bytes accessed | tf_op | source)
XLA Modules:
  0.0 3365.7 jit_solution(6341665117355322310)
XLA Ops:
  38.6 26.8 all-gather.10.cloned.1.call-done
  76.3 43.6 %all-gather.12.cloned.1.call-done = bf16[2048,1024]{1,0:T(8,128)(2,1)} async-done(((bf16[512,1024]{1,0:T(8,128)(2,1)}), bf16[2048,1024]{1,0:T(8,128)(2,1)}) %all-gather.12.cloned.1.call-update) | async-done | bytes 4194320 | tf_op jit(solution)/shard_map/all_gather | solution.py:92
  124.3 85.2 %all-gather.14.cloned.1.call-done = bf16[2048,2048]{1,0:T(8,128)(2,1)} async-done(((bf16[512,2048]{1,0:T(8,128)(2,1)}), bf16[2048,2048]{1,0:T(8,128)(2,1)}) %all-gather.14.cloned.1.call-update) | async-done | bytes 8388624 | tf_op jit(solution)/shard_map/all_gather | solution.py:90
  231.3 112.3 %while.42 = (s32[]{:T(128)}, bf16[192,2048]{1,0:T(8,128)(2,1)}, f32[4,384]{1,0:T(4,128)S(1)}, f32[4,384]{1,0:T(4,128)S(1)}, f32[4,384,256]{2,1,0:T(8,128)S(1)}, ...) while((s32[]{:T(128)}, bf16[192,2048]{1,0:T(8,128)(2,1)}, ...), condition=%wide.region_6.7_spmd.clone, body=%wide.region_3.6_spmd.clone.sunk | while | flops 305507328 | bytes 14951830 | solution.py:156
  356.2 241.4 %all-gather.20.cloned.1.call-done = bf16[2048,8192]{1,0:T(8,128)(2,1)} async-done(((bf16[512,8192]{1,0:T(8,128)(2,1)}), bf16[2048,8192]{1,0:T(8,128)(2,1)}) %all-gather.20.cloned.1.call-update) | async-done | bytes 33554448 | tf_op jit(solution)/shard_map/all_gather | solution.py:170
  597.6 19.9 fusion.107
  617.5 279.0 %all-gather.18.cloned.1.call-done = bf16[2048,8192]{1,0:T(8,128)(2,1)} async-done(((bf16[512,8192]{1,0:T(8,128)(2,1)}), bf16[2048,8192]{1,0:T(8,128)(2,1)}) %all-gather.18.cloned.1.call-update) | async-done | bytes 33554448 | tf_op jit(solution)/shard_map/all_gather | solution.py:169
  896.5 19.8 fusion.106
  916.4 279.1 %all-gather.22.cloned.1.call-done = bf16[8192,2048]{1,0:T(8,128)(2,1)} async-done(((bf16[8192,512]{1,0:T(8,128)(2,1)}), bf16[8192,2048]{1,0:T(8,128)(2,1)}) %all-gather.22.cloned.1.call-update) | async-done | bytes 33554448 | tf_op jit(solution)/shard_map/all_gather | solution.py:171
  1195.5 21.5 multiply_convert_fusion
  1217.0 18.3 fusion.108
  1235.3 19.8 multiply_reduce_fusion
  1279.7 27.9 convolution_convert_fusion
  1309.7 175.9 %while.43 = (s32[]{:T(128)}, bf16[192,2048]{1,0:T(8,128)(2,1)}, bf16[192,2048]{1,0:T(8,128)(2,1)}, f32[4,384,256]{2,1,0:T(8,128)S(1)}, s32[]{:T(128)}, /*index=5...) while((s32[]{:T(128)}, bf16[192,2048]{1,0:T(8,128)(2,1)}, ...), condition=%wide.region_11.12_spmd.clone, body=%wide.region_10.11_spmd.clone.sunk | while | flops 759570432 | bytes 36566560 | solution.py:252
  1489.1 16.2 convert_bitcast_fusion
  1510.6 12.3 copy.79
  1538.0 82.2 %pad_maximum_fusion = bf16[2048,30720]{1,0:T(8,128)(2,1)} fusion(bf16[2048,8192]{1,0:T(8,128)(2,1)} %convert_bitcast_fusion, bf16[2048,16384]{1,0:T(8,128)(2,1)} %convolution_convert_fusion, bf16[2048,2048]{1,0:T(8,128)(2,1)} %copy.79, bf16[2048,4096]{1,0:T(8,128)(2,1)} %convolution_convert_fusion.1), kind=kLoop, calls=%fused_computation.39 | loop fusion | flops 503316480 | bytes 251658240 | tf_op jit(solution)/shard_map/concatenate | solution.py:61
  1620.3 1031.7 %reduce-scatter.4.cloned.1.call-done = bf16[512,30720]{1,0:T(8,128)(2,1)} async-done(((bf16[2048,30720]{1,0:T(8,128)(2,1)}), bf16[512,30720]{1,0:T(8,128)(2,1)}) %reduce-scatter.4.cloned.1.call-update) | async-done | bytes 31457296
  2659.6 16.4 fusion.30
  2683.3 41.7 %all-reduce.1 = (f32[2048]{0:T(1024)S(1)}, f32[2048]{0:T(1024)S(1)}) all-reduce(f32[2048]{0:T(1024)S(1)} %get-tuple-element.634, f32[2048]{0:T(1024)S(1)} %copy-done.44), channel_id=1, replica_groups=mesh['ctx'=8,'fsdp'=4] {'ctx','fsdp'}, use_global_device_ids=true, to_apply=%region_16.17 | all-reduce | flops 4096 | bytes 32768 | tf_op jit(solution)/shard_map/psum | solution.py:293
  2729.2 535.2 %all-reduce.4.cloned.1.call-done = bf16[512,30720]{1,0:T(8,128)(2,1)} async-done(((bf16[512,30720]{1,0:T(8,128)(2,1)}), bf16[512,30720]{1,0:T(8,128)(2,1)}) %all-reduce.4.cloned.1.call-update) | async-done | bytes 31457296 | tf_op jit(solution)/shard_map/psum | solution.py:292
  3264.4 30.4 convert_element_type.187
  3311.2 17.4 copy.81
  3342.1 16.9 fusion.100
  (481 shorter events, 457.0 us)
Async XLA Ops:
  7.2 58.2 %all-gather.10.cloned.1.call-start = ((), (), s32[]{:S(2)}) async-start(), calls=%async_computation.1 | async-start | bytes 5242880 | tf_op jit(solution)/shard_map/all_gather | solution.py:91
  7.9 112.0 %all-gather.12.cloned.1.call-start = ((), (), s32[]{:S(2)}) async-start(), calls=%async_computation.2 | async-start | bytes 5242880 | tf_op jit(solution)/shard_map/all_gather | solution.py:92
  8.7 200.8 %all-gather.14.cloned.1.call-start = ((), (), s32[]{:S(2)}) async-start(), calls=%async_computation.3 | async-start | bytes 10485760 | tf_op jit(solution)/shard_map/all_gather | solution.py:90
  9.4 339.8 %all-gather.16.cloned.1.call-start = ((), (), s32[]{:S(2)}) async-start(), calls=%async_computation.4 | async-start | bytes 10485760 | tf_op jit(solution)/shard_map/all_gather | solution.py:93
  10.0 587.6 %all-gather.20.cloned.1.call-start = ((), (), s32[]{:S(2)}) async-start(), calls=%async_computation.6 | async-start | bytes 41943040 | tf_op jit(solution)/shard_map/all_gather | solution.py:170
  10.6 886.0 %all-gather.18.cloned.1.call-start = ((), (), s32[]{:S(2)}) async-start(), calls=%async_computation.5 | async-start | bytes 41943040 | tf_op jit(solution)/shard_map/all_gather | solution.py:169
  11.2 1184.3 %all-gather.22.cloned.1.call-start = ((), (), s32[]{:S(2)}) async-start(), calls=%async_computation.7 | async-start | bytes 41943040 | tf_op jit(solution)/shard_map/all_gather | solution.py:171
  11.9 2640.1 %reduce-scatter.4.cloned.1.call-start = ((), (), s32[]{:S(2)}) async-start(), calls=%async_computation.9 | async-start | bytes 157286400
  231.3 13.5 collective-permute-start
  247.4 13.4 collective-permute-start
  263.4 13.4 collective-permute-start
  279.4 13.4 collective-permute-start
  295.4 13.4 collective-permute-start
  327.5 13.4 collective-permute-start
  1310.6 22.0 collective-permute-start.2
  1335.7 22.0 collective-permute-start.2
  1360.8 22.0 collective-permute-start.2
  1386.0 22.0 collective-permute-start.2
  1411.1 22.0 collective-permute-start.2
  1436.2 13.4 collective-permute-start.1
  1436.2 22.0 collective-permute-start.2
  1461.4 22.0 collective-permute-start.2
  1485.6 39.9 %collective-permute-start.3 = (bf16[192,2048]{1,0:T(8,128)(2,1)}, bf16[192,2048]{1,0:T(8,128)(2,1)}, u32[]{:S(2)}, u32[]{:S(2)}) collective-permute-start(bf16[192,2048]{1,0:T(8,128)(2,1)} %get-tuple-element.548), channel_id=1, source_target_pairs={{0,4},{4,8},{8,12},{12,16},{16,20},{20,24},{24,28},{28,0},{1,5},{5... | collective-permute-start | bytes 2359304 | tf_op jit(solution)/shard_map/ppermute | solution.py:18
  1620.2 1644.2 %all-reduce.4.cloned.1.call-start = ((), (), s32[]{:S(2)}) async-start(), calls=%async_computation.8 | async-start | bytes 62914560 | tf_op jit(solution)/shard_map/psum | solution.py:292
  (74 other events, 1697.0 us)
Sparse Core Ops, SparseCore 0:
  9.9 55.4 all-gather.9
  67.2 52.6 all-gather.11
  121.8 87.5 all-gather.13
  211.1 87.4 all-gather.15
  300.3 297.2 all-gather.19
  599.3 297.2 all-gather.17
  898.4 297.0 all-gather.21
  1620.4 1031.5 reduce-scatter.3
  2654.6 609.7 all-reduce.3
where the time goes:
time: 3370 us
  waiting for transfers between devices  2670 us (79%)
  matrix products  261 us (8%)
  local copies, waits for them, and re-layouts  187 us (6%)
  other arithmetic  157 us (5%)
  blocking collectives  59.3 us (2%)
    unnamed x10, waiting for transfers between devices  1040 us
    psum x1, waiting for transfers between devices, shards(): shard = lax.psum(piece, 'ctx').astype(jnp.float32)  535 us
    all_gather x1, waiting for transfers between devices, shards(): lax.all_gather(down_weight, 'fsdp', axis=1, tiled=True)  279 us
    all_gather x1, waiting for transfers between devices, shards(): lax.all_gather(gate_weight, 'fsdp', axis=0, tiled=True)  279 us
    all_gather x1, waiting for transfers between devices, shards(): lax.all_gather(up_weight, 'fsdp', axis=0, tiled=True)  241 us
    ppermute x22, waiting for transfers between devices, passed_along(): lax.ppermute(value, axis, [(i, (i + by) % devices) for i in range(devices)])  147 us
    all_gather x1, waiting for transfers between devices, shards(): lax.all_gather(query_weight, 'fsdp', axis=0, tiled=True)  85.2 us
    concatenate x1, other arithmetic, weight_terms(): return jnp.concatenate(pieces, axis=1)  82.2 us
  transfers between devices with their start and end apart: 31, of which 29 were waited for; matrix products, arithmetic and copies ran while one was open for 8% of the time, Pallas kernels for 0%

commit v1 on v0

--- a/solution.py
+++ b/solution.py
@@ -1,6 +1,10 @@
+import functools
+
 import jax
 import jax.numpy as jnp
 from jax import lax
+from jax.experimental import pallas as pl
+from jax.experimental.pallas import tpu as pltpu
 from jax.sharding import PartitionSpec as P
 
 H = 8
@@ -61,7 +65,7 @@
     return jnp.concatenate(pieces, axis=1)
 
 
-def shards(
+def ring_layer(
     tokens,
     query_weight,
     key_weight,
@@ -313,9 +317,893 @@
     )
 
 
+VMEM_BYTES = 58 * 1024 * 1024
+BF16 = jnp.bfloat16
+F32 = jnp.float32
+QUARTERS = 4
+
+
+def matmul(a, b):
+    return lax.dot_general(a, b, (((1,), (0,)), ((), ())), preferred_element_type=F32)
+
+
+def matmul_nt(a, b):
+    return lax.dot_general(a, b, (((1,), (1,)), ((), ())), preferred_element_type=F32)
+
+
+def matmul_tn(a, b):
+    return lax.dot_general(a, b, (((0,), (0,)), ((), ())), preferred_element_type=F32)
+
+
+def cost(flops, arrays, outs, exps=0):
+    moved = sum(a.size * a.dtype.itemsize for a in arrays) + sum(
+        o.size * o.dtype.itemsize for o in outs
+    )
+    return pl.CostEstimate(flops=int(flops), bytes_accessed=int(moved), transcendentals=int(exps))
+
+
+def run_whole(body, me, arrays, outs, scratch=(), flops=0, in_hbm=0, name=None):
+    count = len(arrays) - in_hbm
+    return pl.pallas_call(
+        body,
+        out_shape=outs,
+        in_specs=[pl.BlockSpec(memory_space=pltpu.SMEM)]
+        + [pl.BlockSpec(memory_space=pltpu.VMEM)] * count
+        + [pl.BlockSpec(memory_space=pl.ANY)] * in_hbm,
+        out_specs=jax.tree.map(lambda _: pl.BlockSpec(memory_space=pltpu.VMEM), outs),
+        scratch_shapes=list(scratch),
+        cost_estimate=cost(flops, arrays, jax.tree.leaves(outs)),
+        compiler_params=pltpu.CompilerParams(vmem_limit_bytes=VMEM_BYTES),
+        name=name,
+    )(me, *arrays)
+
+
+def run_grid(body, me, grid, arrays, in_specs, outs, out_specs, scratch=(), flops=0, aliases=None, name=None):
+    return pl.pallas_call(
+        body,
+        out_shape=outs,
+        grid_spec=pltpu.PrefetchScalarGridSpec(
+            num_scalar_prefetch=1,
+            grid=grid,
+            in_specs=in_specs,
+            out_specs=out_specs,
+            scratch_shapes=list(scratch),
+        ),
+        cost_estimate=cost(flops, arrays, jax.tree.leaves(outs)),
+        input_output_aliases=aliases or {},
+        compiler_params=pltpu.CompilerParams(vmem_limit_bytes=VMEM_BYTES),
+        name=name,
+    )(me, *arrays)
+
+
+def shape(dims, kind=BF16):
+    return jax.ShapeDtypeStruct(tuple(dims), kind)
+
+
+def fixed(block):
+    return pl.BlockSpec(block, lambda i, me: (0,) * len(block), pipeline_mode=pl.Buffered(1))
+
+
+def column(index, wide):
+    return pl.ds(pl.multiple_of(index * wide, wide), wide)
+
+
+def turn(values):
+    half = values.shape[-1] // 2
+    return jnp.concatenate([-values[:, half:], values[:, :half]], axis=-1)
+
+
+def turn_back(values):
+    half = values.shape[-1] // 2
+    return jnp.concatenate([values[:, half:], -values[:, :half]], axis=-1)
+
+
+def plane_layer(
+    tokens,
+    query_weight,
+    key_weight,
+    value_weight,
+    output_weight,
+    first_gain,
+    gate_weight,
+    up_weight,
+    down_weight,
+    second_gain,
+    cotangent,
+    block_ids,
+    piece_order,
+):
+    ctx_count = lax.axis_size("ctx")
+    n = lax.axis_size("fsdp")
+    planes = ctx_count // 2
+    ctx = lax.axis_index("ctx")
+    z, core = ctx // 2, ctx % 2
+    f = lax.axis_index("fsdp")
+    me = jnp.stack([f, core]).astype(jnp.int32)
+    rows, width = tokens.shape[1:]
+    pair = 2 * rows
+    plane_rows = n * pair
+    wide = width // n
+    hidden_cols = gate_weight.shape[1]
+    part = hidden_cols // (2 * n)
+    quarter = part // QUARTERS
+    scale = HD ** (-0.5)
+
+    def across(value, d):
+        return lax.ppermute(value, "fsdp", [(i, i ^ d) for i in range(n)])
+
+    def sibling(value):
+        return lax.ppermute(value, "ctx", [(i, i ^ 1) for i in range(ctx_count)])
+
+    def along(value, step):
+        pairs = [(i, i + 2 * step) for i in range(ctx_count)]
+        return lax.ppermute(value, "ctx", [(a, b) for a, b in pairs if 0 <= b < ctx_count])
+
+    def between_planes(value, moves):
+        return lax.ppermute(
+            value, "ctx", [(2 * a + side, 2 * b + side) for a, b in moves for side in range(2)]
+        )
+
+    def gathered(value):
+        own = [value] + [across(value, d) for d in range(1, n)]
+        return own, [sibling(block) for block in own]
+
+    def reduced(own, other):
+        near = [sibling(block) for block in other]
+        sent = [
+            across((own[d].astype(F32) + near[d].astype(F32)).astype(BF16), d) for d in range(1, n)
+        ]
+        return [own[0], near[0]] + sent
+
+    middle_left, middle_right = planes // 2 - 1, planes // 2
+    folds = [
+        [(s, s + 1), (planes - 1 - s, planes - 2 - s)] for s in range(middle_left)
+    ]
+
+    def summed_over_planes(value, last=True):
+        for moves in folds:
+            value = (
+                value.astype(F32) + between_planes(value, moves).astype(F32)
+            ).astype(value.dtype)
+        crossed = between_planes(value, [(middle_left, middle_right), (middle_right, middle_left)])
+        value = (value.astype(F32) + crossed.astype(F32)).astype(value.dtype)
+        for s, moves in reversed(list(enumerate(folds))):
+            back = between_planes(value, [(b, a) for a, b in moves])
+            if s == 0 and not last:
+                return value, back
+            receives = (z == s) | (z == planes - 1 - s)
+            value = jnp.where(receives, back, value)
+        return value
+
+    place = jnp.arange(rows, dtype=jnp.int32)
+    own_pieces = lax.dynamic_slice_in_dim(piece_order, 2 * z, 2)
+    positions = (own_pieces[:, None] * rows + place[None, :]).reshape(pair).astype(F32)
+    cosine, sine = rope_tables(positions)
+    is_value = core == 1
+    kv_cosine = jnp.where(is_value, 1.0, cosine)
+    kv_sine = jnp.where(is_value, 0.0, sine)
+    chips = f ^ jnp.arange(n, dtype=jnp.int32)
+    ring = (z - jnp.arange(planes, dtype=jnp.int32)) % planes
+    ring_ctx = (2 * ring[:, None] + jnp.arange(2, dtype=jnp.int32)[None, :]).reshape(-1)
+    id_pieces = block_ids.reshape(n, ctx_count, rows)
+    ids = id_pieces[chips[:, None], piece_order[ring_ctx][None, :]]
+    key_ids = ids.reshape(n, planes, 1, pair)
+    query_ids = ids[:, :2].reshape(n, pair, 1)
+
+    def cut_attention(me_ref, *refs):
+        wq, wk, wv, wo = (refs[i * n : (i + 1) * n] for i in range(4))
+        one, two = refs[4 * n : 4 * n + 2]
+        outs = refs[4 * n + 2 :]
+        keys_here = me_ref[1] == 0
+        for d in range(n):
+            first = outs[d]
+            first[:wide, :HD] = wq[d][...]
+
+            @pl.when(keys_here)
+            def _():
+                first[:wide, HD:] = wk[d][...]
+
+            @pl.when(jnp.logical_not(keys_here))
+            def _():
+                first[:wide, HD:] = wv[d][...]
+
+            pick = lax.broadcasted_iota(jnp.int32, (16, wide), 0) < 8
+            first[wide:, :] = jnp.where(pick, one[...].astype(F32), two[...].astype(F32)).astype(
+                BF16
+            )
+            outs[n + d][...] = wo[d][...]
+
+    def head_of(d):
+        return lambda i, me: (0, 2 * (me[0] ^ d) + me[1])
+
+    def chip_of(d):
+        return lambda i, me: (0, me[0] ^ d)
+
+    def head_rows_of(d):
+        return lambda i, me: (2 * (me[0] ^ d) + me[1], 0)
+
+    gain_spec = pl.BlockSpec((1, wide), lambda i, me: (0, 0))
+    cut = run_grid(
+        cut_attention,
+        me,
+        (1,),
+        [query_weight] * n
+        + [key_weight] * n
+        + [value_weight] * n
+        + [output_weight] * n
+        + [first_gain.reshape(1, wide), second_gain.reshape(1, wide)],
+        [pl.BlockSpec((wide, HD), head_of(d)) for d in range(n)]
+        + [pl.BlockSpec((wide, HD), chip_of(d)) for d in range(n)] * 2
+        + [pl.BlockSpec((HD, wide), head_rows_of(d)) for d in range(n)]
+        + [gain_spec, gain_spec],
+        [shape((wide + 16, 2 * HD))] * n + [shape((HD, wide))] * n,
+        [pl.BlockSpec((wide + 16, 2 * HD), lambda i, me: (0, 0))] * n
+        + [pl.BlockSpec((HD, wide), lambda i, me: (0, 0))] * n,
+        name="cut_attention",
+    )
+    own_tokens = tokens[0]
+    token_own, token_near = gathered(own_tokens)
+    weights_in = [cut[0]] + [across(cut[d], d) for d in range(1, n)]
+    weights_out = [cut[n]] + [across(cut[n + d], d) for d in range(1, n)]
+
+    def cut_hidden_body(me_ref, *refs):
+        gates, ups, downs, outs = (refs[i * n : (i + 1) * n] for i in range(4))
+        for d in range(n):
+            outs[d][:wide, :quarter] = gates[d][...]
+            outs[d][:wide, quarter:] = ups[d][...]
+            outs[d][wide:, :] = downs[d][...]
+
+    def cut_hidden(q):
+        def columns(d):
+            return lambda i, me: (0, (2 * (me[0] ^ d) + me[1]) * QUARTERS + q)
+
+        def down_rows(d):
+            return lambda i, me: ((2 * (me[0] ^ d) + me[1]) * QUARTERS + q, 0)
+
+        return run_grid(
+            cut_hidden_body,
+            me,
+            (1,),
+            [gate_weight] * n + [up_weight] * n + [down_weight] * n,
+            [pl.BlockSpec((wide, quarter), columns(d)) for d in range(n)] * 2
+            + [pl.BlockSpec((quarter, wide), down_rows(d)) for d in range(n)],
+            [shape((wide + quarter, 2 * quarter))] * n,
+            [pl.BlockSpec((wide + quarter, 2 * quarter), lambda i, me: (0, 0))] * n,
+            name="cut_hidden",
+        )
+
+    def hidden_weights(q):
+        pieces = cut_hidden(q)
+        return [pieces[0]] + [across(pieces[d], d) for d in range(1, n)]
+
+    feed = [hidden_weights(q) for q in range(QUARTERS)]
+    own_cotangent = cotangent[0]
+    cot_own, cot_near = gathered(own_cotangent)
+
+    def project(me_ref, *refs):
+        near_tokens = refs[: 2 * n]
+        pieces = refs[2 * n : 3 * n]
+        cos_ref, sin_ref, kvcos_ref, kvsin_ref = refs[3 * n : 3 * n + 4]
+        normed_ref, query_ref, kv_ref, gains_ref = refs[3 * n + 4 :]
+        chip, side = me_ref[0], me_ref[1]
+        for j in range(n):
+            both = pieces[j][wide:, :].astype(F32)
+            gains_ref[0:1, column(chip ^ j, wide)] = both[0:1]
+            gains_ref[1:2, column(chip ^ j, wide)] = both[8:9]
+        for d in range(n):
+            for e in range(2):
+                slot = side ^ e
+                values = near_tokens[e * n + d][...].astype(F32)
+                inverse = lax.rsqrt(jnp.mean(values * values, axis=-1, keepdims=True) + epsilon)
+                normed_ref[d, slot] = (values * inverse * gains_ref[0:1, :]).astype(BF16)
+                both = jnp.zeros((rows, 2 * HD), F32)
+                for j in range(n):
+                    both += matmul(
+                        normed_ref[d, slot, :, column(chip ^ j, wide)], pieces[j][:wide, :]
+                    )
+                query, kv = both[:, :HD], both[:, HD:]
+                query_ref[d, slot] = (
+                    query * cos_ref[slot] + turn(query) * sin_ref[slot]
+                ).astype(BF16)
+                kv_ref[d, slot] = (kv * kvcos_ref[slot] + turn(kv) * kvsin_ref[slot]).astype(BF16)
+
+    head_shape = (n, 2, rows, HD)
+    tables = [t.reshape(2, rows, HD) for t in (cosine, sine, kv_cosine, kv_sine)]
+    normed, query_rot, own_kv, gains = run_whole(
+        project,
+        me,
+        token_own + token_near + weights_in + tables,
+        [
+            shape((n, 2, rows, width)),
+            shape(head_shape),
+            shape(head_shape),
+            shape((2, width), F32),
+        ],
+        flops=2 * plane_rows * width * 2 * HD,
+        name="project",
+    )
+
+    rightward, leftward = [own_kv], [own_kv]
+    for _ in range(planes - 1):
+        rightward.append(along(rightward[-1], 1))
+        leftward.append(along(leftward[-1], -1))
+    kv_mine = [own_kv] + [rightward[k] + leftward[planes - k] for k in range(1, planes)]
+    kv_near = [sibling(block) for block in kv_mine]
+
+    head_spec = pl.BlockSpec((1, 2, rows, HD), lambda i, me: (i, 0, 0, 0))
+    id_specs = [
+        pl.BlockSpec((1, pair, 1), lambda i, me: (i, 0, 0)),
+        pl.BlockSpec((1, planes, 1, pair), lambda i, me: (i, 0, 0, 0)),
+    ]
+
+    def scored(side, query, query_id, key_id, mine, near):
+        keys, values, scores = [], [], []
+        for k in range(planes):
+            a = mine[k][0].reshape(pair, HD)
+            b = near[k][0].reshape(pair, HD)
+            keys.append(jnp.where(side == 0, a, b))
+            values.append(jnp.where(side == 0, b, a))
+            score = matmul_nt(query, keys[k]) * scale
+            scores.append(jnp.where(key_id[0, k] <= query_id[0], score, masked_score))
+        top = functools.reduce(jnp.maximum, [jnp.max(s, axis=-1, keepdims=True) for s in scores])
+        raised = [jnp.exp(s - top) for s in scores]
+        inverse = 1.0 / sum(jnp.sum(r, axis=-1, keepdims=True) for r in raised)
+        return keys, values, [r * inverse for r in raised]
+
+    def spread(step, side, whole, own_refs, near_refs):
+        for d in range(n):
+
+            @pl.when(step == d)
+            def _():
+                own_refs[d][...] = whole[side]
+                near_refs[d][...] = whole[1 - side]
+
+    def attend(me_ref, query_ref, query_id, key_id, *refs):
+        mine, near, out_w = refs[:planes], refs[planes : 2 * planes], refs[2 * planes : 2 * planes + n]
+        attended_ref = refs[2 * planes + n]
+        own_refs = refs[2 * planes + n + 1 : 2 * planes + 2 * n + 1]
+        near_refs = refs[2 * planes + 2 * n + 1 : 2 * planes + 3 * n + 1]
+        whole = refs[-1]
+        chip, side = me_ref[0], me_ref[1]
+        query = query_ref[0].reshape(pair, HD)
+        _, values, probs = scored(side, query, query_id, key_id, mine, near)
+        total = jnp.zeros((pair, HD), F32)
+        for k in range(planes):
+            total += matmul(probs[k].astype(BF16), values[k])
+        attended = total.astype(BF16)
+        attended_ref[0] = attended.reshape(2, rows, HD)
+        for j in range(n):
+            whole[:, :, column(chip ^ j, wide)] = (
+                matmul(attended, out_w[j][...]).astype(BF16).reshape(2, rows, wide)
+            )
+        spread(pl.program_id(0), side, whole, own_refs, near_refs)
+
+    block = (rows, width)
+    attend_flops = 4 * plane_rows * planes * pair * HD + 2 * plane_rows * HD * width
+    attended, *partial = run_grid(
+        attend,
+        me,
+        (n,),
+        [query_rot, query_ids, key_ids] + kv_mine + kv_near + weights_out,
+        [head_spec] + id_specs + [head_spec] * (2 * planes) + [fixed((HD, wide))] * n,
+        [shape(head_shape)] + [shape(block)] * (2 * n),
+        [head_spec] + [pl.BlockSpec(block, lambda i, me: (0, 0))] * (2 * n),
+        scratch=[pltpu.VMEM((2, rows, width), BF16)],
+        flops=attend_flops,
+        name="attend",
+    )
+    middle_terms = reduced(partial[:n], partial[n:])
+
+    def second_norm(me_ref, token_ref, gains_ref, *refs):
+        terms, (middle_ref, normed_ref) = refs[:-2], refs[-2:]
+        middle = token_ref[...].astype(F32)
+        middle += sum(t[...].astype(F32) for t in terms)
+        inverse = lax.rsqrt(jnp.mean(middle * middle, axis=-1, keepdims=True) + epsilon)
+        middle_ref[...] = middle
+        normed_ref[...] = (middle * inverse * gains_ref[1:2, :]).astype(BF16)
+
+    middle, own_normed_two = run_whole(
+        second_norm,
+        me,
+        [own_tokens, gains] + middle_terms,
+        [shape(block, F32), shape(block)],
+        name="second_norm",
+    )
+    two_own, two_near = gathered(own_normed_two)
+
+    tile = plane_rows // 3
+
+    def feed_forward(me_ref, *refs):
+        pieces = refs[:n]
+        two_refs, cot_refs = refs[n : 3 * n], refs[3 * n : 5 * n]
+        hidden_ref, gate_ref, up_ref, dgate, dup, ddown = refs[5 * n : 5 * n + 6]
+        two, cot, turned, two_sem, cot_sem = refs[5 * n + 6 :]
+        chip = me_ref[0]
+        copies = []
+        for source, target, sems in ((two_refs, two, two_sem), (cot_refs, cot, cot_sem)):
+            for i in range(2 * n):
+                copies.append(
+                    pltpu.make_async_copy(
+                        source[i], target.at[pl.ds(i * rows, rows)], sems.at[i]
+                    )
+                )
+        for copy in copies:
+            copy.start()
+        for copy in copies:
+            copy.wait()
+
+        def forward(t, _):
+            here = pl.ds(pl.multiple_of(t * tile, tile), tile)
+            both = jnp.zeros((tile, 2 * quarter), F32)
+            hidden_grad = jnp.zeros((tile, quarter), F32)
+            for j in range(n):
+                both += matmul(two[here, column(chip ^ j, wide)], pieces[j][:wide, :])
+                hidden_grad += matmul_nt(cot[here, column(chip ^ j, wide)], pieces[j][wide:, :])
+            gate, up = both[:, :quarter], both[:, quarter:]
+            share = 1.0 / (1.0 + jnp.exp(-gate))
+            activated = gate * share
+            results = (
+                activated * up,
+                hidden_grad * up * share * (1.0 + gate * (1.0 - share)),
+                hidden_grad * activated,
+            )
+            for i, (result, ref) in enumerate(zip(results, (hidden_ref, gate_ref, up_ref))):
+                ref[here, :] = result.astype(BF16)
+                turned[i, :, here] = result.T.astype(BF16)
+            return 0
+
+        lax.fori_loop(0, plane_rows // tile, forward, 0)
+        for j in range(n):
+            here = column(chip ^ j, wide)
+            dgate[j] = matmul(turned[1], two[:, here]).astype(BF16)
+            dup[j] = matmul(turned[2], two[:, here]).astype(BF16)
+            ddown[j] = matmul(turned[0], cot[:, here]).astype(BF16)
+
+    grad_tile = (n, quarter, wide)
+    hiddens, gate_grads, up_grads, hidden_tiles = [], [], [], []
+    for q in range(QUARTERS):
+        hidden, gate_grad, up_grad, *tiles = run_whole(
+            feed_forward,
+            me,
+            feed[q] + two_own + two_near + cot_own + cot_near,
+            [shape((plane_rows, quarter))] * 3 + [shape(grad_tile)] * 3,
+            scratch=[
+                pltpu.VMEM((plane_rows, width), BF16),
+                pltpu.VMEM((plane_rows, width), BF16),
+                pltpu.VMEM((3, quarter, plane_rows), BF16),
+                pltpu.SemaphoreType.DMA((2 * n,)),
+                pltpu.SemaphoreType.DMA((2 * n,)),
+            ],
+            flops=12 * plane_rows * width * quarter,
+            in_hbm=4 * n,
+            name="feed_forward",
+        )
+        hiddens.append(hidden)
+        gate_grads.append(gate_grad)
+        up_grads.append(up_grad)
+        hidden_tiles.append(tiles)
+
+    pieces = [feed[q][j] for q in range(QUARTERS) for j in range(n)]
+    piece_specs = [fixed((wide + quarter, 2 * quarter))] * (QUARTERS * n)
+    pair_spec = pl.BlockSpec((2, 1, rows, quarter), lambda i, me: (0, i, 0, 0))
+    out_specs = [pl.BlockSpec(block, lambda i, me: (0, 0))] * (2 * n)
+
+    def put(step, results, own_refs, near_refs, chip):
+        for d in range(n):
+
+            @pl.when(step == d)
+            def _():
+                for j in range(n):
+                    here = column(chip ^ j, wide)
+                    own_refs[d][:, here] = results[j][:rows]
+                    near_refs[d][:, here] = results[j][rows:]
+
+    def feed_forward_back(me_ref, *refs):
+        gates, ups = refs[:QUARTERS], refs[QUARTERS : 2 * QUARTERS]
+        pieces = refs[2 * QUARTERS : 2 * QUARTERS + QUARTERS * n]
+        outs = refs[2 * QUARTERS + QUARTERS * n :]
+        lefts = [
+            jnp.concatenate(
+                [g[:, 0].reshape(pair, quarter), u[:, 0].reshape(pair, quarter)], axis=1
+            )
+            for g, u in zip(gates, ups)
+        ]
+        results = []
+        for j in range(n):
+            total = jnp.zeros((pair, wide), F32)
+            for q in range(QUARTERS):
+                total += matmul_nt(lefts[q], pieces[q * n + j][:wide, :])
+            results.append(total.astype(BF16))
+        put(pl.program_id(0), results, outs[:n], outs[n:], me_ref[0])
+
+    def by_block(value):
+        return value.reshape(2, n, rows, quarter)
+
+    back = run_grid(
+        feed_forward_back,
+        me,
+        (n,),
+        [by_block(g) for g in gate_grads] + [by_block(u) for u in up_grads] + pieces,
+        [pair_spec] * (2 * QUARTERS) + piece_specs,
+        [shape(block)] * (2 * n),
+        out_specs,
+        flops=4 * plane_rows * width * part,
+        name="feed_forward_back",
+    )
+    two_grad_terms = reduced(back[:n], back[n:])
+
+    def norm_back(values, inverse, gain, grad):
+        unit = values * inverse
+        scaled = grad * gain
+        return inverse * (scaled - unit * jnp.mean(scaled * unit, axis=-1, keepdims=True)), jnp.sum(
+            grad * unit, axis=0, keepdims=True
+        )
+
+    def second_norm_back(me_ref, middle_ref, cot_ref, gains_ref, *refs):
+        terms, (middle_grad_ref, branch_ref, gain_ref, flat) = refs[:-4], refs[-4:]
+        middle = middle_ref[...]
+        inverse = lax.rsqrt(jnp.mean(middle * middle, axis=-1, keepdims=True) + epsilon)
+        grad = sum(t[...].astype(F32) for t in terms)
+        back, gain_term = norm_back(middle, inverse, gains_ref[1:2, :], grad)
+        middle_grad = cot_ref[...].astype(F32) + back
+        middle_grad_ref[...] = middle_grad
+        branch_ref[...] = middle_grad.astype(BF16)
+        flat[...] = gain_term
+        for j in range(n):
+            gain_ref[j] = flat[:, column(me_ref[0] ^ j, wide)]
+
+    gain_shape = shape((n, 1, wide), F32)
+    middle_grad, branch_grad, gain_two_term = run_whole(
+        second_norm_back,
+        me,
+        [middle, own_cotangent, gains] + two_grad_terms,
+        [shape(block, F32), shape(block), gain_shape],
+        scratch=[pltpu.VMEM((1, width), F32)],
+        name="second_norm_back",
+    )
+    branch_own, branch_near = gathered(branch_grad)
+
+    def attend_back(me_ref, query_ref, query_id, key_id, cos_ref, sin_ref, *refs):
+        mine, near, out_w = refs[:planes], refs[planes : 2 * planes], refs[2 * planes : 2 * planes + n]
+        branch_refs = refs[2 * planes + n : 2 * planes + 3 * n]
+        query_grad_ref = refs[2 * planes + 3 * n]
+        keep_refs = refs[2 * planes + 3 * n + 1 : 3 * planes + 3 * n + 1]
+        send_refs = refs[3 * planes + 3 * n + 1 : 4 * planes + 3 * n + 1]
+        branch = refs[-1]
+        chip, side = me_ref[0], me_ref[1]
+        for d in range(n):
+
+            @pl.when(pl.program_id(0) == d)
+            def _():
+                branch[side] = branch_refs[d][...]
+                branch[1 - side] = branch_refs[n + d][...]
+
+        query = query_ref[0].reshape(pair, HD)
+        attended_grad = jnp.zeros((pair, HD), F32)
+        for j in range(n):
+            attended_grad += matmul_nt(
+                branch[:, :, column(chip ^ j, wide)].reshape(pair, wide), out_w[j][...]
+            )
+        attended_grad = attended_grad.astype(BF16)
+        keys, values, probs = scored(side, query, query_id, key_id, mine, near)
+        low = [p.astype(BF16) for p in probs]
+        shares = [matmul_nt(attended_grad, values[k]) for k in range(planes)]
+        delta = sum(
+            jnp.sum(low[k].astype(F32) * shares[k], axis=-1, keepdims=True) for k in range(planes)
+        )
+        query_grad = jnp.zeros((pair, HD), F32)
+        for k in range(planes):
+            score_grad = (probs[k] * (shares[k] - delta)).astype(BF16)
+            query_grad += matmul(score_grad, keys[k])
+            key_grad = matmul_tn(score_grad, query) * scale
+            value_grad = matmul_tn(low[k], attended_grad)
+            keep_refs[k][0] = jnp.where(side == 0, key_grad, value_grad).astype(BF16).reshape(
+                2, rows, HD
+            )
+            send_refs[k][0] = jnp.where(side == 0, value_grad, key_grad).astype(BF16).reshape(
+                2, rows, HD
+            )
+        query_grad = query_grad * scale
+        query_grad = query_grad * cos_ref[...] + turn_back(query_grad * sin_ref[...])
+        query_grad_ref[0] = query_grad.astype(BF16).reshape(2, rows, HD)
+
+    query_grad, *kv_grads = run_grid(
+        attend_back,
+        me,
+        (n,),
+        [query_rot, query_ids, key_ids, cosine, sine]
+        + kv_mine
+        + kv_near
+        + weights_out
+        + branch_own
+        + branch_near,
+        [head_spec]
+        + id_specs
+        + [fixed((pair, HD))] * 2
+        + [head_spec] * (2 * planes)
+        + [fixed((HD, wide))] * n
+        + [fixed(block)] * (2 * n),
+        [shape(head_shape)] * (1 + 2 * planes),
+        [head_spec] * (1 + 2 * planes),
+        scratch=[pltpu.VMEM((2, rows, width), BF16)],
+        flops=10 * plane_rows * planes * pair * HD + 2 * plane_rows * HD * width,
+        name="attend_back",
+    )
+    kept, handed = kv_grads[:planes], kv_grads[planes:]
+    kv_sums = [
+        (kept[k].astype(F32) + sibling(handed[k]).astype(F32)).astype(BF16) for k in range(planes)
+    ]
+    from_above = jnp.zeros_like(own_kv)
+    from_below = jnp.zeros_like(own_kv)
+    for k in range(planes - 1, 0, -1):
+        below = jnp.where(z >= k, kv_sums[k], 0).astype(F32) + from_above.astype(F32)
+        above = jnp.where(z + k < planes, kv_sums[planes - k], 0).astype(F32) + from_below.astype(F32)
+        from_above = along(below.astype(BF16), -1)
+        from_below = along(above.astype(BF16), 1)
+
+    def project_back(me_ref, *refs):
+        own_ref, above_ref, below_ref, query_grad_ref, kvcos_ref, kvsin_ref = refs[:6]
+        pieces = refs[6 : 6 + n]
+        kv_ref = refs[6 + n]
+        own_refs, near_refs = refs[7 + n : 7 + 2 * n], refs[7 + 2 * n : 7 + 3 * n]
+        chip, side = me_ref[0], me_ref[1]
+        for d in range(n):
+            for e in range(2):
+                slot = side ^ e
+                grad = own_ref[d, slot].astype(F32) + above_ref[d, slot].astype(F32)
+                grad = grad + below_ref[d, slot].astype(F32)
+                grad = grad * kvcos_ref[slot] + turn_back(grad * kvsin_ref[slot])
+                grad = grad.astype(BF16)
+                kv_ref[d, slot] = grad
+                left = jnp.concatenate([query_grad_ref[d, slot], grad], axis=1)
+                target = (own_refs, near_refs)[e][d]
+                for j in range(n):
+                    target[:, column(chip ^ j, wide)] = matmul_nt(left, pieces[j][:wide, :]).astype(
+                        BF16
+                    )
+
+    kv_grad, *partial = run_whole(
+        project_back,
+        me,
+        [kv_sums[0], from_above, from_below, query_grad] + tables[2:] + weights_in,
+        [shape(head_shape)] + [shape(block)] * (2 * n),
+        flops=4 * plane_rows * width * HD,
+        name="project_back",
+    )
+    one_grad_terms = reduced(partial[:n], partial[n:])
+
+    def first_norm_back(me_ref, token_ref, middle_grad_ref, gains_ref, *refs):
+        terms, (grad_ref, gain_ref, flat) = refs[:-3], refs[-3:]
+        values = token_ref[...].astype(F32)
+        inverse = lax.rsqrt(jnp.mean(values * values, axis=-1, keepdims=True) + epsilon)
+        grad = sum(t[...].astype(F32) for t in terms)
+        back, gain_term = norm_back(values, inverse, gains_ref[0:1, :], grad)
+        grad_ref[...] = middle_grad_ref[...] + back
+        flat[...] = gain_term
+        for j in range(n):
+            gain_ref[j] = flat[:, column(me_ref[0] ^ j, wide)]
+
+    tokens_grad, gain_one_term = run_whole(
+        first_norm_back,
+        me,
+        [own_tokens, middle_grad, gains] + one_grad_terms,
+        [shape(block, F32), gain_shape],
+        scratch=[pltpu.VMEM((1, width), F32)],
+        name="first_norm_back",
+    )
+    gain_terms = jnp.concatenate([gain_one_term, gain_two_term], axis=1)
+    gain_sum = gain_terms[0] + sum(across(gain_terms[d], d) for d in range(1, n))
+    gain_sum = gain_sum + sibling(gain_sum)
+    gain_sum = summed_over_planes(gain_sum)
+
+    def outer(me_ref, left_ref, right_ref, out_ref):
+        turned = left_ref[...].reshape(plane_rows, HD).astype(F32).T.astype(BF16)
+        for j in range(n):
+            right = right_ref[:, :, :, column(me_ref[0] ^ j, wide)].reshape(plane_rows, wide)
+            out_ref[j] = matmul(turned, right).astype(BF16)
+
+    def outer_branch(me_ref, left_ref, *refs):
+        branch_refs, (out_ref, right_ref, sems) = refs[: 2 * n], refs[2 * n :]
+        copies = []
+        for e in range(2):
+            for d in range(n):
+                copies.append(
+                    pltpu.make_async_copy(
+                        branch_refs[e * n + d],
+                        right_ref.at[d, me_ref[1] ^ e],
+                        sems.at[e * n + d],
+                    )
+                )
+        for copy in copies:
+            copy.start()
+        for copy in copies:
+            copy.wait()
+        outer(me_ref, left_ref, right_ref, out_ref)
+
+    outer_flops = 2 * plane_rows * width * HD
+    outer_tile = shape((n, HD, wide))
+    query_tile = run_whole(
+        outer, me, [query_grad, normed], outer_tile, flops=outer_flops, name="query_outer"
+    )
+    output_tile = run_whole(
+        outer_branch,
+        me,
+        [attended] + branch_own + branch_near,
+        outer_tile,
+        scratch=[pltpu.VMEM((n, 2, rows, width), BF16), pltpu.SemaphoreType.DMA((2 * n,))],
+        flops=outer_flops,
+        in_hbm=2 * n,
+        name="output_outer",
+    )
+    kv_tile = run_whole(outer, me, [kv_grad, normed], outer_tile, flops=outer_flops, name="kv_outer")
+
+    def deal(me_ref, *refs):
+        count = (len(refs) - n) // 2
+        sums, backs, outs = refs[:count], refs[count : 2 * count], refs[2 * count :]
+        outer_plane = me_ref[2] == 1
+
+        @pl.when(outer_plane)
+        def _():
+            for d in range(n):
+                for w in range(count):
+                    outs[d][w] = backs[w][d]
+
+        @pl.when(jnp.logical_not(outer_plane))
+        def _():
+            for d in range(n):
+                for w in range(count):
+                    outs[d][w] = sums[w][d]
+
+    is_outer = ((z == 0) | (z == planes - 1)).astype(jnp.int32)
+    me_and_plane = jnp.concatenate([me, is_outer[None]])
+
+    def owned(tiles):
+        ends = [summed_over_planes(t, last=False) for t in tiles]
+        dealt = run_whole(
+            deal,
+            me_and_plane,
+            [a for a, _ in ends] + [b for _, b in ends],
+            [shape((len(tiles),) + tiles[0].shape[1:])] * n,
+            name="deal",
+        )
+        own = [dealt[0]] + [across(dealt[d], d) for d in range(1, n)]
+        return own + [sibling(block) for block in own]
+
+    full = lambda count: [fixed((count, HD, wide))] * (2 * n)
+
+    def slot_of(q, count):
+        def where(i, me):
+            return (2 * (me[0] ^ (i % n)) + (me[1] ^ (i // n))) * count + q
+
+        return where
+
+    def place_hidden(me_ref, *refs):
+        tiles = refs[: 2 * n]
+        gate_out, up_out, down_out = refs[-3:]
+        for i in range(2 * n):
+
+            @pl.when(pl.program_id(0) == i)
+            def _():
+                gate_out[...] = tiles[i][0].astype(F32).T
+                up_out[...] = tiles[i][1].astype(F32).T
+                down_out[...] = tiles[i][2].astype(F32)
+
+    hidden_outs = [
+        shape(gate_weight.shape, F32),
+        shape(up_weight.shape, F32),
+        shape(down_weight.shape, F32),
+    ]
+    held = None
+    for q in range(QUARTERS):
+        tiles = owned(hidden_tiles[q])
+        where = slot_of(q, QUARTERS)
+        by_columns = pl.BlockSpec((wide, quarter), lambda i, me, w=where: (0, w(i, me)))
+        by_rows = pl.BlockSpec((quarter, wide), lambda i, me, w=where: (w(i, me), 0))
+        rest = [] if held is None else list(held)
+        held = run_grid(
+            place_hidden,
+            me,
+            (2 * n,),
+            tiles + rest,
+            [fixed((3, quarter, wide))] * (2 * n) + [pl.BlockSpec(memory_space=pl.ANY)] * len(rest),
+            hidden_outs,
+            [by_columns, by_columns, by_rows],
+            aliases={1 + 2 * n + i: i for i in range(len(rest))},
+            name="place_hidden",
+        )
+
+    def place_query(me_ref, *refs):
+        tiles, (query_out, output_out) = refs[: 2 * n], refs[2 * n :]
+        for i in range(2 * n):
+
+            @pl.when(pl.program_id(0) == i)
+            def _():
+                query_out[...] = tiles[i][0].astype(F32).T
+                output_out[...] = tiles[i][1].astype(F32)
+
+    where = slot_of(0, 1)
+    query_weight_grad, output_weight_grad = run_grid(
+        place_query,
+        me,
+        (2 * n,),
+        owned([query_tile, output_tile]),
+        [fixed((2, HD, wide))] * (2 * n),
+        [shape(query_weight.shape, F32), shape(output_weight.shape, F32)],
+        [
+            pl.BlockSpec((wide, HD), lambda i, me: (0, where(i, me))),
+            pl.BlockSpec((HD, wide), lambda i, me: (where(i, me), 0)),
+        ],
+        name="place_query",
+    )
+
+    def place_kv(me_ref, *refs):
+        tiles, (key_out, value_out) = refs[: 2 * n], refs[2 * n :]
+        keys_here = me_ref[1] == 0
+        for d in range(n):
+
+            @pl.when(pl.program_id(0) == d)
+            def _():
+                own, near = tiles[d][0].astype(F32).T, tiles[n + d][0].astype(F32).T
+                key_out[...] = jnp.where(keys_here, own, near)
+                value_out[...] = jnp.where(keys_here, near, own)
+
+    by_chip = pl.BlockSpec((wide, HD), lambda i, me: (0, me[0] ^ i))
+    key_weight_grad, value_weight_grad = run_grid(
+        place_kv,
+        me,
+        (n,),
+        owned([kv_tile]),
+        [fixed((1, HD, wide))] * (2 * n),
+        [shape(key_weight.shape, F32), shape(value_weight.shape, F32)],
+        [by_chip, by_chip],
+        name="place_kv",
+    )
+
+    def feed_forward_out(me_ref, *refs):
+        hiddens = refs[:QUARTERS]
+        pieces = refs[QUARTERS : QUARTERS + QUARTERS * n]
+        outs = refs[QUARTERS + QUARTERS * n :]
+        results = []
+        for j in range(n):
+            total = jnp.zeros((pair, wide), F32)
+            for q in range(QUARTERS):
+                total += matmul(hiddens[q][:, 0].reshape(pair, quarter), pieces[q * n + j][wide:, :])
+            results.append(total.astype(BF16))
+        put(pl.program_id(0), results, outs[:n], outs[n:], me_ref[0])
+
+    partial = run_grid(
+        feed_forward_out,
+        me,
+        (n,),
+        [by_block(h) for h in hiddens] + pieces,
+        [pair_spec] * QUARTERS + piece_specs,
+        [shape(block)] * (2 * n),
+        out_specs,
+        flops=2 * plane_rows * width * part,
+        name="feed_forward_out",
+    )
+    output = middle + sum(t.astype(F32) for t in reduced(partial[:n], partial[n:]))
+
+    return (
+        output.astype(BF16)[None],
+        tokens_grad[None],
+        query_weight_grad,
+        key_weight_grad,
+        value_weight_grad,
+        output_weight_grad,
+        gain_sum[0],
+        held[0],
+        held[1],
+        held[2],
+        gain_sum[1],
+    )
+
+
 def solution(mesh):
+    chips, pieces = mesh.shape["fsdp"], mesh.shape["ctx"]
+    one_head_each = 2 * chips == H and chips == KVH and pieces % 4 == 0 and pieces > 4
     return jax.shard_map(
-        shards,
+        plane_layer if one_head_each else ring_layer,
         mesh=mesh,
         in_specs=(
             P("fsdp", "ctx", None),

time: 3370 us -> 1700 us (0.50)
  waiting for transfers between devices: 2670 us -> 1080 us
  Pallas kernels: 0 us -> 309 us
  matrix products: 261 us -> 0 us
  starting transfers between devices: 2.05 us -> 209 us
  local copies, waits for them, and re-layouts: 187 us -> 23.1 us
  other arithmetic: 157 us -> 61 us
  blocking collectives: 59.3 us -> 0 us
    unnamed x10 -> x0, waiting for transfers between devices: 1040 us -> none
    all_gather x7 -> x0, waiting for transfers between devices: 955 us -> none  [the longest x1 279 us: shards(): lax.all_gather(down_weight, 'fsdp', axis=1, tiled=True)]
    ppermute x22 -> x188, waiting for transfers between devices: 147 us -> 1080 us  [the longest x48 642 us: between_planes(): lax.ppermute(value, 'ctx', [(2 * a + side, 2 * b + side) for a, b in move...]
    psum x1 -> x0, waiting for transfers between devices: 535 us -> none  [shards(): shard = lax.psum(piece, 'ctx').astype(jnp.float32)]
    pallas_call x0 -> x33, Pallas kernels: none -> 309 us  [the longest x18 159 us: run_whole(): pl.pallas_call(body, out_shape=outs, in_specs=[pl.BlockSpec(memory_space=...]
    dot_general x73 -> x0, matrix products: 261 us -> none  [the longest x4 58.7 us: weight_terms(): jnp.einsum('tc,tn->cn', column, rights[index], preferred_element_type=jnp...]
    ppermute x22 -> x188, starting transfers between devices: 1.71 us -> 209 us  [the longest x48 97.5 us: between_planes(): lax.ppermute(value, 'ctx', [(2 * a + side, 2 * b + side) for a, b in move...]
    concatenate x3 -> x4, other arithmetic: 83.2 us -> 0.69 us  [the longest x1 0.6 us: plane_layer(): me_and_plane = jnp.concatenate([me, is_outer[None]])]
  transfers between devices with their start and end apart: 31 -> 188, of which waited for: 29 -> 64; matrix products, arithmetic and copies ran while one was open for 8% -> 4% of each run, Pallas kernels for 0% -> 14%
where the time goes in v1:
time: 1700 us; the launch traced here: 1690 us
  waiting for transfers between devices  1080 us (64%)
  Pallas kernels  309 us (18%)
  starting transfers between devices  209 us (12%)
  other arithmetic  61 us (4%)
  local copies, waits for them, and re-layouts  23.1 us (1%)
    ppermute x48, waiting for transfers between devices, between_planes(): lax.ppermute(value, 'ctx', [(2 * a + side, 2 * b + side) for a, b in move...  642 us
    ppermute x63, waiting for transfers between devices, across(): return lax.ppermute(value, 'fsdp', [(i, i ^ d) for i in range(n)])  395 us
    pallas_call x18, Pallas kernels, run_whole(): pl.pallas_call(body, out_shape=outs, in_specs=[pl.BlockSpec(memory_space=...  159 us
    pallas_call x15, Pallas kernels, run_grid(): pl.pallas_call(body, out_shape=outs, grid_spec=pltpu.PrefetchScalarGridSp...  150 us
    ppermute x48, starting transfers between devices, between_planes(): lax.ppermute(value, 'ctx', [(2 * a + side, 2 * b + side) for a, b in move...  97.5 us
    ppermute x63, starting transfers between devices, across(): return lax.ppermute(value, 'fsdp', [(i, i ^ d) for i in range(n)])  68.8 us
    ppermute x12, waiting for transfers between devices, along(): lax.ppermute(value, 'ctx', [(a, b) for a, b in pairs if 0 <= b < ctx_count])  41.1 us
  transfers between devices with their start and end apart: 188, of which 64 were waited for; matrix products, arithmetic and copies ran while one was open for 4% of the time, Pallas kernels for 14%

profile of v1, /device:TPU:0, one launch (start us, length us, event | category | flops | bytes accessed | tf_op | source)
XLA Modules:
  0.0 1687.9 jit_solution(8472857469226947433)
XLA Ops:
  16.7 34.5 %collective-permute-done.7.refs_9_.refs_7_ = bf16[528,512]{1,0:T(8,128)(2,1)} collective-permute-done((bf16[528,512]{1,0:T(8,128)(2,1)}, bf16[528,512]{1,0:T(8,128)(2,1)}, u32[]{:S(2)}, u32[]{:S(2)}) %collective-permute-start.7) | collective-permute-done | bytes 540704 | tf_op jit(solution)/shard_map/ppermute | solution.py:433
  219.3 30.6 %collective-permute-done.27.refs_3_ = bf16[192,2048]{1,0:T(8,128)(2,1)S(1)} collective-permute-done((bf16[192,2048]{1,0:T(8,128)(2,1)S(1)}, bf16[192,2048]{1,0:T(8,128)(2,1)S(1)}, u32[]{:S(2)}, u32[]{:S(2)}) %collective-permute-start.27) | collective-permute-done | bytes 786464 | tf_op jit(solution)/shard_map/ppermute | solution.py:433
  336.2 19.1 %feed_forward.7 = (bf16[1536,256]{1,0:T(8,128)(2,1)}, bf16[1536,256]{1,0:T(8,128)(2,1)}, bf16[1536,256]{1,0:T(8,128)(2,1)}, bf16[4,256,512]{2,1,0:T(8,128)(2,1)}...) custom-call(s32[2]{0:T(128)} %pad_add_fusion.me_ref, ...), custom_call_target="tpu_custom_call" | custom-call | flops 9663676416 | bytes 21233664 | tf_op jit(solution)/shard_map/feed_forward/pallas_call | solution.py:347
  369.6 33.7 %collective-permute-done.51.refs_2_.refs_14_.refs_18_ = bf16[768,512]{1,0:T(8,128)(2,1)S(1)} collective-permute-done((bf16[768,512]{1,0:T(8,128)(2,1)}, bf16[768,512]{1,0:T(8,128)(2,1)S(1)}, u32[]{:S(2)}, u32[]{:S(2)}) %collective-permute-start.51) | collective-permute-done | bytes 786464 | tf_op jit(solution)/shard_map/ppermute | solution.py:433
  404.5 18.8 %feed_forward.6 = (bf16[1536,256]{1,0:T(8,128)(2,1)}, bf16[1536,256]{1,0:T(8,128)(2,1)}, bf16[1536,256]{1,0:T(8,128)(2,1)}, bf16[4,256,512]{2,1,0:T(8,128)(2,1)}...) custom-call(s32[2]{0:T(128)} %pad_add_fusion.me_ref, ...), custom_call_target="tpu_custom_call" | custom-call | flops 9663676416 | bytes 21233664 | tf_op jit(solution)/shard_map/feed_forward/pallas_call | solution.py:347
  426.9 19.2 %feed_forward.5 = (bf16[1536,256]{1,0:T(8,128)(2,1)}, bf16[1536,256]{1,0:T(8,128)(2,1)}, bf16[1536,256]{1,0:T(8,128)(2,1)}, bf16[4,256,512]{2,1,0:T(8,128)(2,1)}...) custom-call(s32[2]{0:T(128)} %pad_add_fusion.me_ref, ...), custom_call_target="tpu_custom_call" | custom-call | flops 9663676416 | bytes 21233664 | tf_op jit(solution)/shard_map/feed_forward/pallas_call | solution.py:347
  447.4 19.0 %feed_forward.4 = (bf16[1536,256]{1,0:T(8,128)(2,1)}, bf16[1536,256]{1,0:T(8,128)(2,1)}, bf16[1536,256]{1,0:T(8,128)(2,1)}, bf16[4,256,512]{2,1,0:T(8,128)(2,1)}...) custom-call(s32[2]{0:T(128)} %pad_add_fusion.me_ref, ...), custom_call_target="tpu_custom_call" | custom-call | flops 9663676416 | bytes 21233664 | tf_op jit(solution)/shard_map/feed_forward/pallas_call | solution.py:347
  466.4 23.3 %feed_forward_back.1 = (bf16[192,2048]{1,0:T(8,128)(2,1)}, bf16[192,2048]{1,0:T(8,128)(2,1)}, bf16[192,2048]{1,0:T(8,128)(2,1)}, bf16[192,2048]{1,0:T(8,128)(2,1...) custom-call(s32[2]{0:T(128)} %pad_add_fusion.me_ref, ...), custom_call_target="tpu_custom_call" | custom-call | flops 12884901888 | bytes 25165824 | tf_op jit(solution)/shard_map/feed_forward_back/pallas_call | solution.py:362
  607.8 18.0 %collective-permute-done.142 = bf16[4,256,512]{2,1,0:T(8,128)(2,1)S(1)} collective-permute-done((bf16[4,256,512]{2,1,0:T(8,128)(2,1)S(1)}, bf16[4,256,512]{2,1,0:T(8,128)(2,1)S(1)}, u32[]{:S(2)}, u32[]{:S(2)}) %collective-permute-start.142) | collective-permute-done | bytes 1048608 | tf_op jit(solution)/shard_map/ppermute | solution.py:443
  693.3 22.4 %collective-permute-done.160 = bf16[4,256,512]{2,1,0:T(8,128)(2,1)S(1)} collective-permute-done((bf16[4,256,512]{2,1,0:T(8,128)(2,1)S(1)}, bf16[4,256,512]{2,1,0:T(8,128)(2,1)S(1)}, u32[]{:S(2)}, u32[]{:S(2)}) %collective-permute-start.160) | collective-permute-done | bytes 1048608 | tf_op jit(solution)/shard_map/ppermute | solution.py:443
  716.5 21.6 %collective-permute-done.172 = bf16[4,256,512]{2,1,0:T(8,128)(2,1)S(1)} collective-permute-done((bf16[4,256,512]{2,1,0:T(8,128)(2,1)S(1)}, bf16[4,256,512]{2,1,0:T(8,128)(2,1)S(1)}, u32[]{:S(2)}, u32[]{:S(2)}) %collective-permute-start.172) | collective-permute-done | bytes 1048608 | tf_op jit(solution)/shard_map/ppermute | solution.py:443
  738.7 21.9 %collective-permute-done.174 = bf16[4,256,512]{2,1,0:T(8,128)(2,1)S(1)} collective-permute-done((bf16[4,256,512]{2,1,0:T(8,128)(2,1)S(1)}, bf16[4,256,512]{2,1,0:T(8,128)(2,1)S(1)}, u32[]{:S(2)}, u32[]{:S(2)}) %collective-permute-start.174) | collective-permute-done | bytes 1048608 | tf_op jit(solution)/shard_map/ppermute | solution.py:443
  761.6 21.0 %collective-permute-done.176 = bf16[4,256,512]{2,1,0:T(8,128)(2,1)S(1)} collective-permute-done((bf16[4,256,512]{2,1,0:T(8,128)(2,1)S(1)}, bf16[4,256,512]{2,1,0:T(8,128)(2,1)S(1)}, u32[]{:S(2)}, u32[]{:S(2)}) %collective-permute-start.176) | collective-permute-done | bytes 1048608 | tf_op jit(solution)/shard_map/ppermute | solution.py:443
  787.5 31.1 %collective-permute-done.60 = bf16[192,2048]{1,0:T(8,128)(2,1)S(1)} collective-permute-done((bf16[192,2048]{1,0:T(8,128)(2,1)S(1)}, bf16[192,2048]{1,0:T(8,128)(2,1)S(1)}, u32[]{:S(2)}, u32[]{:S(2)}) %collective-permute-start.60) | collective-permute-done | bytes 786464 | tf_op jit(solution)/shard_map/ppermute | solution.py:433
  885.1 200.4 %collective-permute-done.130.refs_3_ = bf16[4,256,512]{2,1,0:T(8,128)(2,1)S(1)} collective-permute-done((bf16[4,256,512]{2,1,0:T(8,128)(2,1)S(1)}, bf16[4,256,512]{2,1,0:T(8,128)(2,1)S(1)}, u32[]{:S(2)}, u32[]{:S(2)}) %collective-permute-start.130) | collective-permute-done | bytes 1048608 | tf_op jit(solution)/shard_map/ppermute | solution.py:443
  1086.8 21.2 %collective-permute-done.131.refs_4_ = bf16[4,256,512]{2,1,0:T(8,128)(2,1)S(1)} collective-permute-done((bf16[4,256,512]{2,1,0:T(8,128)(2,1)S(1)}, bf16[4,256,512]{2,1,0:T(8,128)(2,1)S(1)}, u32[]{:S(2)}, u32[]{:S(2)}) %collective-permute-start.131) | collective-permute-done | bytes 1048608 | tf_op jit(solution)/shard_map/ppermute | solution.py:443
  1131.7 21.2 %collective-permute-done.146.refs_3_ = bf16[4,256,512]{2,1,0:T(8,128)(2,1)S(1)} collective-permute-done((bf16[4,256,512]{2,1,0:T(8,128)(2,1)S(1)}, bf16[4,256,512]{2,1,0:T(8,128)(2,1)S(1)}, u32[]{:S(2)}, u32[]{:S(2)}) %collective-permute-start.146) | collective-permute-done | bytes 1048608 | tf_op jit(solution)/shard_map/ppermute | solution.py:443
  1155.9 19.6 %collective-permute-done.147.refs_4_ = bf16[4,256,512]{2,1,0:T(8,128)(2,1)} collective-permute-done((bf16[4,256,512]{2,1,0:T(8,128)(2,1)S(1)}, bf16[4,256,512]{2,1,0:T(8,128)(2,1)}, u32[]{:S(2)}, u32[]{:S(2)}) %collective-permute-start.147) | collective-permute-done | bytes 1048608 | tf_op jit(solution)/shard_map/ppermute | solution.py:443
  1177.4 20.6 %collective-permute-done.148.refs_5_ = bf16[4,256,512]{2,1,0:T(8,128)(2,1)} collective-permute-done((bf16[4,256,512]{2,1,0:T(8,128)(2,1)}, bf16[4,256,512]{2,1,0:T(8,128)(2,1)}, u32[]{:S(2)}, u32[]{:S(2)}) %collective-permute-start.148) | collective-permute-done | bytes 1048608 | tf_op jit(solution)/shard_map/ppermute | solution.py:443
  1198.0 22.5 %collective-permute-done.162.refs_3_ = bf16[4,256,512]{2,1,0:T(8,128)(2,1)} collective-permute-done((bf16[4,256,512]{2,1,0:T(8,128)(2,1)S(1)}, bf16[4,256,512]{2,1,0:T(8,128)(2,1)}, u32[]{:S(2)}, u32[]{:S(2)}) %collective-permute-start.162) | collective-permute-done | bytes 1048608 | tf_op jit(solution)/shard_map/ppermute | solution.py:443
  1223.9 19.0 %collective-permute-done.163.refs_4_ = bf16[4,256,512]{2,1,0:T(8,128)(2,1)} collective-permute-done((bf16[4,256,512]{2,1,0:T(8,128)(2,1)S(1)}, bf16[4,256,512]{2,1,0:T(8,128)(2,1)}, u32[]{:S(2)}, u32[]{:S(2)}) %collective-permute-start.163) | collective-permute-done | bytes 1048608 | tf_op jit(solution)/shard_map/ppermute | solution.py:443
  1244.2 21.2 %collective-permute-done.164.refs_5_ = bf16[4,256,512]{2,1,0:T(8,128)(2,1)} collective-permute-done((bf16[4,256,512]{2,1,0:T(8,128)(2,1)}, bf16[4,256,512]{2,1,0:T(8,128)(2,1)}, u32[]{:S(2)}, u32[]{:S(2)}) %collective-permute-start.164) | collective-permute-done | bytes 1048608 | tf_op jit(solution)/shard_map/ppermute | solution.py:443
  1277.8 20.2 %attend_back.1 = (bf16[4,2,192,256]{3,2,1,0:T(8,128)(2,1)}, bf16[4,2,192,256]{3,2,1,0:T(8,128)(2,1)}, bf16[4,2,192,256]{3,2,1,0:T(8,128)(2,1)}, bf16[4,2,192,256...) custom-call(s32[2]{0:T(128)} %pad_add_fusion.me_ref, ...), custom_call_target="tpu_custom_call" | custom-call | flops 7650410496 | bytes 22312960 | tf_op jit(solution)/shard_map/attend_back/pallas_call | solution.py:362
  1310.2 20.2 %collective-permute-done.180.refs_5_ = bf16[4,256,512]{2,1,0:T(8,128)(2,1)} collective-permute-done((bf16[4,256,512]{2,1,0:T(8,128)(2,1)S(1)}, bf16[4,256,512]{2,1,0:T(8,128)(2,1)}, u32[]{:S(2)}, u32[]{:S(2)}) %collective-permute-start.180) | collective-permute-done | bytes 1048608 | tf_op jit(solution)/shard_map/ppermute | solution.py:443
  (787 shorter events, 963.8 us)
Async XLA Ops:
  330.6 92.7 %collective-permute-start.47 = (bf16[768,512]{1,0:T(8,128)(2,1)}, bf16[768,512]{1,0:T(8,128)(2,1)S(1)}, u32[]{:S(2)}, u32[]{:S(2)}) collective-permute-start(bf16[768,512]{1,0:T(8,128)(2,1)} %get-tuple-element.180), channel_id=1, source_target_pairs={{0,1},{1,0},{2,3},{3,2},{4,5},{5,4},{6,7},{7,6},{8,9},{9,8},{10,11... | collective-permute-start | bytes 2359304 | tf_op jit(solution)/shard_map/ppermute | solution.py:433
  332.2 93.6 %collective-permute-start.48 = (bf16[768,512]{1,0:T(8,128)(2,1)}, bf16[768,512]{1,0:T(8,128)(2,1)S(1)}, u32[]{:S(2)}, u32[]{:S(2)}) collective-permute-start(bf16[768,512]{1,0:T(8,128)(2,1)} %get-tuple-element.181), channel_id=1, source_target_pairs={{0,2},{1,3},{2,0},{3,1},{4,6},{5,7},{6,4},{7,5},{8,10},{9,11},{10,... | collective-permute-start | bytes 2359304 | tf_op jit(solution)/shard_map/ppermute | solution.py:433
  333.2 70.1 %collective-permute-start.51 = (bf16[768,512]{1,0:T(8,128)(2,1)}, bf16[768,512]{1,0:T(8,128)(2,1)S(1)}, u32[]{:S(2)}, u32[]{:S(2)}) collective-permute-start(bf16[768,512]{1,0:T(8,128)(2,1)} %get-tuple-element.186), channel_id=1, source_target_pairs={{0,2},{1,3},{2,0},{3,1},{4,6},{5,7},{6,4},{7,5},{8,10},{9,11},{10,... | collective-permute-start | bytes 2359304 | tf_op jit(solution)/shard_map/ppermute | solution.py:433
  518.0 85.3 %collective-permute-start.140 = (bf16[4,256,512]{2,1,0:T(8,128)(2,1)S(1)}, bf16[4,256,512]{2,1,0:T(8,128)(2,1)S(1)}, u32[]{:S(2)}, u32[]{:S(2)}) collective-permute-start(bf16[4,256,512]{2,1,0:T(8,128)(2,1)S(1)} %copy-done.46), channel_id=1, source_target_pairs={{0,8},{4,12},{24,16},{28,20},{1,9},{5,13},{25,17},{29,21},{2,10},{... | collective-permute-start | bytes 3145736 | tf_op jit(solution)/shard_map/ppermute | solution.py:443
  519.4 106.4 %collective-permute-start.142 = (bf16[4,256,512]{2,1,0:T(8,128)(2,1)S(1)}, bf16[4,256,512]{2,1,0:T(8,128)(2,1)S(1)}, u32[]{:S(2)}, u32[]{:S(2)}) collective-permute-start(bf16[4,256,512]{2,1,0:T(8,128)(2,1)S(1)} %copy-done.42), channel_id=1, source_target_pairs={{0,8},{4,12},{24,16},{28,20},{1,9},{5,13},{25,17},{29,21},{2,10},{... | collective-permute-start | bytes 3145736 | tf_op jit(solution)/shard_map/ppermute | solution.py:443
  535.9 112.4 %collective-permute-start.144 = (bf16[4,256,512]{2,1,0:T(8,128)(2,1)S(1)}, bf16[4,256,512]{2,1,0:T(8,128)(2,1)S(1)}, u32[]{:S(2)}, u32[]{:S(2)}) collective-permute-start(bf16[4,256,512]{2,1,0:T(8,128)(2,1)S(1)} %copy-done.40), channel_id=1, source_target_pairs={{0,8},{4,12},{24,16},{28,20},{1,9},{5,13},{25,17},{29,21},{2,10},{... | collective-permute-start | bytes 3145736 | tf_op jit(solution)/shard_map/ppermute | solution.py:443
  558.4 112.4 %collective-permute-start.156 = (bf16[4,256,512]{2,1,0:T(8,128)(2,1)S(1)}, bf16[4,256,512]{2,1,0:T(8,128)(2,1)S(1)}, u32[]{:S(2)}, u32[]{:S(2)}) collective-permute-start(bf16[4,256,512]{2,1,0:T(8,128)(2,1)S(1)} %copy-done.45), channel_id=1, source_target_pairs={{0,8},{4,12},{24,16},{28,20},{1,9},{5,13},{25,17},{29,21},{2,10},{... | collective-permute-start | bytes 3145736 | tf_op jit(solution)/shard_map/ppermute | solution.py:443
  580.8 112.4 %collective-permute-start.158 = (bf16[4,256,512]{2,1,0:T(8,128)(2,1)S(1)}, bf16[4,256,512]{2,1,0:T(8,128)(2,1)S(1)}, u32[]{:S(2)}, u32[]{:S(2)}) collective-permute-start(bf16[4,256,512]{2,1,0:T(8,128)(2,1)S(1)} %copy-done.41), channel_id=1, source_target_pairs={{0,8},{4,12},{24,16},{28,20},{1,9},{5,13},{25,17},{29,21},{2,10},{... | collective-permute-start | bytes 3145736 | tf_op jit(solution)/shard_map/ppermute | solution.py:443
  603.3 112.4 %collective-permute-start.160 = (bf16[4,256,512]{2,1,0:T(8,128)(2,1)S(1)}, bf16[4,256,512]{2,1,0:T(8,128)(2,1)S(1)}, u32[]{:S(2)}, u32[]{:S(2)}) collective-permute-start(bf16[4,256,512]{2,1,0:T(8,128)(2,1)S(1)} %copy-done.37), channel_id=1, source_target_pairs={{0,8},{4,12},{24,16},{28,20},{1,9},{5,13},{25,17},{29,21},{2,10},{... | collective-permute-start | bytes 3145736 | tf_op jit(solution)/shard_map/ppermute | solution.py:443
  625.8 112.4 %collective-permute-start.172 = (bf16[4,256,512]{2,1,0:T(8,128)(2,1)S(1)}, bf16[4,256,512]{2,1,0:T(8,128)(2,1)S(1)}, u32[]{:S(2)}, u32[]{:S(2)}) collective-permute-start(bf16[4,256,512]{2,1,0:T(8,128)(2,1)S(1)} %copy-done.39), channel_id=1, source_target_pairs={{0,8},{4,12},{24,16},{28,20},{1,9},{5,13},{25,17},{29,21},{2,10},{... | collective-permute-start | bytes 3145736 | tf_op jit(solution)/shard_map/ppermute | solution.py:443
  648.2 112.4 %collective-permute-start.174 = (bf16[4,256,512]{2,1,0:T(8,128)(2,1)S(1)}, bf16[4,256,512]{2,1,0:T(8,128)(2,1)S(1)}, u32[]{:S(2)}, u32[]{:S(2)}) collective-permute-start(bf16[4,256,512]{2,1,0:T(8,128)(2,1)S(1)} %copy-done.38), channel_id=1, source_target_pairs={{0,8},{4,12},{24,16},{28,20},{1,9},{5,13},{25,17},{29,21},{2,10},{... | collective-permute-start | bytes 3145736 | tf_op jit(solution)/shard_map/ppermute | solution.py:443
  670.7 111.9 %collective-permute-start.176 = (bf16[4,256,512]{2,1,0:T(8,128)(2,1)S(1)}, bf16[4,256,512]{2,1,0:T(8,128)(2,1)S(1)}, u32[]{:S(2)}, u32[]{:S(2)}) collective-permute-start(bf16[4,256,512]{2,1,0:T(8,128)(2,1)S(1)} %copy-done.36), channel_id=1, source_target_pairs={{0,8},{4,12},{24,16},{28,20},{1,9},{5,13},{25,17},{29,21},{2,10},{... | collective-permute-start | bytes 3145736 | tf_op jit(solution)/shard_map/ppermute | solution.py:443
  693.2 90.3 %collective-permute-start.65 = (bf16[192,2048]{1,0:T(8,128)(2,1)S(1)}, bf16[192,2048]{1,0:T(8,128)(2,1)S(1)}, u32[]{:S(2)}, u32[]{:S(2)}) collective-permute-start(bf16[192,2048]{1,0:T(8,128)(2,1)S(1)} %add_convert_fusion.43), channel_id=1, source_target_pairs={{0,1},{1,0},{2,3},{3,2},{4,5},{5,4},{6,7},{7,6},{8,9},{9,8},{10,11... | collective-permute-start | bytes 2359304 | tf_op jit(solution)/shard_map/ppermute | solution.py:433
  847.7 237.8 %collective-permute-start.130 = (bf16[4,256,512]{2,1,0:T(8,128)(2,1)S(1)}, bf16[4,256,512]{2,1,0:T(8,128)(2,1)S(1)}, u32[]{:S(2)}, u32[]{:S(2)}) collective-permute-start(bf16[4,256,512]{2,1,0:T(8,128)(2,1)S(1)} %add_convert_fusion.22.refs_0_), channel_id=1, source_target_pairs={{8,0},{12,4},{16,24},{20,28},{9,1},{13,5},{17,25},{21,29},{10,2},{... | collective-permute-start | bytes 3145736 | tf_op jit(solution)/shard_map/ppermute | solution.py:443
  849.0 258.9 %collective-permute-start.131 = (bf16[4,256,512]{2,1,0:T(8,128)(2,1)S(1)}, bf16[4,256,512]{2,1,0:T(8,128)(2,1)S(1)}, u32[]{:S(2)}, u32[]{:S(2)}) collective-permute-start(bf16[4,256,512]{2,1,0:T(8,128)(2,1)S(1)} %add_convert_fusion.20.refs_1_), channel_id=1, source_target_pairs={{8,0},{12,4},{16,24},{20,28},{9,1},{13,5},{17,25},{21,29},{10,2},{... | collective-permute-start | bytes 3145736 | tf_op jit(solution)/shard_map/ppermute | solution.py:443
  865.1 265.3 %collective-permute-start.132 = (bf16[4,256,512]{2,1,0:T(8,128)(2,1)S(1)}, bf16[4,256,512]{2,1,0:T(8,128)(2,1)S(1)}, u32[]{:S(2)}, u32[]{:S(2)}) collective-permute-start(bf16[4,256,512]{2,1,0:T(8,128)(2,1)S(1)} %add_convert_fusion.18.refs_2_), channel_id=1, source_target_pairs={{8,0},{12,4},{16,24},{20,28},{9,1},{13,5},{17,25},{21,29},{10,2},{... | collective-permute-start | bytes 3145736 | tf_op jit(solution)/shard_map/ppermute | solution.py:443
  880.8 272.1 %collective-permute-start.146 = (bf16[4,256,512]{2,1,0:T(8,128)(2,1)S(1)}, bf16[4,256,512]{2,1,0:T(8,128)(2,1)S(1)}, u32[]{:S(2)}, u32[]{:S(2)}) collective-permute-start(bf16[4,256,512]{2,1,0:T(8,128)(2,1)S(1)} %add_convert_fusion.16.refs_0_), channel_id=1, source_target_pairs={{8,0},{12,4},{16,24},{20,28},{9,1},{13,5},{17,25},{21,29},{10,2},{... | collective-permute-start | bytes 3145736 | tf_op jit(solution)/shard_map/ppermute | solution.py:443
  883.5 292.0 %collective-permute-start.147 = (bf16[4,256,512]{2,1,0:T(8,128)(2,1)S(1)}, bf16[4,256,512]{2,1,0:T(8,128)(2,1)}, u32[]{:S(2)}, u32[]{:S(2)}) collective-permute-start(bf16[4,256,512]{2,1,0:T(8,128)(2,1)S(1)} %add_convert_fusion.14.refs_1_), channel_id=1, source_target_pairs={{8,0},{12,4},{16,24},{20,28},{9,1},{13,5},{17,25},{21,29},{10,2},{... | collective-permute-start | bytes 3145736 | tf_op jit(solution)/shard_map/ppermute | solution.py:443
  1085.5 112.5 %collective-permute-start.148 = (bf16[4,256,512]{2,1,0:T(8,128)(2,1)}, bf16[4,256,512]{2,1,0:T(8,128)(2,1)}, u32[]{:S(2)}, u32[]{:S(2)}) collective-permute-start(bf16[4,256,512]{2,1,0:T(8,128)(2,1)} %add_convert_fusion.12.refs_2_), channel_id=1, source_target_pairs={{8,0},{12,4},{16,24},{20,28},{9,1},{13,5},{17,25},{21,29},{10,2},{... | collective-permute-start | bytes 3145736 | tf_op jit(solution)/shard_map/ppermute | solution.py:443
  1108.0 112.5 %collective-permute-start.162 = (bf16[4,256,512]{2,1,0:T(8,128)(2,1)S(1)}, bf16[4,256,512]{2,1,0:T(8,128)(2,1)}, u32[]{:S(2)}, u32[]{:S(2)}) collective-permute-start(bf16[4,256,512]{2,1,0:T(8,128)(2,1)S(1)} %add_convert_fusion.10.refs_0_), channel_id=1, source_target_pairs={{8,0},{12,4},{16,24},{20,28},{9,1},{13,5},{17,25},{21,29},{10,2},{... | collective-permute-start | bytes 3145736 | tf_op jit(solution)/shard_map/ppermute | solution.py:443
  1130.4 112.5 %collective-permute-start.163 = (bf16[4,256,512]{2,1,0:T(8,128)(2,1)S(1)}, bf16[4,256,512]{2,1,0:T(8,128)(2,1)}, u32[]{:S(2)}, u32[]{:S(2)}) collective-permute-start(bf16[4,256,512]{2,1,0:T(8,128)(2,1)S(1)} %add_convert_fusion.8.refs_1_), channel_id=1, source_target_pairs={{8,0},{12,4},{16,24},{20,28},{9,1},{13,5},{17,25},{21,29},{10,2},{... | collective-permute-start | bytes 3145736 | tf_op jit(solution)/shard_map/ppermute | solution.py:443
  1153.9 111.5 %collective-permute-start.164 = (bf16[4,256,512]{2,1,0:T(8,128)(2,1)}, bf16[4,256,512]{2,1,0:T(8,128)(2,1)}, u32[]{:S(2)}, u32[]{:S(2)}) collective-permute-start(bf16[4,256,512]{2,1,0:T(8,128)(2,1)} %add_convert_fusion.6.refs_2_), channel_id=1, source_target_pairs={{8,0},{12,4},{16,24},{20,28},{9,1},{13,5},{17,25},{21,29},{10,2},{... | collective-permute-start | bytes 3145736 | tf_op jit(solution)/shard_map/ppermute | solution.py:443
  1175.5 91.2 %collective-permute-start.76 = (bf16[192,2048]{1,0:T(8,128)(2,1)}, bf16[192,2048]{1,0:T(8,128)(2,1)}, u32[]{:S(2)}, u32[]{:S(2)}) collective-permute-start(bf16[192,2048]{1,0:T(8,128)(2,1)} %copy-done.80), channel_id=1, source_target_pairs={{0,4},{4,0},{8,12},{12,8},{16,20},{20,16},{24,28},{28,24},{1,5},{5... | collective-permute-start | bytes 2359304 | tf_op jit(solution)/shard_map/ppermute | solution.py:436
  1198.0 76.9 %collective-permute-start.75 = (bf16[192,2048]{1,0:T(8,128)(2,1)}, bf16[192,2048]{1,0:T(8,128)(2,1)}, u32[]{:S(2)}, u32[]{:S(2)}) collective-permute-start(bf16[192,2048]{1,0:T(8,128)(2,1)} %collective-permute-done.71.refs_14_.refs_2_), channel_id=1, source_target_pairs={{0,4},{4,0},{8,12},{12,8},{16,20},{20,16},{24,28},{28,24},{1,5},{5... | collective-permute-start | bytes 2359304 | tf_op jit(solution)/shard_map/ppermute | solution.py:436
  (322 other events, 7692.8 us)

commit v2 on v1

--- a/solution.py
+++ b/solution.py
@@ -321,6 +321,7 @@
 BF16 = jnp.bfloat16
 F32 = jnp.float32
 QUARTERS = 4
+LINES = 2
 
 
 def matmul(a, b):
@@ -460,7 +461,7 @@
         [(s, s + 1), (planes - 1 - s, planes - 2 - s)] for s in range(middle_left)
     ]
 
-    def summed_over_planes(value, last=True):
+    def summed_over_planes(value):
         for moves in folds:
             value = (
                 value.astype(F32) + between_planes(value, moves).astype(F32)
@@ -469,8 +470,6 @@
         value = (value.astype(F32) + crossed.astype(F32)).astype(value.dtype)
         for s, moves in reversed(list(enumerate(folds))):
             back = between_planes(value, [(b, a) for a, b in moves])
-            if s == 0 and not last:
-                return value, back
             receives = (z == s) | (z == planes - 1 - s)
             value = jnp.where(receives, back, value)
         return value
@@ -578,7 +577,7 @@
 
     feed = [hidden_weights(q) for q in range(QUARTERS)]
     own_cotangent = cotangent[0]
-    cot_own, cot_near = gathered(own_cotangent)
+    cot_own = [own_cotangent] + [across(own_cotangent, d) for d in range(1, n)]
 
     def project(me_ref, *refs):
         near_tokens = refs[: 2 * n]
@@ -678,6 +677,10 @@
             )
         spread(pl.program_id(0), side, whole, own_refs, near_refs)
 
+    early = lax.optimization_barrier([query_rot] + cot_own[1:] + feed[0][1:])
+    query_rot, cot_own[1:], feed[0][1:] = early[0], early[1:n], early[n:]
+    cot_near = [sibling(block) for block in cot_own]
+
     block = (rows, width)
     attend_flops = 4 * plane_rows * planes * pair * HD + 2 * plane_rows * HD * width
     attended, *partial = run_grid(
@@ -1056,20 +1059,53 @@
 
     is_outer = ((z == 0) | (z == planes - 1)).astype(jnp.int32)
     me_and_plane = jnp.concatenate([me, is_outer[None]])
-
-    def owned(tiles):
-        ends = [summed_over_planes(t, last=False) for t in tiles]
+    stages = len(folds) * 2 + 1
+
+    def stage_moves(stage):
+        if stage < len(folds):
+            return folds[stage]
+        if stage == len(folds):
+            return [(middle_left, middle_right), (middle_right, middle_left)]
+        return [(b, a) for a, b in folds[stages - 1 - stage]]
+
+    def pipelined(tiles):
+        ends = {}
+        for line in range(LINES):
+            waiting = []
+            feed_line = list(range(line, len(tiles), LINES))
+            while feed_line or waiting:
+                if feed_line:
+                    first = feed_line.pop(0)
+                    waiting.append((first, 0, tiles[first]))
+                operands = lax.optimization_barrier([value for _, _, value in waiting])
+                moved = []
+                for (index, stage, _), value in zip(waiting, operands):
+                    other = between_planes(value, stage_moves(stage))
+                    if stage == stages - 1:
+                        ends[index] = (value, other)
+                        continue
+                    if stage <= len(folds):
+                        value = (value.astype(F32) + other.astype(F32)).astype(BF16)
+                    else:
+                        s = stages - 1 - stage
+                        value = jnp.where((z == s) | (z == planes - 1 - s), other, value)
+                    moved.append((index, stage + 1, value))
+                waiting = moved
+        return [ends[i] for i in range(len(tiles))]
+
+    order = [t for q in range(QUARTERS) for t in hidden_tiles[q]] + [query_tile, output_tile, kv_tile]
+    plane_sums = pipelined(order)
+
+    def owned(ends):
         dealt = run_whole(
             deal,
             me_and_plane,
             [a for a, _ in ends] + [b for _, b in ends],
-            [shape((len(tiles),) + tiles[0].shape[1:])] * n,
+            [shape((len(ends),) + ends[0][0].shape[1:])] * n,
             name="deal",
         )
         own = [dealt[0]] + [across(dealt[d], d) for d in range(1, n)]
         return own + [sibling(block) for block in own]
-
-    full = lambda count: [fixed((count, HD, wide))] * (2 * n)
 
     def slot_of(q, count):
         def where(i, me):
@@ -1095,7 +1131,7 @@
     ]
     held = None
     for q in range(QUARTERS):
-        tiles = owned(hidden_tiles[q])
+        tiles = owned(plane_sums[3 * q : 3 * q + 3])
         where = slot_of(q, QUARTERS)
         by_columns = pl.BlockSpec((wide, quarter), lambda i, me, w=where: (0, w(i, me)))
         by_rows = pl.BlockSpec((quarter, wide), lambda i, me, w=where: (w(i, me), 0))
@@ -1126,7 +1162,7 @@
         place_query,
         me,
         (2 * n,),
-        owned([query_tile, output_tile]),
+        owned(plane_sums[3 * QUARTERS : 3 * QUARTERS + 2]),
         [fixed((2, HD, wide))] * (2 * n),
         [shape(query_weight.shape, F32), shape(output_weight.shape, F32)],
         [
@@ -1152,7 +1188,7 @@
         place_kv,
         me,
         (n,),
-        owned([kv_tile]),
+        owned(plane_sums[3 * QUARTERS + 2 :]),
         [fixed((1, HD, wide))] * (2 * n),
         [shape(key_weight.shape, F32), shape(value_weight.shape, F32)],
         [by_chip, by_chip],

time: 1700 us -> 1250 us (0.74)
  waiting for transfers between devices: 1080 us -> 597 us
  starting transfers between devices: 209 us -> 237 us
    ppermute x48, waiting for transfers between devices: 642 us -> 198 us  [between_planes(): lax.ppermute(value, 'ctx', [(2 * a + side, 2 * b + side) for a, b in move...]
    ppermute x63, waiting for transfers between devices: 395 us -> 340 us  [across(): return lax.ppermute(value, 'fsdp', [(i, i ^ d) for i in range(n)])]
    ppermute x48, starting transfers between devices: 97.5 us -> 120 us  [between_planes(): lax.ppermute(value, 'ctx', [(2 * a + side, 2 * b + side) for a, b in move...]
    convert_element_type x30, other arithmetic: 23.7 us -> 42.4 us  [pipelined(): value = (value.astype(F32) + other.astype(F32)).astype(BF16)]
  transfers between devices with their start and end apart: 188 -> 188, of which waited for: 64 -> 57; matrix products, arithmetic and copies ran while one was open for 4% -> 7% of each run, Pallas kernels for 14% -> 17%
where the time goes in v2:
time: 1250 us; the launch traced here: 1240 us
  waiting for transfers between devices  597 us (48%)
  Pallas kernels  308 us (25%)
  starting transfers between devices  237 us (19%)
  other arithmetic  76.8 us (6%)
  local copies, waits for them, and re-layouts  20.7 us (2%)
    ppermute x63, waiting for transfers between devices, across(): return lax.ppermute(value, 'fsdp', [(i, i ^ d) for i in range(n)])  340 us
    ppermute x48, waiting for transfers between devices, between_planes(): lax.ppermute(value, 'ctx', [(2 * a + side, 2 * b + side) for a, b in move...  198 us
    pallas_call x18, Pallas kernels, run_whole(): pl.pallas_call(body, out_shape=outs, in_specs=[pl.BlockSpec(memory_space=...  158 us
    pallas_call x15, Pallas kernels, run_grid(): pl.pallas_call(body, out_shape=outs, grid_spec=pltpu.PrefetchScalarGridSp...  150 us
    ppermute x48, starting transfers between devices, between_planes(): lax.ppermute(value, 'ctx', [(2 * a + side, 2 * b + side) for a, b in move...  120 us
    ppermute x63, starting transfers between devices, across(): return lax.ppermute(value, 'fsdp', [(i, i ^ d) for i in range(n)])  69.5 us
    ppermute x12, waiting for transfers between devices, along(): lax.ppermute(value, 'ctx', [(a, b) for a, b in pairs if 0 <= b < ctx_count])  56.2 us
    convert_element_type x30, other arithmetic, pipelined(): value = (value.astype(F32) + other.astype(F32)).astype(BF16)  42.4 us
  transfers between devices with their start and end apart: 188, of which 57 were waited for; matrix products, arithmetic and copies ran while one was open for 7% of the time, Pallas kernels for 17%

profile of v2, /device:TPU:0, one launch (start us, length us, event | category | flops | bytes accessed | tf_op | source)
XLA Modules:
  0.0 1243.2 jit_solution(701705391337922274)
XLA Ops:
  16.7 34.5 %collective-permute-done.7.refs_9_.refs_7_ = bf16[528,512]{1,0:T(8,128)(2,1)} collective-permute-done((bf16[528,512]{1,0:T(8,128)(2,1)}, bf16[528,512]{1,0:T(8,128)(2,1)}, u32[]{:S(2)}, u32[]{:S(2)}) %collective-permute-start.7) | collective-permute-done | bytes 540704 | tf_op jit(solution)/shard_map/ppermute | solution.py:434
  85.3 14.9 %collective-permute-done.17 = bf16[4,2,192,256]{3,2,1,0:T(8,128)(2,1)S(1)} collective-permute-done((bf16[4,2,192,256]{3,2,1,0:T(8,128)(2,1)}, bf16[4,2,192,256]{3,2,1,0:T(8,128)(2,1)S(1)}, u32[]{:S(2)}, u32[]{:S(2)}) %collective-permute-start.17) | collective-permute-done | bytes 786464 | tf_op jit(solution)/shard_map/ppermute | solution.py:441
  157.5 16.8 %collective-permute-done.13.refs_1_.refs_5_.refs_9_ = bf16[768,512]{1,0:T(8,128)(2,1)} collective-permute-done((bf16[768,512]{1,0:T(8,128)(2,1)}, bf16[768,512]{1,0:T(8,128)(2,1)}, u32[]{:S(2)}, u32[]{:S(2)}) %collective-permute-start.13) | collective-permute-done | bytes 786464 | tf_op jit(solution)/shard_map/ppermute | solution.py:434
  195.4 17.3 %attend.1 = (bf16[4,2,192,256]{3,2,1,0:T(8,128)(2,1)}, bf16[192,2048]{1,0:T(8,128)(2,1)}, bf16[192,2048]{1,0:T(8,128)(2,1)}, bf16[192,2048]{1,0:T(8,128)(2,1)}, ...) custom-call(s32[2]{0:T(128)} %pad_add_fusion.me_ref, ...), custom_call_target="tpu_custom_call" | custom-call | flops 4026531840 | bytes 15235072 | tf_op jit(solution)/shard_map/attend/pallas_call | solution.py:363
  237.8 16.6 %collective-permute-done.33.refs_3_ = bf16[192,2048]{1,0:T(8,128)(2,1)S(1)} collective-permute-done((bf16[192,2048]{1,0:T(8,128)(2,1)S(1)}, bf16[192,2048]{1,0:T(8,128)(2,1)S(1)}, u32[]{:S(2)}, u32[]{:S(2)}) %collective-permute-start.33) | collective-permute-done | bytes 786464 | tf_op jit(solution)/shard_map/ppermute | solution.py:434
  271.3 33.3 %collective-permute-done.54.refs_2_.refs_18_.refs_22_ = bf16[768,512]{1,0:T(8,128)(2,1)} collective-permute-done((bf16[768,512]{1,0:T(8,128)(2,1)}, bf16[768,512]{1,0:T(8,128)(2,1)}, u32[]{:S(2)}, u32[]{:S(2)}) %collective-permute-start.54) | collective-permute-done | bytes 786464 | tf_op jit(solution)/shard_map/ppermute | solution.py:434
  307.2 16.7 %collective-permute-done.37.refs_6_ = bf16[192,2048]{1,0:T(8,128)(2,1)S(1)} collective-permute-done((bf16[192,2048]{1,0:T(8,128)(2,1)}, bf16[192,2048]{1,0:T(8,128)(2,1)S(1)}, u32[]{:S(2)}, u32[]{:S(2)}) %collective-permute-start.37) | collective-permute-done | bytes 786464 | tf_op jit(solution)/shard_map/ppermute | solution.py:434
  338.6 19.1 %feed_forward.7 = (bf16[1536,256]{1,0:T(8,128)(2,1)}, bf16[1536,256]{1,0:T(8,128)(2,1)}, bf16[1536,256]{1,0:T(8,128)(2,1)}, bf16[4,256,512]{2,1,0:T(8,128)(2,1)}...) custom-call(s32[2]{0:T(128)} %pad_add_fusion.me_ref, ...), custom_call_target="tpu_custom_call" | custom-call | flops 9663676416 | bytes 21233664 | tf_op jit(solution)/shard_map/feed_forward/pallas_call | solution.py:348
  371.9 32.8 %collective-permute-done.51.refs_2_.refs_14_.refs_18_ = bf16[768,512]{1,0:T(8,128)(2,1)S(1)} collective-permute-done((bf16[768,512]{1,0:T(8,128)(2,1)}, bf16[768,512]{1,0:T(8,128)(2,1)S(1)}, u32[]{:S(2)}, u32[]{:S(2)}) %collective-permute-start.51) | collective-permute-done | bytes 786464 | tf_op jit(solution)/shard_map/ppermute | solution.py:434
  405.9 18.8 %feed_forward.6 = (bf16[1536,256]{1,0:T(8,128)(2,1)}, bf16[1536,256]{1,0:T(8,128)(2,1)}, bf16[1536,256]{1,0:T(8,128)(2,1)}, bf16[4,256,512]{2,1,0:T(8,128)(2,1)}...) custom-call(s32[2]{0:T(128)} %pad_add_fusion.me_ref, ...), custom_call_target="tpu_custom_call" | custom-call | flops 9663676416 | bytes 21233664 | tf_op jit(solution)/shard_map/feed_forward/pallas_call | solution.py:348
  426.1 19.2 %feed_forward.5 = (bf16[1536,256]{1,0:T(8,128)(2,1)}, bf16[1536,256]{1,0:T(8,128)(2,1)}, bf16[1536,256]{1,0:T(8,128)(2,1)}, bf16[4,256,512]{2,1,0:T(8,128)(2,1)}...) custom-call(s32[2]{0:T(128)} %pad_add_fusion.me_ref, ...), custom_call_target="tpu_custom_call" | custom-call | flops 9663676416 | bytes 21233664 | tf_op jit(solution)/shard_map/feed_forward/pallas_call | solution.py:348
  445.4 19.0 %feed_forward.4 = (bf16[1536,256]{1,0:T(8,128)(2,1)}, bf16[1536,256]{1,0:T(8,128)(2,1)}, bf16[1536,256]{1,0:T(8,128)(2,1)}, bf16[4,256,512]{2,1,0:T(8,128)(2,1)}...) custom-call(s32[2]{0:T(128)} %pad_add_fusion.me_ref, ...), custom_call_target="tpu_custom_call" | custom-call | flops 9663676416 | bytes 21233664 | tf_op jit(solution)/shard_map/feed_forward/pallas_call | solution.py:348
  464.4 23.3 %feed_forward_back.1 = (bf16[192,2048]{1,0:T(8,128)(2,1)}, bf16[192,2048]{1,0:T(8,128)(2,1)}, bf16[192,2048]{1,0:T(8,128)(2,1)}, bf16[192,2048]{1,0:T(8,128)(2,1...) custom-call(s32[2]{0:T(128)} %pad_add_fusion.me_ref, ...), custom_call_target="tpu_custom_call" | custom-call | flops 12884901888 | bytes 25165824 | tf_op jit(solution)/shard_map/feed_forward_back/pallas_call | solution.py:363
  488.8 16.5 %feed_forward_out.1 = (bf16[192,2048]{1,0:T(8,128)(2,1)}, bf16[192,2048]{1,0:T(8,128)(2,1)}, bf16[192,2048]{1,0:T(8,128)(2,1)}, bf16[192,2048]{1,0:T(8,128)(2,1)...) custom-call(s32[2]{0:T(128)} %pad_add_fusion.me_ref, ...), custom_call_target="tpu_custom_call" | custom-call | flops 6442450944 | bytes 22020096 | tf_op jit(solution)/shard_map/feed_forward_out/pallas_call | solution.py:363
  518.2 16.2 %collective-permute-done.94 = bf16[4,256,512]{2,1,0:T(8,128)(2,1)S(1)} collective-permute-done((bf16[4,256,512]{2,1,0:T(8,128)(2,1)S(1)}, bf16[4,256,512]{2,1,0:T(8,128)(2,1)S(1)}, u32[]{:S(2)}, u32[]{:S(2)}) %collective-permute-start.94) | collective-permute-done | bytes 1048608 | tf_op jit(solution)/shard_map/ppermute | solution.py:444
  535.5 20.4 %collective-permute-done.109 = bf16[4,256,512]{2,1,0:T(8,128)(2,1)S(1)} collective-permute-done((bf16[4,256,512]{2,1,0:T(8,128)(2,1)S(1)}, bf16[4,256,512]{2,1,0:T(8,128)(2,1)S(1)}, u32[]{:S(2)}, u32[]{:S(2)}) %collective-permute-start.109) | collective-permute-done | bytes 1048608 | tf_op jit(solution)/shard_map/ppermute | solution.py:444
  570.5 21.0 %collective-permute-done.60 = bf16[192,2048]{1,0:T(8,128)(2,1)S(1)} collective-permute-done((bf16[192,2048]{1,0:T(8,128)(2,1)S(1)}, bf16[192,2048]{1,0:T(8,128)(2,1)S(1)}, u32[]{:S(2)}, u32[]{:S(2)}) %collective-permute-start.60) | collective-permute-done | bytes 786464 | tf_op jit(solution)/shard_map/ppermute | solution.py:434
  624.2 14.0 %collective-permute-done.71.refs_14_.refs_2_ = bf16[192,2048]{1,0:T(8,128)(2,1)} collective-permute-done((bf16[192,2048]{1,0:T(8,128)(2,1)}, bf16[192,2048]{1,0:T(8,128)(2,1)}, u32[]{:S(2)}, u32[]{:S(2)}) %collective-permute-start.71) | collective-permute-done | bytes 786464 | tf_op jit(solution)/shard_map/ppermute | solution.py:434
  659.6 20.2 %attend_back.1 = (bf16[4,2,192,256]{3,2,1,0:T(8,128)(2,1)}, bf16[4,2,192,256]{3,2,1,0:T(8,128)(2,1)}, bf16[4,2,192,256]{3,2,1,0:T(8,128)(2,1)}, bf16[4,2,192,256...) custom-call(s32[2]{0:T(128)} %pad_add_fusion.me_ref, ...), custom_call_target="tpu_custom_call" | custom-call | flops 7650410496 | bytes 22312960 | tf_op jit(solution)/shard_map/attend_back/pallas_call | solution.py:363
  737.6 14.4 %collective-permute-done.115 = bf16[4,256,512]{2,1,0:T(8,128)(2,1)} collective-permute-done((bf16[4,256,512]{2,1,0:T(8,128)(2,1)}, bf16[4,256,512]{2,1,0:T(8,128)(2,1)}, u32[]{:S(2)}, u32[]{:S(2)}) %collective-permute-start.115) | collective-permute-done | bytes 1048608 | tf_op jit(solution)/shard_map/ppermute | solution.py:444
  821.1 18.9 %collective-permute-done.117 = bf16[4,256,512]{2,1,0:T(8,128)(2,1)} collective-permute-done((bf16[4,256,512]{2,1,0:T(8,128)(2,1)}, bf16[4,256,512]{2,1,0:T(8,128)(2,1)}, u32[]{:S(2)}, u32[]{:S(2)}) %collective-permute-start.117) | collective-permute-done | bytes 1048608 | tf_op jit(solution)/shard_map/ppermute | solution.py:444
  1051.4 16.0 %collective-permute-done.162.refs_2_ = bf16[3,256,512]{2,1,0:T(8,128)(2,1)} collective-permute-done((bf16[3,256,512]{2,1,0:T(8,128)(2,1)}, bf16[3,256,512]{2,1,0:T(8,128)(2,1)}, u32[]{:S(2)}, u32[]{:S(2)}) %collective-permute-start.162) | collective-permute-done | bytes 786464 | tf_op jit(solution)/shard_map/ppermute | solution.py:434
  1085.4 19.5 %collective-permute-done.150.refs_5_ = bf16[4,256,512]{2,1,0:T(8,128)(2,1)S(1)} collective-permute-done((bf16[4,256,512]{2,1,0:T(8,128)(2,1)S(1)}, bf16[4,256,512]{2,1,0:T(8,128)(2,1)S(1)}, u32[]{:S(2)}, u32[]{:S(2)}) %collective-permute-start.150) | collective-permute-done | bytes 1048608 | tf_op jit(solution)/shard_map/ppermute | solution.py:444
  1130.5 16.9 %collective-permute-done.124.refs_3_ = bf16[4,256,512]{2,1,0:T(8,128)(2,1)} collective-permute-done((bf16[4,256,512]{2,1,0:T(8,128)(2,1)S(1)}, bf16[4,256,512]{2,1,0:T(8,128)(2,1)}, u32[]{:S(2)}, u32[]{:S(2)}) %collective-permute-start.124) | collective-permute-done | bytes 1048608 | tf_op jit(solution)/shard_map/ppermute | solution.py:444
  (761 shorter events, 763.2 us)
Async XLA Ops:
  0.6 50.6 %collective-permute-start.2 = (bf16[192,2048]{1,0:T(8,128)(2,1)}, bf16[192,2048]{1,0:T(8,128)(2,1)S(1)}, u32[]{:S(2)}, u32[]{:S(2)}) collective-permute-start(bf16[192,2048]{1,0:T(8,128)(2,1)} %bitcast.35), channel_id=1, source_target_pairs={{0,3},{1,2},{2,1},{3,0},{4,7},{5,6},{6,5},{7,4},{8,11},{9,10},{10,... | collective-permute-start | bytes 2359304 | tf_op jit(solution)/shard_map/ppermute | solution.py:434
  4.6 47.1 %collective-permute-start.1 = (bf16[192,2048]{1,0:T(8,128)(2,1)}, bf16[192,2048]{1,0:T(8,128)(2,1)S(1)}, u32[]{:S(2)}, u32[]{:S(2)}) collective-permute-start(bf16[192,2048]{1,0:T(8,128)(2,1)} %bitcast.36), channel_id=1, source_target_pairs={{0,2},{1,3},{2,0},{3,1},{4,6},{5,7},{6,4},{7,5},{8,10},{9,11},{10,... | collective-permute-start | bytes 2359304 | tf_op jit(solution)/shard_map/ppermute | solution.py:434
  5.1 46.7 %collective-permute-start = (bf16[192,2048]{1,0:T(8,128)(2,1)}, bf16[192,2048]{1,0:T(8,128)(2,1)S(1)}, u32[]{:S(2)}, u32[]{:S(2)}) collective-permute-start(bf16[192,2048]{1,0:T(8,128)(2,1)} %bitcast.37), channel_id=1, source_target_pairs={{0,1},{1,0},{2,3},{3,2},{4,5},{5,4},{6,7},{7,6},{8,9},{9,8},{10,11... | collective-permute-start | bytes 2359304 | tf_op jit(solution)/shard_map/ppermute | solution.py:434
  138.9 45.7 %collective-permute-start.14 = (bf16[768,512]{1,0:T(8,128)(2,1)}, bf16[768,512]{1,0:T(8,128)(2,1)}, u32[]{:S(2)}, u32[]{:S(2)}) collective-permute-start(bf16[768,512]{1,0:T(8,128)(2,1)} %get-tuple-element.208), channel_id=1, source_target_pairs={{0,2},{1,3},{2,0},{3,1},{4,6},{5,7},{6,4},{7,5},{8,10},{9,11},{10,... | collective-permute-start | bytes 2359304 | tf_op jit(solution)/shard_map/ppermute | solution.py:434
  140.7 44.7 %collective-permute-start.15 = (bf16[768,512]{1,0:T(8,128)(2,1)}, bf16[768,512]{1,0:T(8,128)(2,1)}, u32[]{:S(2)}, u32[]{:S(2)}) collective-permute-start(bf16[768,512]{1,0:T(8,128)(2,1)} %get-tuple-element.209), channel_id=1, source_target_pairs={{0,3},{1,2},{2,1},{3,0},{4,7},{5,6},{6,5},{7,4},{8,11},{9,10},{10,... | collective-permute-start | bytes 2359304 | tf_op jit(solution)/shard_map/ppermute | solution.py:434
  226.1 45.0 %collective-permute-start.53 = (bf16[768,512]{1,0:T(8,128)(2,1)}, bf16[768,512]{1,0:T(8,128)(2,1)}, u32[]{:S(2)}, u32[]{:S(2)}) collective-permute-start(bf16[768,512]{1,0:T(8,128)(2,1)} %get-tuple-element.245), channel_id=1, source_target_pairs={{0,1},{1,0},{2,3},{3,2},{4,5},{5,4},{6,7},{7,6},{8,9},{9,8},{10,11... | collective-permute-start | bytes 2359304 | tf_op jit(solution)/shard_map/ppermute | solution.py:434
  237.2 67.4 %collective-permute-start.54 = (bf16[768,512]{1,0:T(8,128)(2,1)}, bf16[768,512]{1,0:T(8,128)(2,1)}, u32[]{:S(2)}, u32[]{:S(2)}) collective-permute-start(bf16[768,512]{1,0:T(8,128)(2,1)} %get-tuple-element.246), channel_id=1, source_target_pairs={{0,2},{1,3},{2,0},{3,1},{4,6},{5,7},{6,4},{7,5},{8,10},{9,11},{10,... | collective-permute-start | bytes 2359304 | tf_op jit(solution)/shard_map/ppermute | solution.py:434
  254.4 50.2 %collective-permute-start.55 = (bf16[768,512]{1,0:T(8,128)(2,1)}, bf16[768,512]{1,0:T(8,128)(2,1)S(1)}, u32[]{:S(2)}, u32[]{:S(2)}) collective-permute-start(bf16[768,512]{1,0:T(8,128)(2,1)} %get-tuple-element.247), channel_id=1, source_target_pairs={{0,3},{1,2},{2,1},{3,0},{4,7},{5,6},{6,5},{7,4},{8,11},{9,10},{10,... | collective-permute-start | bytes 2359304 | tf_op jit(solution)/shard_map/ppermute | solution.py:434
  255.8 50.8 %collective-permute-start.44 = (bf16[192,2048]{1,0:T(8,128)(2,1)}, bf16[192,2048]{1,0:T(8,128)(2,1)}, u32[]{:S(2)}, u32[]{:S(2)}) collective-permute-start(bf16[192,2048]{1,0:T(8,128)(2,1)} %collective-permute-done.10.refs_13_), channel_id=1, source_target_pairs={{0,4},{4,0},{8,12},{12,8},{16,20},{20,16},{24,28},{28,24},{1,5},{5... | collective-permute-start | bytes 2359304 | tf_op jit(solution)/shard_map/ppermute | solution.py:437
  261.1 45.5 %collective-permute-start.45 = (bf16[192,2048]{1,0:T(8,128)(2,1)}, bf16[192,2048]{1,0:T(8,128)(2,1)S(1)}, u32[]{:S(2)}, u32[]{:S(2)}) collective-permute-start(bf16[192,2048]{1,0:T(8,128)(2,1)} %collective-permute-done.11.refs_14_), channel_id=1, source_target_pairs={{0,4},{4,0},{8,12},{12,8},{16,20},{20,16},{24,28},{28,24},{1,5},{5... | collective-permute-start | bytes 2359304 | tf_op jit(solution)/shard_map/ppermute | solution.py:437
  332.9 91.8 %collective-permute-start.47 = (bf16[768,512]{1,0:T(8,128)(2,1)}, bf16[768,512]{1,0:T(8,128)(2,1)S(1)}, u32[]{:S(2)}, u32[]{:S(2)}) collective-permute-start(bf16[768,512]{1,0:T(8,128)(2,1)} %get-tuple-element.235), channel_id=1, source_target_pairs={{0,1},{1,0},{2,3},{3,2},{4,5},{5,4},{6,7},{7,6},{8,9},{9,8},{10,11... | collective-permute-start | bytes 2359304 | tf_op jit(solution)/shard_map/ppermute | solution.py:434
  334.3 90.5 %collective-permute-start.48 = (bf16[768,512]{1,0:T(8,128)(2,1)}, bf16[768,512]{1,0:T(8,128)(2,1)S(1)}, u32[]{:S(2)}, u32[]{:S(2)}) collective-permute-start(bf16[768,512]{1,0:T(8,128)(2,1)} %get-tuple-element.236), channel_id=1, source_target_pairs={{0,2},{1,3},{2,0},{3,1},{4,6},{5,7},{6,4},{7,5},{8,10},{9,11},{10,... | collective-permute-start | bytes 2359304 | tf_op jit(solution)/shard_map/ppermute | solution.py:434
  336.3 68.4 %collective-permute-start.51 = (bf16[768,512]{1,0:T(8,128)(2,1)}, bf16[768,512]{1,0:T(8,128)(2,1)S(1)}, u32[]{:S(2)}, u32[]{:S(2)}) collective-permute-start(bf16[768,512]{1,0:T(8,128)(2,1)} %get-tuple-element.241), channel_id=1, source_target_pairs={{0,2},{1,3},{2,0},{3,1},{4,6},{5,7},{6,4},{7,5},{8,10},{9,11},{10,... | collective-permute-start | bytes 2359304 | tf_op jit(solution)/shard_map/ppermute | solution.py:434
  337.1 67.7 %collective-permute-start.52 = (bf16[768,512]{1,0:T(8,128)(2,1)}, bf16[768,512]{1,0:T(8,128)(2,1)S(1)}, u32[]{:S(2)}, u32[]{:S(2)}) collective-permute-start(bf16[768,512]{1,0:T(8,128)(2,1)} %get-tuple-element.242), channel_id=1, source_target_pairs={{0,3},{1,2},{2,1},{3,0},{4,7},{5,6},{6,5},{7,4},{8,11},{9,10},{10,... | collective-permute-start | bytes 2359304 | tf_op jit(solution)/shard_map/ppermute | solution.py:434
  370.5 54.3 %collective-permute-start.49 = (bf16[768,512]{1,0:T(8,128)(2,1)S(1)}, bf16[768,512]{1,0:T(8,128)(2,1)S(1)}, u32[]{:S(2)}, u32[]{:S(2)}) collective-permute-start(bf16[768,512]{1,0:T(8,128)(2,1)S(1)} %copy-done.140), channel_id=1, source_target_pairs={{0,3},{1,2},{2,1},{3,0},{4,7},{5,6},{6,5},{7,4},{8,11},{9,10},{10,... | collective-permute-start | bytes 2359304 | tf_op jit(solution)/shard_map/ppermute | solution.py:434
  511.3 44.6 %collective-permute-start.109 = (bf16[4,256,512]{2,1,0:T(8,128)(2,1)S(1)}, bf16[4,256,512]{2,1,0:T(8,128)(2,1)S(1)}, u32[]{:S(2)}, u32[]{:S(2)}) collective-permute-start(bf16[4,256,512]{2,1,0:T(8,128)(2,1)S(1)} %copy-done.31), channel_id=1, source_target_pairs={{0,8},{4,12},{24,16},{28,20},{1,9},{5,13},{25,17},{29,21},{2,10},{... | collective-permute-start | bytes 3145736 | tf_op jit(solution)/shard_map/ppermute | solution.py:444
  514.7 43.0 %collective-permute-start.67 = (bf16[192,2048]{1,0:T(8,128)(2,1)S(1)}, bf16[192,2048]{1,0:T(8,128)(2,1)S(1)}, u32[]{:S(2)}, u32[]{:S(2)}) collective-permute-start(bf16[192,2048]{1,0:T(8,128)(2,1)S(1)} %add_convert_fusion.42), channel_id=1, source_target_pairs={{0,2},{1,3},{2,0},{3,1},{4,6},{5,7},{6,4},{7,5},{8,10},{9,11},{10,... | collective-permute-start | bytes 2359304 | tf_op jit(solution)/shard_map/ppermute | solution.py:434
  557.1 45.4 %collective-permute-start.62 = (bf16[192,2048]{1,0:T(8,128)(2,1)}, bf16[192,2048]{1,0:T(8,128)(2,1)}, u32[]{:S(2)}, u32[]{:S(2)}) collective-permute-start(bf16[192,2048]{1,0:T(8,128)(2,1)} %add_convert_fusion.45), channel_id=1, source_target_pairs={{0,3},{1,2},{2,1},{3,0},{4,7},{5,6},{6,5},{7,4},{8,11},{9,10},{10,... | collective-permute-start | bytes 2359304 | tf_op jit(solution)/shard_map/ppermute | solution.py:434
  557.8 46.2 %collective-permute-start.95 = (bf16[4,256,512]{2,1,0:T(8,128)(2,1)S(1)}, bf16[4,256,512]{2,1,0:T(8,128)(2,1)}, u32[]{:S(2)}, u32[]{:S(2)}) collective-permute-start(bf16[4,256,512]{2,1,0:T(8,128)(2,1)S(1)} %add_convert_fusion.29), channel_id=1, source_target_pairs={{8,16},{12,20},{16,8},{20,12},{9,17},{13,21},{17,9},{21,13},{10,18... | collective-permute-start | bytes 3145736 | tf_op jit(solution)/shard_map/ppermute | solution.py:444
  559.4 44.8 %collective-permute-start.96 = (bf16[4,256,512]{2,1,0:T(8,128)(2,1)S(1)}, bf16[4,256,512]{2,1,0:T(8,128)(2,1)}, u32[]{:S(2)}, u32[]{:S(2)}) collective-permute-start(bf16[4,256,512]{2,1,0:T(8,128)(2,1)S(1)} %copy-done.29), channel_id=1, source_target_pairs={{0,8},{4,12},{24,16},{28,20},{1,9},{5,13},{25,17},{29,21},{2,10},{... | collective-permute-start | bytes 3145736 | tf_op jit(solution)/shard_map/ppermute | solution.py:444
  807.0 48.5 %collective-permute-start.185 = (bf16[3,256,512]{2,1,0:T(8,128)(2,1)}, bf16[3,256,512]{2,1,0:T(8,128)(2,1)S(1)}, u32[]{:S(2)}, u32[]{:S(2)}) collective-permute-start(bf16[3,256,512]{2,1,0:T(8,128)(2,1)} %collective-permute-done.181.refs_1_), channel_id=1, source_target_pairs={{0,4},{4,0},{8,12},{12,8},{16,20},{20,16},{24,28},{28,24},{1,5},{5... | collective-permute-start | bytes 2359304 | tf_op jit(solution)/shard_map/ppermute | solution.py:437
  1082.5 44.9 %collective-permute-start.123 = (bf16[4,256,512]{2,1,0:T(8,128)(2,1)S(1)}, bf16[4,256,512]{2,1,0:T(8,128)(2,1)S(1)}, u32[]{:S(2)}, u32[]{:S(2)}) collective-permute-start(bf16[4,256,512]{2,1,0:T(8,128)(2,1)S(1)} %add_convert_fusion.16.refs_0_), channel_id=1, source_target_pairs={{8,0},{12,4},{16,24},{20,28},{9,1},{13,5},{17,25},{21,29},{10,2},{... | collective-permute-start | bytes 3145736 | tf_op jit(solution)/shard_map/ppermute | solution.py:444
  1083.8 45.2 %collective-permute-start.132 = (bf16[4,256,512]{2,1,0:T(8,128)(2,1)S(1)}, bf16[4,256,512]{2,1,0:T(8,128)(2,1)}, u32[]{:S(2)}, u32[]{:S(2)}) collective-permute-start(bf16[4,256,512]{2,1,0:T(8,128)(2,1)S(1)} %add_convert_fusion.15), channel_id=1, source_target_pairs={{8,16},{12,20},{16,8},{20,12},{9,17},{13,21},{17,9},{21,13},{10,18... | collective-permute-start | bytes 3145736 | tf_op jit(solution)/shard_map/ppermute | solution.py:444
  1181.4 46.3 %collective-permute-start.131 = (bf16[2,256,512]{2,1,0:T(8,128)(2,1)}, bf16[2,256,512]{2,1,0:T(8,128)(2,1)S(1)}, u32[]{:S(2)}, u32[]{:S(2)}) collective-permute-start(bf16[2,256,512]{2,1,0:T(8,128)(2,1)} %copy-done.103), channel_id=1, source_target_pairs={{0,4},{4,0},{8,12},{12,8},{16,20},{20,16},{24,28},{28,24},{1,5},{5... | collective-permute-start | bytes 1572872 | tf_op jit(solution)/shard_map/ppermute | solution.py:437
  (309 other events, 6518.8 us)

commit v3 on v2

--- a/solution.py
+++ b/solution.py
@@ -321,6 +321,7 @@
 BF16 = jnp.bfloat16
 F32 = jnp.float32
 QUARTERS = 4
+MESH = pl.DeviceIdType.MESH
 LINES = 2
 
 
@@ -545,37 +546,32 @@
     weights_in = [cut[0]] + [across(cut[d], d) for d in range(1, n)]
     weights_out = [cut[n]] + [across(cut[n + d], d) for d in range(1, n)]
 
-    def cut_hidden_body(me_ref, *refs):
-        gates, ups, downs, outs = (refs[i * n : (i + 1) * n] for i in range(4))
+    def cut_hidden(me_ref, *refs):
+        gates, ups, downs = (refs[i * n : (i + 1) * n] for i in range(3))
         for d in range(n):
-            outs[d][:wide, :quarter] = gates[d][...]
-            outs[d][:wide, quarter:] = ups[d][...]
-            outs[d][wide:, :] = downs[d][...]
-
-    def cut_hidden(q):
-        def columns(d):
-            return lambda i, me: (0, (2 * (me[0] ^ d) + me[1]) * QUARTERS + q)
-
-        def down_rows(d):
-            return lambda i, me: ((2 * (me[0] ^ d) + me[1]) * QUARTERS + q, 0)
-
-        return run_grid(
-            cut_hidden_body,
-            me,
-            (1,),
-            [gate_weight] * n + [up_weight] * n + [down_weight] * n,
-            [pl.BlockSpec((wide, quarter), columns(d)) for d in range(n)] * 2
-            + [pl.BlockSpec((quarter, wide), down_rows(d)) for d in range(n)],
-            [shape((wide + quarter, 2 * quarter))] * n,
-            [pl.BlockSpec((wide + quarter, 2 * quarter), lambda i, me: (0, 0))] * n,
-            name="cut_hidden",
-        )
-
-    def hidden_weights(q):
-        pieces = cut_hidden(q)
-        return [pieces[0]] + [across(pieces[d], d) for d in range(1, n)]
-
-    feed = [hidden_weights(q) for q in range(QUARTERS)]
+            refs[-1][0, d, :wide, :quarter] = gates[d][...]
+            refs[-1][0, d, :wide, quarter:] = ups[d][...]
+            refs[-1][0, d, wide:, :] = downs[d][...]
+
+    def columns_of(d):
+        return lambda q, me: (0, (2 * (me[0] ^ d) + me[1]) * QUARTERS + q)
+
+    def down_rows_of(d):
+        return lambda q, me: ((2 * (me[0] ^ d) + me[1]) * QUARTERS + q, 0)
+
+    piece = (wide + quarter, 2 * quarter)
+    hidden_cut = run_grid(
+        cut_hidden,
+        me,
+        (QUARTERS,),
+        [gate_weight] * n + [up_weight] * n + [down_weight] * n,
+        [pl.BlockSpec((wide, quarter), columns_of(d)) for d in range(n)] * 2
+        + [pl.BlockSpec((quarter, wide), down_rows_of(d)) for d in range(n)],
+        shape((QUARTERS, n) + piece),
+        pl.BlockSpec((1, n) + piece, lambda q, me: (q, 0, 0, 0)),
+        name="cut_hidden",
+    )
+    first_pieces = [across(hidden_cut[0, d], d) for d in range(1, n)]
     own_cotangent = cotangent[0]
     cot_own = [own_cotangent] + [across(own_cotangent, d) for d in range(1, n)]
 
@@ -677,8 +673,8 @@
             )
         spread(pl.program_id(0), side, whole, own_refs, near_refs)
 
-    early = lax.optimization_barrier([query_rot] + cot_own[1:] + feed[0][1:])
-    query_rot, cot_own[1:], feed[0][1:] = early[0], early[1:n], early[n:]
+    early = lax.optimization_barrier([query_rot] + cot_own[1:] + first_pieces)
+    query_rot, cot_own[1:], first_pieces = early[0], early[1:n], early[n:]
     cot_near = [sibling(block) for block in cot_own]
 
     block = (rows, width)
@@ -715,124 +711,448 @@
     two_own, two_near = gathered(own_normed_two)
 
     tile = plane_rows // 3
-
-    def feed_forward(me_ref, *refs):
-        pieces = refs[:n]
-        two_refs, cot_refs = refs[n : 3 * n], refs[3 * n : 5 * n]
-        hidden_ref, gate_ref, up_ref, dgate, dup, ddown = refs[5 * n : 5 * n + 6]
-        two, cot, turned, two_sem, cot_sem = refs[5 * n + 6 :]
-        chip = me_ref[0]
-        copies = []
-        for source, target, sems in ((two_refs, two, two_sem), (cot_refs, cot, cot_sem)):
+    tiles_count = 3 * QUARTERS
+    units = 2 * tiles_count
+    unit = (2, quarter, wide)
+    held_sums, held_ends = 4, 3
+
+    def feed_forward(*refs):
+        two_refs, cot_refs, first_refs = refs[: 2 * n], refs[2 * n : 4 * n], refs[4 * n : 5 * n - 1]
+        cut_ref = refs[5 * n - 1]
+        back_refs, out_refs = refs[5 * n : 7 * n], refs[7 * n : 9 * n]
+        tiles, from_end, from_middle, finals, owned_ref, near_ref = refs[9 * n : 9 * n + 6]
+        (
+            work,
+            feed,
+            hidden,
+            turned,
+            stage,
+            mine,
+            theirs,
+            crossed,
+            sums,
+            ends,
+            load_sem,
+            feed_local,
+            feed_send,
+            feed_recv,
+            stage_sem,
+            one_send,
+            one_recv,
+            two_send,
+            two_recv,
+            three_send,
+            three_recv,
+            mine_sem,
+            theirs_sem,
+            crossed_sem,
+            final_sem,
+            deal_local,
+            deal_send,
+            deal_recv,
+            near_send,
+            near_recv,
+        ) = refs[9 * n + 6 :]
+        here = lax.axis_index("ctx")
+        chip = lax.axis_index("fsdp")
+        z, side = here // 2, here % 2
+        is_middle = (z == 1) | (z == 2)
+        is_end = jnp.logical_not(is_middle)
+        chips = [chip, chip + 1 - 2 * (chip % 2), (chip + 2) % 4, 3 - chip]
+        partner = (2 * (z + 1 - 2 * (z % 2)) + side, chip)
+        other_middle = (2 * (3 - z) + side, chip)
+        sibling_core = (here + 1 - 2 * side, chip)
+        blocks = [pl.ds(pl.multiple_of(c * wide, wide), wide) for c in chips]
+
+        barrier = pltpu.get_barrier_semaphore()
+        for peer in [(here, c) for c in chips[1:]] + [partner, sibling_core]:
+            pl.semaphore_signal(barrier, inc=1, device_id=peer, device_id_type=MESH)
+
+        @pl.when(is_middle)
+        def _():
+            pl.semaphore_signal(barrier, inc=1, device_id=other_middle, device_id_type=MESH)
+            pl.semaphore_wait(barrier, n + 2)
+
+        @pl.when(is_end)
+        def _():
+            pl.semaphore_wait(barrier, n + 1)
+
+        def remote(source, target, send, recv, peer):
+            return pltpu.make_async_remote_copy(
+                src_ref=source,
+                dst_ref=target,
+                send_sem=send,
+                recv_sem=recv,
+                device_id=peer,
+                device_id_type=MESH,
+            )
+
+        def feed_copy(q, d):
+            at = q * n + d
+            return remote(
+                cut_ref.at[q, d], feed.at[q, d], feed_send.at[at], feed_recv.at[at], (here, chips[d])
+            )
+
+        def feed_own(q):
+            return pltpu.make_async_copy(cut_ref.at[q, 0], feed.at[q, 0], feed_local.at[q])
+
+        def hop_one(i):
+            return remote(tiles.at[i], from_end.at[i], one_send.at[i], one_recv.at[i], partner)
+
+        def hop_two(i):
+            return remote(
+                sums.at[i % held_sums],
+                from_middle.at[i],
+                two_send.at[i],
+                two_recv.at[i],
+                other_middle,
+            )
+
+        def hop_three(i):
+            return remote(
+                ends.at[i % held_ends], finals.at[i], three_send.at[i], three_recv.at[i], partner
+            )
+
+        def load_mine(i):
+            return pltpu.make_async_copy(tiles.at[i], mine.at[i % 2], mine_sem.at[i % 2])
+
+        def load_theirs(i):
+            return pltpu.make_async_copy(from_end.at[i], theirs.at[i % 2], theirs_sem.at[i % 2])
+
+        def load_crossed(i):
+            return pltpu.make_async_copy(from_middle.at[i], crossed.at[i % 2], crossed_sem.at[i % 2])
+
+        def keep_final(i):
+            return pltpu.make_async_copy(
+                ends.at[i % held_ends], finals.at[i], final_sem.at[i % held_ends]
+            )
+
+        def keep_own(i):
+            return pltpu.make_async_copy(finals.at[i, 0], owned_ref.at[i, 0], deal_local.at[i])
+
+        def deal_to(i, b, d):
+            at = 2 * i + b
+            return remote(
+                finals.at[i, b],
+                owned_ref.at[i, b],
+                deal_send.at[at],
+                deal_recv.at[at],
+                (here, chips[d]),
+            )
+
+        def to_sibling(i):
+            return remote(
+                owned_ref.at[i], near_ref.at[i], near_send.at[i], near_recv.at[i], sibling_core
+            )
+
+        def add(target, a, b):
+            def some(r, _):
+                at = (r // 4, pl.ds(pl.multiple_of((r % 4) * (quarter // 4), quarter // 4), quarter // 4))
+                target[at] = (a[at].astype(F32) + b[at].astype(F32)).astype(BF16)
+                return 0
+
+            lax.fori_loop(0, 8, some, 0)
+
+        def when_in(i, *conditions):
+            return pl.when(functools.reduce(jnp.logical_and, conditions, (i >= 0) & (i < units)))
+
+        def advance(i):
+            @when_in(i - 1, is_middle)
+            def _():
+                at = i - 1
+                load_mine(at).wait()
+                load_theirs(at).wait()
+
+                @pl.when(at >= held_sums)
+                def _():
+                    hop_two(at - held_sums).wait_send()
+
+                add(sums.at[at % held_sums], mine.at[at % 2], theirs.at[at % 2])
+                hop_two(at).start()
+
+            @when_in(i - 4, is_middle)
+            def _():
+                at = i - 4
+                load_crossed(at).wait()
+
+                @pl.when(at >= held_ends)
+                def _():
+                    hop_three(at - held_ends).wait_send()
+
+                add(ends.at[at % held_ends], sums.at[at % held_sums], crossed.at[at % 2])
+                hop_three(at).start()
+                keep_final(at).start()
+
+            @when_in(i, is_middle)
+            def _():
+                hop_one(i).wait_recv()
+                load_mine(i).start()
+                load_theirs(i).start()
+
+            @when_in(i - 3, is_middle)
+            def _():
+                hop_two(i - 3).wait_recv()
+                load_crossed(i - 3).start()
+
+            @when_in(i - 6)
+            def _():
+                at = i - 6
+
+                @pl.when(is_middle)
+                def _():
+                    keep_final(at).wait()
+
+                @pl.when(is_end)
+                def _():
+                    hop_three(at).wait_recv()
+
+                @pl.when(at % 2 == 0)
+                def _():
+                    keep_own(at).start()
+                    deal_to(at, 1, 1).start()
+
+                @pl.when(at % 2 == 1)
+                def _():
+                    deal_to(at, 0, 2).start()
+                    deal_to(at, 1, 3).start()
+
+            @when_in(i - 9)
+            def _():
+                at = i - 9
+
+                @pl.when(at % 2 == 0)
+                def _():
+                    keep_own(at).wait()
+
+                @pl.when(at % 2 == 1)
+                def _():
+                    deal_to(at, 0, 2).wait_recv()
+
+                deal_to(at, 1, 3).wait_recv()
+                to_sibling(at).start()
+
+        def finish():
+            def one(i, _):
+                @pl.when(is_end)
+                def _():
+                    hop_one(i).wait_send()
+
+                @pl.when(is_middle & (i >= units - held_sums))
+                def _():
+                    hop_two(i).wait_send()
+
+                @pl.when(is_middle & (i >= units - held_ends))
+                def _():
+                    hop_three(i).wait_send()
+
+                @pl.when(i % 2 == 1)
+                def _():
+                    deal_to(i, 0, 2).wait_send()
+
+                deal_to(i, 1, 3).wait_send()
+                to_sibling(i).wait()
+                return 0
+
+            lax.fori_loop(0, units, one, 0)
+
+        loads = []
+        for base, sources in ((0, two_refs), (plane_rows, cot_refs)):
             for i in range(2 * n):
-                copies.append(
+                loads.append(
                     pltpu.make_async_copy(
-                        source[i], target.at[pl.ds(i * rows, rows)], sems.at[i]
+                        sources[i],
+                        work.at[pl.ds(base + i * rows, rows)],
+                        load_sem.at[len(loads)],
                     )
                 )
-        for copy in copies:
+        for d in range(1, n):
+            loads.append(
+                pltpu.make_async_copy(first_refs[d - 1], feed.at[0, d], load_sem.at[len(loads)])
+            )
+        for copy in loads:
             copy.start()
-        for copy in copies:
+        for q in range(QUARTERS):
+            feed_own(q).start()
+        for d in range(1, n):
+            feed_copy(1, d).start()
+        for copy in loads:
             copy.wait()
 
-        def forward(t, _):
-            here = pl.ds(pl.multiple_of(t * tile, tile), tile)
-            both = jnp.zeros((tile, 2 * quarter), F32)
-            hidden_grad = jnp.zeros((tile, quarter), F32)
+        def stage_copy(t, h):
+            return pltpu.make_async_copy(
+                stage.at[t % 2, pl.ds(2 * h, 2)], tiles.at[2 * t + h], stage_sem.at[t % 2, h]
+            )
+
+        def quarter_step(q, _):
+            feed_own(q).wait()
+
+            @pl.when(q > 0)
+            def _():
+                for d in range(1, n):
+                    feed_copy(q, d).wait_recv()
+
+            @pl.when((q > 0) & (q < QUARTERS - 1))
+            def _():
+                for d in range(1, n):
+                    feed_copy(q + 1, d).start()
+
+            def forward(t, _):
+                now = pl.ds(pl.multiple_of(t * tile, tile), tile)
+                cot_now = pl.ds(pl.multiple_of(plane_rows + t * tile, tile), tile)
+                both = jnp.zeros((tile, 2 * quarter), F32)
+                hidden_grad = jnp.zeros((tile, quarter), F32)
+                for j in range(n):
+                    both += matmul(work[now, blocks[j]], feed[q, j, :wide, :])
+                    hidden_grad += matmul_nt(work[cot_now, blocks[j]], feed[q, j, wide:, :])
+                gate, up = both[:, :quarter], both[:, quarter:]
+                share = 1.0 / (1.0 + jnp.exp(-gate))
+                activated = gate * share
+                results = (
+                    activated * up,
+                    hidden_grad * up * share * (1.0 + gate * (1.0 - share)),
+                    hidden_grad * activated,
+                )
+                for w, result in enumerate(results):
+                    hidden[q * 3 + w, now, :] = result.astype(BF16)
+                    turned[w, :, now] = result.T.astype(BF16)
+                return 0
+
+            lax.fori_loop(0, plane_rows // tile, forward, 0)
+            advance(2 * q - 2)
+
+            def outer(w, _):
+                t = 3 * q + w
+                base = jnp.where(w == 0, plane_rows, 0)
+                right = pl.ds(pl.multiple_of(base, plane_rows), plane_rows)
+
+                @pl.when(t >= 2)
+                def _():
+                    for h in range(2):
+                        stage_copy(t - 2, h).wait()
+
+                    @pl.when(is_end)
+                    def _():
+                        for h in range(2):
+                            hop_one(2 * (t - 2) + h).start()
+
+                for j in range(n):
+                    stage[t % 2, j] = matmul(turned[w], work[right, blocks[j]]).astype(BF16)
+                for h in range(2):
+                    stage_copy(t, h).start()
+                return 0
+
+            lax.fori_loop(0, 3, outer, 0)
+            advance(2 * q - 1)
+            return 0
+
+        lax.fori_loop(0, QUARTERS, quarter_step, 0)
+        for t in (tiles_count - 2, tiles_count - 1):
+            for h in range(2):
+                stage_copy(t, h).wait()
+
+            @pl.when(is_end)
+            def _():
+                for h in range(2):
+                    hop_one(2 * t + h).start()
+
+        def back_step(r, _):
+            now = pl.ds(pl.multiple_of(r * pair, pair), pair)
+            lefts = [
+                jnp.concatenate([hidden[q * 3 + 1, now, :], hidden[q * 3 + 2, now, :]], axis=1)
+                for q in range(QUARTERS)
+            ]
             for j in range(n):
-                both += matmul(two[here, column(chip ^ j, wide)], pieces[j][:wide, :])
-                hidden_grad += matmul_nt(cot[here, column(chip ^ j, wide)], pieces[j][wide:, :])
-            gate, up = both[:, :quarter], both[:, quarter:]
-            share = 1.0 / (1.0 + jnp.exp(-gate))
-            activated = gate * share
-            results = (
-                activated * up,
-                hidden_grad * up * share * (1.0 + gate * (1.0 - share)),
-                hidden_grad * activated,
-            )
-            for i, (result, ref) in enumerate(zip(results, (hidden_ref, gate_ref, up_ref))):
-                ref[here, :] = result.astype(BF16)
-                turned[i, :, here] = result.T.astype(BF16)
+                total = jnp.zeros((pair, wide), F32)
+                for q in range(QUARTERS):
+                    total += matmul_nt(lefts[q], feed[q, j, :wide, :])
+                work[now, blocks[j]] = total.astype(BF16)
+            advance(2 * QUARTERS - 2 + r)
             return 0
 
-        lax.fori_loop(0, plane_rows // tile, forward, 0)
-        for j in range(n):
-            here = column(chip ^ j, wide)
-            dgate[j] = matmul(turned[1], two[:, here]).astype(BF16)
-            dup[j] = matmul(turned[2], two[:, here]).astype(BF16)
-            ddown[j] = matmul(turned[0], cot[:, here]).astype(BF16)
-
-    grad_tile = (n, quarter, wide)
-    hiddens, gate_grads, up_grads, hidden_tiles = [], [], [], []
-    for q in range(QUARTERS):
-        hidden, gate_grad, up_grad, *tiles = run_whole(
-            feed_forward,
-            me,
-            feed[q] + two_own + two_near + cot_own + cot_near,
-            [shape((plane_rows, quarter))] * 3 + [shape(grad_tile)] * 3,
-            scratch=[
-                pltpu.VMEM((plane_rows, width), BF16),
-                pltpu.VMEM((plane_rows, width), BF16),
-                pltpu.VMEM((3, quarter, plane_rows), BF16),
-                pltpu.SemaphoreType.DMA((2 * n,)),
-                pltpu.SemaphoreType.DMA((2 * n,)),
-            ],
-            flops=12 * plane_rows * width * quarter,
-            in_hbm=4 * n,
-            name="feed_forward",
-        )
-        hiddens.append(hidden)
-        gate_grads.append(gate_grad)
-        up_grads.append(up_grad)
-        hidden_tiles.append(tiles)
-
-    pieces = [feed[q][j] for q in range(QUARTERS) for j in range(n)]
-    piece_specs = [fixed((wide + quarter, 2 * quarter))] * (QUARTERS * n)
-    pair_spec = pl.BlockSpec((2, 1, rows, quarter), lambda i, me: (0, i, 0, 0))
-    out_specs = [pl.BlockSpec(block, lambda i, me: (0, 0))] * (2 * n)
-
-    def put(step, results, own_refs, near_refs, chip):
-        for d in range(n):
-
-            @pl.when(step == d)
-            def _():
-                for j in range(n):
-                    here = column(chip ^ j, wide)
-                    own_refs[d][:, here] = results[j][:rows]
-                    near_refs[d][:, here] = results[j][rows:]
-
-    def feed_forward_back(me_ref, *refs):
-        gates, ups = refs[:QUARTERS], refs[QUARTERS : 2 * QUARTERS]
-        pieces = refs[2 * QUARTERS : 2 * QUARTERS + QUARTERS * n]
-        outs = refs[2 * QUARTERS + QUARTERS * n :]
-        lefts = [
-            jnp.concatenate(
-                [g[:, 0].reshape(pair, quarter), u[:, 0].reshape(pair, quarter)], axis=1
-            )
-            for g, u in zip(gates, ups)
-        ]
-        results = []
-        for j in range(n):
-            total = jnp.zeros((pair, wide), F32)
-            for q in range(QUARTERS):
-                total += matmul_nt(lefts[q], pieces[q * n + j][:wide, :])
-            results.append(total.astype(BF16))
-        put(pl.program_id(0), results, outs[:n], outs[n:], me_ref[0])
-
-    def by_block(value):
-        return value.reshape(2, n, rows, quarter)
-
-    back = run_grid(
-        feed_forward_back,
-        me,
-        (n,),
-        [by_block(g) for g in gate_grads] + [by_block(u) for u in up_grads] + pieces,
-        [pair_spec] * (2 * QUARTERS) + piece_specs,
-        [shape(block)] * (2 * n),
-        out_specs,
-        flops=4 * plane_rows * width * part,
-        name="feed_forward_back",
-    )
+        lax.fori_loop(0, n, back_step, 0)
+
+        def out_step(r, _):
+            now = pl.ds(pl.multiple_of(r * pair, pair), pair)
+            then = pl.ds(pl.multiple_of(plane_rows + r * pair, pair), pair)
+            for j in range(n):
+                total = jnp.zeros((pair, wide), F32)
+                for q in range(QUARTERS):
+                    total += matmul(hidden[q * 3, now, :], feed[q, j, wide:, :])
+                work[then, blocks[j]] = total.astype(BF16)
+            return 0
+
+        lax.fori_loop(0, n, out_step, 0)
+        stores = []
+        for base, targets in ((0, back_refs), (plane_rows, out_refs)):
+            for i in range(2 * n):
+                stores.append(
+                    pltpu.make_async_copy(
+                        work.at[pl.ds(base + i * rows, rows)], targets[i], load_sem.at[len(stores)]
+                    )
+                )
+        for copy in stores:
+            copy.start()
+
+        def rest(i, _):
+            advance(i)
+            return 0
+
+        lax.fori_loop(2 * QUARTERS - 2 + n, units + 10, rest, 0)
+        for copy in stores:
+            copy.wait()
+        for q in range(1, QUARTERS):
+            for d in range(1, n):
+                feed_copy(q, d).wait_send()
+        finish()
+
+    unit_array = shape((units,) + unit)
+    dma = pltpu.SemaphoreType.DMA
+    arrays = two_own + two_near + cot_own + cot_near + first_pieces + [hidden_cut]
+    results = pl.pallas_call(
+        feed_forward,
+        out_shape=[shape(block)] * (4 * n) + [unit_array] * 6,
+        in_specs=[pl.BlockSpec(memory_space=pl.ANY)] * len(arrays),
+        out_specs=[pl.BlockSpec(memory_space=pl.ANY)] * (4 * n + 6),
+        scratch_shapes=[
+            pltpu.VMEM((2 * plane_rows, width), BF16),
+            pltpu.VMEM((QUARTERS, n) + piece, BF16),
+            pltpu.VMEM((3 * QUARTERS, plane_rows, quarter), BF16),
+            pltpu.VMEM((3, quarter, plane_rows), BF16),
+            pltpu.VMEM((2, n, quarter, wide), BF16),
+            pltpu.VMEM((2,) + unit, BF16),
+            pltpu.VMEM((2,) + unit, BF16),
+            pltpu.VMEM((2,) + unit, BF16),
+            pltpu.VMEM((held_sums,) + unit, BF16),
+            pltpu.VMEM((held_ends,) + unit, BF16),
+            dma((4 * n + n - 1,)),
+            dma((QUARTERS,)),
+            dma((QUARTERS * n,)),
+            dma((QUARTERS * n,)),
+            dma((2, 2)),
+            dma((units,)),
+            dma((units,)),
+            dma((units,)),
+            dma((units,)),
+            dma((units,)),
+            dma((units,)),
+            dma((2,)),
+            dma((2,)),
+            dma((2,)),
+            dma((held_ends,)),
+            dma((units,)),
+            dma((2 * units,)),
+            dma((2 * units,)),
+            dma((units,)),
+            dma((units,)),
+        ],
+        cost_estimate=cost(18 * plane_rows * width * part, arrays, [unit_array] * 6),
+        compiler_params=pltpu.CompilerParams(
+            collective_id=0, has_side_effects=True, vmem_limit_bytes=62 * 1024 * 1024
+        ),
+        name="feed_forward",
+    )(*arrays)
+    back, out_partial = results[: 2 * n], results[2 * n : 4 * n]
+    hidden_own, hidden_near = results[-2:]
     two_grad_terms = reduced(back[:n], back[n:])
 
     def norm_back(values, inverse, gain, grad):
@@ -1093,8 +1413,7 @@
                 waiting = moved
         return [ends[i] for i in range(len(tiles))]
 
-    order = [t for q in range(QUARTERS) for t in hidden_tiles[q]] + [query_tile, output_tile, kv_tile]
-    plane_sums = pipelined(order)
+    plane_sums = pipelined([query_tile, output_tile, kv_tile])
 
     def owned(ends):
         dealt = run_whole(
@@ -1113,40 +1432,37 @@
 
         return where
 
-    def place_hidden(me_ref, *refs):
-        tiles = refs[: 2 * n]
-        gate_out, up_out, down_out = refs[-3:]
-        for i in range(2 * n):
-
-            @pl.when(pl.program_id(0) == i)
+    def place_hidden(me_ref, own_ref, near_ref, gate_out, up_out, down_out):
+        for source, e in ((own_ref, 0), (near_ref, 1)):
+
+            @pl.when(pl.program_id(0) // n == e)
             def _():
-                gate_out[...] = tiles[i][0].astype(F32).T
-                up_out[...] = tiles[i][1].astype(F32).T
-                down_out[...] = tiles[i][2].astype(F32)
-
-    hidden_outs = [
-        shape(gate_weight.shape, F32),
-        shape(up_weight.shape, F32),
-        shape(down_weight.shape, F32),
-    ]
-    held = None
-    for q in range(QUARTERS):
-        tiles = owned(plane_sums[3 * q : 3 * q + 3])
-        where = slot_of(q, QUARTERS)
-        by_columns = pl.BlockSpec((wide, quarter), lambda i, me, w=where: (0, w(i, me)))
-        by_rows = pl.BlockSpec((quarter, wide), lambda i, me, w=where: (w(i, me), 0))
-        rest = [] if held is None else list(held)
-        held = run_grid(
-            place_hidden,
-            me,
-            (2 * n,),
-            tiles + rest,
-            [fixed((3, quarter, wide))] * (2 * n) + [pl.BlockSpec(memory_space=pl.ANY)] * len(rest),
-            hidden_outs,
-            [by_columns, by_columns, by_rows],
-            aliases={1 + 2 * n + i: i for i in range(len(rest))},
-            name="place_hidden",
-        )
+                down_out[...] = source[0, 0].astype(F32)
+                gate_out[...] = source[1, 0].astype(F32).T
+                up_out[...] = source[2, 0].astype(F32).T
+
+    def hidden_slot(i, q, me):
+        return (2 * (me[0] ^ (i % n)) + (me[1] ^ (i // n))) * QUARTERS + q
+
+    by_columns = pl.BlockSpec((wide, quarter), lambda i, q, me: (0, hidden_slot(i, q, me)))
+    by_rows = pl.BlockSpec((quarter, wide), lambda i, q, me: (hidden_slot(i, q, me), 0))
+    held = run_grid(
+        place_hidden,
+        me,
+        (2 * n, QUARTERS),
+        [t.reshape(3 * QUARTERS, n, quarter, wide) for t in (hidden_own, hidden_near)],
+        [
+            pl.BlockSpec((3, 1, quarter, wide), lambda i, q, me: (q, jnp.where(i < n, i, n - 1), 0, 0)),
+            pl.BlockSpec((3, 1, quarter, wide), lambda i, q, me: (q, jnp.where(i < n, 0, i - n), 0, 0)),
+        ],
+        [
+            shape(gate_weight.shape, F32),
+            shape(up_weight.shape, F32),
+            shape(down_weight.shape, F32),
+        ],
+        [by_columns, by_columns, by_rows],
+        name="place_hidden",
+    )
 
     def place_query(me_ref, *refs):
         tiles, (query_out, output_out) = refs[: 2 * n], refs[2 * n :]
@@ -1162,7 +1478,7 @@
         place_query,
         me,
         (2 * n,),
-        owned(plane_sums[3 * QUARTERS : 3 * QUARTERS + 2]),
+        owned(plane_sums[:2]),
         [fixed((2, HD, wide))] * (2 * n),
         [shape(query_weight.shape, F32), shape(output_weight.shape, F32)],
         [
@@ -1188,37 +1504,14 @@
         place_kv,
         me,
         (n,),
-        owned(plane_sums[3 * QUARTERS + 2 :]),
+        owned(plane_sums[2:]),
         [fixed((1, HD, wide))] * (2 * n),
         [shape(key_weight.shape, F32), shape(value_weight.shape, F32)],
         [by_chip, by_chip],
         name="place_kv",
     )
 
-    def feed_forward_out(me_ref, *refs):
-        hiddens = refs[:QUARTERS]
-        pieces = refs[QUARTERS : QUARTERS + QUARTERS * n]
-        outs = refs[QUARTERS + QUARTERS * n :]
-        results = []
-        for j in range(n):
-            total = jnp.zeros((pair, wide), F32)
-            for q in range(QUARTERS):
-                total += matmul(hiddens[q][:, 0].reshape(pair, quarter), pieces[q * n + j][wide:, :])
-            results.append(total.astype(BF16))
-        put(pl.program_id(0), results, outs[:n], outs[n:], me_ref[0])
-
-    partial = run_grid(
-        feed_forward_out,
-        me,
-        (n,),
-        [by_block(h) for h in hiddens] + pieces,
-        [pair_spec] * QUARTERS + piece_specs,
-        [shape(block)] * (2 * n),
-        out_specs,
-        flops=2 * plane_rows * width * part,
-        name="feed_forward_out",
-    )
-    output = middle + sum(t.astype(F32) for t in reduced(partial[:n], partial[n:]))
+    output = middle + sum(t.astype(F32) for t in reduced(out_partial[:n], out_partial[n:]))
 
     return (
         output.astype(BF16)[None],
@@ -1237,7 +1530,7 @@
 
 def solution(mesh):
     chips, pieces = mesh.shape["fsdp"], mesh.shape["ctx"]
-    one_head_each = 2 * chips == H and chips == KVH and pieces % 4 == 0 and pieces > 4
+    one_head_each = 2 * chips == H and chips == KVH and pieces == 8
     return jax.shard_map(
         plane_layer if one_head_each else ring_layer,
         mesh=mesh,

time: 1250 us -> 1190 us (0.952)
  Pallas kernels: 308 us -> 573 us
  waiting for transfers between devices: 597 us -> 415 us
  starting transfers between devices: 237 us -> 123 us
  other arithmetic: 76.8 us -> 46.4 us
    pallas_call x0 -> x1, Pallas kernels: none -> 399 us  [plane_layer(): pl.pallas_call(feed_forward, out_shape=[shape(block)] * (4 * n) + [unit_a...]
    ppermute x48 -> x12, waiting for transfers between devices: 198 us -> 61.9 us  [between_planes(): lax.ppermute(value, 'ctx', [(2 * a + side, 2 * b + side) for a, b in move...]
    pallas_call x18 -> x10, Pallas kernels: 158 us -> 63.1 us  [run_whole(): pl.pallas_call(body, out_shape=outs, in_specs=[pl.BlockSpec(memory_space=...]
    ppermute x48 -> x12, starting transfers between devices: 120 us -> 26.5 us  [between_planes(): lax.ppermute(value, 'ctx', [(2 * a + side, 2 * b + side) for a, b in move...]
    ppermute x63 -> x42, waiting for transfers between devices: 340 us -> 283 us  [across(): return lax.ppermute(value, 'fsdp', [(i, i ^ d) for i in range(n)])]
    pallas_call x15 -> x7, Pallas kernels: 150 us -> 111 us  [run_grid(): pl.pallas_call(body, out_shape=outs, grid_spec=pltpu.PrefetchScalarGridSp...]
    convert_element_type x30 -> x6, other arithmetic: 42.4 us -> 4.23 us  [pipelined(): value = (value.astype(F32) + other.astype(F32)).astype(BF16)]
    ppermute x63 -> x42, starting transfers between devices: 69.5 us -> 53 us  [across(): return lax.ppermute(value, 'fsdp', [(i, i ^ d) for i in range(n)])]
  transfers between devices with their start and end apart: 188 -> 115, of which waited for: 57 -> 40; matrix products, arithmetic and copies ran while one was open for 7% -> 4% of each run, Pallas kernels for 17% -> 10%
where the time goes in v3:
time: 1190 us; the launch traced here: 1180 us
  Pallas kernels  573 us (48%)
  waiting for transfers between devices  415 us (35%)
  starting transfers between devices  123 us (10%)
  other arithmetic  46.4 us (4%)
  local copies, waits for them, and re-layouts  17.1 us (1%)
    pallas_call x1, Pallas kernels, plane_layer(): pl.pallas_call(feed_forward, out_shape=[shape(block)] * (4 * n) + [unit_a...  399 us
    ppermute x42, waiting for transfers between devices, across(): return lax.ppermute(value, 'fsdp', [(i, i ^ d) for i in range(n)])  283 us
    pallas_call x7, Pallas kernels, run_grid(): pl.pallas_call(body, out_shape=outs, grid_spec=pltpu.PrefetchScalarGridSp...  111 us
    pallas_call x10, Pallas kernels, run_whole(): pl.pallas_call(body, out_shape=outs, in_specs=[pl.BlockSpec(memory_space=...  63.1 us
    ppermute x12, waiting for transfers between devices, along(): lax.ppermute(value, 'ctx', [(a, b) for a, b in pairs if 0 <= b < ctx_count])  62 us
    ppermute x12, waiting for transfers between devices, between_planes(): lax.ppermute(value, 'ctx', [(2 * a + side, 2 * b + side) for a, b in move...  61.9 us
    ppermute x42, starting transfers between devices, across(): return lax.ppermute(value, 'fsdp', [(i, i ^ d) for i in range(n)])  53 us
    ppermute x12, starting transfers between devices, along(): lax.ppermute(value, 'ctx', [(a, b) for a, b in pairs if 0 <= b < ctx_count])  35.6 us
  transfers between devices with their start and end apart: 115, of which 40 were waited for; matrix products, arithmetic and copies ran while one was open for 4% of the time, Pallas kernels for 10%

profile of v3, /device:TPU:0, one launch (start us, length us, event | category | flops | bytes accessed | tf_op | source)
XLA Modules:
  0.0 1177.2 jit_solution(4721629121030562907)
XLA Ops:
  16.7 33.3 %collective-permute-done.7.refs_9_.refs_7_ = bf16[528,512]{1,0:T(8,128)(2,1)} collective-permute-done((bf16[528,512]{1,0:T(8,128)(2,1)}, bf16[528,512]{1,0:T(8,128)(2,1)}, u32[]{:S(2)}, u32[]{:S(2)}) %collective-permute-start.7) | collective-permute-done | bytes 540704 | tf_op jit(solution)/shard_map/ppermute | solution.py:435
  84.2 14.9 %collective-permute-done.17 = bf16[4,2,192,256]{3,2,1,0:T(8,128)(2,1)S(1)} collective-permute-done((bf16[4,2,192,256]{3,2,1,0:T(8,128)(2,1)}, bf16[4,2,192,256]{3,2,1,0:T(8,128)(2,1)S(1)}, u32[]{:S(2)}, u32[]{:S(2)}) %collective-permute-start.17) | collective-permute-done | bytes 786464 | tf_op jit(solution)/shard_map/ppermute | solution.py:442
  106.8 12.0 %collective-permute-done.18 = bf16[4,2,192,256]{3,2,1,0:T(8,128)(2,1)S(1)} collective-permute-done((bf16[4,2,192,256]{3,2,1,0:T(8,128)(2,1)S(1)}, bf16[4,2,192,256]{3,2,1,0:T(8,128)(2,1)S(1)}, u32[]{:S(2)}, u32[]{:S(2)}) %collective-permute-start.18) | collective-permute-done | bytes 786464 | tf_op jit(solution)/shard_map/ppermute | solution.py:442
  154.4 38.3 %collective-permute-done.11.refs_10_ = bf16[192,2048]{1,0:T(8,128)(2,1)} collective-permute-done((bf16[192,2048]{1,0:T(8,128)(2,1)S(1)}, bf16[192,2048]{1,0:T(8,128)(2,1)}, u32[]{:S(2)}, u32[]{:S(2)}) %collective-permute-start.11) | collective-permute-done | bytes 786464 | tf_op jit(solution)/shard_map/ppermute | solution.py:435
  193.3 15.0 %collective-permute-done.14.refs_17_ = bf16[768,512]{1,0:T(8,128)(2,1)} collective-permute-done((bf16[768,512]{1,0:T(8,128)(2,1)S(1)}, bf16[768,512]{1,0:T(8,128)(2,1)}, u32[]{:S(2)}, u32[]{:S(2)}) %collective-permute-start.14) | collective-permute-done | bytes 786464 | tf_op jit(solution)/shard_map/ppermute | solution.py:435
  219.8 17.3 %attend.1 = (bf16[4,2,192,256]{3,2,1,0:T(8,128)(2,1)}, bf16[192,2048]{1,0:T(8,128)(2,1)}, bf16[192,2048]{1,0:T(8,128)(2,1)}, bf16[192,2048]{1,0:T(8,128)(2,1)}, ...) custom-call(s32[2]{0:T(128)} %pad_add_fusion.me_ref, ...), custom_call_target="tpu_custom_call" | custom-call | flops 4026531840 | bytes 15235072 | tf_op jit(solution)/shard_map/attend/pallas_call | solution.py:364
  245.9 15.7 %collective-permute-done.31.refs_2_ = bf16[192,2048]{1,0:T(8,128)(2,1)S(1)} collective-permute-done((bf16[192,2048]{1,0:T(8,128)(2,1)S(1)}, bf16[192,2048]{1,0:T(8,128)(2,1)S(1)}, u32[]{:S(2)}, u32[]{:S(2)}) %collective-permute-start.31) | collective-permute-done | bytes 786464 | tf_op jit(solution)/shard_map/ppermute | solution.py:435
  261.6 16.5 %collective-permute-done.33.refs_3_ = bf16[192,2048]{1,0:T(8,128)(2,1)S(1)} collective-permute-done((bf16[192,2048]{1,0:T(8,128)(2,1)S(1)}, bf16[192,2048]{1,0:T(8,128)(2,1)S(1)}, u32[]{:S(2)}, u32[]{:S(2)}) %collective-permute-start.33) | collective-permute-done | bytes 786464 | tf_op jit(solution)/shard_map/ppermute | solution.py:435
  287.7 16.7 %collective-permute-done.36.refs_1_ = bf16[192,2048]{1,0:T(8,128)(2,1)S(1)} collective-permute-done((bf16[192,2048]{1,0:T(8,128)(2,1)}, bf16[192,2048]{1,0:T(8,128)(2,1)S(1)}, u32[]{:S(2)}, u32[]{:S(2)}) %collective-permute-start.36) | collective-permute-done | bytes 786464 | tf_op jit(solution)/shard_map/ppermute | solution.py:435
  305.3 15.3 %collective-permute-done.37.refs_2_ = bf16[192,2048]{1,0:T(8,128)(2,1)S(1)} collective-permute-done((bf16[192,2048]{1,0:T(8,128)(2,1)}, bf16[192,2048]{1,0:T(8,128)(2,1)S(1)}, u32[]{:S(2)}, u32[]{:S(2)}) %collective-permute-start.37) | collective-permute-done | bytes 786464 | tf_op jit(solution)/shard_map/ppermute | solution.py:435
  324.1 399.2 %feed_forward.1 = (bf16[192,2048]{1,0:T(8,128)(2,1)}, bf16[192,2048]{1,0:T(8,128)(2,1)}, bf16[192,2048]{1,0:T(8,128)(2,1)}, bf16[192,2048]{1,0:T(8,128)(2,1)}, b...) custom-call(bf16[192,2048]{1,0:T(8,128)(2,1)} %get-tuple-element.122, ...), custom_call_target="tpu_custom_call" | custom-call | flops 57982058496 | bytes 103022592 | tf_op jit(solution)/shard_map/feed_forward/pallas_call | solution.py:1111
  731.8 15.9 %collective-permute-done.56.refs_2_ = bf16[192,2048]{1,0:T(8,128)(2,1)S(1)} collective-permute-done((bf16[192,2048]{1,0:T(8,128)(2,1)S(1)}, bf16[192,2048]{1,0:T(8,128)(2,1)S(1)}, u32[]{:S(2)}, u32[]{:S(2)}) %collective-permute-start.56) | collective-permute-done | bytes 786464 | tf_op jit(solution)/shard_map/ppermute | solution.py:435
  747.7 16.7 %collective-permute-done.58.refs_3_ = bf16[192,2048]{1,0:T(8,128)(2,1)S(1)} collective-permute-done((bf16[192,2048]{1,0:T(8,128)(2,1)S(1)}, bf16[192,2048]{1,0:T(8,128)(2,1)S(1)}, u32[]{:S(2)}, u32[]{:S(2)}) %collective-permute-start.58) | collective-permute-done | bytes 786464 | tf_op jit(solution)/shard_map/ppermute | solution.py:435
  775.7 17.2 %collective-permute-done.61.refs_13_.refs_1_ = bf16[192,2048]{1,0:T(8,128)(2,1)S(1)} collective-permute-done((bf16[192,2048]{1,0:T(8,128)(2,1)}, bf16[192,2048]{1,0:T(8,128)(2,1)S(1)}, u32[]{:S(2)}, u32[]{:S(2)}) %collective-permute-start.61) | collective-permute-done | bytes 786464 | tf_op jit(solution)/shard_map/ppermute | solution.py:435
  792.9 15.3 %collective-permute-done.62.refs_14_.refs_2_ = bf16[192,2048]{1,0:T(8,128)(2,1)S(1)} collective-permute-done((bf16[192,2048]{1,0:T(8,128)(2,1)}, bf16[192,2048]{1,0:T(8,128)(2,1)S(1)}, u32[]{:S(2)}, u32[]{:S(2)}) %collective-permute-start.62) | collective-permute-done | bytes 786464 | tf_op jit(solution)/shard_map/ppermute | solution.py:435
  812.3 20.2 %attend_back.1 = (bf16[4,2,192,256]{3,2,1,0:T(8,128)(2,1)}, bf16[4,2,192,256]{3,2,1,0:T(8,128)(2,1)}, bf16[4,2,192,256]{3,2,1,0:T(8,128)(2,1)}, bf16[4,2,192,256...) custom-call(s32[2]{0:T(128)} %pad_add_fusion.me_ref, ...), custom_call_target="tpu_custom_call" | custom-call | flops 7650410496 | bytes 22312960 | tf_op jit(solution)/shard_map/attend_back/pallas_call | solution.py:364
  842.1 14.6 %collective-permute-done.75 = bf16[4,2,192,256]{3,2,1,0:T(8,128)(2,1)} collective-permute-done((bf16[4,2,192,256]{3,2,1,0:T(8,128)(2,1)}, bf16[4,2,192,256]{3,2,1,0:T(8,128)(2,1)}, u32[]{:S(2)}, u32[]{:S(2)}) %collective-permute-start.75) | collective-permute-done | bytes 786464 | tf_op jit(solution)/shard_map/ppermute | solution.py:442
  873.1 14.5 %collective-permute-done.73 = bf16[4,2,192,256]{3,2,1,0:T(8,128)(2,1)} collective-permute-done((bf16[4,2,192,256]{3,2,1,0:T(8,128)(2,1)}, bf16[4,2,192,256]{3,2,1,0:T(8,128)(2,1)}, u32[]{:S(2)}, u32[]{:S(2)}) %collective-permute-start.73) | collective-permute-done | bytes 786464 | tf_op jit(solution)/shard_map/ppermute | solution.py:442
  940.1 16.6 %collective-permute-done.85 = bf16[4,256,512]{2,1,0:T(8,128)(2,1)S(1)} collective-permute-done((bf16[4,256,512]{2,1,0:T(8,128)(2,1)}, bf16[4,256,512]{2,1,0:T(8,128)(2,1)S(1)}, u32[]{:S(2)}, u32[]{:S(2)}) %collective-permute-start.85) | collective-permute-done | bytes 1048608 | tf_op jit(solution)/shard_map/ppermute | solution.py:445
  981.0 12.9 %collective-permute-done.80.refs_2_ = bf16[192,2048]{1,0:T(8,128)(2,1)} collective-permute-done((bf16[192,2048]{1,0:T(8,128)(2,1)S(1)}, bf16[192,2048]{1,0:T(8,128)(2,1)}, u32[]{:S(2)}, u32[]{:S(2)}) %collective-permute-start.80) | collective-permute-done | bytes 786464 | tf_op jit(solution)/shard_map/ppermute | solution.py:435
  993.9 16.8 %collective-permute-done.82.refs_3_ = bf16[192,2048]{1,0:T(8,128)(2,1)} collective-permute-done((bf16[192,2048]{1,0:T(8,128)(2,1)S(1)}, bf16[192,2048]{1,0:T(8,128)(2,1)}, u32[]{:S(2)}, u32[]{:S(2)}) %collective-permute-start.82) | collective-permute-done | bytes 786464 | tf_op jit(solution)/shard_map/ppermute | solution.py:435
  1033.8 15.7 %collective-permute-done.91.refs_3_ = bf16[4,256,512]{2,1,0:T(8,128)(2,1)S(1)} collective-permute-done((bf16[4,256,512]{2,1,0:T(8,128)(2,1)S(1)}, bf16[4,256,512]{2,1,0:T(8,128)(2,1)S(1)}, u32[]{:S(2)}, u32[]{:S(2)}) %collective-permute-start.91) | collective-permute-done | bytes 1048608 | tf_op jit(solution)/shard_map/ppermute | solution.py:445
  1056.4 14.4 %collective-permute-done.90.refs_2_ = bf16[4,256,512]{2,1,0:T(8,128)(2,1)S(1)} collective-permute-done((bf16[4,256,512]{2,1,0:T(8,128)(2,1)S(1)}, bf16[4,256,512]{2,1,0:T(8,128)(2,1)S(1)}, u32[]{:S(2)}, u32[]{:S(2)}) %collective-permute-start.90) | collective-permute-done | bytes 1048608 | tf_op jit(solution)/shard_map/ppermute | solution.py:445
  1098.2 45.8 %place_hidden.1 = (f32[512,8192]{1,0:T(8,128)}, f32[512,8192]{1,0:T(8,128)}, f32[8192,512]{1,0:T(8,128)}) custom-call(s32[2]{0:T(128)} %pad_add_fusion.me_ref, bf16[12,4,256,512]{3,2,1,0:T(8,128)(2,1)} %bitcast.31, bf16[12,4,256,512]{3,2,1,0:T(8,128)(2,1)} %bitcast.32), custom_call_target="tpu_custom_call" | custom-call | bytes 75497472 | tf_op jit(solution)/shard_map/place_hidden/pallas_call | solution.py:364
  (445 shorter events, 344.3 us)
Async XLA Ops:
  0.6 49.4 %collective-permute-start = (bf16[192,2048]{1,0:T(8,128)(2,1)}, bf16[192,2048]{1,0:T(8,128)(2,1)S(1)}, u32[]{:S(2)}, u32[]{:S(2)}) collective-permute-start(bf16[192,2048]{1,0:T(8,128)(2,1)} %bitcast.33), channel_id=1, source_target_pairs={{0,1},{1,0},{2,3},{3,2},{4,5},{5,4},{6,7},{7,6},{8,9},{9,8},{10,11... | collective-permute-start | bytes 2359304 | tf_op jit(solution)/shard_map/ppermute | solution.py:435
  3.6 46.9 %collective-permute-start.1 = (bf16[192,2048]{1,0:T(8,128)(2,1)}, bf16[192,2048]{1,0:T(8,128)(2,1)S(1)}, u32[]{:S(2)}, u32[]{:S(2)}) collective-permute-start(bf16[192,2048]{1,0:T(8,128)(2,1)} %bitcast.34), channel_id=1, source_target_pairs={{0,2},{1,3},{2,0},{3,1},{4,6},{5,7},{6,4},{7,5},{8,10},{9,11},{10,... | collective-permute-start | bytes 2359304 | tf_op jit(solution)/shard_map/ppermute | solution.py:435
  5.2 45.4 %collective-permute-start.2 = (bf16[192,2048]{1,0:T(8,128)(2,1)}, bf16[192,2048]{1,0:T(8,128)(2,1)}, u32[]{:S(2)}, u32[]{:S(2)}) collective-permute-start(bf16[192,2048]{1,0:T(8,128)(2,1)} %bitcast.35), channel_id=1, source_target_pairs={{0,3},{1,2},{2,1},{3,0},{4,7},{5,6},{6,5},{7,4},{8,11},{9,10},{10,... | collective-permute-start | bytes 2359304 | tf_op jit(solution)/shard_map/ppermute | solution.py:435
  141.8 50.9 %collective-permute-start.11 = (bf16[192,2048]{1,0:T(8,128)(2,1)S(1)}, bf16[192,2048]{1,0:T(8,128)(2,1)}, u32[]{:S(2)}, u32[]{:S(2)}) collective-permute-start(bf16[192,2048]{1,0:T(8,128)(2,1)S(1)} %bitcast.43), channel_id=1, source_target_pairs={{0,2},{1,3},{2,0},{3,1},{4,6},{5,7},{6,4},{7,5},{8,10},{9,11},{10,... | collective-permute-start | bytes 2359304 | tf_op jit(solution)/shard_map/ppermute | solution.py:435
  142.3 50.4 %collective-permute-start.12 = (bf16[192,2048]{1,0:T(8,128)(2,1)S(1)}, bf16[192,2048]{1,0:T(8,128)(2,1)}, u32[]{:S(2)}, u32[]{:S(2)}) collective-permute-start(bf16[192,2048]{1,0:T(8,128)(2,1)S(1)} %bitcast.44), channel_id=1, source_target_pairs={{0,3},{1,2},{2,1},{3,0},{4,7},{5,6},{6,5},{7,4},{8,11},{9,10},{10,... | collective-permute-start | bytes 2359304 | tf_op jit(solution)/shard_map/ppermute | solution.py:435
  143.7 49.5 %collective-permute-start.13 = (bf16[768,512]{1,0:T(8,128)(2,1)}, bf16[768,512]{1,0:T(8,128)(2,1)}, u32[]{:S(2)}, u32[]{:S(2)}) collective-permute-start(bf16[768,512]{1,0:T(8,128)(2,1)} %get-tuple-element.193), channel_id=1, source_target_pairs={{0,1},{1,0},{2,3},{3,2},{4,5},{5,4},{6,7},{7,6},{8,9},{9,8},{10,11... | collective-permute-start | bytes 2359304 | tf_op jit(solution)/shard_map/ppermute | solution.py:435
  145.3 63.0 %collective-permute-start.14 = (bf16[768,512]{1,0:T(8,128)(2,1)S(1)}, bf16[768,512]{1,0:T(8,128)(2,1)}, u32[]{:S(2)}, u32[]{:S(2)}) collective-permute-start(bf16[768,512]{1,0:T(8,128)(2,1)S(1)} %get-tuple-element.192), channel_id=1, source_target_pairs={{0,2},{1,3},{2,0},{3,1},{4,6},{5,7},{6,4},{7,5},{8,10},{9,11},{10,... | collective-permute-start | bytes 2359304 | tf_op jit(solution)/shard_map/ppermute | solution.py:435
  145.8 63.2 %collective-permute-start.15 = (bf16[768,512]{1,0:T(8,128)(2,1)S(1)}, bf16[768,512]{1,0:T(8,128)(2,1)}, u32[]{:S(2)}, u32[]{:S(2)}) collective-permute-start(bf16[768,512]{1,0:T(8,128)(2,1)S(1)} %get-tuple-element.191), channel_id=1, source_target_pairs={{0,3},{1,2},{2,1},{3,0},{4,7},{5,6},{6,5},{7,4},{8,11},{9,10},{10,... | collective-permute-start | bytes 2359304 | tf_op jit(solution)/shard_map/ppermute | solution.py:435
  245.4 40.5 %collective-permute-start.43 = (bf16[192,2048]{1,0:T(8,128)(2,1)S(1)}, bf16[192,2048]{1,0:T(8,128)(2,1)S(1)}, u32[]{:S(2)}, u32[]{:S(2)}) collective-permute-start(bf16[192,2048]{1,0:T(8,128)(2,1)S(1)} %bitcast.45), channel_id=1, source_target_pairs={{0,4},{4,0},{8,12},{12,8},{16,20},{20,16},{24,28},{28,24},{1,5},{5... | collective-permute-start | bytes 2359304 | tf_op jit(solution)/shard_map/ppermute | solution.py:438
  245.4 41.8 %collective-permute-start.44 = (bf16[192,2048]{1,0:T(8,128)(2,1)}, bf16[192,2048]{1,0:T(8,128)(2,1)}, u32[]{:S(2)}, u32[]{:S(2)}) collective-permute-start(bf16[192,2048]{1,0:T(8,128)(2,1)} %collective-permute-done.10.refs_9_), channel_id=1, source_target_pairs={{0,4},{4,0},{8,12},{12,8},{16,20},{20,16},{24,28},{28,24},{1,5},{5... | collective-permute-start | bytes 2359304 | tf_op jit(solution)/shard_map/ppermute | solution.py:438
  873.1 41.6 %collective-permute-start.68 = (bf16[4,2,192,256]{3,2,1,0:T(8,128)(2,1)}, bf16[4,2,192,256]{3,2,1,0:T(8,128)(2,1)S(1)}, u32[]{:S(2)}, u32[]{:S(2)}) collective-permute-start(bf16[4,2,192,256]{3,2,1,0:T(8,128)(2,1)} %get-tuple-element.148), channel_id=1, source_target_pairs={{0,4},{4,0},{8,12},{12,8},{16,20},{20,16},{24,28},{28,24},{1,5},{5... | collective-permute-start | bytes 2359304 | tf_op jit(solution)/shard_map/ppermute | solution.py:438
  913.1 43.6 %collective-permute-start.85 = (bf16[4,256,512]{2,1,0:T(8,128)(2,1)}, bf16[4,256,512]{2,1,0:T(8,128)(2,1)S(1)}, u32[]{:S(2)}, u32[]{:S(2)}) collective-permute-start(bf16[4,256,512]{2,1,0:T(8,128)(2,1)} %query_outer.1), channel_id=1, source_target_pairs={{0,8},{4,12},{24,16},{28,20},{1,9},{5,13},{25,17},{29,21},{2,10},{... | collective-permute-start | bytes 3145736 | tf_op jit(solution)/shard_map/ppermute | solution.py:445
  926.7 46.6 %collective-permute-start.52 = (bf16[192,2048]{1,0:T(8,128)(2,1)}, bf16[192,2048]{1,0:T(8,128)(2,1)}, u32[]{:S(2)}, u32[]{:S(2)}) collective-permute-start(bf16[192,2048]{1,0:T(8,128)(2,1)} %get-tuple-element.136), channel_id=1, source_target_pairs={{0,4},{4,0},{8,12},{12,8},{16,20},{20,16},{24,28},{28,24},{1,5},{5... | collective-permute-start | bytes 2359304 | tf_op jit(solution)/shard_map/ppermute | solution.py:438
  967.3 51.7 %collective-permute-start.87 = (bf16[4,256,512]{2,1,0:T(8,128)(2,1)S(1)}, bf16[4,256,512]{2,1,0:T(8,128)(2,1)S(1)}, u32[]{:S(2)}, u32[]{:S(2)}) collective-permute-start(bf16[4,256,512]{2,1,0:T(8,128)(2,1)S(1)} %copy-done.5), channel_id=1, source_target_pairs={{0,8},{4,12},{24,16},{28,20},{1,9},{5,13},{25,17},{29,21},{2,10},{... | collective-permute-start | bytes 3145736 | tf_op jit(solution)/shard_map/ppermute | solution.py:445
  979.1 41.7 %collective-permute-start.50 = (bf16[192,2048]{1,0:T(8,128)(2,1)}, bf16[192,2048]{1,0:T(8,128)(2,1)}, u32[]{:S(2)}, u32[]{:S(2)}) collective-permute-start(bf16[192,2048]{1,0:T(8,128)(2,1)} %get-tuple-element.134), channel_id=1, source_target_pairs={{0,4},{4,0},{8,12},{12,8},{16,20},{20,16},{24,28},{28,24},{1,5},{5... | collective-permute-start | bytes 2359304 | tf_op jit(solution)/shard_map/ppermute | solution.py:438
  1022.9 48.0 %collective-permute-start.90 = (bf16[4,256,512]{2,1,0:T(8,128)(2,1)S(1)}, bf16[4,256,512]{2,1,0:T(8,128)(2,1)S(1)}, u32[]{:S(2)}, u32[]{:S(2)}) collective-permute-start(bf16[4,256,512]{2,1,0:T(8,128)(2,1)S(1)} %add_convert_fusion.4.refs_0_), channel_id=1, source_target_pairs={{8,0},{12,4},{16,24},{20,28},{9,1},{13,5},{17,25},{21,29},{10,2},{... | collective-permute-start | bytes 3145736 | tf_op jit(solution)/shard_map/ppermute | solution.py:445
  1029.9 47.3 %collective-permute-start.53 = (bf16[192,2048]{1,0:T(8,128)(2,1)}, bf16[192,2048]{1,0:T(8,128)(2,1)}, u32[]{:S(2)}, u32[]{:S(2)}) collective-permute-start(bf16[192,2048]{1,0:T(8,128)(2,1)} %add_convert_fusion.21), channel_id=1, source_target_pairs={{0,3},{1,2},{2,1},{3,0},{4,7},{5,6},{6,5},{7,4},{8,11},{9,10},{10,... | collective-permute-start | bytes 2359304 | tf_op jit(solution)/shard_map/ppermute | solution.py:435
  1031.3 46.6 %collective-permute-start.51 = (bf16[192,2048]{1,0:T(8,128)(2,1)}, bf16[192,2048]{1,0:T(8,128)(2,1)}, u32[]{:S(2)}, u32[]{:S(2)}) collective-permute-start(bf16[192,2048]{1,0:T(8,128)(2,1)} %add_convert_fusion.22), channel_id=1, source_target_pairs={{0,2},{1,3},{2,0},{3,1},{4,6},{5,7},{6,4},{7,5},{8,10},{9,11},{10,... | collective-permute-start | bytes 2359304 | tf_op jit(solution)/shard_map/ppermute | solution.py:435
  1032.0 47.2 %collective-permute-start.49 = (bf16[192,2048]{1,0:T(8,128)(2,1)}, bf16[192,2048]{1,0:T(8,128)(2,1)}, u32[]{:S(2)}, u32[]{:S(2)}) collective-permute-start(bf16[192,2048]{1,0:T(8,128)(2,1)} %add_convert_fusion.23), channel_id=1, source_target_pairs={{0,1},{1,0},{2,3},{3,2},{4,5},{5,4},{6,7},{7,6},{8,9},{9,8},{10,11... | collective-permute-start | bytes 2359304 | tf_op jit(solution)/shard_map/ppermute | solution.py:435
  1077.8 68.9 %collective-permute-start.93 = (bf16[2,256,512]{2,1,0:T(8,128)(2,1)}, bf16[2,256,512]{2,1,0:T(8,128)(2,1)S(1)}, u32[]{:S(2)}, u32[]{:S(2)}) collective-permute-start(bf16[2,256,512]{2,1,0:T(8,128)(2,1)} %get-tuple-element.173), channel_id=1, source_target_pairs={{0,2},{1,3},{2,0},{3,1},{4,6},{5,7},{6,4},{7,5},{8,10},{9,11},{10,... | collective-permute-start | bytes 1572872 | tf_op jit(solution)/shard_map/ppermute | solution.py:435
  1079.2 67.6 %collective-permute-start.94 = (bf16[2,256,512]{2,1,0:T(8,128)(2,1)}, bf16[2,256,512]{2,1,0:T(8,128)(2,1)S(1)}, u32[]{:S(2)}, u32[]{:S(2)}) collective-permute-start(bf16[2,256,512]{2,1,0:T(8,128)(2,1)} %get-tuple-element.174), channel_id=1, source_target_pairs={{0,3},{1,2},{2,1},{3,0},{4,7},{5,6},{6,5},{7,4},{8,11},{9,10},{10,... | collective-permute-start | bytes 1572872 | tf_op jit(solution)/shard_map/ppermute | solution.py:435
  1080.7 67.2 %collective-permute-start.95 = (bf16[2,256,512]{2,1,0:T(8,128)(2,1)}, bf16[2,256,512]{2,1,0:T(8,128)(2,1)S(1)}, u32[]{:S(2)}, u32[]{:S(2)}) collective-permute-start(bf16[2,256,512]{2,1,0:T(8,128)(2,1)} %get-tuple-element.171.refs_0_), channel_id=1, source_target_pairs={{0,4},{4,0},{8,12},{12,8},{16,20},{20,16},{24,28},{28,24},{1,5},{5... | collective-permute-start | bytes 1572872 | tf_op jit(solution)/shard_map/ppermute | solution.py:438
  1091.6 57.7 %collective-permute-start.96 = (bf16[2,256,512]{2,1,0:T(8,128)(2,1)S(1)}, bf16[2,256,512]{2,1,0:T(8,128)(2,1)}, u32[]{:S(2)}, u32[]{:S(2)}) collective-permute-start(bf16[2,256,512]{2,1,0:T(8,128)(2,1)S(1)} %collective-permute-done.92.refs_1_), channel_id=1, source_target_pairs={{0,4},{4,0},{8,12},{12,8},{16,20},{20,16},{24,28},{28,24},{1,5},{5... | collective-permute-start | bytes 1572872 | tf_op jit(solution)/shard_map/ppermute | solution.py:438
  1096.9 50.4 %collective-permute-start.114 = (f32[2,512]{1,0:T(2,128)S(1)}, f32[2,512]{1,0:T(2,128)S(1)}, u32[]{:S(2)}, u32[]{:S(2)}) collective-permute-start(f32[2,512]{1,0:T(2,128)S(1)} %add.273), channel_id=1, source_target_pairs={{8,0},{12,4},{16,24},{20,28},{9,1},{13,5},{17,25},{21,29},{10,2},{... | collective-permute-start | bytes 12296 | tf_op jit(solution)/shard_map/ppermute | solution.py:445
  (170 other events, 2979.8 us)

commit v4 on v3

--- a/solution.py
+++ b/solution.py
@@ -1,4 +1,5 @@
 import functools
+import types
 
 import jax
 import jax.numpy as jnp
@@ -322,6 +323,7 @@
 F32 = jnp.float32
 QUARTERS = 4
 MESH = pl.DeviceIdType.MESH
+TICKS = (1, 1, 1, 2, 4, 2, 1, 2, 1, 3, 2, 1, 1)
 LINES = 2
 
 
@@ -711,48 +713,123 @@
     two_own, two_near = gathered(own_normed_two)
 
     tile = plane_rows // 3
-    tiles_count = 3 * QUARTERS
+    tiles_count = 3 * QUARTERS + 3
+    query_at, output_at, kv_at = tiles_count - 3, tiles_count - 2, tiles_count - 1
     units = 2 * tiles_count
     unit = (2, quarter, wide)
     held_sums, held_ends = 4, 3
-
-    def feed_forward(*refs):
-        two_refs, cot_refs, first_refs = refs[: 2 * n], refs[2 * n : 4 * n], refs[4 * n : 5 * n - 1]
-        cut_ref = refs[5 * n - 1]
-        back_refs, out_refs = refs[5 * n : 7 * n], refs[7 * n : 9 * n]
-        tiles, from_end, from_middle, finals, owned_ref, near_ref = refs[9 * n : 9 * n + 6]
-        (
-            work,
-            feed,
-            hidden,
-            turned,
-            stage,
-            mine,
-            theirs,
-            crossed,
-            sums,
-            ends,
-            load_sem,
-            feed_local,
-            feed_send,
-            feed_recv,
-            stage_sem,
-            one_send,
-            one_recv,
-            two_send,
-            two_recv,
-            three_send,
-            three_recv,
-            mine_sem,
-            theirs_sem,
-            crossed_sem,
-            final_sem,
-            deal_local,
-            deal_send,
-            deal_recv,
-            near_send,
-            near_recv,
-        ) = refs[9 * n + 6 :]
+    BACK, OUT, ONE = range(3)
+    columns = (plane_rows, HD)
+    lanes = (8, wide)
+    dma = pltpu.SemaphoreType.DMA
+
+    in_hbm = dict(
+        two=two_own + two_near,
+        cot=cot_own + cot_near,
+        first=first_pieces,
+        in_weight=weights_in,
+        out_weight=weights_out,
+        kv_mine=[a.reshape(columns) for a in kv_mine],
+        kv_near=[a.reshape(columns) for a in kv_near],
+        cut=hidden_cut,
+        query=query_rot.reshape(columns),
+        attended=attended.reshape(columns),
+        normed=normed.reshape(plane_rows, width),
+        middle=middle,
+        tokens=own_tokens,
+    )
+    in_vmem = dict(
+        gains=gains,
+        tables=jnp.stack([cosine, sine, kv_cosine, kv_sine]),
+        query_ids=query_ids,
+        key_ids=key_ids,
+    )
+    unit_array = shape((units,) + unit)
+    out_hbm = dict(
+        tiles=unit_array,
+        from_end=unit_array,
+        from_middle=unit_array,
+        finals=unit_array,
+        owned=unit_array,
+        near=unit_array,
+        row_near=shape((3, n) + block),
+        row_far=shape((3, n) + block),
+        branch_all=shape((n, 2) + block),
+        kv_other=shape((planes,) + columns),
+        kv_down=shape((planes,) + columns),
+        kv_up=shape((planes,) + columns),
+        out_own=shape(block),
+        tokens_grad=shape(block, F32),
+        gain_out=shape(lanes, F32),
+    )
+    scratch = dict(
+        work=pltpu.VMEM((2 * plane_rows, width), BF16),
+        feed=pltpu.VMEM((QUARTERS, n) + piece, BF16),
+        heads=pltpu.VMEM((3 * QUARTERS, plane_rows, HD), BF16),
+        turned=pltpu.VMEM((3, HD, plane_rows), BF16),
+        stage=pltpu.VMEM((2, n, quarter, wide), BF16),
+        mine=pltpu.VMEM((2,) + unit, BF16),
+        theirs=pltpu.VMEM((2,) + unit, BF16),
+        crossed=pltpu.VMEM((2,) + unit, BF16),
+        sums=pltpu.VMEM((held_sums,) + unit, BF16),
+        ends=pltpu.VMEM((held_ends,) + unit, BF16),
+        some_rows=pltpu.VMEM((n,) + block, BF16),
+        wide_rows=pltpu.VMEM(block, F32),
+        own_rows=pltpu.VMEM(block, BF16),
+        kv_some=pltpu.VMEM((2,) + columns, BF16),
+        flat=pltpu.VMEM((8, width), F32),
+        gain_mine=pltpu.VMEM((n,) + lanes, F32),
+        gain_far=pltpu.VMEM((n,) + lanes, F32),
+        gain_sum=pltpu.VMEM((4,) + lanes, F32),
+        gain_in=pltpu.VMEM((4,) + lanes, F32),
+        load_sem=dma((4 * n + n - 1,)),
+        feed_local=dma((QUARTERS,)),
+        feed_send=dma((QUARTERS * n,)),
+        feed_recv=dma((QUARTERS * n,)),
+        stage_sem=dma((2, 2)),
+        one_send=dma((units,)),
+        one_recv=dma((units,)),
+        two_send=dma((units,)),
+        two_recv=dma((units,)),
+        three_send=dma((units,)),
+        three_recv=dma((units,)),
+        mine_sem=dma((2,)),
+        theirs_sem=dma((2,)),
+        crossed_sem=dma((2,)),
+        final_sem=dma((held_ends,)),
+        deal_local=dma((units,)),
+        deal_send=dma((2 * units,)),
+        deal_recv=dma((2 * units,)),
+        sib_send=dma((units,)),
+        sib_recv=dma((units,)),
+        row_sem=dma((n,)),
+        row_near_send=dma((3 * n,)),
+        row_near_recv=dma((3 * n,)),
+        row_far_send=dma((3 * n,)),
+        row_far_recv=dma((3 * n,)),
+        branch_local=dma((1,)),
+        branch_send=dma((n,)),
+        branch_recv=dma((n,)),
+        branch_near_send=dma((n,)),
+        branch_near_recv=dma((n,)),
+        kv_sem=dma((2,)),
+        kv_send=dma((planes,)),
+        kv_recv=dma((planes,)),
+        down_send=dma((planes,)),
+        down_recv=dma((planes,)),
+        up_send=dma((planes,)),
+        up_recv=dma((planes,)),
+        gain_send=dma((n + 4,)),
+        gain_recv=dma((n + 4,)),
+    )
+
+    def backward(*refs):
+        r, first = types.SimpleNamespace(), 0
+        for group in (in_hbm, in_vmem, out_hbm):
+            leaves, form = jax.tree.flatten(group)
+            vars(r).update(jax.tree.unflatten(form, refs[first : first + len(leaves)]))
+            first += len(leaves)
+        vars(r).update(zip(scratch, refs[first:]))
         here = lax.axis_index("ctx")
         chip = lax.axis_index("fsdp")
         z, side = here // 2, here % 2
@@ -761,11 +838,13 @@
         chips = [chip, chip + 1 - 2 * (chip % 2), (chip + 2) % 4, 3 - chip]
         partner = (2 * (z + 1 - 2 * (z % 2)) + side, chip)
         other_middle = (2 * (3 - z) + side, chip)
-        sibling_core = (here + 1 - 2 * side, chip)
+        other_core = (here + 1 - 2 * side, chip)
+        below, above = (here - 2, chip), (here + 2, chip)
         blocks = [pl.ds(pl.multiple_of(c * wide, wide), wide) for c in chips]
+        work, feed, heads, turned, stage = r.work, r.feed, r.heads, r.turned, r.stage
 
         barrier = pltpu.get_barrier_semaphore()
-        for peer in [(here, c) for c in chips[1:]] + [partner, sibling_core]:
+        for peer in [(here, c) for c in chips[1:]] + [partner, other_core]:
             pl.semaphore_signal(barrier, inc=1, device_id=peer, device_id_type=MESH)
 
         @pl.when(is_middle)
@@ -787,67 +866,68 @@
                 device_id_type=MESH,
             )
 
+        local = pltpu.make_async_copy
+
+        def span(first, count):
+            return pl.ds(pl.multiple_of(first, count), count)
+
         def feed_copy(q, d):
             at = q * n + d
             return remote(
-                cut_ref.at[q, d], feed.at[q, d], feed_send.at[at], feed_recv.at[at], (here, chips[d])
+                r.cut.at[q, d], feed.at[q, d], r.feed_send.at[at], r.feed_recv.at[at], (here, chips[d])
             )
 
         def feed_own(q):
-            return pltpu.make_async_copy(cut_ref.at[q, 0], feed.at[q, 0], feed_local.at[q])
+            return local(r.cut.at[q, 0], feed.at[q, 0], r.feed_local.at[q])
 
         def hop_one(i):
-            return remote(tiles.at[i], from_end.at[i], one_send.at[i], one_recv.at[i], partner)
+            return remote(r.tiles.at[i], r.from_end.at[i], r.one_send.at[i], r.one_recv.at[i], partner)
 
         def hop_two(i):
             return remote(
-                sums.at[i % held_sums],
-                from_middle.at[i],
-                two_send.at[i],
-                two_recv.at[i],
+                r.sums.at[i % held_sums],
+                r.from_middle.at[i],
+                r.two_send.at[i],
+                r.two_recv.at[i],
                 other_middle,
             )
 
         def hop_three(i):
             return remote(
-                ends.at[i % held_ends], finals.at[i], three_send.at[i], three_recv.at[i], partner
+                r.ends.at[i % held_ends], r.finals.at[i], r.three_send.at[i], r.three_recv.at[i], partner
             )
 
         def load_mine(i):
-            return pltpu.make_async_copy(tiles.at[i], mine.at[i % 2], mine_sem.at[i % 2])
+            return local(r.tiles.at[i], r.mine.at[i % 2], r.mine_sem.at[i % 2])
 
         def load_theirs(i):
-            return pltpu.make_async_copy(from_end.at[i], theirs.at[i % 2], theirs_sem.at[i % 2])
+            return local(r.from_end.at[i], r.theirs.at[i % 2], r.theirs_sem.at[i % 2])
 
         def load_crossed(i):
-            return pltpu.make_async_copy(from_middle.at[i], crossed.at[i % 2], crossed_sem.at[i % 2])
+            return local(r.from_middle.at[i], r.crossed.at[i % 2], r.crossed_sem.at[i % 2])
 
         def keep_final(i):
-            return pltpu.make_async_copy(
-                ends.at[i % held_ends], finals.at[i], final_sem.at[i % held_ends]
-            )
+            return local(r.ends.at[i % held_ends], r.finals.at[i], r.final_sem.at[i % held_ends])
 
         def keep_own(i):
-            return pltpu.make_async_copy(finals.at[i, 0], owned_ref.at[i, 0], deal_local.at[i])
+            return local(r.finals.at[i, 0], r.owned.at[i, 0], r.deal_local.at[i])
 
         def deal_to(i, b, d):
             at = 2 * i + b
             return remote(
-                finals.at[i, b],
-                owned_ref.at[i, b],
-                deal_send.at[at],
-                deal_recv.at[at],
+                r.finals.at[i, b],
+                r.owned.at[i, b],
+                r.deal_send.at[at],
+                r.deal_recv.at[at],
                 (here, chips[d]),
             )
 
         def to_sibling(i):
-            return remote(
-                owned_ref.at[i], near_ref.at[i], near_send.at[i], near_recv.at[i], sibling_core
-            )
+            return remote(r.owned.at[i], r.near.at[i], r.sib_send.at[i], r.sib_recv.at[i], other_core)
 
         def add(target, a, b):
-            def some(r, _):
-                at = (r // 4, pl.ds(pl.multiple_of((r % 4) * (quarter // 4), quarter // 4), quarter // 4))
+            def some(s, _):
+                at = (s // 4, span((s % 4) * (quarter // 4), quarter // 4))
                 target[at] = (a[at].astype(F32) + b[at].astype(F32)).astype(BF16)
                 return 0
 
@@ -856,7 +936,7 @@
         def when_in(i, *conditions):
             return pl.when(functools.reduce(jnp.logical_and, conditions, (i >= 0) & (i < units)))
 
-        def advance(i):
+        def step(i, _=0):
             @when_in(i - 1, is_middle)
             def _():
                 at = i - 1
@@ -867,7 +947,7 @@
                 def _():
                     hop_two(at - held_sums).wait_send()
 
-                add(sums.at[at % held_sums], mine.at[at % 2], theirs.at[at % 2])
+                add(r.sums.at[at % held_sums], r.mine.at[at % 2], r.theirs.at[at % 2])
                 hop_two(at).start()
 
             @when_in(i - 4, is_middle)
@@ -879,7 +959,7 @@
                 def _():
                     hop_three(at - held_ends).wait_send()
 
-                add(ends.at[at % held_ends], sums.at[at % held_sums], crossed.at[at % 2])
+                add(r.ends.at[at % held_ends], r.sums.at[at % held_sums], r.crossed.at[at % 2])
                 hop_three(at).start()
                 keep_final(at).start()
 
@@ -930,6 +1010,15 @@
 
                 deal_to(at, 1, 3).wait_recv()
                 to_sibling(at).start()
+
+            return 0
+
+        steps_done = [0]
+
+        def advance(count):
+            first = steps_done[0]
+            steps_done[0] = first + count
+            lax.fori_loop(first, first + count, step, 0)
 
         def finish():
             def one(i, _):
@@ -955,35 +1044,143 @@
 
             lax.fori_loop(0, units, one, 0)
 
+        def stage_copy(t, h):
+            return local(r.stage.at[t % 2, pl.ds(2 * h, 2)], r.tiles.at[2 * t + h], r.stage_sem.at[t % 2, h])
+
+        def staged(t):
+            for h in range(2):
+                stage_copy(t, h).wait()
+
+            @pl.when(is_end)
+            def _():
+                for h in range(2):
+                    hop_one(2 * t + h).start()
+
+        def outer(t, left, right_rows):
+            for j in range(n):
+                stage[t % 2, j] = matmul(left, work[right_rows, blocks[j]]).astype(BF16)
+            for h in range(2):
+                stage_copy(t, h).start()
+
+        def row_near(s, base, d):
+            at = s * n + d
+            return remote(
+                work.at[pl.ds(base + (n + d) * rows, rows)],
+                r.row_near.at[s, d],
+                r.row_near_send.at[at],
+                r.row_near_recv.at[at],
+                other_core,
+            )
+
+        def row_far(s, base, d):
+            at = s * n + d
+            return remote(
+                work.at[pl.ds(base + d * rows, rows)],
+                r.row_far.at[s, d],
+                r.row_far_send.at[at],
+                r.row_far_recv.at[at],
+                (here, chips[d]),
+            )
+
+        def near_load(s, d):
+            return local(r.row_near.at[s, d], r.some_rows.at[d], r.row_sem.at[d])
+
+        def far_load(s, d):
+            return local(r.row_far.at[s, d], r.some_rows.at[d], r.row_sem.at[d])
+
+        few = 16
+
+        def rows_hand_over(s, base):
+            for d in (3, 1, 2, 0):
+                row_near(s, base, d).start()
+
+        def rows_send(s, base):
+            for d in (3, 1, 2):
+                row_near(s, base, d).wait_recv()
+                near_load(s, d).start()
+            for d in (3, 1, 2):
+                near_load(s, d).wait()
+
+                def some(c, _, d=d):
+                    at = span(c * few, few)
+                    own = pl.ds(pl.multiple_of(base + d * rows + c * few, few), few)
+                    work[own, :] = (
+                        work[own, :].astype(F32) + r.some_rows[d, at, :].astype(F32)
+                    ).astype(BF16)
+                    return 0
+
+                lax.fori_loop(0, rows // few, some, 0)
+                row_far(s, base, d).start()
+
+        def rows_arrive(s, base):
+            row_near(s, base, 0).wait_recv()
+            near_load(s, 0).start()
+            for d in range(1, n):
+                row_far(s, base, d).wait_recv()
+                far_load(s, d).start()
+            near_load(s, 0).wait()
+            for d in range(1, n):
+                far_load(s, d).wait()
+
+        def rows_sent(s, base):
+            for d in range(n):
+                row_near(s, base, d).wait_send()
+            for d in range(1, n):
+                row_far(s, base, d).wait_send()
+
+        def norm_rows_back(base, value_ref, gain_row, use):
+            r.flat[...] = jnp.zeros_like(r.flat)
+
+            def some(c, _):
+                at = span(c * few, few)
+                grad = work[pl.ds(pl.multiple_of(base + c * few, few), few), :].astype(F32)
+                for d in range(n):
+                    grad += r.some_rows[d, at, :].astype(F32)
+                values = value_ref[at, :].astype(F32)
+                inverse = lax.rsqrt(jnp.mean(values * values, axis=-1, keepdims=True) + epsilon)
+                unit_rows = values * inverse
+                scaled = grad * gain_row
+                back = inverse * (
+                    scaled - unit_rows * jnp.mean(scaled * unit_rows, axis=-1, keepdims=True)
+                )
+                use(at, back)
+                terms = grad * unit_rows
+                r.flat[...] += terms[:8] + terms[8:]
+                return 0
+
+            lax.fori_loop(0, rows // few, some, 0)
+
+        def gain_terms(at):
+            total = jnp.sum(r.flat[...], axis=0, keepdims=True)
+            r.flat[0:1, :] = total
+            for j in range(n):
+                r.gain_mine[j, at : at + 1, :] = r.flat[0:1, blocks[j]]
+
+        r.gain_mine[...] = jnp.zeros_like(r.gain_mine)
         loads = []
-        for base, sources in ((0, two_refs), (plane_rows, cot_refs)):
+
+        def load(source, target):
+            copy = local(source, target, r.load_sem.at[len(loads)])
+            copy.start()
+            loads.append(copy)
+
+        def loaded():
+            while loads:
+                loads.pop().wait()
+
+        for base, sources in ((0, r.two), (plane_rows, r.cot)):
             for i in range(2 * n):
-                loads.append(
-                    pltpu.make_async_copy(
-                        sources[i],
-                        work.at[pl.ds(base + i * rows, rows)],
-                        load_sem.at[len(loads)],
-                    )
-                )
+                load(sources[i], work.at[pl.ds(base + i * rows, rows)])
         for d in range(1, n):
-            loads.append(
-                pltpu.make_async_copy(first_refs[d - 1], feed.at[0, d], load_sem.at[len(loads)])
-            )
-        for copy in loads:
-            copy.start()
+            load(r.first[d - 1], feed.at[0, d])
         for q in range(QUARTERS):
             feed_own(q).start()
         for d in range(1, n):
             feed_copy(1, d).start()
-        for copy in loads:
-            copy.wait()
-
-        def stage_copy(t, h):
-            return pltpu.make_async_copy(
-                stage.at[t % 2, pl.ds(2 * h, 2)], tiles.at[2 * t + h], stage_sem.at[t % 2, h]
-            )
+        loaded()
 
         def quarter_step(q, _):
+            step(3 * q - 3)
             feed_own(q).wait()
 
             @pl.when(q > 0)
@@ -997,7 +1194,7 @@
                     feed_copy(q + 1, d).start()
 
             def forward(t, _):
-                now = pl.ds(pl.multiple_of(t * tile, tile), tile)
+                now = span(t * tile, tile)
                 cot_now = pl.ds(pl.multiple_of(plane_rows + t * tile, tile), tile)
                 both = jnp.zeros((tile, 2 * quarter), F32)
                 hidden_grad = jnp.zeros((tile, quarter), F32)
@@ -1013,52 +1210,36 @@
                     hidden_grad * activated,
                 )
                 for w, result in enumerate(results):
-                    hidden[q * 3 + w, now, :] = result.astype(BF16)
+                    heads[q * 3 + w, now, :] = result.astype(BF16)
                     turned[w, :, now] = result.T.astype(BF16)
                 return 0
 
             lax.fori_loop(0, plane_rows // tile, forward, 0)
-            advance(2 * q - 2)
-
-            def outer(w, _):
+            step(3 * q - 2)
+
+            def one(w, _):
                 t = 3 * q + w
-                base = jnp.where(w == 0, plane_rows, 0)
-                right = pl.ds(pl.multiple_of(base, plane_rows), plane_rows)
 
                 @pl.when(t >= 2)
                 def _():
-                    for h in range(2):
-                        stage_copy(t - 2, h).wait()
-
-                    @pl.when(is_end)
-                    def _():
-                        for h in range(2):
-                            hop_one(2 * (t - 2) + h).start()
-
-                for j in range(n):
-                    stage[t % 2, j] = matmul(turned[w], work[right, blocks[j]]).astype(BF16)
-                for h in range(2):
-                    stage_copy(t, h).start()
+                    staged(t - 2)
+
+                outer(t, turned[w], span(jnp.where(w == 0, plane_rows, 0), plane_rows))
                 return 0
 
-            lax.fori_loop(0, 3, outer, 0)
-            advance(2 * q - 1)
+            lax.fori_loop(0, 3, one, 0)
+            step(3 * q - 1)
             return 0
 
         lax.fori_loop(0, QUARTERS, quarter_step, 0)
-        for t in (tiles_count - 2, tiles_count - 1):
-            for h in range(2):
-                stage_copy(t, h).wait()
-
-            @pl.when(is_end)
-            def _():
-                for h in range(2):
-                    hop_one(2 * t + h).start()
-
-        def back_step(r, _):
-            now = pl.ds(pl.multiple_of(r * pair, pair), pair)
+        steps_done[0] = 3 * QUARTERS - 3
+        for t in (query_at - 2, query_at - 1):
+            staged(t)
+
+        def back_step(s, _):
+            now = span(s * pair, pair)
             lefts = [
-                jnp.concatenate([hidden[q * 3 + 1, now, :], hidden[q * 3 + 2, now, :]], axis=1)
+                jnp.concatenate([heads[q * 3 + 1, now, :], heads[q * 3 + 2, now, :]], axis=1)
                 for q in range(QUARTERS)
             ]
             for j in range(n):
@@ -1066,371 +1247,340 @@
                 for q in range(QUARTERS):
                     total += matmul_nt(lefts[q], feed[q, j, :wide, :])
                 work[now, blocks[j]] = total.astype(BF16)
-            advance(2 * QUARTERS - 2 + r)
             return 0
 
-        lax.fori_loop(0, n, back_step, 0)
-
-        def out_step(r, _):
-            now = pl.ds(pl.multiple_of(r * pair, pair), pair)
-            then = pl.ds(pl.multiple_of(plane_rows + r * pair, pair), pair)
+        half = n // 2
+        lax.fori_loop(half, n, back_step, 0)
+        rows_hand_over(BACK, 0)
+        advance(TICKS[0])
+        lax.fori_loop(0, half, back_step, 0)
+        rows_send(BACK, 0)
+        advance(TICKS[1])
+
+        def out_step(s, _):
+            now = span(s * pair, pair)
+            then = pl.ds(pl.multiple_of(plane_rows + s * pair, pair), pair)
             for j in range(n):
                 total = jnp.zeros((pair, wide), F32)
                 for q in range(QUARTERS):
-                    total += matmul(hidden[q * 3, now, :], feed[q, j, wide:, :])
+                    total += matmul(heads[q * 3, now, :], feed[q, j, wide:, :])
                 work[then, blocks[j]] = total.astype(BF16)
             return 0
 
-        lax.fori_loop(0, n, out_step, 0)
-        stores = []
-        for base, targets in ((0, back_refs), (plane_rows, out_refs)):
-            for i in range(2 * n):
-                stores.append(
-                    pltpu.make_async_copy(
-                        work.at[pl.ds(base + i * rows, rows)], targets[i], load_sem.at[len(stores)]
-                    )
-                )
-        for copy in stores:
-            copy.start()
-
-        def rest(i, _):
-            advance(i)
+        load(r.middle, r.wide_rows)
+        lax.fori_loop(half, n, out_step, 0)
+        rows_hand_over(OUT, plane_rows)
+        advance(TICKS[2])
+        lax.fori_loop(0, half, out_step, 0)
+        advance(TICKS[3])
+
+        for k in range(planes):
+            load(r.kv_mine[k], heads.at[k])
+            load(r.kv_near[k], heads.at[planes + k])
+        load(r.query, heads.at[2 * planes])
+        load(r.attended, heads.at[2 * planes + 1])
+        for j in range(n):
+            load(r.in_weight[j].at[pl.ds(0, wide)], feed.at[0, j, pl.ds(0, wide)])
+            load(r.out_weight[j], feed.at[0, j, pl.ds(wide, HD)])
+
+        rows_arrive(BACK, 0)
+        loaded()
+        load(r.cot[0], r.own_rows)
+        loaded()
+
+        def second_use(at, back):
+            grad = r.own_rows[at, :].astype(F32) + back
+            r.wide_rows[at, :] = grad
+            r.own_rows[at, :] = grad.astype(BF16)
+
+        norm_rows_back(0, r.wide_rows, r.gains[1:2, :], second_use)
+
+        def branch_far(d):
+            return remote(
+                r.own_rows,
+                r.branch_all.at[d, side],
+                r.branch_send.at[d],
+                r.branch_recv.at[d],
+                (here, chips[d]),
+            )
+
+        def branch_near(d):
+            source = r.own_rows if d == 0 else r.branch_all.at[d, side]
+            return remote(
+                source,
+                r.branch_all.at[d, side],
+                r.branch_near_send.at[d],
+                r.branch_near_recv.at[d],
+                other_core,
+            )
+
+        for d in (3, 1, 2):
+            branch_far(d).start()
+        branch_near(0).start()
+        branch_own = local(r.own_rows, r.branch_all.at[0, side], r.branch_local.at[0])
+        branch_own.start()
+        gain_terms(1)
+        advance(TICKS[4])
+        for d in (1, 2, 3):
+            branch_far(d).wait_recv()
+            branch_near(d).start()
+        rows_sent(BACK, 0)
+        branch_own.wait()
+        for d in range(n):
+            branch_near(d).wait_recv()
+        for d in range(n):
+            for c in range(2):
+                load(r.branch_all.at[d, c], work.at[pl.ds((2 * d + c) * rows, rows)])
+        rows_send(OUT, plane_rows)
+        loaded()
+
+        query_slot, attended_slot, query_grad_slot, kv_grad_slot = range(2 * planes, 2 * planes + 4)
+
+        def attend_back(d, _):
+            now = span(d * pair, pair)
+            query = heads[query_slot, now, :]
+            attended_grad = jnp.zeros((pair, HD), F32)
+            for j in range(n):
+                attended_grad += matmul_nt(work[now, blocks[j]], feed[0, j, wide:, :])
+            attended_grad = attended_grad.astype(BF16)
+            keys, values, scores = [], [], []
+            for k in range(planes):
+                a, b = heads[k, now, :], heads[planes + k, now, :]
+                keys.append(jnp.where(side == 0, a, b))
+                values.append(jnp.where(side == 0, b, a))
+                score = matmul_nt(query, keys[k]) * scale
+                scores.append(jnp.where(r.key_ids[d, k] <= r.query_ids[d], score, masked_score))
+            top = functools.reduce(jnp.maximum, [jnp.max(s, axis=-1, keepdims=True) for s in scores])
+            raised = [jnp.exp(s - top) for s in scores]
+            inverse = 1.0 / sum(jnp.sum(e, axis=-1, keepdims=True) for e in raised)
+            probs = [e * inverse for e in raised]
+            low = [p.astype(BF16) for p in probs]
+            shares = [matmul_nt(attended_grad, values[k]) for k in range(planes)]
+            delta = sum(
+                jnp.sum(low[k].astype(F32) * shares[k], axis=-1, keepdims=True) for k in range(planes)
+            )
+            query_grad = jnp.zeros((pair, HD), F32)
+            for k in range(planes):
+                score_grad = (probs[k] * (shares[k] - delta)).astype(BF16)
+                query_grad += matmul(score_grad, keys[k])
+                key_grad = matmul_tn(score_grad, query) * scale
+                value_grad = matmul_tn(low[k], attended_grad)
+                heads[k, now, :] = jnp.where(side == 0, key_grad, value_grad).astype(BF16)
+                heads[planes + k, now, :] = jnp.where(side == 0, value_grad, key_grad).astype(BF16)
+            query_grad = query_grad * scale
+            query_grad = query_grad * r.tables[0] + turn_back(query_grad * r.tables[1])
+            heads[query_grad_slot, now, :] = query_grad.astype(BF16)
             return 0
 
-        lax.fori_loop(2 * QUARTERS - 2 + n, units + 10, rest, 0)
-        for copy in stores:
-            copy.wait()
+        lax.fori_loop(0, half, attend_back, 0)
+        advance(TICKS[5])
+        lax.fori_loop(half, n, attend_back, 0)
+
+        def kv_hand_over(k):
+            return remote(
+                heads.at[planes + k], r.kv_other.at[k], r.kv_send.at[k], r.kv_recv.at[k], other_core
+            )
+
+        def kv_load(source, slot):
+            return local(source, r.kv_some.at[slot], r.kv_sem.at[slot])
+
+        def kv_add(k, slot):
+            def some(c, _):
+                at = span(c * 64, 64)
+                heads[k, at, :] = (
+                    heads[k, at, :].astype(F32) + r.kv_some[slot, at, :].astype(F32)
+                ).astype(BF16)
+                return 0
+
+            lax.fori_loop(0, plane_rows // 64, some, 0)
+
+        def kv_down(k):
+            return remote(heads.at[k], r.kv_down.at[k], r.down_send.at[k], r.down_recv.at[k], below)
+
+        def kv_up(k):
+            return remote(
+                heads.at[planes - k], r.kv_up.at[k], r.up_send.at[k], r.up_recv.at[k], above
+            )
+
+        order = list(range(planes - 1, -1, -1))
+        for k in order:
+            kv_hand_over(k).start()
+        for at, k in enumerate(order):
+            kv_hand_over(k).wait_recv()
+            kv_load(r.kv_other.at[k], at % 2).start()
+            kv_load(r.kv_other.at[k], at % 2).wait()
+            kv_add(k, at % 2)
+
+        def kv_send(k):
+            @pl.when(z >= k)
+            def _():
+                kv_down(k).start()
+
+            @pl.when(z + k < planes)
+            def _():
+                kv_up(k).start()
+
+        def kv_receive(k, down_to, up_to):
+            @pl.when((z + 1 >= k) & (z + 1 < planes))
+            def _():
+                kv_down(k).wait_recv()
+                if down_to is not None:
+                    copy = kv_load(r.kv_down.at[k], 0)
+                    copy.start()
+                    copy.wait()
+                    kv_add(down_to, 0)
+
+            @pl.when((z >= 1) & (z - 1 + k < planes))
+            def _():
+                kv_up(k).wait_recv()
+                if up_to is not None:
+                    copy = kv_load(r.kv_up.at[k], 1)
+                    copy.start()
+                    copy.wait()
+                    kv_add(up_to, 1)
+
+        kv_send(3)
+        rows_sent(OUT, plane_rows)
+        load(work.at[pl.ds(plane_rows, rows)], r.out_own)
+        loaded()
+        load(r.normed, work.at[pl.ds(plane_rows, plane_rows)])
+        low_half, high_half = pl.ds(0, plane_rows), pl.ds(plane_rows, plane_rows)
+        advance(TICKS[6])
+        turned[0] = heads[attended_slot].astype(F32).T.astype(BF16)
+        turned[1] = heads[query_grad_slot].astype(F32).T.astype(BF16)
+        loaded()
+        outer(query_at, turned[1], high_half)
+        outer(output_at, turned[0], low_half)
+        advance(TICKS[7])
+        kv_receive(3, 2, 2)
+        kv_send(2)
+        staged(query_at)
+        staged(output_at)
+        advance(TICKS[8])
+        kv_receive(2, 1, 3)
+        kv_send(1)
+        advance(TICKS[9])
+        kv_receive(1, 0, 0)
+
+        def project_back(d, _):
+            now = span(d * pair, pair)
+            grad = heads[0, now, :].astype(F32)
+            grad = grad * r.tables[2] + turn_back(grad * r.tables[3])
+            heads[kv_grad_slot, now, :] = grad.astype(BF16)
+            left = jnp.concatenate([heads[query_grad_slot, now, :], grad.astype(BF16)], axis=1)
+            first = span((side * n + d) * rows, rows)
+            second = span(((1 - side) * n + d) * rows, rows)
+            for j in range(n):
+                total = matmul_nt(left, feed[0, j, :wide, :]).astype(BF16)
+                work[first, blocks[j]] = total[:rows]
+                work[second, blocks[j]] = total[rows:]
+            return 0
+
+        lax.fori_loop(0, n, project_back, 0)
+        rows_hand_over(ONE, 0)
+        turned[2] = heads[kv_grad_slot].astype(F32).T.astype(BF16)
+        outer(kv_at, turned[2], high_half)
+        rows_send(ONE, 0)
+        staged(kv_at)
+        advance(TICKS[10])
+
+        for d in range(1, n):
+            branch_far(d).wait_send()
+        for d in range(n):
+            branch_near(d).wait_send()
+        load(r.tokens, r.own_rows)
+        rows_arrive(ONE, 0)
+        loaded()
+
+        def first_use(at, back):
+            r.wide_rows[at, :] = r.wide_rows[at, :] + back
+
+        norm_rows_back(0, r.own_rows, r.gains[0:1, :], first_use)
+        load(r.wide_rows, r.tokens_grad)
+        gain_terms(0)
+
+        def gain_copy(at, source, target, peer):
+            return remote(source, target, r.gain_send.at[at], r.gain_recv.at[at], peer)
+
+        def gain_far(d):
+            return gain_copy(d, r.gain_mine.at[d], r.gain_far.at[d], (here, chips[d]))
+
+        def gain_hop(s, peer):
+            return gain_copy(n + s, r.gain_sum.at[s], r.gain_in.at[s], peer)
+
+        for d in range(1, n):
+            gain_far(d).start()
+        advance(TICKS[11])
+        for d in range(1, n):
+            gain_far(d).wait()
+        r.gain_sum[0] = r.gain_mine[0] + r.gain_far[1] + r.gain_far[2] + r.gain_far[3]
+        gain_hop(0, other_core).start()
+        gain_hop(0, other_core).wait()
+        r.gain_sum[1] = r.gain_sum[0] + r.gain_in[0]
+
+        @pl.when(is_end)
+        def _():
+            gain_hop(1, partner).start()
+            gain_hop(1, partner).wait_send()
+
+        advance(TICKS[12])
+
+        @pl.when(is_middle)
+        def _():
+            gain_hop(1, partner).wait_recv()
+            r.gain_sum[2] = r.gain_sum[1] + r.gain_in[1]
+            gain_hop(2, other_middle).start()
+            gain_hop(2, other_middle).wait()
+            r.gain_sum[3] = r.gain_sum[2] + r.gain_in[2]
+            gain_hop(3, partner).start()
+            gain_hop(3, partner).wait_send()
+
+        @pl.when(is_end)
+        def _():
+            gain_hop(3, partner).wait_recv()
+            r.gain_sum[3] = r.gain_in[3]
+
+        load(r.gain_sum.at[3], r.gain_out)
+        advance(units + 9 - steps_done[0])
+
+        loaded()
+        rows_arrive(OUT, plane_rows)
+        rows_sent(ONE, 0)
         for q in range(1, QUARTERS):
             for d in range(1, n):
                 feed_copy(q, d).wait_send()
+        for k in range(planes):
+            kv_hand_over(k).wait_send()
+        for k in range(1, planes):
+
+            @pl.when(z >= k)
+            def _():
+                kv_down(k).wait_send()
+
+            @pl.when(z + k < planes)
+            def _():
+                kv_up(k).wait_send()
+
         finish()
 
-    unit_array = shape((units,) + unit)
-    dma = pltpu.SemaphoreType.DMA
-    arrays = two_own + two_near + cot_own + cot_near + first_pieces + [hidden_cut]
+    arrays = jax.tree.leaves((in_hbm, in_vmem))
     results = pl.pallas_call(
-        feed_forward,
-        out_shape=[shape(block)] * (4 * n) + [unit_array] * 6,
-        in_specs=[pl.BlockSpec(memory_space=pl.ANY)] * len(arrays),
-        out_specs=[pl.BlockSpec(memory_space=pl.ANY)] * (4 * n + 6),
-        scratch_shapes=[
-            pltpu.VMEM((2 * plane_rows, width), BF16),
-            pltpu.VMEM((QUARTERS, n) + piece, BF16),
-            pltpu.VMEM((3 * QUARTERS, plane_rows, quarter), BF16),
-            pltpu.VMEM((3, quarter, plane_rows), BF16),
-            pltpu.VMEM((2, n, quarter, wide), BF16),
-            pltpu.VMEM((2,) + unit, BF16),
-            pltpu.VMEM((2,) + unit, BF16),
-            pltpu.VMEM((2,) + unit, BF16),
-            pltpu.VMEM((held_sums,) + unit, BF16),
-            pltpu.VMEM((held_ends,) + unit, BF16),
-            dma((4 * n + n - 1,)),
-            dma((QUARTERS,)),
-            dma((QUARTERS * n,)),
-            dma((QUARTERS * n,)),
-            dma((2, 2)),
-            dma((units,)),
-            dma((units,)),
-            dma((units,)),
-            dma((units,)),
-            dma((units,)),
-            dma((units,)),
-            dma((2,)),
-            dma((2,)),
-            dma((2,)),
-            dma((held_ends,)),
-            dma((units,)),
-            dma((2 * units,)),
-            dma((2 * units,)),
-            dma((units,)),
-            dma((units,)),
-        ],
-        cost_estimate=cost(18 * plane_rows * width * part, arrays, [unit_array] * 6),
+        backward,
+        out_shape=jax.tree.leaves(out_hbm),
+        in_specs=[pl.BlockSpec(memory_space=pl.ANY)] * len(jax.tree.leaves(in_hbm))
+        + [pl.BlockSpec(memory_space=pltpu.VMEM)] * len(in_vmem),
+        out_specs=[pl.BlockSpec(memory_space=pl.ANY)] * len(out_hbm),
+        scratch_shapes=list(scratch.values()),
+        cost_estimate=cost(30 * plane_rows * width * part, arrays, [unit_array] * 6),
         compiler_params=pltpu.CompilerParams(
-            collective_id=0, has_side_effects=True, vmem_limit_bytes=62 * 1024 * 1024
+            collective_id=0, has_side_effects=True, vmem_limit_bytes=63 * 1024 * 1024
         ),
-        name="feed_forward",
+        name="backward",
     )(*arrays)
-    back, out_partial = results[: 2 * n], results[2 * n : 4 * n]
-    hidden_own, hidden_near = results[-2:]
-    two_grad_terms = reduced(back[:n], back[n:])
-
-    def norm_back(values, inverse, gain, grad):
-        unit = values * inverse
-        scaled = grad * gain
-        return inverse * (scaled - unit * jnp.mean(scaled * unit, axis=-1, keepdims=True)), jnp.sum(
-            grad * unit, axis=0, keepdims=True
-        )
-
-    def second_norm_back(me_ref, middle_ref, cot_ref, gains_ref, *refs):
-        terms, (middle_grad_ref, branch_ref, gain_ref, flat) = refs[:-4], refs[-4:]
-        middle = middle_ref[...]
-        inverse = lax.rsqrt(jnp.mean(middle * middle, axis=-1, keepdims=True) + epsilon)
-        grad = sum(t[...].astype(F32) for t in terms)
-        back, gain_term = norm_back(middle, inverse, gains_ref[1:2, :], grad)
-        middle_grad = cot_ref[...].astype(F32) + back
-        middle_grad_ref[...] = middle_grad
-        branch_ref[...] = middle_grad.astype(BF16)
-        flat[...] = gain_term
-        for j in range(n):
-            gain_ref[j] = flat[:, column(me_ref[0] ^ j, wide)]
-
-    gain_shape = shape((n, 1, wide), F32)
-    middle_grad, branch_grad, gain_two_term = run_whole(
-        second_norm_back,
-        me,
-        [middle, own_cotangent, gains] + two_grad_terms,
-        [shape(block, F32), shape(block), gain_shape],
-        scratch=[pltpu.VMEM((1, width), F32)],
-        name="second_norm_back",
-    )
-    branch_own, branch_near = gathered(branch_grad)
-
-    def attend_back(me_ref, query_ref, query_id, key_id, cos_ref, sin_ref, *refs):
-        mine, near, out_w = refs[:planes], refs[planes : 2 * planes], refs[2 * planes : 2 * planes + n]
-        branch_refs = refs[2 * planes + n : 2 * planes + 3 * n]
-        query_grad_ref = refs[2 * planes + 3 * n]
-        keep_refs = refs[2 * planes + 3 * n + 1 : 3 * planes + 3 * n + 1]
-        send_refs = refs[3 * planes + 3 * n + 1 : 4 * planes + 3 * n + 1]
-        branch = refs[-1]
-        chip, side = me_ref[0], me_ref[1]
-        for d in range(n):
-
-            @pl.when(pl.program_id(0) == d)
-            def _():
-                branch[side] = branch_refs[d][...]
-                branch[1 - side] = branch_refs[n + d][...]
-
-        query = query_ref[0].reshape(pair, HD)
-        attended_grad = jnp.zeros((pair, HD), F32)
-        for j in range(n):
-            attended_grad += matmul_nt(
-                branch[:, :, column(chip ^ j, wide)].reshape(pair, wide), out_w[j][...]
-            )
-        attended_grad = attended_grad.astype(BF16)
-        keys, values, probs = scored(side, query, query_id, key_id, mine, near)
-        low = [p.astype(BF16) for p in probs]
-        shares = [matmul_nt(attended_grad, values[k]) for k in range(planes)]
-        delta = sum(
-            jnp.sum(low[k].astype(F32) * shares[k], axis=-1, keepdims=True) for k in range(planes)
-        )
-        query_grad = jnp.zeros((pair, HD), F32)
-        for k in range(planes):
-            score_grad = (probs[k] * (shares[k] - delta)).astype(BF16)
-            query_grad += matmul(score_grad, keys[k])
-            key_grad = matmul_tn(score_grad, query) * scale
-            value_grad = matmul_tn(low[k], attended_grad)
-            keep_refs[k][0] = jnp.where(side == 0, key_grad, value_grad).astype(BF16).reshape(
-                2, rows, HD
-            )
-            send_refs[k][0] = jnp.where(side == 0, value_grad, key_grad).astype(BF16).reshape(
-                2, rows, HD
-            )
-        query_grad = query_grad * scale
-        query_grad = query_grad * cos_ref[...] + turn_back(query_grad * sin_ref[...])
-        query_grad_ref[0] = query_grad.astype(BF16).reshape(2, rows, HD)
-
-    query_grad, *kv_grads = run_grid(
-        attend_back,
-        me,
-        (n,),
-        [query_rot, query_ids, key_ids, cosine, sine]
-        + kv_mine
-        + kv_near
-        + weights_out
-        + branch_own
-        + branch_near,
-        [head_spec]
-        + id_specs
-        + [fixed((pair, HD))] * 2
-        + [head_spec] * (2 * planes)
-        + [fixed((HD, wide))] * n
-        + [fixed(block)] * (2 * n),
-        [shape(head_shape)] * (1 + 2 * planes),
-        [head_spec] * (1 + 2 * planes),
-        scratch=[pltpu.VMEM((2, rows, width), BF16)],
-        flops=10 * plane_rows * planes * pair * HD + 2 * plane_rows * HD * width,
-        name="attend_back",
-    )
-    kept, handed = kv_grads[:planes], kv_grads[planes:]
-    kv_sums = [
-        (kept[k].astype(F32) + sibling(handed[k]).astype(F32)).astype(BF16) for k in range(planes)
-    ]
-    from_above = jnp.zeros_like(own_kv)
-    from_below = jnp.zeros_like(own_kv)
-    for k in range(planes - 1, 0, -1):
-        below = jnp.where(z >= k, kv_sums[k], 0).astype(F32) + from_above.astype(F32)
-        above = jnp.where(z + k < planes, kv_sums[planes - k], 0).astype(F32) + from_below.astype(F32)
-        from_above = along(below.astype(BF16), -1)
-        from_below = along(above.astype(BF16), 1)
-
-    def project_back(me_ref, *refs):
-        own_ref, above_ref, below_ref, query_grad_ref, kvcos_ref, kvsin_ref = refs[:6]
-        pieces = refs[6 : 6 + n]
-        kv_ref = refs[6 + n]
-        own_refs, near_refs = refs[7 + n : 7 + 2 * n], refs[7 + 2 * n : 7 + 3 * n]
-        chip, side = me_ref[0], me_ref[1]
-        for d in range(n):
-            for e in range(2):
-                slot = side ^ e
-                grad = own_ref[d, slot].astype(F32) + above_ref[d, slot].astype(F32)
-                grad = grad + below_ref[d, slot].astype(F32)
-                grad = grad * kvcos_ref[slot] + turn_back(grad * kvsin_ref[slot])
-                grad = grad.astype(BF16)
-                kv_ref[d, slot] = grad
-                left = jnp.concatenate([query_grad_ref[d, slot], grad], axis=1)
-                target = (own_refs, near_refs)[e][d]
-                for j in range(n):
-                    target[:, column(chip ^ j, wide)] = matmul_nt(left, pieces[j][:wide, :]).astype(
-                        BF16
-                    )
-
-    kv_grad, *partial = run_whole(
-        project_back,
-        me,
-        [kv_sums[0], from_above, from_below, query_grad] + tables[2:] + weights_in,
-        [shape(head_shape)] + [shape(block)] * (2 * n),
-        flops=4 * plane_rows * width * HD,
-        name="project_back",
-    )
-    one_grad_terms = reduced(partial[:n], partial[n:])
-
-    def first_norm_back(me_ref, token_ref, middle_grad_ref, gains_ref, *refs):
-        terms, (grad_ref, gain_ref, flat) = refs[:-3], refs[-3:]
-        values = token_ref[...].astype(F32)
-        inverse = lax.rsqrt(jnp.mean(values * values, axis=-1, keepdims=True) + epsilon)
-        grad = sum(t[...].astype(F32) for t in terms)
-        back, gain_term = norm_back(values, inverse, gains_ref[0:1, :], grad)
-        grad_ref[...] = middle_grad_ref[...] + back
-        flat[...] = gain_term
-        for j in range(n):
-            gain_ref[j] = flat[:, column(me_ref[0] ^ j, wide)]
-
-    tokens_grad, gain_one_term = run_whole(
-        first_norm_back,
-        me,
-        [own_tokens, middle_grad, gains] + one_grad_terms,
-        [shape(block, F32), gain_shape],
-        scratch=[pltpu.VMEM((1, width), F32)],
-        name="first_norm_back",
-    )
-    gain_terms = jnp.concatenate([gain_one_term, gain_two_term], axis=1)
-    gain_sum = gain_terms[0] + sum(across(gain_terms[d], d) for d in range(1, n))
-    gain_sum = gain_sum + sibling(gain_sum)
-    gain_sum = summed_over_planes(gain_sum)
-
-    def outer(me_ref, left_ref, right_ref, out_ref):
-        turned = left_ref[...].reshape(plane_rows, HD).astype(F32).T.astype(BF16)
-        for j in range(n):
-            right = right_ref[:, :, :, column(me_ref[0] ^ j, wide)].reshape(plane_rows, wide)
-            out_ref[j] = matmul(turned, right).astype(BF16)
-
-    def outer_branch(me_ref, left_ref, *refs):
-        branch_refs, (out_ref, right_ref, sems) = refs[: 2 * n], refs[2 * n :]
-        copies = []
-        for e in range(2):
-            for d in range(n):
-                copies.append(
-                    pltpu.make_async_copy(
-                        branch_refs[e * n + d],
-                        right_ref.at[d, me_ref[1] ^ e],
-                        sems.at[e * n + d],
-                    )
-                )
-        for copy in copies:
-            copy.start()
-        for copy in copies:
-            copy.wait()
-        outer(me_ref, left_ref, right_ref, out_ref)
-
-    outer_flops = 2 * plane_rows * width * HD
-    outer_tile = shape((n, HD, wide))
-    query_tile = run_whole(
-        outer, me, [query_grad, normed], outer_tile, flops=outer_flops, name="query_outer"
-    )
-    output_tile = run_whole(
-        outer_branch,
-        me,
-        [attended] + branch_own + branch_near,
-        outer_tile,
-        scratch=[pltpu.VMEM((n, 2, rows, width), BF16), pltpu.SemaphoreType.DMA((2 * n,))],
-        flops=outer_flops,
-        in_hbm=2 * n,
-        name="output_outer",
-    )
-    kv_tile = run_whole(outer, me, [kv_grad, normed], outer_tile, flops=outer_flops, name="kv_outer")
-
-    def deal(me_ref, *refs):
-        count = (len(refs) - n) // 2
-        sums, backs, outs = refs[:count], refs[count : 2 * count], refs[2 * count :]
-        outer_plane = me_ref[2] == 1
-
-        @pl.when(outer_plane)
-        def _():
-            for d in range(n):
-                for w in range(count):
-                    outs[d][w] = backs[w][d]
-
-        @pl.when(jnp.logical_not(outer_plane))
-        def _():
-            for d in range(n):
-                for w in range(count):
-                    outs[d][w] = sums[w][d]
-
-    is_outer = ((z == 0) | (z == planes - 1)).astype(jnp.int32)
-    me_and_plane = jnp.concatenate([me, is_outer[None]])
-    stages = len(folds) * 2 + 1
-
-    def stage_moves(stage):
-        if stage < len(folds):
-            return folds[stage]
-        if stage == len(folds):
-            return [(middle_left, middle_right), (middle_right, middle_left)]
-        return [(b, a) for a, b in folds[stages - 1 - stage]]
-
-    def pipelined(tiles):
-        ends = {}
-        for line in range(LINES):
-            waiting = []
-            feed_line = list(range(line, len(tiles), LINES))
-            while feed_line or waiting:
-                if feed_line:
-                    first = feed_line.pop(0)
-                    waiting.append((first, 0, tiles[first]))
-                operands = lax.optimization_barrier([value for _, _, value in waiting])
-                moved = []
-                for (index, stage, _), value in zip(waiting, operands):
-                    other = between_planes(value, stage_moves(stage))
-                    if stage == stages - 1:
-                        ends[index] = (value, other)
-                        continue
-                    if stage <= len(folds):
-                        value = (value.astype(F32) + other.astype(F32)).astype(BF16)
-                    else:
-                        s = stages - 1 - stage
-                        value = jnp.where((z == s) | (z == planes - 1 - s), other, value)
-                    moved.append((index, stage + 1, value))
-                waiting = moved
-        return [ends[i] for i in range(len(tiles))]
-
-    plane_sums = pipelined([query_tile, output_tile, kv_tile])
-
-    def owned(ends):
-        dealt = run_whole(
-            deal,
-            me_and_plane,
-            [a for a, _ in ends] + [b for _, b in ends],
-            [shape((len(ends),) + ends[0][0].shape[1:])] * n,
-            name="deal",
-        )
-        own = [dealt[0]] + [across(dealt[d], d) for d in range(1, n)]
-        return own + [sibling(block) for block in own]
-
-    def slot_of(q, count):
-        def where(i, me):
-            return (2 * (me[0] ^ (i % n)) + (me[1] ^ (i // n))) * count + q
-
-        return where
+    results = types.SimpleNamespace(**jax.tree.unflatten(jax.tree.structure(out_hbm), results))
+    owned_tiles, near_tiles = (
+        a.reshape(tiles_count, n, quarter, wide) for a in (results.owned, results.near)
+    )
 
     def place_hidden(me_ref, own_ref, near_ref, gate_out, up_out, down_out):
         for source, e in ((own_ref, 0), (near_ref, 1)):
@@ -1438,11 +1588,17 @@
             @pl.when(pl.program_id(0) // n == e)
             def _():
                 down_out[...] = source[0, 0].astype(F32)
-                gate_out[...] = source[1, 0].astype(F32).T
-                up_out[...] = source[2, 0].astype(F32).T
+                gate_out[...] = source[1, 0].T.astype(F32)
+                up_out[...] = source[2, 0].T.astype(F32)
 
     def hidden_slot(i, q, me):
         return (2 * (me[0] ^ (i % n)) + (me[1] ^ (i // n))) * QUARTERS + q
+
+    def own_hidden(i, q, me):
+        return (jnp.where(i < n, q, QUARTERS - 1), jnp.minimum(i, n - 1), 0, 0)
+
+    def near_hidden(i, q, me):
+        return (jnp.where(i < n, 0, q), jnp.maximum(i - n, 0), 0, 0)
 
     by_columns = pl.BlockSpec((wide, quarter), lambda i, q, me: (0, hidden_slot(i, q, me)))
     by_rows = pl.BlockSpec((quarter, wide), lambda i, q, me: (hidden_slot(i, q, me), 0))
@@ -1450,10 +1606,10 @@
         place_hidden,
         me,
         (2 * n, QUARTERS),
-        [t.reshape(3 * QUARTERS, n, quarter, wide) for t in (hidden_own, hidden_near)],
+        [owned_tiles, near_tiles],
         [
-            pl.BlockSpec((3, 1, quarter, wide), lambda i, q, me: (q, jnp.where(i < n, i, n - 1), 0, 0)),
-            pl.BlockSpec((3, 1, quarter, wide), lambda i, q, me: (q, jnp.where(i < n, 0, i - n), 0, 0)),
+            pl.BlockSpec((3, 1, quarter, wide), own_hidden),
+            pl.BlockSpec((3, 1, quarter, wide), near_hidden),
         ],
         [
             shape(gate_weight.shape, F32),
@@ -1464,67 +1620,67 @@
         name="place_hidden",
     )
 
-    def place_query(me_ref, *refs):
-        tiles, (query_out, output_out) = refs[: 2 * n], refs[2 * n :]
-        for i in range(2 * n):
-
-            @pl.when(pl.program_id(0) == i)
-            def _():
-                query_out[...] = tiles[i][0].astype(F32).T
-                output_out[...] = tiles[i][1].astype(F32)
-
-    where = slot_of(0, 1)
+    def place_query(me_ref, own_ref, near_ref, query_out, output_out):
+        for source, e in ((own_ref, 0), (near_ref, 1)):
+
+            @pl.when(pl.program_id(0) // n == e)
+            def _():
+                query_out[...] = source[0, 0].T.astype(F32)
+                output_out[...] = source[1, 0].astype(F32)
+
+    def head_slot(i, me):
+        return 2 * (me[0] ^ (i % n)) + (me[1] ^ (i // n))
+
+    own_spec = lambda i, me: (query_at // 2, jnp.where(i < n, i, n - 1), 0, 0)
+    near_spec = lambda i, me: (query_at // 2, jnp.where(i < n, 0, i - n), 0, 0)
     query_weight_grad, output_weight_grad = run_grid(
         place_query,
         me,
         (2 * n,),
-        owned(plane_sums[:2]),
-        [fixed((2, HD, wide))] * (2 * n),
+        [owned_tiles, near_tiles],
+        [pl.BlockSpec((2, 1, HD, wide), own_spec), pl.BlockSpec((2, 1, HD, wide), near_spec)],
         [shape(query_weight.shape, F32), shape(output_weight.shape, F32)],
         [
-            pl.BlockSpec((wide, HD), lambda i, me: (0, where(i, me))),
-            pl.BlockSpec((HD, wide), lambda i, me: (where(i, me), 0)),
+            pl.BlockSpec((wide, HD), lambda i, me: (0, head_slot(i, me))),
+            pl.BlockSpec((HD, wide), lambda i, me: (head_slot(i, me), 0)),
         ],
         name="place_query",
     )
 
-    def place_kv(me_ref, *refs):
-        tiles, (key_out, value_out) = refs[: 2 * n], refs[2 * n :]
+    def place_kv(me_ref, own_ref, near_ref, key_out, value_out):
         keys_here = me_ref[1] == 0
-        for d in range(n):
-
-            @pl.when(pl.program_id(0) == d)
-            def _():
-                own, near = tiles[d][0].astype(F32).T, tiles[n + d][0].astype(F32).T
-                key_out[...] = jnp.where(keys_here, own, near)
-                value_out[...] = jnp.where(keys_here, near, own)
+        own, near = own_ref[0, 0].T.astype(F32), near_ref[0, 0].T.astype(F32)
+        key_out[...] = jnp.where(keys_here, own, near)
+        value_out[...] = jnp.where(keys_here, near, own)
 
     by_chip = pl.BlockSpec((wide, HD), lambda i, me: (0, me[0] ^ i))
+    kv_spec = pl.BlockSpec((1, 1, HD, wide), lambda i, me: (kv_at, i, 0, 0))
     key_weight_grad, value_weight_grad = run_grid(
         place_kv,
         me,
         (n,),
-        owned(plane_sums[2:]),
-        [fixed((1, HD, wide))] * (2 * n),
+        [owned_tiles, near_tiles],
+        [kv_spec, kv_spec],
         [shape(key_weight.shape, F32), shape(value_weight.shape, F32)],
         [by_chip, by_chip],
         name="place_kv",
     )
 
-    output = middle + sum(t.astype(F32) for t in reduced(out_partial[:n], out_partial[n:]))
+    output = middle + results.out_own.astype(F32) + results.row_near[OUT, 0].astype(F32)
+    output = output + sum(results.row_far[OUT, d].astype(F32) for d in range(1, n))
 
     return (
         output.astype(BF16)[None],
-        tokens_grad[None],
+        results.tokens_grad[None],
         query_weight_grad,
         key_weight_grad,
         value_weight_grad,
         output_weight_grad,
-        gain_sum[0],
+        results.gain_out[0],
         held[0],
         held[1],
         held[2],
-        gain_sum[1],
+        results.gain_out[1],
     )
 
 

time: 1190 us -> 895 us (0.75)
  waiting for transfers between devices: 415 us -> 184 us
  starting transfers between devices: 123 us -> 48.8 us
  Pallas kernels: 573 us -> 621 us
  other arithmetic: 46.4 us -> 17 us
    ppermute x42 -> x21, waiting for transfers between devices: 283 us -> 155 us  [across(): return lax.ppermute(value, 'fsdp', [(i, i ^ d) for i in range(n)])]
    pallas_call x1, Pallas kernels: 399 us -> 525 us  [plane_layer(): pl.pallas_call(backward, out_shape=jax.tree.leaves(out_hbm), in_specs=[pl...]
    ppermute x12 -> x0, waiting for transfers between devices: 61.9 us -> none  [between_planes(): lax.ppermute(value, 'ctx', [(2 * a + side, 2 * b + side) for a, b in move...]
    pallas_call x10 -> x2, Pallas kernels: 63.1 us -> 15.9 us  [run_whole(): pl.pallas_call(body, out_shape=outs, in_specs=[pl.BlockSpec(memory_space=...]
    ppermute x12 -> x6, waiting for transfers between devices: 62 us -> 27.1 us  [along(): lax.ppermute(value, 'ctx', [(a, b) for a, b in pairs if 0 <= b < ctx_count])]
    pallas_call x7 -> x6, Pallas kernels: 111 us -> 80.8 us  [run_grid(): pl.pallas_call(body, out_shape=outs, grid_spec=pltpu.PrefetchScalarGridSp...]
    ppermute x12 -> x0, starting transfers between devices: 26.5 us -> none  [between_planes(): lax.ppermute(value, 'ctx', [(2 * a + side, 2 * b + side) for a, b in move...]
    ppermute x42 -> x21, starting transfers between devices: 53 us -> 26.8 us  [across(): return lax.ppermute(value, 'fsdp', [(i, i ^ d) for i in range(n)])]
  transfers between devices with their start and end apart: 115 -> 47, of which waited for: 40 -> 16; matrix products, arithmetic and copies ran while one was open for 4% -> 2% of each run, Pallas kernels for 10% -> 2%
where the time goes in v4:
time: 895 us; the launch traced here: 886 us
  Pallas kernels  621 us (69%)
  waiting for transfers between devices  184 us (21%)
  starting transfers between devices  48.8 us (5%)
  other arithmetic  17 us (2%)
  local copies, waits for them, and re-layouts  13.8 us (2%)
    pallas_call x1, Pallas kernels, plane_layer(): pl.pallas_call(backward, out_shape=jax.tree.leaves(out_hbm), in_specs=[pl...  525 us
    ppermute x21, waiting for transfers between devices, across(): return lax.ppermute(value, 'fsdp', [(i, i ^ d) for i in range(n)])  155 us
    pallas_call x6, Pallas kernels, run_grid(): pl.pallas_call(body, out_shape=outs, grid_spec=pltpu.PrefetchScalarGridSp...  80.8 us
    ppermute x6, waiting for transfers between devices, along(): lax.ppermute(value, 'ctx', [(a, b) for a, b in pairs if 0 <= b < ctx_count])  27.1 us
    ppermute x21, starting transfers between devices, across(): return lax.ppermute(value, 'fsdp', [(i, i ^ d) for i in range(n)])  26.8 us
    ppermute x6, starting transfers between devices, along(): lax.ppermute(value, 'ctx', [(a, b) for a, b in pairs if 0 <= b < ctx_count])  17.9 us
  transfers between devices with their start and end apart: 47, of which 16 were waited for; matrix products, arithmetic and copies ran while one was open for 2% of the time, Pallas kernels for 2%

profile of v4, /device:TPU:0, one launch (start us, length us, event | category | flops | bytes accessed | tf_op | source)
XLA Modules:
  0.0 886.3 jit_solution(5640508139084914905)
XLA Ops:
  0.6 4.0 collective-permute-start.2
  8.4 4.9 cut_attention.1
  16.8 34.4 %collective-permute-done.7.refs_9_.refs_14_ = bf16[528,512]{1,0:T(8,128)(2,1)} collective-permute-done((bf16[528,512]{1,0:T(8,128)(2,1)}, bf16[528,512]{1,0:T(8,128)(2,1)}, u32[]{:S(2)}, u32[]{:S(2)}) %collective-permute-start.7) | collective-permute-done | bytes 540704 | tf_op jit(solution)/shard_map/ppermute | solution.py:437
  56.3 11.5 %collective-permute-done.9.refs_11_.refs_16_ = bf16[528,512]{1,0:T(8,128)(2,1)} collective-permute-done((bf16[528,512]{1,0:T(8,128)(2,1)}, bf16[528,512]{1,0:T(8,128)(2,1)}, u32[]{:S(2)}, u32[]{:S(2)}) %collective-permute-start.9) | collective-permute-done | bytes 540704 | tf_op jit(solution)/shard_map/ppermute | solution.py:437
  67.9 11.5 %project.1 = (bf16[4,2,192,2048]{3,2,1,0:T(8,128)(2,1)}, bf16[4,2,192,256]{3,2,1,0:T(8,128)(2,1)}, bf16[4,2,192,256]{3,2,1,0:T(8,128)(2,1)}, f32[2,2048]{1,0:T(2,128)}) custom-call(s32[2]{0:T(128)} %pad_add_fusion.me_ref, bf16[192,2048]{1,0:T(8,128)(2,1)} %bitcast.52, bf16[192,2048]{1,0:T(8,128)(2,1)} %copy-done.26, bf16[192,2048]{1,0:T(8,128)(2,1)} %copy-done.25, ...), custom_call_target="tpu_custom_call" | custom-call | flops 3221225472 | bytes 17907712 | tf_op jit(solution)/shard_map/project/pallas_call | solution.py:351
  80.6 4.6 collective-permute-start.16
  85.2 14.9 %collective-permute-done.17 = bf16[4,2,192,256]{3,2,1,0:T(8,128)(2,1)S(1)} collective-permute-done((bf16[4,2,192,256]{3,2,1,0:T(8,128)(2,1)}, bf16[4,2,192,256]{3,2,1,0:T(8,128)(2,1)S(1)}, u32[]{:S(2)}, u32[]{:S(2)}) %collective-permute-start.17) | collective-permute-done | bytes 786464 | tf_op jit(solution)/shard_map/ppermute | solution.py:444
  102.3 4.6 collective-permute-start.20
  108.4 12.2 %collective-permute-done.18 = bf16[4,2,192,256]{3,2,1,0:T(8,128)(2,1)S(1)} collective-permute-done((bf16[4,2,192,256]{3,2,1,0:T(8,128)(2,1)S(1)}, bf16[4,2,192,256]{3,2,1,0:T(8,128)(2,1)S(1)}, u32[]{:S(2)}, u32[]{:S(2)}) %collective-permute-start.18) | collective-permute-done | bytes 786464 | tf_op jit(solution)/shard_map/ppermute | solution.py:444
  122.0 4.9 collective-permute-start.21
  128.9 10.1 %cut_hidden.1.refs_9_ = bf16[4,4,768,512]{3,2,1,0:T(8,128)(2,1)} custom-call(s32[2]{0:T(128)} %pad_add_fusion.me_ref, bf16[512,8192]{1,0:T(8,128)(2,1)} %refs_3_.3, bf16[512,8192]{1,0:T(8,128)(2,1)} %refs_3_.3, bf16[512,8192]{1,0:T(8,128)(2,1)} %refs_3_.3, bf16[512,8192]{1,0:T(8,128)(2,1)} %refs_3_.3, bf16[512,8192]{1,0:T(8,128)(2,1)} %refs_7_.3, ...), custom_call_target="tpu_custom_call" | custom-call | bytes 113246208 | tf_op jit(solution)/shard_map/cut_hidden/pallas_call | solution.py:366
  152.2 24.8 %collective-permute-done.11.refs_3_ = bf16[192,2048]{1,0:T(8,128)(2,1)} collective-permute-done((bf16[192,2048]{1,0:T(8,128)(2,1)}, bf16[192,2048]{1,0:T(8,128)(2,1)}, u32[]{:S(2)}, u32[]{:S(2)}) %collective-permute-start.11) | collective-permute-done | bytes 786464 | tf_op jit(solution)/shard_map/ppermute | solution.py:437
  180.0 10.7 %collective-permute-done.14.refs_11_ = bf16[768,512]{1,0:T(8,128)(2,1)} collective-permute-done((bf16[768,512]{1,0:T(8,128)(2,1)S(1)}, bf16[768,512]{1,0:T(8,128)(2,1)}, u32[]{:S(2)}, u32[]{:S(2)}) %collective-permute-start.14) | collective-permute-done | bytes 786464 | tf_op jit(solution)/shard_map/ppermute | solution.py:437
  196.1 5.2 collective-permute-done.28.refs_11_.refs_30_
  202.3 17.3 %attend.1 = (bf16[4,2,192,256]{3,2,1,0:T(8,128)(2,1)}, bf16[192,2048]{1,0:T(8,128)(2,1)}, bf16[192,2048]{1,0:T(8,128)(2,1)}, bf16[192,2048]{1,0:T(8,128)(2,1)}, ...) custom-call(s32[2]{0:T(128)} %pad_add_fusion.me_ref, ...), custom_call_target="tpu_custom_call" | custom-call | flops 4026531840 | bytes 15235072 | tf_op jit(solution)/shard_map/attend/pallas_call | solution.py:366
  228.4 15.7 %collective-permute-done.31.refs_2_ = bf16[192,2048]{1,0:T(8,128)(2,1)S(1)} collective-permute-done((bf16[192,2048]{1,0:T(8,128)(2,1)S(1)}, bf16[192,2048]{1,0:T(8,128)(2,1)S(1)}, u32[]{:S(2)}, u32[]{:S(2)}) %collective-permute-start.31) | collective-permute-done | bytes 786464 | tf_op jit(solution)/shard_map/ppermute | solution.py:437
  244.1 15.7 %collective-permute-done.33.refs_3_ = bf16[192,2048]{1,0:T(8,128)(2,1)S(1)} collective-permute-done((bf16[192,2048]{1,0:T(8,128)(2,1)S(1)}, bf16[192,2048]{1,0:T(8,128)(2,1)S(1)}, u32[]{:S(2)}, u32[]{:S(2)}) %collective-permute-start.33) | collective-permute-done | bytes 786464 | tf_op jit(solution)/shard_map/ppermute | solution.py:437
  261.9 4.4 second_norm.1
  270.3 17.7 %collective-permute-done.42.refs_36_ = bf16[192,2048]{1,0:T(8,128)(2,1)} collective-permute-done((bf16[192,2048]{1,0:T(8,128)(2,1)}, bf16[192,2048]{1,0:T(8,128)(2,1)}, u32[]{:S(2)}, u32[]{:S(2)}) %collective-permute-start.42) | collective-permute-done | bytes 786464 | tf_op jit(solution)/shard_map/ppermute | solution.py:437
  288.1 15.1 %collective-permute-done.41.refs_35_ = bf16[192,2048]{1,0:T(8,128)(2,1)} collective-permute-done((bf16[192,2048]{1,0:T(8,128)(2,1)}, bf16[192,2048]{1,0:T(8,128)(2,1)}, u32[]{:S(2)}, u32[]{:S(2)}) %collective-permute-start.41) | collective-permute-done | bytes 786464 | tf_op jit(solution)/shard_map/ppermute | solution.py:437
  306.9 524.5 %backward.1 = (bf16[4,2,192,2048]{3,2,1,0:T(8,128)(2,1)}, bf16[30,2,256,512]{3,2,1,0:T(8,128)(2,1)}, bf16[30,2,256,512]{3,2,1,0:T(8,128)(2,1)}, bf16[30,2,256,51...) custom-call(bf16[1536,256]{1,0:T(8,128)(2,1)} %bitcast.63, ...), custom_call_target="tpu_custom_call" | custom-call | flops 96636764160 | bytes 143243264 | tf_op jit(solution)/shard_map/backward/pallas_call | solution.py:1567
  831.4 5.1 place_kv.1
  836.5 8.4 place_query.1
  844.9 35.1 %place_hidden.1 = (f32[512,8192]{1,0:T(8,128)}, f32[512,8192]{1,0:T(8,128)}, f32[8192,512]{1,0:T(8,128)}) custom-call(s32[2]{0:T(128)} %pad_add_fusion.me_ref, bf16[15,4,256,512]{3,2,1,0:T(8,128)(2,1)} %bitcast.47, bf16[15,4,256,512]{3,2,1,0:T(8,128)(2,1)} %bitcast.44), custom_call_target="tpu_custom_call" | custom-call | bytes 81788928 | tf_op jit(solution)/shard_map/place_hidden/pallas_call | solution.py:366
  (180 shorter events, 67.8 us)
Async XLA Ops:
  0.6 50.6 %collective-permute-start.2 = (bf16[192,2048]{1,0:T(8,128)(2,1)}, bf16[192,2048]{1,0:T(8,128)(2,1)S(1)}, u32[]{:S(2)}, u32[]{:S(2)}) collective-permute-start(bf16[192,2048]{1,0:T(8,128)(2,1)} %bitcast.49), channel_id=1, source_target_pairs={{0,3},{1,2},{2,1},{3,0},{4,7},{5,6},{6,5},{7,4},{8,11},{9,10},{10,... | collective-permute-start | bytes 2359304 | tf_op jit(solution)/shard_map/ppermute | solution.py:437
  4.6 47.1 %collective-permute-start.1 = (bf16[192,2048]{1,0:T(8,128)(2,1)}, bf16[192,2048]{1,0:T(8,128)(2,1)S(1)}, u32[]{:S(2)}, u32[]{:S(2)}) collective-permute-start(bf16[192,2048]{1,0:T(8,128)(2,1)} %bitcast.50), channel_id=1, source_target_pairs={{0,2},{1,3},{2,0},{3,1},{4,6},{5,7},{6,4},{7,5},{8,10},{9,11},{10,... | collective-permute-start | bytes 2359304 | tf_op jit(solution)/shard_map/ppermute | solution.py:437
  5.1 46.7 %collective-permute-start = (bf16[192,2048]{1,0:T(8,128)(2,1)}, bf16[192,2048]{1,0:T(8,128)(2,1)S(1)}, u32[]{:S(2)}, u32[]{:S(2)}) collective-permute-start(bf16[192,2048]{1,0:T(8,128)(2,1)} %bitcast.51), channel_id=1, source_target_pairs={{0,1},{1,0},{2,3},{3,2},{4,5},{5,4},{6,7},{7,6},{8,9},{9,8},{10,11... | collective-permute-start | bytes 2359304 | tf_op jit(solution)/shard_map/ppermute | solution.py:437
  13.3 37.9 %collective-permute-start.7 = (bf16[528,512]{1,0:T(8,128)(2,1)}, bf16[528,512]{1,0:T(8,128)(2,1)}, u32[]{:S(2)}, u32[]{:S(2)}) collective-permute-start(bf16[528,512]{1,0:T(8,128)(2,1)} %get-tuple-element.56), channel_id=1, source_target_pairs={{0,1},{1,0},{2,3},{3,2},{4,5},{5,4},{6,7},{7,6},{8,9},{9,8},{10,11... | collective-permute-start | bytes 1622024 | tf_op jit(solution)/shard_map/ppermute | solution.py:437
  15.2 37.1 %collective-permute-start.8 = (bf16[528,512]{1,0:T(8,128)(2,1)}, bf16[528,512]{1,0:T(8,128)(2,1)}, u32[]{:S(2)}, u32[]{:S(2)}) collective-permute-start(bf16[528,512]{1,0:T(8,128)(2,1)} %get-tuple-element.57), channel_id=1, source_target_pairs={{0,2},{1,3},{2,0},{3,1},{4,6},{5,7},{6,4},{7,5},{8,10},{9,11},{10,... | collective-permute-start | bytes 1622024 | tf_op jit(solution)/shard_map/ppermute | solution.py:437
  106.9 36.0 %collective-permute-start.12 = (bf16[192,2048]{1,0:T(8,128)(2,1)}, bf16[192,2048]{1,0:T(8,128)(2,1)}, u32[]{:S(2)}, u32[]{:S(2)}) collective-permute-start(bf16[192,2048]{1,0:T(8,128)(2,1)} %bitcast.3.refs_1_), channel_id=1, source_target_pairs={{0,3},{1,2},{2,1},{3,0},{4,7},{5,6},{6,5},{7,4},{8,11},{9,10},{10,... | collective-permute-start | bytes 2359304 | tf_op jit(solution)/shard_map/ppermute | solution.py:437
  120.7 23.7 %collective-permute-start.19 = (bf16[4,2,192,256]{3,2,1,0:T(8,128)(2,1)S(1)}, bf16[4,2,192,256]{3,2,1,0:T(8,128)(2,1)S(1)}, u32[]{:S(2)}, u32[]{:S(2)}) collective-permute-start(bf16[4,2,192,256]{3,2,1,0:T(8,128)(2,1)S(1)} %collective-permute-done.18), channel_id=1, source_target_pairs={{8,0},{12,4},{16,8},{20,12},{24,16},{28,20},{9,1},{13,5},{17,9},{2... | collective-permute-start | bytes 2359304 | tf_op jit(solution)/shard_map/ppermute | solution.py:444
  122.0 23.9 %collective-permute-start.21 = (bf16[4,2,192,256]{3,2,1,0:T(8,128)(2,1)S(1)}, bf16[4,2,192,256]{3,2,1,0:T(8,128)(2,1)S(1)}, u32[]{:S(2)}, u32[]{:S(2)}) collective-permute-start(bf16[4,2,192,256]{3,2,1,0:T(8,128)(2,1)S(1)} %collective-permute-done.20), channel_id=1, source_target_pairs={{0,8},{4,12},{8,16},{12,20},{16,24},{20,28},{1,9},{5,13},{9,17},{1... | collective-permute-start | bytes 2359304 | tf_op jit(solution)/shard_map/ppermute | solution.py:444
  140.8 36.2 %collective-permute-start.11 = (bf16[192,2048]{1,0:T(8,128)(2,1)}, bf16[192,2048]{1,0:T(8,128)(2,1)}, u32[]{:S(2)}, u32[]{:S(2)}) collective-permute-start(bf16[192,2048]{1,0:T(8,128)(2,1)} %bitcast.3.refs_1_), channel_id=1, source_target_pairs={{0,2},{1,3},{2,0},{3,1},{4,6},{5,7},{6,4},{7,5},{8,10},{9,11},{10,... | collective-permute-start | bytes 2359304 | tf_op jit(solution)/shard_map/ppermute | solution.py:437
  142.4 34.6 %collective-permute-start.10 = (bf16[192,2048]{1,0:T(8,128)(2,1)}, bf16[192,2048]{1,0:T(8,128)(2,1)}, u32[]{:S(2)}, u32[]{:S(2)}) collective-permute-start(bf16[192,2048]{1,0:T(8,128)(2,1)} %bitcast.3.refs_1_), channel_id=1, source_target_pairs={{0,1},{1,0},{2,3},{3,2},{4,5},{5,4},{6,7},{7,6},{8,9},{9,8},{10,11... | collective-permute-start | bytes 2359304 | tf_op jit(solution)/shard_map/ppermute | solution.py:437
  142.9 37.1 %collective-permute-start.15 = (bf16[768,512]{1,0:T(8,128)(2,1)S(1)}, bf16[768,512]{1,0:T(8,128)(2,1)}, u32[]{:S(2)}, u32[]{:S(2)}) collective-permute-start(bf16[768,512]{1,0:T(8,128)(2,1)S(1)} %get-tuple-element.99), channel_id=1, source_target_pairs={{0,3},{1,2},{2,1},{3,0},{4,7},{5,6},{6,5},{7,4},{8,11},{9,10},{10,... | collective-permute-start | bytes 2359304 | tf_op jit(solution)/shard_map/ppermute | solution.py:437
  144.4 46.4 %collective-permute-start.14 = (bf16[768,512]{1,0:T(8,128)(2,1)S(1)}, bf16[768,512]{1,0:T(8,128)(2,1)}, u32[]{:S(2)}, u32[]{:S(2)}) collective-permute-start(bf16[768,512]{1,0:T(8,128)(2,1)S(1)} %get-tuple-element.100), channel_id=1, source_target_pairs={{0,2},{1,3},{2,0},{3,1},{4,6},{5,7},{6,4},{7,5},{8,10},{9,11},{10,... | collective-permute-start | bytes 2359304 | tf_op jit(solution)/shard_map/ppermute | solution.py:437
  145.9 46.1 %collective-permute-start.13 = (bf16[768,512]{1,0:T(8,128)(2,1)S(1)}, bf16[768,512]{1,0:T(8,128)(2,1)}, u32[]{:S(2)}, u32[]{:S(2)}) collective-permute-start(bf16[768,512]{1,0:T(8,128)(2,1)S(1)} %get-tuple-element.101), channel_id=1, source_target_pairs={{0,1},{1,0},{2,3},{3,2},{4,5},{5,4},{6,7},{7,6},{8,9},{9,8},{10,11... | collective-permute-start | bytes 2359304 | tf_op jit(solution)/shard_map/ppermute | solution.py:437
  177.0 24.3 %collective-permute-start.22 = (bf16[4,2,192,256]{3,2,1,0:T(8,128)(2,1)}, bf16[4,2,192,256]{3,2,1,0:T(8,128)(2,1)}, u32[]{:S(2)}, u32[]{:S(2)}) collective-permute-start(bf16[4,2,192,256]{3,2,1,0:T(8,128)(2,1)} %get-tuple-element.62.refs_0_), channel_id=1, source_target_pairs={{0,4},{4,0},{8,12},{12,8},{16,20},{20,16},{24,28},{28,24},{1,5},{5... | collective-permute-start | bytes 2359304 | tf_op jit(solution)/shard_map/ppermute | solution.py:440
  177.0 24.3 %collective-permute-start.24 = (bf16[4,2,192,256]{3,2,1,0:T(8,128)(2,1)S(1)}, bf16[4,2,192,256]{3,2,1,0:T(8,128)(2,1)}, u32[]{:S(2)}, u32[]{:S(2)}) collective-permute-start(bf16[4,2,192,256]{3,2,1,0:T(8,128)(2,1)S(1)} %add.138.refs_2_), channel_id=1, source_target_pairs={{0,4},{4,0},{8,12},{12,8},{16,20},{20,16},{24,28},{28,24},{1,5},{5... | collective-permute-start | bytes 2359304 | tf_op jit(solution)/shard_map/ppermute | solution.py:440
  224.4 35.4 %collective-permute-start.33 = (bf16[192,2048]{1,0:T(8,128)(2,1)S(1)}, bf16[192,2048]{1,0:T(8,128)(2,1)S(1)}, u32[]{:S(2)}, u32[]{:S(2)}) collective-permute-start(bf16[192,2048]{1,0:T(8,128)(2,1)S(1)} %add_convert_fusion.1), channel_id=1, source_target_pairs={{0,2},{1,3},{2,0},{3,1},{4,6},{5,7},{6,4},{7,5},{8,10},{9,11},{10,... | collective-permute-start | bytes 2359304 | tf_op jit(solution)/shard_map/ppermute | solution.py:437
  226.4 34.7 %collective-permute-start.35 = (bf16[192,2048]{1,0:T(8,128)(2,1)S(1)}, bf16[192,2048]{1,0:T(8,128)(2,1)S(1)}, u32[]{:S(2)}, u32[]{:S(2)}) collective-permute-start(bf16[192,2048]{1,0:T(8,128)(2,1)S(1)} %add_convert_fusion), channel_id=1, source_target_pairs={{0,3},{1,2},{2,1},{3,0},{4,7},{5,6},{6,5},{7,4},{8,11},{9,10},{10,... | collective-permute-start | bytes 2359304 | tf_op jit(solution)/shard_map/ppermute | solution.py:437
  227.9 41.3 %collective-permute-start.36 = (bf16[192,2048]{1,0:T(8,128)(2,1)}, bf16[192,2048]{1,0:T(8,128)(2,1)S(1)}, u32[]{:S(2)}, u32[]{:S(2)}) collective-permute-start(bf16[192,2048]{1,0:T(8,128)(2,1)} %bitcast.3.refs_1_), channel_id=1, source_target_pairs={{0,4},{4,0},{8,12},{12,8},{16,20},{20,16},{24,28},{28,24},{1,5},{5... | collective-permute-start | bytes 2359304 | tf_op jit(solution)/shard_map/ppermute | solution.py:440
  227.9 42.0 %collective-permute-start.37 = (bf16[192,2048]{1,0:T(8,128)(2,1)}, bf16[192,2048]{1,0:T(8,128)(2,1)S(1)}, u32[]{:S(2)}, u32[]{:S(2)}) collective-permute-start(bf16[192,2048]{1,0:T(8,128)(2,1)} %collective-permute-done.10.refs_2_), channel_id=1, source_target_pairs={{0,4},{4,0},{8,12},{12,8},{16,20},{20,16},{24,28},{28,24},{1,5},{5... | collective-permute-start | bytes 2359304 | tf_op jit(solution)/shard_map/ppermute | solution.py:440
  244.1 25.8 %collective-permute-start.38 = (bf16[192,2048]{1,0:T(8,128)(2,1)}, bf16[192,2048]{1,0:T(8,128)(2,1)S(1)}, u32[]{:S(2)}, u32[]{:S(2)}) collective-permute-start(bf16[192,2048]{1,0:T(8,128)(2,1)} %collective-permute-done.11.refs_3_), channel_id=1, source_target_pairs={{0,4},{4,0},{8,12},{12,8},{16,20},{20,16},{24,28},{28,24},{1,5},{5... | collective-permute-start | bytes 2359304 | tf_op jit(solution)/shard_map/ppermute | solution.py:440
  268.7 34.5 %collective-permute-start.41 = (bf16[192,2048]{1,0:T(8,128)(2,1)}, bf16[192,2048]{1,0:T(8,128)(2,1)}, u32[]{:S(2)}, u32[]{:S(2)}) collective-permute-start(bf16[192,2048]{1,0:T(8,128)(2,1)} %get-tuple-element.84.refs_33_), channel_id=1, source_target_pairs={{0,2},{1,3},{2,0},{3,1},{4,6},{5,7},{6,4},{7,5},{8,10},{9,11},{10,... | collective-permute-start | bytes 2359304 | tf_op jit(solution)/shard_map/ppermute | solution.py:437
  269.2 34.0 %collective-permute-start.40 = (bf16[192,2048]{1,0:T(8,128)(2,1)}, bf16[192,2048]{1,0:T(8,128)(2,1)}, u32[]{:S(2)}, u32[]{:S(2)}) collective-permute-start(bf16[192,2048]{1,0:T(8,128)(2,1)} %get-tuple-element.84.refs_33_), channel_id=1, source_target_pairs={{0,1},{1,0},{2,3},{3,2},{4,5},{5,4},{6,7},{7,6},{8,9},{9,8},{10,11... | collective-permute-start | bytes 2359304 | tf_op jit(solution)/shard_map/ppermute | solution.py:437
  269.8 36.7 %collective-permute-start.39 = (bf16[192,2048]{1,0:T(8,128)(2,1)}, bf16[192,2048]{1,0:T(8,128)(2,1)}, u32[]{:S(2)}, u32[]{:S(2)}) collective-permute-start(bf16[192,2048]{1,0:T(8,128)(2,1)} %collective-permute-done.12.refs_4_), channel_id=1, source_target_pairs={{0,4},{4,0},{8,12},{12,8},{16,20},{20,16},{24,28},{28,24},{1,5},{5... | collective-permute-start | bytes 2359304 | tf_op jit(solution)/shard_map/ppermute | solution.py:440
  269.8 36.7 %collective-permute-start.43 = (bf16[192,2048]{1,0:T(8,128)(2,1)}, bf16[192,2048]{1,0:T(8,128)(2,1)}, u32[]{:S(2)}, u32[]{:S(2)}) collective-permute-start(bf16[192,2048]{1,0:T(8,128)(2,1)} %get-tuple-element.84.refs_33_), channel_id=1, source_target_pairs={{0,4},{4,0},{8,12},{12,8},{16,20},{20,16},{24,28},{28,24},{1,5},{5... | collective-permute-start | bytes 2359304 | tf_op jit(solution)/shard_map/ppermute | solution.py:440
  (55 other events, 903.0 us)

commit v5 on v4

--- a/solution.py
+++ b/solution.py
@@ -545,8 +545,6 @@
     )
     own_tokens = tokens[0]
     token_own, token_near = gathered(own_tokens)
-    weights_in = [cut[0]] + [across(cut[d], d) for d in range(1, n)]
-    weights_out = [cut[n]] + [across(cut[n + d], d) for d in range(1, n)]
 
     def cut_hidden(me_ref, *refs):
         gates, ups, downs = (refs[i * n : (i + 1) * n] for i in range(3))
@@ -573,144 +571,10 @@
         pl.BlockSpec((1, n) + piece, lambda q, me: (q, 0, 0, 0)),
         name="cut_hidden",
     )
-    first_pieces = [across(hidden_cut[0, d], d) for d in range(1, n)]
+    cut, hidden_cut = lax.optimization_barrier((cut, hidden_cut))
+    weights_in = [cut[0]] + [across(cut[d], d) for d in range(1, n)]
     own_cotangent = cotangent[0]
-    cot_own = [own_cotangent] + [across(own_cotangent, d) for d in range(1, n)]
-
-    def project(me_ref, *refs):
-        near_tokens = refs[: 2 * n]
-        pieces = refs[2 * n : 3 * n]
-        cos_ref, sin_ref, kvcos_ref, kvsin_ref = refs[3 * n : 3 * n + 4]
-        normed_ref, query_ref, kv_ref, gains_ref = refs[3 * n + 4 :]
-        chip, side = me_ref[0], me_ref[1]
-        for j in range(n):
-            both = pieces[j][wide:, :].astype(F32)
-            gains_ref[0:1, column(chip ^ j, wide)] = both[0:1]
-            gains_ref[1:2, column(chip ^ j, wide)] = both[8:9]
-        for d in range(n):
-            for e in range(2):
-                slot = side ^ e
-                values = near_tokens[e * n + d][...].astype(F32)
-                inverse = lax.rsqrt(jnp.mean(values * values, axis=-1, keepdims=True) + epsilon)
-                normed_ref[d, slot] = (values * inverse * gains_ref[0:1, :]).astype(BF16)
-                both = jnp.zeros((rows, 2 * HD), F32)
-                for j in range(n):
-                    both += matmul(
-                        normed_ref[d, slot, :, column(chip ^ j, wide)], pieces[j][:wide, :]
-                    )
-                query, kv = both[:, :HD], both[:, HD:]
-                query_ref[d, slot] = (
-                    query * cos_ref[slot] + turn(query) * sin_ref[slot]
-                ).astype(BF16)
-                kv_ref[d, slot] = (kv * kvcos_ref[slot] + turn(kv) * kvsin_ref[slot]).astype(BF16)
-
-    head_shape = (n, 2, rows, HD)
-    tables = [t.reshape(2, rows, HD) for t in (cosine, sine, kv_cosine, kv_sine)]
-    normed, query_rot, own_kv, gains = run_whole(
-        project,
-        me,
-        token_own + token_near + weights_in + tables,
-        [
-            shape((n, 2, rows, width)),
-            shape(head_shape),
-            shape(head_shape),
-            shape((2, width), F32),
-        ],
-        flops=2 * plane_rows * width * 2 * HD,
-        name="project",
-    )
-
-    rightward, leftward = [own_kv], [own_kv]
-    for _ in range(planes - 1):
-        rightward.append(along(rightward[-1], 1))
-        leftward.append(along(leftward[-1], -1))
-    kv_mine = [own_kv] + [rightward[k] + leftward[planes - k] for k in range(1, planes)]
-    kv_near = [sibling(block) for block in kv_mine]
-
-    head_spec = pl.BlockSpec((1, 2, rows, HD), lambda i, me: (i, 0, 0, 0))
-    id_specs = [
-        pl.BlockSpec((1, pair, 1), lambda i, me: (i, 0, 0)),
-        pl.BlockSpec((1, planes, 1, pair), lambda i, me: (i, 0, 0, 0)),
-    ]
-
-    def scored(side, query, query_id, key_id, mine, near):
-        keys, values, scores = [], [], []
-        for k in range(planes):
-            a = mine[k][0].reshape(pair, HD)
-            b = near[k][0].reshape(pair, HD)
-            keys.append(jnp.where(side == 0, a, b))
-            values.append(jnp.where(side == 0, b, a))
-            score = matmul_nt(query, keys[k]) * scale
-            scores.append(jnp.where(key_id[0, k] <= query_id[0], score, masked_score))
-        top = functools.reduce(jnp.maximum, [jnp.max(s, axis=-1, keepdims=True) for s in scores])
-        raised = [jnp.exp(s - top) for s in scores]
-        inverse = 1.0 / sum(jnp.sum(r, axis=-1, keepdims=True) for r in raised)
-        return keys, values, [r * inverse for r in raised]
-
-    def spread(step, side, whole, own_refs, near_refs):
-        for d in range(n):
-
-            @pl.when(step == d)
-            def _():
-                own_refs[d][...] = whole[side]
-                near_refs[d][...] = whole[1 - side]
-
-    def attend(me_ref, query_ref, query_id, key_id, *refs):
-        mine, near, out_w = refs[:planes], refs[planes : 2 * planes], refs[2 * planes : 2 * planes + n]
-        attended_ref = refs[2 * planes + n]
-        own_refs = refs[2 * planes + n + 1 : 2 * planes + 2 * n + 1]
-        near_refs = refs[2 * planes + 2 * n + 1 : 2 * planes + 3 * n + 1]
-        whole = refs[-1]
-        chip, side = me_ref[0], me_ref[1]
-        query = query_ref[0].reshape(pair, HD)
-        _, values, probs = scored(side, query, query_id, key_id, mine, near)
-        total = jnp.zeros((pair, HD), F32)
-        for k in range(planes):
-            total += matmul(probs[k].astype(BF16), values[k])
-        attended = total.astype(BF16)
-        attended_ref[0] = attended.reshape(2, rows, HD)
-        for j in range(n):
-            whole[:, :, column(chip ^ j, wide)] = (
-                matmul(attended, out_w[j][...]).astype(BF16).reshape(2, rows, wide)
-            )
-        spread(pl.program_id(0), side, whole, own_refs, near_refs)
-
-    early = lax.optimization_barrier([query_rot] + cot_own[1:] + first_pieces)
-    query_rot, cot_own[1:], first_pieces = early[0], early[1:n], early[n:]
-    cot_near = [sibling(block) for block in cot_own]
-
     block = (rows, width)
-    attend_flops = 4 * plane_rows * planes * pair * HD + 2 * plane_rows * HD * width
-    attended, *partial = run_grid(
-        attend,
-        me,
-        (n,),
-        [query_rot, query_ids, key_ids] + kv_mine + kv_near + weights_out,
-        [head_spec] + id_specs + [head_spec] * (2 * planes) + [fixed((HD, wide))] * n,
-        [shape(head_shape)] + [shape(block)] * (2 * n),
-        [head_spec] + [pl.BlockSpec(block, lambda i, me: (0, 0))] * (2 * n),
-        scratch=[pltpu.VMEM((2, rows, width), BF16)],
-        flops=attend_flops,
-        name="attend",
-    )
-    middle_terms = reduced(partial[:n], partial[n:])
-
-    def second_norm(me_ref, token_ref, gains_ref, *refs):
-        terms, (middle_ref, normed_ref) = refs[:-2], refs[-2:]
-        middle = token_ref[...].astype(F32)
-        middle += sum(t[...].astype(F32) for t in terms)
-        inverse = lax.rsqrt(jnp.mean(middle * middle, axis=-1, keepdims=True) + epsilon)
-        middle_ref[...] = middle
-        normed_ref[...] = (middle * inverse * gains_ref[1:2, :]).astype(BF16)
-
-    middle, own_normed_two = run_whole(
-        second_norm,
-        me,
-        [own_tokens, gains] + middle_terms,
-        [shape(block, F32), shape(block)],
-        name="second_norm",
-    )
-    two_own, two_near = gathered(own_normed_two)
 
     tile = plane_rows // 3
     tiles_count = 3 * QUARTERS + 3
@@ -718,28 +582,22 @@
     units = 2 * tiles_count
     unit = (2, quarter, wide)
     held_sums, held_ends = 4, 3
-    BACK, OUT, ONE = range(3)
+    MID, BACK, OUT, ONE = range(4)
+    query_slot, attended_slot, query_grad_slot, kv_grad_slot = range(2 * planes, 2 * planes + 4)
+    kept_slots = 2 * planes + 2
     columns = (plane_rows, HD)
     lanes = (8, wide)
     dma = pltpu.SemaphoreType.DMA
 
     in_hbm = dict(
-        two=two_own + two_near,
-        cot=cot_own + cot_near,
-        first=first_pieces,
+        near_tokens=token_own + token_near,
         in_weight=weights_in,
-        out_weight=weights_out,
-        kv_mine=[a.reshape(columns) for a in kv_mine],
-        kv_near=[a.reshape(columns) for a in kv_near],
+        out_cut=cut[n:],
         cut=hidden_cut,
-        query=query_rot.reshape(columns),
-        attended=attended.reshape(columns),
-        normed=normed.reshape(plane_rows, width),
-        middle=middle,
+        cotangent=own_cotangent,
         tokens=own_tokens,
     )
     in_vmem = dict(
-        gains=gains,
         tables=jnp.stack([cosine, sine, kv_cosine, kv_sine]),
         query_ids=query_ids,
         key_ids=key_ids,
@@ -752,8 +610,13 @@
         finals=unit_array,
         owned=unit_array,
         near=unit_array,
-        row_near=shape((3, n) + block),
-        row_far=shape((3, n) + block),
+        row_near=shape((4, n) + block),
+        row_far=shape((4, n) + block),
+        cot_all=shape((2, n) + block),
+        kept=shape((kept_slots,) + columns),
+        out_weight=shape((2, 2, HD, wide)),
+        normed=shape((plane_rows, width)),
+        middle=shape(block, F32),
         branch_all=shape((n, 2) + block),
         kv_other=shape((planes,) + columns),
         kv_down=shape((planes,) + columns),
@@ -782,7 +645,9 @@
         gain_far=pltpu.VMEM((n,) + lanes, F32),
         gain_sum=pltpu.VMEM((4,) + lanes, F32),
         gain_in=pltpu.VMEM((4,) + lanes, F32),
-        load_sem=dma((4 * n + n - 1,)),
+        load_sem=dma((4 * n + n,)),
+        gains=pltpu.VMEM((8, width), F32),
+        gain_rows=pltpu.VMEM((n, 16, wide), BF16),
         feed_local=dma((QUARTERS,)),
         feed_send=dma((QUARTERS * n,)),
         feed_recv=dma((QUARTERS * n,)),
@@ -803,10 +668,28 @@
         sib_send=dma((units,)),
         sib_recv=dma((units,)),
         row_sem=dma((n,)),
-        row_near_send=dma((3 * n,)),
-        row_near_recv=dma((3 * n,)),
-        row_far_send=dma((3 * n,)),
-        row_far_recv=dma((3 * n,)),
+        row_near_send=dma((4 * n,)),
+        row_near_recv=dma((4 * n,)),
+        row_far_send=dma((4 * n,)),
+        row_far_recv=dma((4 * n,)),
+        out_send=dma((n,)),
+        out_recv=dma((n,)),
+        cot_send=dma((n,)),
+        cot_recv=dma((n,)),
+        cot_near_send=dma((n,)),
+        cot_near_recv=dma((n,)),
+        two_local=dma((1,)),
+        two_far_send=dma((n,)),
+        two_far_recv=dma((n,)),
+        two_near_send=dma((n,)),
+        two_near_recv=dma((n,)),
+        climb_send=dma((planes,)),
+        climb_recv=dma((planes,)),
+        fall_send=dma((planes,)),
+        fall_recv=dma((planes,)),
+        pass_send=dma((planes,)),
+        pass_recv=dma((planes,)),
+        keep_sem=dma((3,)),
         branch_local=dma((1,)),
         branch_send=dma((n,)),
         branch_recv=dma((n,)),
@@ -1168,16 +1051,267 @@
             while loads:
                 loads.pop().wait()
 
-        for base, sources in ((0, r.two), (plane_rows, r.cot)):
-            for i in range(2 * n):
-                load(sources[i], work.at[pl.ds(base + i * rows, rows)])
+        def out_far(d):
+            return remote(
+                r.out_cut[d],
+                r.theirs.at[d // 2, d % 2],
+                r.out_send.at[d],
+                r.out_recv.at[d],
+                (here, chips[d]),
+            )
+
+        def cot_far(d):
+            return remote(
+                r.cotangent, r.cot_all.at[0, d], r.cot_send.at[d], r.cot_recv.at[d], (here, chips[d])
+            )
+
+        def cot_near(d):
+            source = r.cotangent if d == 0 else r.cot_all.at[0, d]
+            return remote(
+                source, r.cot_all.at[1, d], r.cot_near_send.at[d], r.cot_near_recv.at[d], other_core
+            )
+
         for d in range(1, n):
-            load(r.first[d - 1], feed.at[0, d])
+            out_far(d).start()
+        for d in range(1, n):
+            feed_copy(0, d).start()
+        for d in range(1, n):
+            cot_far(d).start()
+        cot_near(0).start()
+        for i in range(2 * n):
+            load(r.near_tokens[i], work.at[pl.ds(plane_rows + i * rows, rows)])
+        for j in range(n):
+            for h in range(2):
+                load(r.in_weight[j].at[pl.ds(h * HD, HD)], r.sums.at[j, h])
+            load(r.in_weight[j].at[pl.ds(wide, 16)], r.gain_rows.at[j])
+        loaded()
+        load(r.out_cut[0], r.theirs.at[0, 0])
         for q in range(QUARTERS):
             feed_own(q).start()
+        for j in range(n):
+            both = r.gain_rows[j].astype(F32)
+            r.gains[0:1, blocks[j]] = both[0:1]
+            r.gains[1:2, blocks[j]] = both[8:9]
+
+        def project(d, _):
+            for c in range(2):
+                first = ((side + c) % 2 * n + d) * rows
+
+                def some(s, _, c=c, first=first):
+                    now = pl.ds(pl.multiple_of(plane_rows + first + s * few, few), few)
+                    then = pl.ds(pl.multiple_of((2 * d + c) * rows + s * few, few), few)
+                    values = work[now, :].astype(F32)
+                    inverse = lax.rsqrt(jnp.mean(values * values, axis=-1, keepdims=True) + epsilon)
+                    work[then, :] = (values * inverse * r.gains[0:1, :]).astype(BF16)
+                    return 0
+
+                lax.fori_loop(0, rows // few, some, 0)
+            now = span(d * pair, pair)
+            both = jnp.zeros((pair, 2 * HD), F32)
+            for j in range(n):
+                for h in range(2):
+                    here_half = pl.ds(pl.multiple_of(chips[j] * wide + h * HD, HD), HD)
+                    both += matmul(work[now, here_half], r.sums[j, h])
+            query, kv = both[:, :HD], both[:, HD:]
+            query = query * r.tables[0] + turn(query) * r.tables[1]
+            heads[query_slot, now, :] = query.astype(BF16)
+            kv = kv * r.tables[2] + turn(kv) * r.tables[3]
+            heads[0, now, :] = kv.astype(BF16)
+            return 0
+
+        lax.fori_loop(0, n, project, 0)
+        keep_normed = local(work.at[pl.ds(0, plane_rows)], r.normed, r.keep_sem.at[0])
+        keep_normed.start()
+
+        def climb(s):
+            return remote(heads.at[s - 1], heads.at[s], r.climb_send.at[s], r.climb_recv.at[s], above)
+
+        def fall(s):
+            return remote(
+                heads.at[(planes - s + 1) % planes],
+                heads.at[planes - s],
+                r.fall_send.at[s],
+                r.fall_recv.at[s],
+                below,
+            )
+
+        def pass_on(k):
+            return remote(
+                heads.at[k], heads.at[planes + k], r.pass_send.at[k], r.pass_recv.at[k], other_core
+            )
+
+        def kv_leave(s):
+            @pl.when((z - s + 1 >= 0) & (z + 1 < planes))
+            def _():
+                climb(s).start()
+
+            @pl.when((z + s - 1 < planes) & (z >= 1))
+            def _():
+                fall(s).start()
+
+        def kv_come(s):
+            @pl.when(z - s >= 0)
+            def _():
+                climb(s).wait_recv()
+
+            @pl.when(z + s < planes)
+            def _():
+                fall(s).wait_recv()
+
+        kv_leave(1)
+        pass_on(0).start()
         for d in range(1, n):
+            out_far(d).wait_recv()
+        loaded()
+        keep_out = local(r.theirs, r.out_weight, r.keep_sem.at[1])
+        keep_out.start()
+        kv_come(1)
+        kv_leave(2)
+
+        @pl.when(z >= 1)
+        def _():
+            pass_on(1).start()
+
+        @pl.when(z + 1 < planes)
+        def _():
+            pass_on(3).start()
+
+        kv_come(2)
+        kv_leave(3)
+        pass_on(2).start()
+        for d in range(1, n):
+            cot_far(d).wait_recv()
+            cot_near(d).start()
+        keep_normed.wait()
+        kv_come(3)
+
+        @pl.when(z == 0)
+        def _():
+            pass_on(1).start()
+
+        @pl.when(z == planes - 1)
+        def _():
+            pass_on(3).start()
+
+        for k in range(planes):
+            pass_on(k).wait_recv()
+
+        def scored(d, now):
+            keys, values, scores = [], [], []
+            for k in range(planes):
+                a, b = heads[k, now, :], heads[planes + k, now, :]
+                keys.append(jnp.where(side == 0, a, b))
+                values.append(jnp.where(side == 0, b, a))
+                score = matmul_nt(heads[query_slot, now, :], keys[k]) * scale
+                scores.append(jnp.where(r.key_ids[d, k] <= r.query_ids[d], score, masked_score))
+            top = functools.reduce(jnp.maximum, [jnp.max(s, axis=-1, keepdims=True) for s in scores])
+            raised = [jnp.exp(s - top) for s in scores]
+            inverse = 1.0 / sum(jnp.sum(e, axis=-1, keepdims=True) for e in raised)
+            return keys, values, [e * inverse for e in raised]
+
+        def put_rows(base, d, now_values, block_at):
+            first = pl.ds(pl.multiple_of(base + (side * n + d) * rows, rows), rows)
+            second = pl.ds(pl.multiple_of(base + ((1 - side) * n + d) * rows, rows), rows)
+            work[first, block_at] = now_values[:rows]
+            work[second, block_at] = now_values[rows:]
+
+        def attend(d, _):
+            now = span(d * pair, pair)
+            _, values, probs = scored(d, now)
+            total = jnp.zeros((pair, HD), F32)
+            for k in range(planes):
+                total += matmul(probs[k].astype(BF16), values[k])
+            low_total = total.astype(BF16)
+            heads[attended_slot, now, :] = low_total
+            for j in range(n):
+                put_rows(
+                    plane_rows,
+                    d,
+                    matmul(low_total, r.theirs[j // 2, j % 2]).astype(BF16),
+                    blocks[j],
+                )
+            return 0
+
+        lax.fori_loop(0, n, attend, 0)
+        rows_hand_over(MID, plane_rows)
+        keep_heads = local(heads.at[pl.ds(0, kept_slots)], r.kept, r.keep_sem.at[2])
+        keep_heads.start()
+        load(r.tokens, r.own_rows)
+        rows_send(MID, plane_rows)
+        loaded()
+        keep_out.wait()
+        for s in range(1, planes):
+
+            @pl.when((z - s + 1 >= 0) & (z + 1 < planes))
+            def _():
+                climb(s).wait_send()
+
+            @pl.when((z + s - 1 < planes) & (z >= 1))
+            def _():
+                fall(s).wait_send()
+
+        for k in range(planes):
+            pass_on(k).wait_send()
+
+        rows_arrive(MID, plane_rows)
+
+        def second_norm(c, _):
+            at = span(c * few, few)
+            total = r.own_rows[at, :].astype(F32)
+            total += work[pl.ds(pl.multiple_of(plane_rows + c * few, few), few), :].astype(F32)
+            for d in range(n):
+                total += r.some_rows[d, at, :].astype(F32)
+            inverse = lax.rsqrt(jnp.mean(total * total, axis=-1, keepdims=True) + epsilon)
+            r.wide_rows[at, :] = total
+            r.own_rows[at, :] = (total * inverse * r.gains[1:2, :]).astype(BF16)
+            return 0
+
+        lax.fori_loop(0, rows // few, second_norm, 0)
+
+        def two_far(d):
+            return remote(
+                r.own_rows,
+                work.at[pl.ds(d * rows, rows)],
+                r.two_far_send.at[d],
+                r.two_far_recv.at[d],
+                (here, chips[d]),
+            )
+
+        def two_near(d):
+            source = r.own_rows if d == 0 else work.at[pl.ds(d * rows, rows)]
+            return remote(
+                source,
+                work.at[pl.ds((n + d) * rows, rows)],
+                r.two_near_send.at[d],
+                r.two_near_recv.at[d],
+                other_core,
+            )
+
+        for d in (3, 1, 2):
+            two_far(d).start()
+        two_near(0).start()
+        two_own = local(r.own_rows, work.at[pl.ds(0, rows)], r.two_local.at[0])
+        two_own.start()
+        load(r.wide_rows, r.middle)
+        rows_sent(MID, plane_rows)
+        for d in range(n):
+            cot_near(d).wait_recv()
+            if d > 0:
+                load(r.cot_all.at[0, d], work.at[pl.ds(plane_rows + d * rows, rows)])
+            else:
+                load(r.cotangent, work.at[pl.ds(plane_rows, rows)])
+            load(r.cot_all.at[1, d], work.at[pl.ds(plane_rows + (n + d) * rows, rows)])
+        keep_heads.wait()
+        for d in (1, 2, 3):
+            two_far(d).wait_recv()
+            two_near(d).start()
+        for d in range(1, n):
+            feed_copy(0, d).wait_recv()
             feed_copy(1, d).start()
+        two_own.wait()
         loaded()
+        for d in range(n):
+            two_near(d).wait_recv()
 
         def quarter_step(q, _):
             step(3 * q - 3)
@@ -1236,6 +1370,9 @@
         for t in (query_at - 2, query_at - 1):
             staged(t)
 
+        for d in range(1, n):
+            two_near(d).wait_send()
+
         def back_step(s, _):
             now = span(s * pair, pair)
             lefts = [
@@ -1267,25 +1404,23 @@
                 work[then, blocks[j]] = total.astype(BF16)
             return 0
 
-        load(r.middle, r.wide_rows)
         lax.fori_loop(half, n, out_step, 0)
         rows_hand_over(OUT, plane_rows)
         advance(TICKS[2])
         lax.fori_loop(0, half, out_step, 0)
         advance(TICKS[3])
 
-        for k in range(planes):
-            load(r.kv_mine[k], heads.at[k])
-            load(r.kv_near[k], heads.at[planes + k])
-        load(r.query, heads.at[2 * planes])
-        load(r.attended, heads.at[2 * planes + 1])
+        load(r.kept, heads.at[pl.ds(0, kept_slots)])
         for j in range(n):
             load(r.in_weight[j].at[pl.ds(0, wide)], feed.at[0, j, pl.ds(0, wide)])
-            load(r.out_weight[j], feed.at[0, j, pl.ds(wide, HD)])
+            load(r.out_weight.at[j // 2, j % 2], feed.at[0, j, pl.ds(wide, HD)])
 
         rows_arrive(BACK, 0)
         loaded()
-        load(r.cot[0], r.own_rows)
+        for d in range(1, n):
+            two_far(d).wait_send()
+        two_near(0).wait_send()
+        load(r.cotangent, r.own_rows)
         loaded()
 
         def second_use(at, back):
@@ -1334,8 +1469,6 @@
         rows_send(OUT, plane_rows)
         loaded()
 
-        query_slot, attended_slot, query_grad_slot, kv_grad_slot = range(2 * planes, 2 * planes + 4)
-
         def attend_back(d, _):
             now = span(d * pair, pair)
             query = heads[query_slot, now, :]
@@ -1343,17 +1476,7 @@
             for j in range(n):
                 attended_grad += matmul_nt(work[now, blocks[j]], feed[0, j, wide:, :])
             attended_grad = attended_grad.astype(BF16)
-            keys, values, scores = [], [], []
-            for k in range(planes):
-                a, b = heads[k, now, :], heads[planes + k, now, :]
-                keys.append(jnp.where(side == 0, a, b))
-                values.append(jnp.where(side == 0, b, a))
-                score = matmul_nt(query, keys[k]) * scale
-                scores.append(jnp.where(r.key_ids[d, k] <= r.query_ids[d], score, masked_score))
-            top = functools.reduce(jnp.maximum, [jnp.max(s, axis=-1, keepdims=True) for s in scores])
-            raised = [jnp.exp(s - top) for s in scores]
-            inverse = 1.0 / sum(jnp.sum(e, axis=-1, keepdims=True) for e in raised)
-            probs = [e * inverse for e in raised]
+            keys, values, probs = scored(d, now)
             low = [p.astype(BF16) for p in probs]
             shares = [matmul_nt(attended_grad, values[k]) for k in range(planes)]
             delta = sum(
@@ -1468,12 +1591,8 @@
             grad = grad * r.tables[2] + turn_back(grad * r.tables[3])
             heads[kv_grad_slot, now, :] = grad.astype(BF16)
             left = jnp.concatenate([heads[query_grad_slot, now, :], grad.astype(BF16)], axis=1)
-            first = span((side * n + d) * rows, rows)
-            second = span(((1 - side) * n + d) * rows, rows)
             for j in range(n):
-                total = matmul_nt(left, feed[0, j, :wide, :]).astype(BF16)
-                work[first, blocks[j]] = total[:rows]
-                work[second, blocks[j]] = total[rows:]
+                put_rows(0, d, matmul_nt(left, feed[0, j, :wide, :]).astype(BF16), blocks[j])
             return 0
 
         lax.fori_loop(0, n, project_back, 0)
@@ -1546,9 +1665,14 @@
         loaded()
         rows_arrive(OUT, plane_rows)
         rows_sent(ONE, 0)
-        for q in range(1, QUARTERS):
+        for q in range(QUARTERS):
             for d in range(1, n):
                 feed_copy(q, d).wait_send()
+        for d in range(1, n):
+            out_far(d).wait_send()
+            cot_far(d).wait_send()
+        for d in range(n):
+            cot_near(d).wait_send()
         for k in range(planes):
             kv_hand_over(k).wait_send()
         for k in range(1, planes):
@@ -1666,7 +1790,7 @@
         name="place_kv",
     )
 
-    output = middle + results.out_own.astype(F32) + results.row_near[OUT, 0].astype(F32)
+    output = results.middle + results.out_own.astype(F32) + results.row_near[OUT, 0].astype(F32)
     output = output + sum(results.row_far[OUT, d].astype(F32) for d in range(1, n))
 
     return (

time: 895 us -> 824 us (0.921)
  waiting for transfers between devices: 184 us -> 31.4 us
  Pallas kernels: 621 us -> 762 us
  starting transfers between devices: 48.8 us -> 10.5 us
  other arithmetic: 17 us -> 7.33 us
    pallas_call x1, Pallas kernels: 525 us -> 699 us  [plane_layer(): pl.pallas_call(backward, out_shape=jax.tree.leaves(out_hbm), in_specs=[pl...]
    ppermute x21 -> x6, waiting for transfers between devices: 155 us -> 31.4 us  [across(): return lax.ppermute(value, 'fsdp', [(i, i ^ d) for i in range(n)])]
    ppermute x6 -> x0, waiting for transfers between devices: 27.1 us -> none  [along(): lax.ppermute(value, 'ctx', [(a, b) for a, b in pairs if 0 <= b < ctx_count])]
    ppermute x6 -> x0, starting transfers between devices: 17.9 us -> none  [along(): lax.ppermute(value, 'ctx', [(a, b) for a, b in pairs if 0 <= b < ctx_count])]
    ppermute x21 -> x6, starting transfers between devices: 26.8 us -> 9.49 us  [across(): return lax.ppermute(value, 'fsdp', [(i, i ^ d) for i in range(n)])]
    pallas_call x6 -> x5, Pallas kernels: 80.8 us -> 63.6 us  [run_grid(): pl.pallas_call(body, out_shape=outs, grid_spec=pltpu.PrefetchScalarGridSp...]
    pallas_call x2 -> x0, Pallas kernels: 15.9 us -> none  [run_whole(): pl.pallas_call(body, out_shape=outs, in_specs=[pl.BlockSpec(memory_space=...]
  transfers between devices with their start and end apart: 47 -> 10, of which waited for: 16 -> 2; matrix products, arithmetic and copies ran while one was open for 2% -> 1% of each run, Pallas kernels for 2% -> 2%
where the time goes in v5:
time: 824 us; the launch traced here: 821 us
  Pallas kernels  762 us (92%)
  waiting for transfers between devices  31.4 us (4%)
  starting transfers between devices  10.5 us (1%)
  local copies, waits for them, and re-layouts  8.96 us (1%)
    pallas_call x1, Pallas kernels, plane_layer(): pl.pallas_call(backward, out_shape=jax.tree.leaves(out_hbm), in_specs=[pl...  699 us
    pallas_call x5, Pallas kernels, run_grid(): pl.pallas_call(body, out_shape=outs, grid_spec=pltpu.PrefetchScalarGridSp...  63.6 us
    ppermute x6, waiting for transfers between devices, across(): return lax.ppermute(value, 'fsdp', [(i, i ^ d) for i in range(n)])  31.4 us
  transfers between devices with their start and end apart: 10, of which 2 were waited for; matrix products, arithmetic and copies ran while one was open for 1% of the time, Pallas kernels for 2%

profile of v5, /device:TPU:0, one launch (start us, length us, event | category | flops | bytes accessed | tf_op | source)
XLA Modules:
  0.0 821.2 jit_solution(4945109934736698055)
XLA Ops:
  0.6 4.0 collective-permute-start.5
  5.2 1.3 reshape.290.refs_16_
  6.5 1.3 reshape.291.refs_17_
  7.8 0.6 pad_add_fusion.me_ref
  8.4 10.1 %cut_hidden.1.refs_1_ = bf16[4,4,768,512]{3,2,1,0:T(8,128)(2,1)} custom-call(s32[2]{0:T(128)} %pad_add_fusion.me_ref, bf16[512,8192]{1,0:T(8,128)(2,1)} %refs_3_.3, bf16[512,8192]{1,0:T(8,128)(2,1)} %refs_3_.3, bf16[512,8192]{1,0:T(8,128)(2,1)} %refs_3_.3, bf16[512,8192]{1,0:T(8,128)(2,1)} %refs_3_.3, bf16[512,8192]{1,0:T(8,128)(2,1)} %refs_7_.3, ...), custom_call_target="tpu_custom_call" | custom-call | bytes 113246208 | tf_op jit(solution)/shard_map/cut_hidden/pallas_call | solution.py:366
  18.5 4.9 cut_attention.1
  23.4 1.9 collective-permute-start
  25.3 1.5 collective-permute-start.1
  27.0 0.6 gather_fusion
  27.9 23.3 %collective-permute-done.refs_3_ = bf16[528,512]{1,0:T(8,128)(2,1)} collective-permute-done((bf16[528,512]{1,0:T(8,128)(2,1)}, bf16[528,512]{1,0:T(8,128)(2,1)}, u32[]{:S(2)}, u32[]{:S(2)}) %collective-permute-start) | collective-permute-done | bytes 540704 | tf_op jit(solution)/shard_map/ppermute | solution.py:437
  52.3 1.4 collective-permute-start.2
  54.0 0.7 gather_fusion.1
  54.7 0.7 reshape.293.refs_19_
  55.4 1.5 reshape.313.refs_20_
  57.0 1.4 fusion.4
  58.5 1.2 pad_maximum_fusion.refs_21_
  59.7 8.1 collective-permute-done.2.refs_5_
  67.8 698.7 %backward.1 = (bf16[4,2,192,2048]{3,2,1,0:T(8,128)(2,1)}, bf16[2,4,192,2048]{3,2,1,0:T(8,128)(2,1)}, bf16[30,2,256,512]{3,2,1,0:T(8,128)(2,1)}, bf16[30,2,256,51...) custom-call(bf16[192,2048]{1,0:T(8,128)(2,1)} %bitcast.35, ...), custom_call_target="tpu_custom_call" | custom-call | flops 96636764160 | bytes 119633920 | tf_op jit(solution)/shard_map/backward/pallas_call | solution.py:1691
  766.5 5.1 place_kv.1
  771.6 8.4 %place_query.1 = (f32[512,2048]{1,0:T(8,128)}, f32[2048,512]{1,0:T(8,128)}) custom-call(s32[2]{0:T(128)} %pad_add_fusion.me_ref, bf16[15,4,256,512]{3,2,1,0:T(8,128)(2,1)} %bitcast.29, bf16[15,4,256,512]{3,2,1,0:T(8,128)(2,1)} %bitcast.26), custom_call_target="tpu_custom_call" | custom-call | bytes 39845888 | tf_op jit(solution)/shard_map/place_query/pallas_call | solution.py:366
  780.0 35.1 %place_hidden.1 = (f32[512,8192]{1,0:T(8,128)}, f32[512,8192]{1,0:T(8,128)}, f32[8192,512]{1,0:T(8,128)}) custom-call(s32[2]{0:T(128)} %pad_add_fusion.me_ref, bf16[15,4,256,512]{3,2,1,0:T(8,128)(2,1)} %bitcast.30, bf16[15,4,256,512]{3,2,1,0:T(8,128)(2,1)} %bitcast.27), custom_call_target="tpu_custom_call" | custom-call | bytes 81788928 | tf_op jit(solution)/shard_map/place_hidden/pallas_call | solution.py:366
  815.1 1.4 fusion.12
  816.5 3.6 fusion.2
  820.1 1.1 copy.26
  (48 shorter events, 2.5 us)
Async XLA Ops:
  0.6 50.6 %collective-permute-start.5 = (bf16[192,2048]{1,0:T(8,128)(2,1)}, bf16[192,2048]{1,0:T(8,128)(2,1)S(1)}, u32[]{:S(2)}, u32[]{:S(2)}) collective-permute-start(bf16[192,2048]{1,0:T(8,128)(2,1)} %bitcast.36), channel_id=1, source_target_pairs={{0,3},{1,2},{2,1},{3,0},{4,7},{5,6},{6,5},{7,4},{8,11},{9,10},{10,... | collective-permute-start | bytes 2359304 | tf_op jit(solution)/shard_map/ppermute | solution.py:437
  4.6 47.1 %collective-permute-start.4 = (bf16[192,2048]{1,0:T(8,128)(2,1)}, bf16[192,2048]{1,0:T(8,128)(2,1)S(1)}, u32[]{:S(2)}, u32[]{:S(2)}) collective-permute-start(bf16[192,2048]{1,0:T(8,128)(2,1)} %bitcast.37), channel_id=1, source_target_pairs={{0,2},{1,3},{2,0},{3,1},{4,6},{5,7},{6,4},{7,5},{8,10},{9,11},{10,... | collective-permute-start | bytes 2359304 | tf_op jit(solution)/shard_map/ppermute | solution.py:437
  5.1 46.7 %collective-permute-start.3 = (bf16[192,2048]{1,0:T(8,128)(2,1)}, bf16[192,2048]{1,0:T(8,128)(2,1)S(1)}, u32[]{:S(2)}, u32[]{:S(2)}) collective-permute-start(bf16[192,2048]{1,0:T(8,128)(2,1)} %bitcast.38), channel_id=1, source_target_pairs={{0,1},{1,0},{2,3},{3,2},{4,5},{5,4},{6,7},{7,6},{8,9},{9,8},{10,11... | collective-permute-start | bytes 2359304 | tf_op jit(solution)/shard_map/ppermute | solution.py:437
  18.4 8.6 %copy-start = (s32[8]{0:T(128)S(1)}, s32[8]{0:T(128)}, u32[]{:S(2)}) copy-start(s32[8]{0:T(128)} %param.25) | copy-start | bytes 100
  18.4 32.7 %copy-start.5 = (bf16[1,192,2048]{2,1,0:T(8,128)(2,1)S(1)}, bf16[1,192,2048]{2,1,0:T(8,128)(2,1)}, u32[]{:S(2)}) copy-start(bf16[1,192,2048]{2,1,0:T(8,128)(2,1)} %param.13) | copy-start | bytes 2359300
  18.5 35.5 %copy-start.4 = (s32[4,1536]{1,0:T(4,128)S(1)}, s32[4,1536]{1,0:T(4,128)}, u32[]{:S(2)}) copy-start(s32[4,1536]{1,0:T(4,128)} %param.24) | copy-start | bytes 73732
  23.4 27.8 %collective-permute-start = (bf16[528,512]{1,0:T(8,128)(2,1)}, bf16[528,512]{1,0:T(8,128)(2,1)}, u32[]{:S(2)}, u32[]{:S(2)}) collective-permute-start(bf16[528,512]{1,0:T(8,128)(2,1)} %get-tuple-element.53), channel_id=1, source_target_pairs={{0,1},{1,0},{2,3},{3,2},{4,5},{5,4},{6,7},{7,6},{8,9},{9,8},{10,11... | collective-permute-start | bytes 1622024 | tf_op jit(solution)/shard_map/ppermute | solution.py:437
  25.3 27.0 %collective-permute-start.1 = (bf16[528,512]{1,0:T(8,128)(2,1)}, bf16[528,512]{1,0:T(8,128)(2,1)}, u32[]{:S(2)}, u32[]{:S(2)}) collective-permute-start(bf16[528,512]{1,0:T(8,128)(2,1)} %get-tuple-element.54), channel_id=1, source_target_pairs={{0,2},{1,3},{2,0},{3,1},{4,6},{5,7},{6,4},{7,5},{8,10},{9,11},{10,... | collective-permute-start | bytes 1622024 | tf_op jit(solution)/shard_map/ppermute | solution.py:437
  51.2 16.6 %collective-permute-start.6 = (bf16[192,2048]{1,0:T(8,128)(2,1)S(1)}, bf16[192,2048]{1,0:T(8,128)(2,1)}, u32[]{:S(2)}, u32[]{:S(2)}) collective-permute-start(bf16[192,2048]{1,0:T(8,128)(2,1)S(1)} %bitcast.41), channel_id=1, source_target_pairs={{0,4},{4,0},{8,12},{12,8},{16,20},{20,16},{24,28},{28,24},{1,5},{5... | collective-permute-start | bytes 2359304 | tf_op jit(solution)/shard_map/ppermute | solution.py:440
  51.2 8.5 %copy-start.6 = (bf16[192,2048]{1,0:T(8,128)(2,1)}, bf16[192,2048]{1,0:T(8,128)(2,1)S(1)}, u32[]{:S(2)}) copy-start(bf16[192,2048]{1,0:T(8,128)(2,1)S(1)} %collective-permute-done.5.refs_9_) | copy-start | bytes 2359300
  51.2 16.6 %collective-permute-start.9 = (bf16[192,2048]{1,0:T(8,128)(2,1)S(1)}, bf16[192,2048]{1,0:T(8,128)(2,1)}, u32[]{:S(2)}, u32[]{:S(2)}) collective-permute-start(bf16[192,2048]{1,0:T(8,128)(2,1)S(1)} %collective-permute-done.5.refs_9_), channel_id=1, source_target_pairs={{0,4},{4,0},{8,12},{12,8},{16,20},{20,16},{24,28},{28,24},{1,5},{5... | collective-permute-start | bytes 2359304 | tf_op jit(solution)/shard_map/ppermute | solution.py:440
  51.7 8.0 copy-start.7
  51.7 16.1 %collective-permute-start.8 = (bf16[192,2048]{1,0:T(8,128)(2,1)S(1)}, bf16[192,2048]{1,0:T(8,128)(2,1)}, u32[]{:S(2)}, u32[]{:S(2)}) collective-permute-start(bf16[192,2048]{1,0:T(8,128)(2,1)S(1)} %collective-permute-done.4.refs_8_), channel_id=1, source_target_pairs={{0,4},{4,0},{8,12},{12,8},{16,20},{20,16},{24,28},{28,24},{1,5},{5... | collective-permute-start | bytes 2359304 | tf_op jit(solution)/shard_map/ppermute | solution.py:440
  51.8 7.9 copy-start.8
  51.8 16.0 %collective-permute-start.7 = (bf16[192,2048]{1,0:T(8,128)(2,1)S(1)}, bf16[192,2048]{1,0:T(8,128)(2,1)}, u32[]{:S(2)}, u32[]{:S(2)}) collective-permute-start(bf16[192,2048]{1,0:T(8,128)(2,1)S(1)} %collective-permute-done.3.refs_7_), channel_id=1, source_target_pairs={{0,4},{4,0},{8,12},{12,8},{16,20},{20,16},{24,28},{28,24},{1,5},{5... | collective-permute-start | bytes 2359304 | tf_op jit(solution)/shard_map/ppermute | solution.py:440
  52.3 15.5 %collective-permute-start.2 = (bf16[528,512]{1,0:T(8,128)(2,1)}, bf16[528,512]{1,0:T(8,128)(2,1)}, u32[]{:S(2)}, u32[]{:S(2)}) collective-permute-start(bf16[528,512]{1,0:T(8,128)(2,1)} %get-tuple-element.55), channel_id=1, source_target_pairs={{0,3},{1,2},{2,1},{3,0},{4,7},{5,6},{6,5},{7,4},{8,11},{9,10},{10,... | collective-permute-start | bytes 1622024 | tf_op jit(solution)/shard_map/ppermute | solution.py:437
  780.0 36.5 %copy-start.2 = (f32[192,2048]{1,0:T(8,128)S(1)}, f32[192,2048]{1,0:T(8,128)}, u32[]{:S(2)}) copy-start(f32[192,2048]{1,0:T(8,128)} %get-tuple-element.60) | copy-start | bytes 4718596
  780.0 36.5 %copy-start.3 = (bf16[192,2048]{1,0:T(8,128)(2,1)S(1)}, bf16[192,2048]{1,0:T(8,128)(2,1)}, u32[]{:S(2)}) copy-start(bf16[192,2048]{1,0:T(8,128)(2,1)} %get-tuple-element.61) | copy-start | bytes 2359300
  816.5 3.6 copy-start.1

commit v6 on v5

--- a/solution.py
+++ b/solution.py
@@ -323,7 +323,7 @@
 F32 = jnp.float32
 QUARTERS = 4
 MESH = pl.DeviceIdType.MESH
-TICKS = (1, 1, 1, 2, 4, 2, 1, 2, 1, 3, 2, 1, 1)
+TICKS = (2, 1, 2, 2, 3, 2, 1, 1, 1, 4, 4, 2, 2)
 LINES = 2
 
 
@@ -499,21 +499,21 @@
         keys_here = me_ref[1] == 0
         for d in range(n):
             first = outs[d]
-            first[:wide, :HD] = wq[d][...]
+            outs[n + d][...] = wq[d][...]
 
             @pl.when(keys_here)
             def _():
-                first[:wide, HD:] = wk[d][...]
+                first[:wide, :] = wk[d][...]
 
             @pl.when(jnp.logical_not(keys_here))
             def _():
-                first[:wide, HD:] = wv[d][...]
-
-            pick = lax.broadcasted_iota(jnp.int32, (16, wide), 0) < 8
-            first[wide:, :] = jnp.where(pick, one[...].astype(F32), two[...].astype(F32)).astype(
-                BF16
-            )
-            outs[n + d][...] = wo[d][...]
+                first[:wide, :] = wv[d][...]
+
+            pick = lax.broadcasted_iota(jnp.int32, (16, HD), 0) < 8
+            for g, gain in enumerate((one, two)):
+                halves = [gain[:, h * HD : (h + 1) * HD].astype(F32) for h in range(2)]
+                first[wide + 16 * g : wide + 16 * (g + 1), :] = jnp.where(pick, *halves).astype(BF16)
+            outs[2 * n + d][...] = wo[d][...]
 
     def head_of(d):
         return lambda i, me: (0, 2 * (me[0] ^ d) + me[1])
@@ -538,13 +538,14 @@
         + [pl.BlockSpec((wide, HD), chip_of(d)) for d in range(n)] * 2
         + [pl.BlockSpec((HD, wide), head_rows_of(d)) for d in range(n)]
         + [gain_spec, gain_spec],
-        [shape((wide + 16, 2 * HD))] * n + [shape((HD, wide))] * n,
-        [pl.BlockSpec((wide + 16, 2 * HD), lambda i, me: (0, 0))] * n
+        [shape((wide + 32, HD))] * n + [shape((wide, HD))] * n + [shape((HD, wide))] * n,
+        [pl.BlockSpec((wide + 32, HD), lambda i, me: (0, 0))] * n
+        + [pl.BlockSpec((wide, HD), lambda i, me: (0, 0))] * n
         + [pl.BlockSpec((HD, wide), lambda i, me: (0, 0))] * n,
         name="cut_attention",
     )
     own_tokens = tokens[0]
-    token_own, token_near = gathered(own_tokens)
+    near_tokens = [own_tokens] + [across(own_tokens, d) for d in range(1, n)]
 
     def cut_hidden(me_ref, *refs):
         gates, ups, downs = (refs[i * n : (i + 1) * n] for i in range(3))
@@ -576,7 +577,6 @@
     own_cotangent = cotangent[0]
     block = (rows, width)
 
-    tile = plane_rows // 3
     tiles_count = 3 * QUARTERS + 3
     query_at, output_at, kv_at = tiles_count - 3, tiles_count - 2, tiles_count - 1
     units = 2 * tiles_count
@@ -590,9 +590,10 @@
     dma = pltpu.SemaphoreType.DMA
 
     in_hbm = dict(
-        near_tokens=token_own + token_near,
+        near_tokens=near_tokens,
         in_weight=weights_in,
-        out_cut=cut[n:],
+        query_cut=cut[n : 2 * n],
+        out_cut=cut[2 * n :],
         cut=hidden_cut,
         cotangent=own_cotangent,
         tokens=own_tokens,
@@ -613,6 +614,7 @@
         row_near=shape((4, n) + block),
         row_far=shape((4, n) + block),
         cot_all=shape((2, n) + block),
+        query_in=shape((n, wide, HD)),
         kept=shape((kept_slots,) + columns),
         out_weight=shape((2, 2, HD, wide)),
         normed=shape((plane_rows, width)),
@@ -623,6 +625,7 @@
         kv_up=shape((planes,) + columns),
         out_own=shape(block),
         tokens_grad=shape(block, F32),
+        output=shape(block),
         gain_out=shape(lanes, F32),
     )
     scratch = dict(
@@ -647,7 +650,7 @@
         gain_in=pltpu.VMEM((4,) + lanes, F32),
         load_sem=dma((4 * n + n,)),
         gains=pltpu.VMEM((8, width), F32),
-        gain_rows=pltpu.VMEM((n, 16, wide), BF16),
+        gain_rows=pltpu.VMEM((n, 32, HD), BF16),
         feed_local=dma((QUARTERS,)),
         feed_send=dma((QUARTERS * n,)),
         feed_recv=dma((QUARTERS * n,)),
@@ -672,6 +675,10 @@
         row_near_recv=dma((4 * n,)),
         row_far_send=dma((4 * n,)),
         row_far_recv=dma((4 * n,)),
+        token_send=dma((n,)),
+        token_recv=dma((n,)),
+        query_send=dma((n,)),
+        query_recv=dma((n,)),
         out_send=dma((n,)),
         out_recv=dma((n,)),
         cot_send=dma((n,)),
@@ -683,10 +690,15 @@
         two_far_recv=dma((n,)),
         two_near_send=dma((n,)),
         two_near_recv=dma((n,)),
-        climb_send=dma((planes,)),
-        climb_recv=dma((planes,)),
-        fall_send=dma((planes,)),
-        fall_recv=dma((planes,)),
+        two_half_send=dma((n,)),
+        two_half_recv=dma((n,)),
+        branch_half_send=dma((n,)),
+        branch_half_recv=dma((n,)),
+        climb_send=dma((2 * planes,)),
+        climb_recv=dma((2 * planes,)),
+        fall_send=dma((2 * planes,)),
+        fall_recv=dma((2 * planes,)),
+        soft=pltpu.VMEM((2 * n, pair, 1), F32),
         pass_send=dma((planes,)),
         pass_recv=dma((planes,)),
         keep_sem=dma((3,)),
@@ -948,7 +960,7 @@
         def row_near(s, base, d):
             at = s * n + d
             return remote(
-                work.at[pl.ds(base + (n + d) * rows, rows)],
+                work.at[pl.ds(base + (2 * d + 1) * rows, rows)],
                 r.row_near.at[s, d],
                 r.row_near_send.at[at],
                 r.row_near_recv.at[at],
@@ -958,7 +970,7 @@
         def row_far(s, base, d):
             at = s * n + d
             return remote(
-                work.at[pl.ds(base + d * rows, rows)],
+                work.at[pl.ds(base + 2 * d * rows, rows)],
                 r.row_far.at[s, d],
                 r.row_far_send.at[at],
                 r.row_far_recv.at[at],
@@ -973,27 +985,47 @@
 
         few = 16
 
-        def rows_hand_over(s, base):
-            for d in (3, 1, 2, 0):
-                row_near(s, base, d).start()
-
-        def rows_send(s, base):
-            for d in (3, 1, 2):
-                row_near(s, base, d).wait_recv()
-                near_load(s, d).start()
-            for d in (3, 1, 2):
-                near_load(s, d).wait()
-
-                def some(c, _, d=d):
-                    at = span(c * few, few)
-                    own = pl.ds(pl.multiple_of(base + d * rows + c * few, few), few)
-                    work[own, :] = (
-                        work[own, :].astype(F32) + r.some_rows[d, at, :].astype(F32)
-                    ).astype(BF16)
-                    return 0
-
-                lax.fori_loop(0, rows // few, some, 0)
-                row_far(s, base, d).start()
+        def row_send(s, base, d):
+            row_near(s, base, d).wait_recv()
+            near_load(s, d).start()
+            near_load(s, d).wait()
+
+            def some(c, _):
+                at = span(c * few, few)
+                own = pl.ds(pl.multiple_of(base + 2 * d * rows + c * few, few), few)
+                work[own, :] = (
+                    work[own, :].astype(F32) + r.some_rows[d, at, :].astype(F32)
+                ).astype(BF16)
+                return 0
+
+            lax.fori_loop(0, rows // few, some, 0)
+            row_far(s, base, d).start()
+
+        far_first = (3, 1, 2, 0)
+
+        def rows_reduced(s, base, compute, send=True, ticks=0):
+            def one(i, _):
+                d = jnp.where(i == 0, 3, jnp.where(i == n - 1, 0, i))
+                compute(d)
+                for at in range(n):
+
+                    @pl.when(i == at)
+                    def _():
+                        row_near(s, base, far_first[at]).start()
+                        if send and at > 0:
+                            row_send(s, base, far_first[at - 1])
+
+                if ticks:
+
+                    @pl.when(i >= n - ticks)
+                    def _():
+                        step(first + i - (n - ticks))
+
+                return 0
+
+            first = steps_done[0]
+            steps_done[0] = first + ticks
+            lax.fori_loop(0, n, one, 0)
 
         def rows_arrive(s, base):
             row_near(s, base, 0).wait_recv()
@@ -1071,6 +1103,23 @@
                 source, r.cot_all.at[1, d], r.cot_near_send.at[d], r.cot_near_recv.at[d], other_core
             )
 
+        def query_far(d):
+            return remote(
+                r.query_cut[d],
+                r.query_in.at[d],
+                r.query_send.at[d],
+                r.query_recv.at[d],
+                (here, chips[d]),
+            )
+
+        def kv_piece(j):
+            return r.kv_some.at[j // 3, pl.ds(j % 3 * wide, wide)]
+
+        def query_piece(j):
+            return heads.at[query_grad_slot + j // 3, pl.ds(j % 3 * wide, wide)]
+
+        for d in range(1, n):
+            query_far(d).start()
         for d in range(1, n):
             out_far(d).start()
         for d in range(1, n):
@@ -1078,24 +1127,39 @@
         for d in range(1, n):
             cot_far(d).start()
         cot_near(0).start()
-        for i in range(2 * n):
-            load(r.near_tokens[i], work.at[pl.ds(plane_rows + i * rows, rows)])
+        def token_near(d):
+            return remote(
+                r.near_tokens[d],
+                work.at[pl.ds(plane_rows + (2 * d + 1) * rows, rows)],
+                r.token_send.at[d],
+                r.token_recv.at[d],
+                other_core,
+            )
+
+        for d in range(n):
+            token_near(d).start()
+            load(r.near_tokens[d], work.at[pl.ds(plane_rows + 2 * d * rows, rows)])
         for j in range(n):
-            for h in range(2):
-                load(r.in_weight[j].at[pl.ds(h * HD, HD)], r.sums.at[j, h])
-            load(r.in_weight[j].at[pl.ds(wide, 16)], r.gain_rows.at[j])
+            load(r.in_weight[j].at[pl.ds(0, wide)], kv_piece(j))
+            load(r.in_weight[j].at[pl.ds(wide, 32)], r.gain_rows.at[j])
         loaded()
         load(r.out_cut[0], r.theirs.at[0, 0])
+        load(r.query_cut[0], query_piece(0))
         for q in range(QUARTERS):
             feed_own(q).start()
         for j in range(n):
             both = r.gain_rows[j].astype(F32)
-            r.gains[0:1, blocks[j]] = both[0:1]
-            r.gains[1:2, blocks[j]] = both[8:9]
+            for g in range(2):
+                for h in range(2):
+                    here_half = pl.ds(pl.multiple_of(chips[j] * wide + h * HD, HD), HD)
+                    r.gains[g : g + 1, here_half] = both[16 * g + 8 * h : 16 * g + 8 * h + 1]
+
+        for d in range(n):
+            token_near(d).wait_recv()
 
         def project(d, _):
             for c in range(2):
-                first = ((side + c) % 2 * n + d) * rows
+                first = (2 * d + (side + c) % 2) * rows
 
                 def some(s, _, c=c, first=first):
                     now = pl.ds(pl.multiple_of(plane_rows + first + s * few, few), few)
@@ -1107,14 +1171,9 @@
 
                 lax.fori_loop(0, rows // few, some, 0)
             now = span(d * pair, pair)
-            both = jnp.zeros((pair, 2 * HD), F32)
+            kv = jnp.zeros((pair, HD), F32)
             for j in range(n):
-                for h in range(2):
-                    here_half = pl.ds(pl.multiple_of(chips[j] * wide + h * HD, HD), HD)
-                    both += matmul(work[now, here_half], r.sums[j, h])
-            query, kv = both[:, :HD], both[:, HD:]
-            query = query * r.tables[0] + turn(query) * r.tables[1]
-            heads[query_slot, now, :] = query.astype(BF16)
+                kv += matmul(work[now, blocks[j]], kv_piece(j)[...])
             kv = kv * r.tables[2] + turn(kv) * r.tables[3]
             heads[0, now, :] = kv.astype(BF16)
             return 0
@@ -1123,15 +1182,25 @@
         keep_normed = local(work.at[pl.ds(0, plane_rows)], r.normed, r.keep_sem.at[0])
         keep_normed.start()
 
-        def climb(s):
-            return remote(heads.at[s - 1], heads.at[s], r.climb_send.at[s], r.climb_recv.at[s], above)
-
-        def fall(s):
-            return remote(
-                heads.at[(planes - s + 1) % planes],
-                heads.at[planes - s],
-                r.fall_send.at[s],
-                r.fall_recv.at[s],
+        kv_halves = [pl.ds(h * (plane_rows // 2), plane_rows // 2) for h in range(2)]
+
+        def climb(s, h):
+            at = 2 * s + h
+            return remote(
+                heads.at[s - 1, kv_halves[h]],
+                heads.at[s, kv_halves[h]],
+                r.climb_send.at[at],
+                r.climb_recv.at[at],
+                above,
+            )
+
+        def fall(s, h):
+            at = 2 * s + h
+            return remote(
+                heads.at[(planes - s + 1) % planes, kv_halves[h]],
+                heads.at[planes - s, kv_halves[h]],
+                r.fall_send.at[at],
+                r.fall_recv.at[at],
                 below,
             )
 
@@ -1140,88 +1209,134 @@
                 heads.at[k], heads.at[planes + k], r.pass_send.at[k], r.pass_recv.at[k], other_core
             )
 
-        def kv_leave(s):
+        def kv_leave(s, h):
             @pl.when((z - s + 1 >= 0) & (z + 1 < planes))
             def _():
-                climb(s).start()
+                climb(s, h).start()
 
             @pl.when((z + s - 1 < planes) & (z >= 1))
             def _():
-                fall(s).start()
-
-        def kv_come(s):
+                fall(s, h).start()
+
+        def kv_come(s, h):
             @pl.when(z - s >= 0)
             def _():
-                climb(s).wait_recv()
+                climb(s, h).wait_recv()
 
             @pl.when(z + s < planes)
             def _():
-                fall(s).wait_recv()
-
-        kv_leave(1)
+                fall(s, h).wait_recv()
+
+        def kv_forward(s):
+            for h in range(2):
+                kv_come(s, h)
+                if s + 1 < planes:
+                    kv_leave(s + 1, h)
+
+        for h in range(2):
+            kv_leave(1, h)
         pass_on(0).start()
         for d in range(1, n):
+            query_far(d).wait_recv()
+            load(r.query_in.at[d], query_piece(d))
+        loaded()
+
+        def project_query(d, _):
+            now = span(d * pair, pair)
+            query = jnp.zeros((pair, HD), F32)
+            for j in range(n):
+                query += matmul(work[now, blocks[j]], query_piece(j)[...])
+            query = query * r.tables[0] + turn(query) * r.tables[1]
+            heads[query_slot, now, :] = query.astype(BF16)
+            return 0
+
+        lax.fori_loop(0, n, project_query, 0)
+        for d in range(1, n):
             out_far(d).wait_recv()
-        loaded()
         keep_out = local(r.theirs, r.out_weight, r.keep_sem.at[1])
         keep_out.start()
-        kv_come(1)
-        kv_leave(2)
-
-        @pl.when(z >= 1)
-        def _():
-            pass_on(1).start()
-
-        @pl.when(z + 1 < planes)
-        def _():
-            pass_on(3).start()
-
-        kv_come(2)
-        kv_leave(3)
+
+        def put_rows(base, d, now_values, block_at):
+            first = pl.ds(pl.multiple_of(base + (2 * d + side) * rows, rows), rows)
+            second = pl.ds(pl.multiple_of(base + (2 * d + 1 - side) * rows, rows), rows)
+            work[first, block_at] = now_values[:rows]
+            work[second, block_at] = now_values[rows:]
+
+        def totals(d):
+            return [r.wide_rows.at[:, span((2 * d + c) * HD, HD)] for c in range(2)]
+
+        def attend_block(k, d, first, last):
+            now = span(d * pair, pair)
+            a, b = heads[k, now, :], heads[planes + k, now, :]
+            keys, values = jnp.where(side == 0, a, b), jnp.where(side == 0, b, a)
+            score = matmul_nt(heads[query_slot, now, :], keys) * scale
+            score = jnp.where(r.key_ids[d, k] <= r.query_ids[d], score, masked_score)
+            top = jnp.max(score, axis=-1, keepdims=True)
+            if not first:
+                before = r.soft[d]
+                top = jnp.maximum(top, before)
+                factor = jnp.exp(before - top)
+            raised = jnp.exp(score - top)
+            weight = jnp.sum(raised, axis=-1, keepdims=True)
+            total = matmul(raised.astype(BF16), values)
+            if not first:
+                weight += r.soft[n + d] * factor
+                total += jnp.concatenate([t[...] for t in totals(d)], axis=0) * factor
+            if last:
+                return total, weight
+            r.soft[d] = top
+            r.soft[n + d] = weight
+            for c, target in enumerate(totals(d)):
+                target[...] = total[c * rows : (c + 1) * rows]
+            return None
+
+        def attend_to(k, first=False):
+            def one(d, _):
+                attend_block(k, d, first, False)
+                return 0
+
+            lax.fori_loop(0, n, one, 0)
+
+        def when_middle(there, otherwise):
+            return jnp.where(is_middle, there, otherwise)
+
+        def passed(condition, k):
+            @pl.when(condition)
+            def _():
+                pass_on(k).wait_recv()
+
+        def passing(condition, k):
+            @pl.when(condition)
+            def _():
+                pass_on(k).start()
+
+        pass_on(0).wait_recv()
+        attend_to(0, first=True)
+        kv_forward(1)
+        passing(z >= 1, 1)
+        passing(z + 1 < planes, 3)
+        passed(z >= 1, 1)
+        passed(z + 1 < planes, 3)
+        attend_to(jnp.where(z >= 1, 1, 3))
+        kv_forward(2)
         pass_on(2).start()
         for d in range(1, n):
             cot_far(d).wait_recv()
             cot_near(d).start()
+        pass_on(2).wait_recv()
+        attend_to(when_middle(3, 2))
         keep_normed.wait()
-        kv_come(3)
-
-        @pl.when(z == 0)
-        def _():
-            pass_on(1).start()
-
-        @pl.when(z == planes - 1)
-        def _():
-            pass_on(3).start()
-
-        for k in range(planes):
-            pass_on(k).wait_recv()
-
-        def scored(d, now):
-            keys, values, scores = [], [], []
-            for k in range(planes):
-                a, b = heads[k, now, :], heads[planes + k, now, :]
-                keys.append(jnp.where(side == 0, a, b))
-                values.append(jnp.where(side == 0, b, a))
-                score = matmul_nt(heads[query_slot, now, :], keys[k]) * scale
-                scores.append(jnp.where(r.key_ids[d, k] <= r.query_ids[d], score, masked_score))
-            top = functools.reduce(jnp.maximum, [jnp.max(s, axis=-1, keepdims=True) for s in scores])
-            raised = [jnp.exp(s - top) for s in scores]
-            inverse = 1.0 / sum(jnp.sum(e, axis=-1, keepdims=True) for e in raised)
-            return keys, values, [e * inverse for e in raised]
-
-        def put_rows(base, d, now_values, block_at):
-            first = pl.ds(pl.multiple_of(base + (side * n + d) * rows, rows), rows)
-            second = pl.ds(pl.multiple_of(base + ((1 - side) * n + d) * rows, rows), rows)
-            work[first, block_at] = now_values[:rows]
-            work[second, block_at] = now_values[rows:]
-
-        def attend(d, _):
+        kv_forward(3)
+        passing(z == 0, 1)
+        passing(z == planes - 1, 3)
+        passed(z == 0, 1)
+        passed(z == planes - 1, 3)
+
+        def attend(d):
             now = span(d * pair, pair)
-            _, values, probs = scored(d, now)
-            total = jnp.zeros((pair, HD), F32)
-            for k in range(planes):
-                total += matmul(probs[k].astype(BF16), values[k])
-            low_total = total.astype(BF16)
+            last_block = jnp.where(z == 0, 1, when_middle(2, 3))
+            total, weight = attend_block(last_block, d, False, True)
+            low_total = (total * (1.0 / weight)).astype(BF16)
             heads[attended_slot, now, :] = low_total
             for j in range(n):
                 put_rows(
@@ -1230,25 +1345,23 @@
                     matmul(low_total, r.theirs[j // 2, j % 2]).astype(BF16),
                     blocks[j],
                 )
-            return 0
-
-        lax.fori_loop(0, n, attend, 0)
-        rows_hand_over(MID, plane_rows)
+
+        rows_reduced(MID, plane_rows, attend)
         keep_heads = local(heads.at[pl.ds(0, kept_slots)], r.kept, r.keep_sem.at[2])
         keep_heads.start()
         load(r.tokens, r.own_rows)
-        rows_send(MID, plane_rows)
         loaded()
         keep_out.wait()
         for s in range(1, planes):
-
-            @pl.when((z - s + 1 >= 0) & (z + 1 < planes))
-            def _():
-                climb(s).wait_send()
-
-            @pl.when((z + s - 1 < planes) & (z >= 1))
-            def _():
-                fall(s).wait_send()
+            for h in range(2):
+
+                @pl.when((z - s + 1 >= 0) & (z + 1 < planes))
+                def _():
+                    climb(s, h).wait_send()
+
+                @pl.when((z + s - 1 < planes) & (z >= 1))
+                def _():
+                    fall(s, h).wait_send()
 
         for k in range(planes):
             pass_on(k).wait_send()
@@ -1271,23 +1384,34 @@
         def two_far(d):
             return remote(
                 r.own_rows,
-                work.at[pl.ds(d * rows, rows)],
+                work.at[pl.ds(2 * d * rows, rows)],
                 r.two_far_send.at[d],
                 r.two_far_recv.at[d],
                 (here, chips[d]),
             )
 
         def two_near(d):
-            source = r.own_rows if d == 0 else work.at[pl.ds(d * rows, rows)]
+            source = r.own_rows if d == 0 else work.at[pl.ds(2 * d * rows, rows)]
             return remote(
                 source,
-                work.at[pl.ds((n + d) * rows, rows)],
+                work.at[pl.ds((2 * d + 1) * rows, rows)],
                 r.two_near_send.at[d],
                 r.two_near_recv.at[d],
                 other_core,
             )
 
-        for d in (3, 1, 2):
+        half_rows = rows // 2
+
+        def two_half(d):
+            return remote(
+                work.at[pl.ds(2 * d * rows + (d - 1) * half_rows, half_rows)],
+                work.at[pl.ds(2 * 3 * rows + (d - 1) * half_rows, half_rows)],
+                r.two_half_send.at[d],
+                r.two_half_recv.at[d],
+                (here, chips[3 - d]),
+            )
+
+        for d in (1, 2):
             two_far(d).start()
         two_near(0).start()
         two_own = local(r.own_rows, work.at[pl.ds(0, rows)], r.two_local.at[0])
@@ -1296,22 +1420,30 @@
         rows_sent(MID, plane_rows)
         for d in range(n):
             cot_near(d).wait_recv()
-            if d > 0:
-                load(r.cot_all.at[0, d], work.at[pl.ds(plane_rows + d * rows, rows)])
-            else:
-                load(r.cotangent, work.at[pl.ds(plane_rows, rows)])
-            load(r.cot_all.at[1, d], work.at[pl.ds(plane_rows + (n + d) * rows, rows)])
+            source = r.cotangent if d == 0 else r.cot_all.at[0, d]
+            load(source, work.at[pl.ds(plane_rows + 2 * d * rows, rows)])
+            load(r.cot_all.at[1, d], work.at[pl.ds(plane_rows + (2 * d + 1) * rows, rows)])
         keep_heads.wait()
-        for d in (1, 2, 3):
-            two_far(d).wait_recv()
-            two_near(d).start()
         for d in range(1, n):
             feed_copy(0, d).wait_recv()
-            feed_copy(1, d).start()
+        loaded()
+
+        def rows_of_chip(t, arrive, half_way, pass_along):
+            for at in range(n):
+
+                @pl.when(t == at)
+                def _():
+                    for d in ((), (1, 2), (), ())[at]:
+                        arrive(d).wait_recv()
+                        half_way(d).start()
+                        pass_along(d).start()
+                    if at == 2:
+                        half_way(1).wait_recv()
+                        half_way(2).wait_recv()
+                        pass_along(3).start()
+                    pass_along(at).wait_recv()
+
         two_own.wait()
-        loaded()
-        for d in range(n):
-            two_near(d).wait_recv()
 
         def quarter_step(q, _):
             step(3 * q - 3)
@@ -1328,10 +1460,14 @@
                     feed_copy(q + 1, d).start()
 
             def forward(t, _):
-                now = span(t * tile, tile)
-                cot_now = pl.ds(pl.multiple_of(plane_rows + t * tile, tile), tile)
-                both = jnp.zeros((tile, 2 * quarter), F32)
-                hidden_grad = jnp.zeros((tile, quarter), F32)
+                @pl.when(q == 0)
+                def _():
+                    rows_of_chip(t, two_far, two_half, two_near)
+
+                now = span(t * pair, pair)
+                cot_now = pl.ds(pl.multiple_of(plane_rows + t * pair, pair), pair)
+                both = jnp.zeros((pair, 2 * quarter), F32)
+                hidden_grad = jnp.zeros((pair, quarter), F32)
                 for j in range(n):
                     both += matmul(work[now, blocks[j]], feed[q, j, :wide, :])
                     hidden_grad += matmul_nt(work[cot_now, blocks[j]], feed[q, j, wide:, :])
@@ -1348,7 +1484,13 @@
                     turned[w, :, now] = result.T.astype(BF16)
                 return 0
 
-            lax.fori_loop(0, plane_rows // tile, forward, 0)
+            lax.fori_loop(0, n, forward, 0)
+
+            @pl.when(q == 0)
+            def _():
+                for d in range(1, n):
+                    feed_copy(1, d).start()
+
             step(3 * q - 2)
 
             def one(w, _):
@@ -1372,9 +1514,11 @@
 
         for d in range(1, n):
             two_near(d).wait_send()
-
-        def back_step(s, _):
-            now = span(s * pair, pair)
+        for d in (1, 2):
+            two_half(d).wait_send()
+
+        def back_step(d):
+            now = span(d * pair, pair)
             lefts = [
                 jnp.concatenate([heads[q * 3 + 1, now, :], heads[q * 3 + 2, now, :]], axis=1)
                 for q in range(QUARTERS)
@@ -1384,40 +1528,31 @@
                 for q in range(QUARTERS):
                     total += matmul_nt(lefts[q], feed[q, j, :wide, :])
                 work[now, blocks[j]] = total.astype(BF16)
-            return 0
 
         half = n // 2
-        lax.fori_loop(half, n, back_step, 0)
-        rows_hand_over(BACK, 0)
-        advance(TICKS[0])
-        lax.fori_loop(0, half, back_step, 0)
-        rows_send(BACK, 0)
-        advance(TICKS[1])
-
-        def out_step(s, _):
-            now = span(s * pair, pair)
-            then = pl.ds(pl.multiple_of(plane_rows + s * pair, pair), pair)
+        rows_reduced(BACK, 0, back_step, ticks=TICKS[0] + TICKS[1])
+
+        def out_step(d):
+            now = span(d * pair, pair)
+            then = pl.ds(pl.multiple_of(plane_rows + d * pair, pair), pair)
             for j in range(n):
                 total = jnp.zeros((pair, wide), F32)
                 for q in range(QUARTERS):
                     total += matmul(heads[q * 3, now, :], feed[q, j, wide:, :])
                 work[then, blocks[j]] = total.astype(BF16)
-            return 0
-
-        lax.fori_loop(half, n, out_step, 0)
-        rows_hand_over(OUT, plane_rows)
-        advance(TICKS[2])
-        lax.fori_loop(0, half, out_step, 0)
-        advance(TICKS[3])
+
+        rows_reduced(OUT, plane_rows, out_step, send=False, ticks=TICKS[2] + TICKS[3])
 
         load(r.kept, heads.at[pl.ds(0, kept_slots)])
         for j in range(n):
-            load(r.in_weight[j].at[pl.ds(0, wide)], feed.at[0, j, pl.ds(0, wide)])
+            query_source = r.query_cut[0] if j == 0 else r.query_in.at[j]
+            load(query_source, feed.at[0, j, pl.ds(0, wide), pl.ds(0, HD)])
+            load(r.in_weight[j].at[pl.ds(0, wide)], feed.at[0, j, pl.ds(0, wide), pl.ds(HD, HD)])
             load(r.out_weight.at[j // 2, j % 2], feed.at[0, j, pl.ds(wide, HD)])
 
         rows_arrive(BACK, 0)
         loaded()
-        for d in range(1, n):
+        for d in (1, 2):
             two_far(d).wait_send()
         two_near(0).wait_send()
         load(r.cotangent, r.own_rows)
@@ -1449,28 +1584,52 @@
                 other_core,
             )
 
-        for d in (3, 1, 2):
+        def branch_half(d):
+            some = pl.ds((d - 1) * half_rows, half_rows)
+            return remote(
+                r.branch_all.at[d, side, some],
+                r.branch_all.at[3, side, some],
+                r.branch_half_send.at[d],
+                r.branch_half_recv.at[d],
+                (here, chips[3 - d]),
+            )
+
+        for d in (1, 2):
             branch_far(d).start()
         branch_near(0).start()
         branch_own = local(r.own_rows, r.branch_all.at[0, side], r.branch_local.at[0])
         branch_own.start()
         gain_terms(1)
         advance(TICKS[4])
-        for d in (1, 2, 3):
-            branch_far(d).wait_recv()
-            branch_near(d).start()
         rows_sent(BACK, 0)
         branch_own.wait()
-        for d in range(n):
-            branch_near(d).wait_recv()
-        for d in range(n):
+        loaded()
+
+        def scored(d, now):
+            keys, values, scores = [], [], []
+            for k in range(planes):
+                a, b = heads[k, now, :], heads[planes + k, now, :]
+                keys.append(jnp.where(side == 0, a, b))
+                values.append(jnp.where(side == 0, b, a))
+                score = matmul_nt(heads[query_slot, now, :], keys[k]) * scale
+                scores.append(jnp.where(r.key_ids[d, k] <= r.query_ids[d], score, masked_score))
+            top = functools.reduce(jnp.maximum, [jnp.max(s, axis=-1, keepdims=True) for s in scores])
+            raised = [jnp.exp(s - top) for s in scores]
+            inverse = 1.0 / sum(jnp.sum(e, axis=-1, keepdims=True) for e in raised)
+            return keys, values, [e * inverse for e in raised]
+
+        def attend_back(d, _):
+            rows_of_chip(d, branch_far, branch_half, branch_near)
+
+            @pl.when(d == half)
+            def _():
+                for at in (3, 1, 2):
+                    row_send(OUT, plane_rows, at)
+
+            now = span(d * pair, pair)
             for c in range(2):
-                load(r.branch_all.at[d, c], work.at[pl.ds((2 * d + c) * rows, rows)])
-        rows_send(OUT, plane_rows)
-        loaded()
-
-        def attend_back(d, _):
-            now = span(d * pair, pair)
+                load(r.branch_all.at[d, c], work.at[pl.ds(pl.multiple_of((2 * d + c) * rows, rows), rows)])
+            loaded()
             query = heads[query_slot, now, :]
             attended_grad = jnp.zeros((pair, HD), F32)
             for j in range(n):
@@ -1585,7 +1744,7 @@
         advance(TICKS[9])
         kv_receive(1, 0, 0)
 
-        def project_back(d, _):
+        def project_back(d):
             now = span(d * pair, pair)
             grad = heads[0, now, :].astype(F32)
             grad = grad * r.tables[2] + turn_back(grad * r.tables[3])
@@ -1593,18 +1752,16 @@
             left = jnp.concatenate([heads[query_grad_slot, now, :], grad.astype(BF16)], axis=1)
             for j in range(n):
                 put_rows(0, d, matmul_nt(left, feed[0, j, :wide, :]).astype(BF16), blocks[j])
-            return 0
-
-        lax.fori_loop(0, n, project_back, 0)
-        rows_hand_over(ONE, 0)
+
+        rows_reduced(ONE, 0, project_back)
         turned[2] = heads[kv_grad_slot].astype(F32).T.astype(BF16)
         outer(kv_at, turned[2], high_half)
-        rows_send(ONE, 0)
         staged(kv_at)
         advance(TICKS[10])
 
-        for d in range(1, n):
+        for d in (1, 2):
             branch_far(d).wait_send()
+            branch_half(d).wait_send()
         for d in range(n):
             branch_near(d).wait_send()
         load(r.tokens, r.own_rows)
@@ -1660,17 +1817,36 @@
             r.gain_sum[3] = r.gain_in[3]
 
         load(r.gain_sum.at[3], r.gain_out)
+
+        loaded()
+        load(r.middle, r.wide_rows)
+        load(r.out_own, r.own_rows)
+        rows_arrive(OUT, plane_rows)
+        loaded()
+
+        def last_rows(c, _):
+            at = span(c * few, few)
+            total = r.wide_rows[at, :] + r.own_rows[at, :].astype(F32)
+            for d in range(n):
+                total += r.some_rows[d, at, :].astype(F32)
+            r.own_rows[at, :] = total.astype(BF16)
+            return 0
+
+        lax.fori_loop(0, rows // few, last_rows, 0)
+        load(r.own_rows, r.output)
         advance(units + 9 - steps_done[0])
 
         loaded()
-        rows_arrive(OUT, plane_rows)
         rows_sent(ONE, 0)
         for q in range(QUARTERS):
             for d in range(1, n):
                 feed_copy(q, d).wait_send()
         for d in range(1, n):
+            query_far(d).wait_send()
             out_far(d).wait_send()
+            token_near(d).wait_send()
             cot_far(d).wait_send()
+        token_near(0).wait_send()
         for d in range(n):
             cot_near(d).wait_send()
         for k in range(planes):
@@ -1706,104 +1882,71 @@
         a.reshape(tiles_count, n, quarter, wide) for a in (results.owned, results.near)
     )
 
-    def place_hidden(me_ref, own_ref, near_ref, gate_out, up_out, down_out):
+    def place(me_ref, own_ref, near_ref, gate, up, down, query, out, key, value):
         for source, e in ((own_ref, 0), (near_ref, 1)):
 
-            @pl.when(pl.program_id(0) // n == e)
-            def _():
-                down_out[...] = source[0, 0].astype(F32)
-                gate_out[...] = source[1, 0].T.astype(F32)
-                up_out[...] = source[2, 0].T.astype(F32)
-
-    def hidden_slot(i, q, me):
-        return (2 * (me[0] ^ (i % n)) + (me[1] ^ (i // n))) * QUARTERS + q
-
-    def own_hidden(i, q, me):
-        return (jnp.where(i < n, q, QUARTERS - 1), jnp.minimum(i, n - 1), 0, 0)
-
-    def near_hidden(i, q, me):
-        return (jnp.where(i < n, 0, q), jnp.maximum(i - n, 0), 0, 0)
-
-    by_columns = pl.BlockSpec((wide, quarter), lambda i, q, me: (0, hidden_slot(i, q, me)))
-    by_rows = pl.BlockSpec((quarter, wide), lambda i, q, me: (hidden_slot(i, q, me), 0))
-    held = run_grid(
-        place_hidden,
+            @pl.when(pl.program_id(1) == e)
+            def _():
+                for q in range(QUARTERS):
+                    here = slice(q * quarter, (q + 1) * quarter)
+                    down[here, :] = source[3 * q, 0].astype(F32)
+                    gate[:, here] = source[3 * q + 1, 0].T.astype(F32)
+                    up[:, here] = source[3 * q + 2, 0].T.astype(F32)
+                query[...] = source[query_at, 0].T.astype(F32)
+                out[...] = source[output_at, 0].astype(F32)
+
+                @pl.when(me_ref[1] == e)
+                def _():
+                    key[...] = source[kv_at, 0].T.astype(F32)
+
+                @pl.when(me_ref[1] != e)
+                def _():
+                    value[...] = source[kv_at, 0].T.astype(F32)
+
+    def owner(d, e, me):
+        return 2 * (me[0] ^ d) + (me[1] ^ e)
+
+    by_chip = pl.BlockSpec((tiles_count, 1, quarter, wide), lambda d, e, me: (0, d, 0, 0))
+    placed = run_grid(
+        place,
         me,
-        (2 * n, QUARTERS),
+        (n, 2),
         [owned_tiles, near_tiles],
+        [by_chip, by_chip],
         [
-            pl.BlockSpec((3, 1, quarter, wide), own_hidden),
-            pl.BlockSpec((3, 1, quarter, wide), near_hidden),
+            shape(a.shape, F32)
+            for a in (
+                gate_weight,
+                up_weight,
+                down_weight,
+                query_weight,
+                output_weight,
+                key_weight,
+                value_weight,
+            )
         ],
-        [
-            shape(gate_weight.shape, F32),
-            shape(up_weight.shape, F32),
-            shape(down_weight.shape, F32),
-        ],
-        [by_columns, by_columns, by_rows],
-        name="place_hidden",
-    )
-
-    def place_query(me_ref, own_ref, near_ref, query_out, output_out):
-        for source, e in ((own_ref, 0), (near_ref, 1)):
-
-            @pl.when(pl.program_id(0) // n == e)
-            def _():
-                query_out[...] = source[0, 0].T.astype(F32)
-                output_out[...] = source[1, 0].astype(F32)
-
-    def head_slot(i, me):
-        return 2 * (me[0] ^ (i % n)) + (me[1] ^ (i // n))
-
-    own_spec = lambda i, me: (query_at // 2, jnp.where(i < n, i, n - 1), 0, 0)
-    near_spec = lambda i, me: (query_at // 2, jnp.where(i < n, 0, i - n), 0, 0)
-    query_weight_grad, output_weight_grad = run_grid(
-        place_query,
-        me,
-        (2 * n,),
-        [owned_tiles, near_tiles],
-        [pl.BlockSpec((2, 1, HD, wide), own_spec), pl.BlockSpec((2, 1, HD, wide), near_spec)],
-        [shape(query_weight.shape, F32), shape(output_weight.shape, F32)],
-        [
-            pl.BlockSpec((wide, HD), lambda i, me: (0, head_slot(i, me))),
-            pl.BlockSpec((HD, wide), lambda i, me: (head_slot(i, me), 0)),
-        ],
-        name="place_query",
-    )
-
-    def place_kv(me_ref, own_ref, near_ref, key_out, value_out):
-        keys_here = me_ref[1] == 0
-        own, near = own_ref[0, 0].T.astype(F32), near_ref[0, 0].T.astype(F32)
-        key_out[...] = jnp.where(keys_here, own, near)
-        value_out[...] = jnp.where(keys_here, near, own)
-
-    by_chip = pl.BlockSpec((wide, HD), lambda i, me: (0, me[0] ^ i))
-    kv_spec = pl.BlockSpec((1, 1, HD, wide), lambda i, me: (kv_at, i, 0, 0))
-    key_weight_grad, value_weight_grad = run_grid(
-        place_kv,
-        me,
-        (n,),
-        [owned_tiles, near_tiles],
-        [kv_spec, kv_spec],
-        [shape(key_weight.shape, F32), shape(value_weight.shape, F32)],
-        [by_chip, by_chip],
-        name="place_kv",
-    )
-
-    output = results.middle + results.out_own.astype(F32) + results.row_near[OUT, 0].astype(F32)
-    output = output + sum(results.row_far[OUT, d].astype(F32) for d in range(1, n))
+        [pl.BlockSpec((wide, part), lambda d, e, me: (0, owner(d, e, me)))] * 2
+        + [
+            pl.BlockSpec((part, wide), lambda d, e, me: (owner(d, e, me), 0)),
+            pl.BlockSpec((wide, HD), lambda d, e, me: (0, owner(d, e, me))),
+            pl.BlockSpec((HD, wide), lambda d, e, me: (owner(d, e, me), 0)),
+        ]
+        + [pl.BlockSpec((wide, HD), lambda d, e, me: (0, me[0] ^ d))] * 2,
+        name="place",
+    )
+    gate_grad, up_grad, down_grad, query_grad, output_grad, key_grad, value_grad = placed
 
     return (
-        output.astype(BF16)[None],
+        results.output[None],
         results.tokens_grad[None],
-        query_weight_grad,
-        key_weight_grad,
-        value_weight_grad,
-        output_weight_grad,
+        query_grad,
+        key_grad,
+        value_grad,
+        output_grad,
         results.gain_out[0],
-        held[0],
-        held[1],
-        held[2],
+        gate_grad,
+        up_grad,
+        down_grad,
         results.gain_out[1],
     )
 

time: 824 us -> 778 us (0.944)
  Pallas kernels: 762 us -> 732 us
  waiting for transfers between devices: 31.4 us -> 18.8 us
    pallas_call x1, Pallas kernels: 699 us -> 678 us  [plane_layer(): pl.pallas_call(backward, out_shape=jax.tree.leaves(out_hbm), in_specs=[pl...]
    ppermute x6, waiting for transfers between devices: 31.4 us -> 18.8 us  [across(): return lax.ppermute(value, 'fsdp', [(i, i ^ d) for i in range(n)])]
    pallas_call x5 -> x3, Pallas kernels: 63.6 us -> 54.6 us  [run_grid(): pl.pallas_call(body, out_shape=outs, grid_spec=pltpu.PrefetchScalarGridSp...]
  transfers between devices with their start and end apart: 10 -> 6, of which waited for: 2 -> 2; matrix products, arithmetic and copies ran while one was open for 1% -> 1% of each run, Pallas kernels for 2% -> 2%
where the time goes in v6:
time: 778 us; the launch traced here: 776 us
  Pallas kernels  732 us (94%)
  waiting for transfers between devices  18.8 us (2%)
  local copies, waits for them, and re-layouts  10.8 us (1%)
  starting transfers between devices  9.51 us (1%)
    pallas_call x1, Pallas kernels, plane_layer(): pl.pallas_call(backward, out_shape=jax.tree.leaves(out_hbm), in_specs=[pl...  678 us
    pallas_call x3, Pallas kernels, run_grid(): pl.pallas_call(body, out_shape=outs, grid_spec=pltpu.PrefetchScalarGridSp...  54.6 us
    ppermute x6, waiting for transfers between devices, across(): return lax.ppermute(value, 'fsdp', [(i, i ^ d) for i in range(n)])  18.8 us
  transfers between devices with their start and end apart: 6, of which 2 were waited for; matrix products, arithmetic and copies ran while one was open for 1% of the time, Pallas kernels for 2%

profile of v6, /device:TPU:0, one launch (start us, length us, event | category | flops | bytes accessed | tf_op | source)
XLA Modules:
  0.0 776.0 jit_solution(8189910937566979232)
XLA Ops:
  0.6 4.0 collective-permute-start.5
  4.6 0.5 collective-permute-start.4
  5.2 1.3 reshape.283.refs_16_
  6.5 1.3 reshape.284.refs_17_
  7.8 0.7 pad_add_fusion.me_ref
  8.4 10.1 %cut_hidden.1.refs_1_ = bf16[4,4,768,512]{3,2,1,0:T(8,128)(2,1)} custom-call(s32[2]{0:T(128)} %pad_add_fusion.me_ref, bf16[512,8192]{1,0:T(8,128)(2,1)} %refs_3_.3, bf16[512,8192]{1,0:T(8,128)(2,1)} %refs_3_.3, bf16[512,8192]{1,0:T(8,128)(2,1)} %refs_3_.3, bf16[512,8192]{1,0:T(8,128)(2,1)} %refs_3_.3, bf16[512,8192]{1,0:T(8,128)(2,1)} %refs_7_.3, ...), custom_call_target="tpu_custom_call" | custom-call | bytes 113246208 | tf_op jit(solution)/shard_map/cut_hidden/pallas_call | solution.py:366
  18.5 4.8 cut_attention.1
  23.3 2.0 collective-permute-start
  25.3 1.5 collective-permute-start.1
  27.1 0.6 gather_fusion
  28.2 0.7 gather_fusion.1
  28.8 0.7 reshape.286.refs_19_
  29.5 1.5 reshape.305.refs_20_
  31.2 14.3 %collective-permute-done.refs_3_ = bf16[544,256]{1,0:T(8,128)(2,1)S(1)} collective-permute-done((bf16[544,256]{1,0:T(8,128)(2,1)}, bf16[544,256]{1,0:T(8,128)(2,1)S(1)}, u32[]{:S(2)}, u32[]{:S(2)}) %collective-permute-start) | collective-permute-done | bytes 278560 | tf_op jit(solution)/shard_map/ppermute | solution.py:437
  45.5 1.4 collective-permute-start.2
  46.9 1.4 fusion.1
  48.3 1.2 pad_maximum_fusion.refs_21_
  49.6 4.5 collective-permute-done.2.refs_5_
  54.2 0.7 copy-done.7
  55.1 677.8 %backward.1 = (bf16[4,2,192,2048]{3,2,1,0:T(8,128)(2,1)}, bf16[2,4,192,2048]{3,2,1,0:T(8,128)(2,1)}, bf16[30,2,256,512]{3,2,1,0:T(8,128)(2,1)}, bf16[30,2,256,51...) custom-call(bf16[192,2048]{1,0:T(8,128)(2,1)} %bitcast.24, ...), custom_call_target="tpu_custom_call" | custom-call | flops 96636764160 | bytes 116488192 | tf_op jit(solution)/shard_map/backward/pallas_call | solution.py:1867
  732.9 1.4 fusion.9
  734.3 39.7 %place.1 = (f32[512,8192]{1,0:T(8,128)}, f32[512,8192]{1,0:T(8,128)}, f32[8192,512]{1,0:T(8,128)}, f32[512,2048]{1,0:T(8,128)}, f32[2048,512]{1,0:T(8,128)}, /*index=5*/f32[512,1024]{1,0:T(8,128)}, f32[512,1024]{1,0:T(8,128)}) custom-call(s32[2]{0:T(128)} %pad_add_fusion.me_ref, bf16[15,4,256,512]{3,2,1,0:T(8,128)(2,1)} %bitcast.18, ...), custom_call_target="tpu_custom_call" | custom-call | bytes 94371840 | tf_op jit(solution)/shard_map/place/pallas_call | solution.py:366
  774.0 0.9 copy.27
  774.9 1.1 copy.28
  (36 shorter events, 1.2 us)
Async XLA Ops:
  0.6 53.5 %collective-permute-start.5 = (bf16[192,2048]{1,0:T(8,128)(2,1)}, bf16[192,2048]{1,0:T(8,128)(2,1)S(1)}, u32[]{:S(2)}, u32[]{:S(2)}) collective-permute-start(bf16[192,2048]{1,0:T(8,128)(2,1)} %bitcast.25), channel_id=1, source_target_pairs={{0,3},{1,2},{2,1},{3,0},{4,7},{5,6},{6,5},{7,4},{8,11},{9,10},{10,... | collective-permute-start | bytes 2359304 | tf_op jit(solution)/shard_map/ppermute | solution.py:437
  4.6 49.5 %collective-permute-start.4 = (bf16[192,2048]{1,0:T(8,128)(2,1)}, bf16[192,2048]{1,0:T(8,128)(2,1)}, u32[]{:S(2)}, u32[]{:S(2)}) collective-permute-start(bf16[192,2048]{1,0:T(8,128)(2,1)} %bitcast.26), channel_id=1, source_target_pairs={{0,2},{1,3},{2,0},{3,1},{4,6},{5,7},{6,4},{7,5},{8,10},{9,11},{10,... | collective-permute-start | bytes 2359304 | tf_op jit(solution)/shard_map/ppermute | solution.py:437
  5.1 49.0 %collective-permute-start.3 = (bf16[192,2048]{1,0:T(8,128)(2,1)}, bf16[192,2048]{1,0:T(8,128)(2,1)}, u32[]{:S(2)}, u32[]{:S(2)}) collective-permute-start(bf16[192,2048]{1,0:T(8,128)(2,1)} %bitcast.27), channel_id=1, source_target_pairs={{0,1},{1,0},{2,3},{3,2},{4,5},{5,4},{6,7},{7,6},{8,9},{9,8},{10,11... | collective-permute-start | bytes 2359304 | tf_op jit(solution)/shard_map/ppermute | solution.py:437
  18.5 8.5 %copy-start = (s32[8]{0:T(128)S(1)}, s32[8]{0:T(128)}, u32[]{:S(2)}) copy-start(s32[8]{0:T(128)} %param.25) | copy-start | bytes 100
  18.5 9.6 %copy-start.3 = (s32[4,1536]{1,0:T(4,128)S(1)}, s32[4,1536]{1,0:T(4,128)}, u32[]{:S(2)}) copy-start(s32[4,1536]{1,0:T(4,128)} %param.24) | copy-start | bytes 73732
  23.3 22.1 %collective-permute-start = (bf16[544,256]{1,0:T(8,128)(2,1)}, bf16[544,256]{1,0:T(8,128)(2,1)S(1)}, u32[]{:S(2)}, u32[]{:S(2)}) collective-permute-start(bf16[544,256]{1,0:T(8,128)(2,1)} %get-tuple-element.62), channel_id=1, source_target_pairs={{0,1},{1,0},{2,3},{3,2},{4,5},{5,4},{6,7},{7,6},{8,9},{9,8},{10,11... | collective-permute-start | bytes 835592 | tf_op jit(solution)/shard_map/ppermute | solution.py:437
  25.3 24.3 %collective-permute-start.1 = (bf16[544,256]{1,0:T(8,128)(2,1)}, bf16[544,256]{1,0:T(8,128)(2,1)S(1)}, u32[]{:S(2)}, u32[]{:S(2)}) collective-permute-start(bf16[544,256]{1,0:T(8,128)(2,1)} %get-tuple-element.63), channel_id=1, source_target_pairs={{0,2},{1,3},{2,0},{3,1},{4,6},{5,7},{6,4},{7,5},{8,10},{9,11},{10,... | collective-permute-start | bytes 835592 | tf_op jit(solution)/shard_map/ppermute | solution.py:437
  45.5 8.6 %copy-start.5 = (bf16[544,256]{1,0:T(8,128)(2,1)}, bf16[544,256]{1,0:T(8,128)(2,1)S(1)}, u32[]{:S(2)}) copy-start(bf16[544,256]{1,0:T(8,128)(2,1)S(1)} %collective-permute-done.refs_3_) | copy-start | bytes 835588
  45.5 8.6 %collective-permute-start.2 = (bf16[544,256]{1,0:T(8,128)(2,1)}, bf16[544,256]{1,0:T(8,128)(2,1)S(1)}, u32[]{:S(2)}, u32[]{:S(2)}) collective-permute-start(bf16[544,256]{1,0:T(8,128)(2,1)} %get-tuple-element.64), channel_id=1, source_target_pairs={{0,3},{1,2},{2,1},{3,0},{4,7},{5,6},{6,5},{7,4},{8,11},{9,10},{10,... | collective-permute-start | bytes 835592 | tf_op jit(solution)/shard_map/ppermute | solution.py:437
  49.6 4.6 copy-start.6
  54.1 0.7 copy-start.7
  54.1 1.0 copy-start.4
  734.2 39.7 %copy-start.2 = (bf16[192,2048]{1,0:T(8,128)(2,1)S(1)}, bf16[192,2048]{1,0:T(8,128)(2,1)}, u32[]{:S(2)}) copy-start(bf16[192,2048]{1,0:T(8,128)(2,1)} %get-tuple-element.73) | copy-start | bytes 2359300
  734.3 40.6 %copy-start.1 = (f32[192,2048]{1,0:T(8,128)S(1)}, f32[192,2048]{1,0:T(8,128)}, u32[]{:S(2)}) copy-start(f32[192,2048]{1,0:T(8,128)} %get-tuple-element.74) | copy-start | bytes 4718596

commit v7 on v6

--- a/solution.py
+++ b/solution.py
@@ -323,7 +323,7 @@
 F32 = jnp.float32
 QUARTERS = 4
 MESH = pl.DeviceIdType.MESH
-TICKS = (2, 1, 2, 2, 3, 2, 1, 1, 1, 4, 4, 2, 2)
+TICKS = (2, 1, 2, 2, 3, 2, 1, 1, 1, 2, 4, 2, 2)
 LINES = 2
 
 
@@ -492,88 +492,44 @@
     key_ids = ids.reshape(n, planes, 1, pair)
     query_ids = ids[:, :2].reshape(n, pair, 1)
 
-    def cut_attention(me_ref, *refs):
-        wq, wk, wv, wo = (refs[i * n : (i + 1) * n] for i in range(4))
-        one, two = refs[4 * n : 4 * n + 2]
-        outs = refs[4 * n + 2 :]
+    def cut_weights(me_ref, *refs):
+        keys, values, (one, two), outs = refs[:n], refs[n : 2 * n], refs[2 * n : 2 * n + 2], refs[2 * n + 2 :]
         keys_here = me_ref[1] == 0
         for d in range(n):
-            first = outs[d]
-            outs[n + d][...] = wq[d][...]
 
             @pl.when(keys_here)
             def _():
-                first[:wide, :] = wk[d][...]
+                outs[d][:wide, :] = keys[d][...]
 
             @pl.when(jnp.logical_not(keys_here))
             def _():
-                first[:wide, :] = wv[d][...]
+                outs[d][:wide, :] = values[d][...]
 
             pick = lax.broadcasted_iota(jnp.int32, (16, HD), 0) < 8
             for g, gain in enumerate((one, two)):
                 halves = [gain[:, h * HD : (h + 1) * HD].astype(F32) for h in range(2)]
-                first[wide + 16 * g : wide + 16 * (g + 1), :] = jnp.where(pick, *halves).astype(BF16)
-            outs[2 * n + d][...] = wo[d][...]
-
-    def head_of(d):
-        return lambda i, me: (0, 2 * (me[0] ^ d) + me[1])
+                outs[d][wide + 16 * g : wide + 16 * (g + 1), :] = jnp.where(pick, *halves).astype(BF16)
 
     def chip_of(d):
         return lambda i, me: (0, me[0] ^ d)
 
-    def head_rows_of(d):
-        return lambda i, me: (2 * (me[0] ^ d) + me[1], 0)
-
+    own_tokens = tokens[0]
+    near_tokens = [own_tokens] + [across(own_tokens, d) for d in (1, 2)]
     gain_spec = pl.BlockSpec((1, wide), lambda i, me: (0, 0))
     cut = run_grid(
-        cut_attention,
+        cut_weights,
         me,
         (1,),
-        [query_weight] * n
-        + [key_weight] * n
+        [key_weight] * n
         + [value_weight] * n
-        + [output_weight] * n
         + [first_gain.reshape(1, wide), second_gain.reshape(1, wide)],
-        [pl.BlockSpec((wide, HD), head_of(d)) for d in range(n)]
-        + [pl.BlockSpec((wide, HD), chip_of(d)) for d in range(n)] * 2
-        + [pl.BlockSpec((HD, wide), head_rows_of(d)) for d in range(n)]
-        + [gain_spec, gain_spec],
-        [shape((wide + 32, HD))] * n + [shape((wide, HD))] * n + [shape((HD, wide))] * n,
-        [pl.BlockSpec((wide + 32, HD), lambda i, me: (0, 0))] * n
-        + [pl.BlockSpec((wide, HD), lambda i, me: (0, 0))] * n
-        + [pl.BlockSpec((HD, wide), lambda i, me: (0, 0))] * n,
-        name="cut_attention",
-    )
-    own_tokens = tokens[0]
-    near_tokens = [own_tokens] + [across(own_tokens, d) for d in range(1, n)]
-
-    def cut_hidden(me_ref, *refs):
-        gates, ups, downs = (refs[i * n : (i + 1) * n] for i in range(3))
-        for d in range(n):
-            refs[-1][0, d, :wide, :quarter] = gates[d][...]
-            refs[-1][0, d, :wide, quarter:] = ups[d][...]
-            refs[-1][0, d, wide:, :] = downs[d][...]
-
-    def columns_of(d):
-        return lambda q, me: (0, (2 * (me[0] ^ d) + me[1]) * QUARTERS + q)
-
-    def down_rows_of(d):
-        return lambda q, me: ((2 * (me[0] ^ d) + me[1]) * QUARTERS + q, 0)
-
+        [pl.BlockSpec((wide, HD), chip_of(d)) for d in range(n)] * 2 + [gain_spec, gain_spec],
+        [shape((wide + 32, HD))] * n,
+        [pl.BlockSpec((wide + 32, HD), lambda i, me: (0, 0))] * n,
+        name="cut_weights",
+    )
+    weights_in = [cut[0]] + [across(cut[d], d) for d in range(1, n)]
     piece = (wide + quarter, 2 * quarter)
-    hidden_cut = run_grid(
-        cut_hidden,
-        me,
-        (QUARTERS,),
-        [gate_weight] * n + [up_weight] * n + [down_weight] * n,
-        [pl.BlockSpec((wide, quarter), columns_of(d)) for d in range(n)] * 2
-        + [pl.BlockSpec((quarter, wide), down_rows_of(d)) for d in range(n)],
-        shape((QUARTERS, n) + piece),
-        pl.BlockSpec((1, n) + piece, lambda q, me: (q, 0, 0, 0)),
-        name="cut_hidden",
-    )
-    cut, hidden_cut = lax.optimization_barrier((cut, hidden_cut))
-    weights_in = [cut[0]] + [across(cut[d], d) for d in range(1, n)]
     own_cotangent = cotangent[0]
     block = (rows, width)
 
@@ -581,7 +537,7 @@
     query_at, output_at, kv_at = tiles_count - 3, tiles_count - 2, tiles_count - 1
     units = 2 * tiles_count
     unit = (2, quarter, wide)
-    held_sums, held_ends = 4, 3
+    held_sums, held_ends, ahead = 4, 3, 2
     MID, BACK, OUT, ONE = range(4)
     query_slot, attended_slot, query_grad_slot, kv_grad_slot = range(2 * planes, 2 * planes + 4)
     kept_slots = 2 * planes + 2
@@ -592,9 +548,11 @@
     in_hbm = dict(
         near_tokens=near_tokens,
         in_weight=weights_in,
-        query_cut=cut[n : 2 * n],
-        out_cut=cut[2 * n :],
-        cut=hidden_cut,
+        query_weight=query_weight,
+        output_weight=output_weight,
+        gate_weight=gate_weight,
+        up_weight=up_weight,
+        down_weight=down_weight,
         cotangent=own_cotangent,
         tokens=own_tokens,
     )
@@ -651,9 +609,9 @@
         load_sem=dma((4 * n + n,)),
         gains=pltpu.VMEM((8, width), F32),
         gain_rows=pltpu.VMEM((n, 32, HD), BF16),
-        feed_local=dma((QUARTERS,)),
-        feed_send=dma((QUARTERS * n,)),
-        feed_recv=dma((QUARTERS * n,)),
+        feed_local=dma((3 * QUARTERS,)),
+        feed_send=dma((3 * QUARTERS * n,)),
+        feed_recv=dma((3 * QUARTERS * n,)),
         stage_sem=dma((2, 2)),
         one_send=dma((units,)),
         one_recv=dma((units,)),
@@ -694,13 +652,19 @@
         two_half_recv=dma((n,)),
         branch_half_send=dma((n,)),
         branch_half_recv=dma((n,)),
-        climb_send=dma((2 * planes,)),
-        climb_recv=dma((2 * planes,)),
-        fall_send=dma((2 * planes,)),
-        fall_recv=dma((2 * planes,)),
+        climb_send=dma((n * planes,)),
+        climb_recv=dma((n * planes,)),
+        fall_send=dma((n * planes,)),
+        fall_recv=dma((n * planes,)),
         soft=pltpu.VMEM((2 * n, pair, 1), F32),
-        pass_send=dma((planes,)),
-        pass_recv=dma((planes,)),
+        pass_send=dma((n * planes,)),
+        pass_recv=dma((n * planes,)),
+        cot_half_send=dma((n,)),
+        cot_half_recv=dma((n,)),
+        share_send=dma((2 * n,)),
+        share_recv=dma((2 * n,)),
+        token_half_send=dma((n,)),
+        token_half_recv=dma((n,)),
         keep_sem=dma((3,)),
         branch_local=dma((1,)),
         branch_send=dma((n,)),
@@ -766,14 +730,47 @@
         def span(first, count):
             return pl.ds(pl.multiple_of(first, count), count)
 
-        def feed_copy(q, d):
-            at = q * n + d
-            return remote(
-                r.cut.at[q, d], feed.at[q, d], r.feed_send.at[at], r.feed_recv.at[at], (here, chips[d])
-            )
+        def head_of(d):
+            return span((2 * chips[d] + side) * HD, HD)
+
+        def feed_parts(q, d, first=0, count=wide):
+            there = span(((2 * chips[d] + side) * QUARTERS + q) * quarter, quarter)
+            rows_in = pl.ds(first, count)
+            below = 0 if count == wide else pl.multiple_of(first // 2, quarter // 2)
+            some = pl.ds(
+                pl.multiple_of(
+                    ((2 * chips[d] + side) * QUARTERS + q) * quarter + below, quarter // 2
+                ),
+                count // 2,
+            )
+            below = wide if count == wide else pl.multiple_of(wide + below, quarter // 2)
+            return (
+                (r.gate_weight.at[rows_in, there], feed.at[q, d, rows_in, pl.ds(0, quarter)]),
+                (r.up_weight.at[rows_in, there], feed.at[q, d, rows_in, pl.ds(quarter, quarter)]),
+                (r.down_weight.at[some], feed.at[q, d, pl.ds(below, count // 2)]),
+            )
+
+        def feed_far(q, d, *rows_of):
+            copies = []
+            for part, (source, target) in enumerate(feed_parts(q, d, *rows_of)):
+                at = (q * n + d) * 3 + part
+                copies.append(
+                    remote(source, target, r.feed_send.at[at], r.feed_recv.at[at], (here, chips[d]))
+                )
+            return copies
 
         def feed_own(q):
-            return local(r.cut.at[q, 0], feed.at[q, 0], r.feed_local.at[q])
+            return [
+                local(source, target, r.feed_local.at[3 * q + part])
+                for part, (source, target) in enumerate(feed_parts(q, 0))
+            ]
+
+        def every(copies, use):
+            for copy in copies:
+                use(copy)
+
+        starts, waits = lambda c: c.start(), lambda c: c.wait()
+        arrives, leaves = lambda c: c.wait_recv(), lambda c: c.wait_send()
 
         def hop_one(i):
             return remote(r.tiles.at[i], r.from_end.at[i], r.one_send.at[i], r.one_recv.at[i], partner)
@@ -823,7 +820,7 @@
         def add(target, a, b):
             def some(s, _):
                 at = (s // 4, span((s % 4) * (quarter // 4), quarter // 4))
-                target[at] = (a[at].astype(F32) + b[at].astype(F32)).astype(BF16)
+                target[at] = a[at] + b[at]
                 return 0
 
             lax.fori_loop(0, 8, some, 0)
@@ -832,6 +829,10 @@
             return pl.when(functools.reduce(jnp.logical_and, conditions, (i >= 0) & (i < units)))
 
         def step(i, _=0):
+            @when_in(i + ahead, is_end, i >= 0)
+            def _():
+                hop_one(i + ahead).start()
+
             @when_in(i - 1, is_middle)
             def _():
                 at = i - 1
@@ -946,10 +947,10 @@
             for h in range(2):
                 stage_copy(t, h).wait()
 
-            @pl.when(is_end)
-            def _():
-                for h in range(2):
-                    hop_one(2 * t + h).start()
+            @pl.when(is_end & (t == 0))
+            def _():
+                for i in range(ahead):
+                    hop_one(i).start()
 
         def outer(t, left, right_rows):
             for j in range(n):
@@ -993,19 +994,17 @@
             def some(c, _):
                 at = span(c * few, few)
                 own = pl.ds(pl.multiple_of(base + 2 * d * rows + c * few, few), few)
-                work[own, :] = (
-                    work[own, :].astype(F32) + r.some_rows[d, at, :].astype(F32)
-                ).astype(BF16)
+                work[own, :] = work[own, :] + r.some_rows[d, at, :]
                 return 0
 
             lax.fori_loop(0, rows // few, some, 0)
             row_far(s, base, d).start()
 
-        far_first = (3, 1, 2, 0)
+        far_first = (1, 2, 3, 0)
 
         def rows_reduced(s, base, compute, send=True, ticks=0):
             def one(i, _):
-                d = jnp.where(i == 0, 3, jnp.where(i == n - 1, 0, i))
+                d = (i + 1) % n
                 compute(d)
                 for at in range(n):
 
@@ -1085,7 +1084,7 @@
 
         def out_far(d):
             return remote(
-                r.out_cut[d],
+                r.output_weight.at[head_of(d)],
                 r.theirs.at[d // 2, d % 2],
                 r.out_send.at[d],
                 r.out_recv.at[d],
@@ -1105,7 +1104,7 @@
 
         def query_far(d):
             return remote(
-                r.query_cut[d],
+                r.query_weight.at[:, head_of(d)],
                 r.query_in.at[d],
                 r.query_send.at[d],
                 r.query_recv.at[d],
@@ -1118,35 +1117,68 @@
         def query_piece(j):
             return heads.at[query_grad_slot + j // 3, pl.ds(j % 3 * wide, wide)]
 
+        half_rows = rows // 2
+
+        def cot_half(d):
+            some = pl.ds((d - 1) * half_rows, half_rows)
+            return remote(
+                r.cot_all.at[0, d, some],
+                r.cot_all.at[0, 3, some],
+                r.cot_half_send.at[d],
+                r.cot_half_recv.at[d],
+                (here, chips[3 - d]),
+            )
+
+        parity = z % 2
+
+        def feed_half(d):
+            return feed_far(0, d, pl.multiple_of(parity * (wide // 2), wide // 2), wide // 2)
+
+        def feed_share(d):
+            copies = []
+            for part, (first, count) in enumerate(((0, wide // 2), (wide, quarter // 2))):
+                some = feed.at[0, d, span(first + parity * count, count)]
+                at = 2 * d + part
+                copies.append(remote(some, some, r.share_send.at[at], r.share_recv.at[at], partner))
+            return copies
+
+        def token_near(d):
+            source = work.at[pl.ds(plane_rows + 2 * d * rows, rows)] if d == 3 else r.near_tokens[d]
+            return remote(
+                source,
+                work.at[pl.ds(plane_rows + (2 * d + 1) * rows, rows)],
+                r.token_send.at[d],
+                r.token_recv.at[d],
+                other_core,
+            )
+
+        def token_half(d):
+            return remote(
+                r.near_tokens[d].at[pl.ds((d - 1) * half_rows, half_rows)],
+                work.at[pl.ds(plane_rows + 6 * rows + (d - 1) * half_rows, half_rows)],
+                r.token_half_send.at[d],
+                r.token_half_recv.at[d],
+                (here, chips[3 - d]),
+            )
+
+        for d in (1, 2):
+            token_half(d).start()
         for d in range(1, n):
             query_far(d).start()
         for d in range(1, n):
             out_far(d).start()
-        for d in range(1, n):
-            feed_copy(0, d).start()
-        for d in range(1, n):
-            cot_far(d).start()
         cot_near(0).start()
-        def token_near(d):
-            return remote(
-                r.near_tokens[d],
-                work.at[pl.ds(plane_rows + (2 * d + 1) * rows, rows)],
-                r.token_send.at[d],
-                r.token_recv.at[d],
-                other_core,
-            )
-
-        for d in range(n):
+        for d in range(n - 1):
             token_near(d).start()
             load(r.near_tokens[d], work.at[pl.ds(plane_rows + 2 * d * rows, rows)])
         for j in range(n):
             load(r.in_weight[j].at[pl.ds(0, wide)], kv_piece(j))
             load(r.in_weight[j].at[pl.ds(wide, 32)], r.gain_rows.at[j])
         loaded()
-        load(r.out_cut[0], r.theirs.at[0, 0])
-        load(r.query_cut[0], query_piece(0))
+        load(r.output_weight.at[head_of(0)], r.theirs.at[0, 0])
+        load(r.query_weight.at[:, head_of(0)], query_piece(0))
         for q in range(QUARTERS):
-            feed_own(q).start()
+            every(feed_own(q), starts)
         for j in range(n):
             both = r.gain_rows[j].astype(F32)
             for g in range(2):
@@ -1154,10 +1186,7 @@
                     here_half = pl.ds(pl.multiple_of(chips[j] * wide + h * HD, HD), HD)
                     r.gains[g : g + 1, here_half] = both[16 * g + 8 * h : 16 * g + 8 * h + 1]
 
-        for d in range(n):
-            token_near(d).wait_recv()
-
-        def project(d, _):
+        def project(d):
             for c in range(2):
                 first = (2 * d + (side + c) % 2) * rows
 
@@ -1176,69 +1205,95 @@
                 kv += matmul(work[now, blocks[j]], kv_piece(j)[...])
             kv = kv * r.tables[2] + turn(kv) * r.tables[3]
             heads[0, now, :] = kv.astype(BF16)
-            return 0
-
-        lax.fori_loop(0, n, project, 0)
-        keep_normed = local(work.at[pl.ds(0, plane_rows)], r.normed, r.keep_sem.at[0])
-        keep_normed.start()
-
-        kv_halves = [pl.ds(h * (plane_rows // 2), plane_rows // 2) for h in range(2)]
-
-        def climb(s, h):
-            at = 2 * s + h
-            return remote(
-                heads.at[s - 1, kv_halves[h]],
-                heads.at[s, kv_halves[h]],
-                r.climb_send.at[at],
-                r.climb_recv.at[at],
-                above,
-            )
-
-        def fall(s, h):
-            at = 2 * s + h
-            return remote(
-                heads.at[(planes - s + 1) % planes, kv_halves[h]],
-                heads.at[planes - s, kv_halves[h]],
+
+        def block_of(k, d):
+            return heads.at[k, span(d * pair, pair)]
+
+        def climb(s, d):
+            at = s * n + d
+            return remote(
+                block_of(s - 1, d), block_of(s, d), r.climb_send.at[at], r.climb_recv.at[at], above
+            )
+
+        def fall(s, d):
+            at = s * n + d
+            return remote(
+                block_of((planes - s + 1) % planes, d),
+                block_of(planes - s, d),
                 r.fall_send.at[at],
                 r.fall_recv.at[at],
                 below,
             )
 
-        def pass_on(k):
-            return remote(
-                heads.at[k], heads.at[planes + k], r.pass_send.at[k], r.pass_recv.at[k], other_core
-            )
-
-        def kv_leave(s, h):
+        def pass_on(k, d):
+            at = k * n + d
+            return remote(
+                block_of(k, d),
+                block_of(planes + k, d),
+                r.pass_send.at[at],
+                r.pass_recv.at[at],
+                other_core,
+            )
+
+        def kv_leave(s, d):
             @pl.when((z - s + 1 >= 0) & (z + 1 < planes))
             def _():
-                climb(s, h).start()
+                climb(s, d).start()
 
             @pl.when((z + s - 1 < planes) & (z >= 1))
             def _():
-                fall(s, h).start()
-
-        def kv_come(s, h):
+                fall(s, d).start()
+
+        def kv_come(s, d):
             @pl.when(z - s >= 0)
             def _():
-                climb(s, h).wait_recv()
+                climb(s, d).wait_recv()
 
             @pl.when(z + s < planes)
             def _():
-                fall(s, h).wait_recv()
-
-        def kv_forward(s):
-            for h in range(2):
-                kv_come(s, h)
-                if s + 1 < planes:
-                    kv_leave(s + 1, h)
-
-        for h in range(2):
-            kv_leave(1, h)
-        pass_on(0).start()
+                fall(s, d).wait_recv()
+
+        def passing(condition, k, d):
+            @pl.when(condition)
+            def _():
+                pass_on(k, d).start()
+
+        def passed(condition, k, d):
+            @pl.when(condition)
+            def _():
+                pass_on(k, d).wait_recv()
+
+        def by_chip(use):
+            def one(i, _):
+                use((i + 1) % n)
+                return 0
+
+            lax.fori_loop(0, n, one, 0)
+
+        def start_kv(d):
+            for at in range(n):
+
+                @pl.when(d == at)
+                def _():
+                    if at == 3:
+                        for far in (1, 2):
+                            token_half(far).wait_recv()
+                        token_near(3).start()
+                    token_near(at).wait_recv()
+
+            project(d)
+            kv_leave(1, d)
+            pass_on(0, d).start()
+
+        by_chip(start_kv)
+        token_near(3).wait_send()
+        keep_normed = local(work.at[pl.ds(0, plane_rows)], r.normed, r.keep_sem.at[0])
+        keep_normed.start()
         for d in range(1, n):
             query_far(d).wait_recv()
             load(r.query_in.at[d], query_piece(d))
+        for d in (1, 2):
+            cot_far(d).start()
         loaded()
 
         def project_query(d, _):
@@ -1291,48 +1346,50 @@
             return None
 
         def attend_to(k, first=False):
-            def one(d, _):
-                attend_block(k, d, first, False)
-                return 0
-
-            lax.fori_loop(0, n, one, 0)
+            by_chip(lambda d: attend_block(k, d, first, False) and None)
 
         def when_middle(there, otherwise):
             return jnp.where(is_middle, there, otherwise)
 
-        def passed(condition, k):
-            @pl.when(condition)
-            def _():
-                pass_on(k).wait_recv()
-
-        def passing(condition, k):
-            @pl.when(condition)
-            def _():
-                pass_on(k).start()
-
-        pass_on(0).wait_recv()
+        by_chip(lambda d: pass_on(0, d).wait_recv())
         attend_to(0, first=True)
-        kv_forward(1)
-        passing(z >= 1, 1)
-        passing(z + 1 < planes, 3)
-        passed(z >= 1, 1)
-        passed(z + 1 < planes, 3)
+
+        def first_come(d):
+            kv_come(1, d)
+            kv_leave(2, d)
+            passing(z >= 1, 1, d)
+            passing(z + 1 < planes, 3, d)
+
+        def first_passed(d):
+            passed(z >= 1, 1, d)
+            passed(z + 1 < planes, 3, d)
+
+        by_chip(first_come)
+        by_chip(first_passed)
         attend_to(jnp.where(z >= 1, 1, 3))
-        kv_forward(2)
-        pass_on(2).start()
+        for d in (1, 2):
+            cot_far(d).wait_recv()
+            cot_half(d).start()
+            cot_near(d).start()
         for d in range(1, n):
-            cot_far(d).wait_recv()
-            cot_near(d).start()
-        pass_on(2).wait_recv()
+            every(feed_half(d), starts)
+
+        def second_come(d):
+            kv_come(2, d)
+            kv_leave(3, d)
+            pass_on(2, d).start()
+
+        by_chip(second_come)
+        by_chip(lambda d: pass_on(2, d).wait_recv())
         attend_to(when_middle(3, 2))
         keep_normed.wait()
-        kv_forward(3)
-        passing(z == 0, 1)
-        passing(z == planes - 1, 3)
-        passed(z == 0, 1)
-        passed(z == planes - 1, 3)
 
         def attend(d):
+            kv_come(3, d)
+            passing(z == 0, 1, d)
+            passing(z == planes - 1, 3, d)
+            passed(z == 0, 1, d)
+            passed(z == planes - 1, 3, d)
             now = span(d * pair, pair)
             last_block = jnp.where(z == 0, 1, when_middle(2, 3))
             total, weight = attend_block(last_block, d, False, True)
@@ -1352,19 +1409,28 @@
         load(r.tokens, r.own_rows)
         loaded()
         keep_out.wait()
-        for s in range(1, planes):
-            for h in range(2):
+        for d in (1, 2):
+            cot_half(d).wait_recv()
+        cot_near(3).start()
+        for d in range(1, n):
+            every(feed_half(d), arrives)
+            every(feed_share(d), starts)
+
+        def kv_left(d):
+            for s in range(1, planes):
 
                 @pl.when((z - s + 1 >= 0) & (z + 1 < planes))
                 def _():
-                    climb(s, h).wait_send()
+                    climb(s, d).wait_send()
 
                 @pl.when((z + s - 1 < planes) & (z >= 1))
                 def _():
-                    fall(s, h).wait_send()
-
-        for k in range(planes):
-            pass_on(k).wait_send()
+                    fall(s, d).wait_send()
+
+            for k in range(planes):
+                pass_on(k, d).wait_send()
+
+        by_chip(kv_left)
 
         rows_arrive(MID, plane_rows)
 
@@ -1399,8 +1465,6 @@
                 r.two_near_recv.at[d],
                 other_core,
             )
-
-        half_rows = rows // 2
 
         def two_half(d):
             return remote(
@@ -1425,7 +1489,7 @@
             load(r.cot_all.at[1, d], work.at[pl.ds(plane_rows + (2 * d + 1) * rows, rows)])
         keep_heads.wait()
         for d in range(1, n):
-            feed_copy(0, d).wait_recv()
+            every(feed_share(d), arrives)
         loaded()
 
         def rows_of_chip(t, arrive, half_way, pass_along):
@@ -1447,17 +1511,17 @@
 
         def quarter_step(q, _):
             step(3 * q - 3)
-            feed_own(q).wait()
+            every(feed_own(q), waits)
 
             @pl.when(q > 0)
             def _():
                 for d in range(1, n):
-                    feed_copy(q, d).wait_recv()
+                    every(feed_far(q, d), arrives)
 
             @pl.when((q > 0) & (q < QUARTERS - 1))
             def _():
                 for d in range(1, n):
-                    feed_copy(q + 1, d).start()
+                    every(feed_far(q + 1, d), starts)
 
             def forward(t, _):
                 @pl.when(q == 0)
@@ -1489,29 +1553,28 @@
             @pl.when(q == 0)
             def _():
                 for d in range(1, n):
-                    feed_copy(1, d).start()
+                    every(feed_far(1, d), starts)
 
             step(3 * q - 2)
 
             def one(w, _):
                 t = 3 * q + w
 
-                @pl.when(t >= 2)
+                outer(t, turned[w], span(jnp.where(w == 0, plane_rows, 0), plane_rows))
+
+                @pl.when(w > 0)
                 def _():
-                    staged(t - 2)
-
-                outer(t, turned[w], span(jnp.where(w == 0, plane_rows, 0), plane_rows))
+                    staged(t - 1)
+
                 return 0
 
             lax.fori_loop(0, 3, one, 0)
             step(3 * q - 1)
+            staged(3 * q + 2)
             return 0
 
         lax.fori_loop(0, QUARTERS, quarter_step, 0)
         steps_done[0] = 3 * QUARTERS - 3
-        for t in (query_at - 2, query_at - 1):
-            staged(t)
-
         for d in range(1, n):
             two_near(d).wait_send()
         for d in (1, 2):
@@ -1543,9 +1606,11 @@
 
         rows_reduced(OUT, plane_rows, out_step, send=False, ticks=TICKS[2] + TICKS[3])
 
+        for d in range(1, n):
+            every(feed_share(d), leaves)
         load(r.kept, heads.at[pl.ds(0, kept_slots)])
         for j in range(n):
-            query_source = r.query_cut[0] if j == 0 else r.query_in.at[j]
+            query_source = r.query_weight.at[:, head_of(0)] if j == 0 else r.query_in.at[j]
             load(query_source, feed.at[0, j, pl.ds(0, wide), pl.ds(0, HD)])
             load(r.in_weight[j].at[pl.ds(0, wide)], feed.at[0, j, pl.ds(0, wide), pl.ds(HD, HD)])
             load(r.out_weight.at[j // 2, j % 2], feed.at[0, j, pl.ds(wide, HD)])
@@ -1669,9 +1734,7 @@
         def kv_add(k, slot):
             def some(c, _):
                 at = span(c * 64, 64)
-                heads[k, at, :] = (
-                    heads[k, at, :].astype(F32) + r.kv_some[slot, at, :].astype(F32)
-                ).astype(BF16)
+                heads[k, at, :] = heads[k, at, :] + r.kv_some[slot, at, :]
                 return 0
 
             lax.fori_loop(0, plane_rows // 64, some, 0)
@@ -1733,30 +1796,36 @@
         loaded()
         outer(query_at, turned[1], high_half)
         outer(output_at, turned[0], low_half)
+        staged(query_at)
+        staged(output_at)
         advance(TICKS[7])
         kv_receive(3, 2, 2)
         kv_send(2)
-        staged(query_at)
-        staged(output_at)
         advance(TICKS[8])
         kv_receive(2, 1, 3)
         kv_send(1)
         advance(TICKS[9])
         kv_receive(1, 0, 0)
 
-        def project_back(d):
+        def kv_back(d, _):
             now = span(d * pair, pair)
             grad = heads[0, now, :].astype(F32)
             grad = grad * r.tables[2] + turn_back(grad * r.tables[3])
             heads[kv_grad_slot, now, :] = grad.astype(BF16)
-            left = jnp.concatenate([heads[query_grad_slot, now, :], grad.astype(BF16)], axis=1)
+            turned[2, :, now] = grad.T.astype(BF16)
+            return 0
+
+        lax.fori_loop(0, n, kv_back, 0)
+        outer(kv_at, turned[2], high_half)
+
+        def project_back(d):
+            now = span(d * pair, pair)
+            left = jnp.concatenate([heads[query_grad_slot, now, :], heads[kv_grad_slot, now, :]], axis=1)
             for j in range(n):
                 put_rows(0, d, matmul_nt(left, feed[0, j, :wide, :]).astype(BF16), blocks[j])
 
+        staged(kv_at)
         rows_reduced(ONE, 0, project_back)
-        turned[2] = heads[kv_grad_slot].astype(F32).T.astype(BF16)
-        outer(kv_at, turned[2], high_half)
-        staged(kv_at)
         advance(TICKS[10])
 
         for d in (1, 2):
@@ -1838,15 +1907,20 @@
 
         loaded()
         rows_sent(ONE, 0)
-        for q in range(QUARTERS):
+        for q in range(1, QUARTERS):
             for d in range(1, n):
-                feed_copy(q, d).wait_send()
+                every(feed_far(q, d), leaves)
+        for d in range(1, n):
+            every(feed_half(d), leaves)
+        for d in (1, 2):
+            token_half(d).wait_send()
+            cot_far(d).wait_send()
+            cot_half(d).wait_send()
         for d in range(1, n):
             query_far(d).wait_send()
             out_far(d).wait_send()
+        for d in range(n - 1):
             token_near(d).wait_send()
-            cot_far(d).wait_send()
-        token_near(0).wait_send()
         for d in range(n):
             cot_near(d).wait_send()
         for k in range(planes):

time: 778 us -> 725 us (0.932)
  Pallas kernels: 732 us -> 688 us
    pallas_call x1, Pallas kernels: 678 us -> 644 us  [plane_layer(): pl.pallas_call(backward, out_shape=jax.tree.leaves(out_hbm), in_specs=[pl...]
    pallas_call x3 -> x2, Pallas kernels: 54.6 us -> 43.1 us  [run_grid(): pl.pallas_call(body, out_shape=outs, grid_spec=pltpu.PrefetchScalarGridSp...]
    ppermute x6 -> x5, waiting for transfers between devices: 18.8 us -> 12.3 us  [across(): return lax.ppermute(value, 'fsdp', [(i, i ^ d) for i in range(n)])]
  transfers between devices with their start and end apart: 6 -> 5, of which waited for: 2 -> 2; matrix products, arithmetic and copies ran while one was open for 1% -> 1% of each run, Pallas kernels for 2% -> 0%
where the time goes in v7:
time: 725 us; the launch traced here: 723 us
  Pallas kernels  688 us (95%)
  waiting for transfers between devices  12.3 us (2%)
  local copies, waits for them, and re-layouts  10.8 us (1%)
  starting transfers between devices  8.01 us (1%)
    pallas_call x1, Pallas kernels, plane_layer(): pl.pallas_call(backward, out_shape=jax.tree.leaves(out_hbm), in_specs=[pl...  644 us
    pallas_call x2, Pallas kernels, run_grid(): pl.pallas_call(body, out_shape=outs, grid_spec=pltpu.PrefetchScalarGridSp...  43.1 us
  transfers between devices with their start and end apart: 5, of which 2 were waited for; matrix products, arithmetic and copies ran while one was open for 1% of the time, Pallas kernels for 0%

profile of v7, /device:TPU:0, one launch (start us, length us, event | category | flops | bytes accessed | tf_op | source)
XLA Modules:
  0.0 723.2 jit_solution(16144816729114304921)
XLA Ops:
  0.6 3.0 collective-permute-start.4
  3.7 1.5 collective-permute-start.3
  5.2 1.3 reshape.283.refs_8_
  6.4 1.3 reshape.284.refs_9_
  7.7 0.6 pad_add_fusion.me_ref
  8.3 3.4 cut_weights.1
  11.7 0.5 collective-permute-start
  12.3 2.9 collective-permute-start.2
  15.6 0.6 gather_fusion
  16.5 0.7 gather_fusion.1
  17.2 0.7 reshape.286.refs_14_
  17.9 1.5 reshape.305.refs_15_
  19.5 0.1 multiply_bitcast_fusion
  19.6 1.4 fusion.1
  21.0 1.2 pad_maximum_fusion.refs_16_
  22.3 8.0 %collective-permute-done.refs_4_ = bf16[544,256]{1,0:T(8,128)(2,1)S(1)} collective-permute-done((bf16[544,256]{1,0:T(8,128)(2,1)}, bf16[544,256]{1,0:T(8,128)(2,1)S(1)}, u32[]{:S(2)}, u32[]{:S(2)}) %collective-permute-start) | collective-permute-done | bytes 278560 | tf_op jit(solution)/shard_map/ppermute | solution.py:437
  30.3 4.3 collective-permute-done.2.refs_6_
  34.7 0.7 copy-done.7
  35.3 0.3 copy-done.4
  35.6 644.5 %backward.1 = (bf16[4,2,192,2048]{3,2,1,0:T(8,128)(2,1)}, bf16[2,4,192,2048]{3,2,1,0:T(8,128)(2,1)}, bf16[30,2,256,512]{3,2,1,0:T(8,128)(2,1)}, bf16[30,2,256,51...) custom-call(bf16[192,2048]{1,0:T(8,128)(2,1)} %bitcast.24, ...), custom_call_target="tpu_custom_call" | custom-call | flops 96636764160 | bytes 130381824 | tf_op jit(solution)/shard_map/backward/pallas_call | solution.py:1941
  680.1 1.4 fusion.9
  681.4 39.7 %place.1 = (f32[512,8192]{1,0:T(8,128)}, f32[512,8192]{1,0:T(8,128)}, f32[8192,512]{1,0:T(8,128)}, f32[512,2048]{1,0:T(8,128)}, f32[2048,512]{1,0:T(8,128)}, /*index=5*/f32[512,1024]{1,0:T(8,128)}, f32[512,1024]{1,0:T(8,128)}) custom-call(s32[2]{0:T(128)} %pad_add_fusion.me_ref, bf16[15,4,256,512]{3,2,1,0:T(8,128)(2,1)} %bitcast.18, ...), custom_call_target="tpu_custom_call" | custom-call | bytes 94371840 | tf_op jit(solution)/shard_map/place/pallas_call | solution.py:366
  721.2 0.9 copy.27
  722.1 1.1 copy.28
  (33 shorter events, 0.8 us)
Async XLA Ops:
  0.6 34.0 %collective-permute-start.4 = (bf16[192,2048]{1,0:T(8,128)(2,1)}, bf16[192,2048]{1,0:T(8,128)(2,1)S(1)}, u32[]{:S(2)}, u32[]{:S(2)}) collective-permute-start(bf16[192,2048]{1,0:T(8,128)(2,1)} %bitcast.25), channel_id=1, source_target_pairs={{0,2},{1,3},{2,0},{3,1},{4,6},{5,7},{6,4},{7,5},{8,10},{9,11},{10,... | collective-permute-start | bytes 2359304 | tf_op jit(solution)/shard_map/ppermute | solution.py:437
  3.7 31.0 %collective-permute-start.3 = (bf16[192,2048]{1,0:T(8,128)(2,1)}, bf16[192,2048]{1,0:T(8,128)(2,1)}, u32[]{:S(2)}, u32[]{:S(2)}) collective-permute-start(bf16[192,2048]{1,0:T(8,128)(2,1)} %bitcast.26), channel_id=1, source_target_pairs={{0,1},{1,0},{2,3},{3,2},{4,5},{5,4},{6,7},{7,6},{8,9},{9,8},{10,11... | collective-permute-start | bytes 2359304 | tf_op jit(solution)/shard_map/ppermute | solution.py:437
  8.3 7.1 copy-start
  8.3 8.2 %copy-start.3 = (s32[4,1536]{1,0:T(4,128)S(1)}, s32[4,1536]{1,0:T(4,128)}, u32[]{:S(2)}) copy-start(s32[4,1536]{1,0:T(4,128)} %param.24) | copy-start | bytes 73732
  11.7 18.6 %collective-permute-start = (bf16[544,256]{1,0:T(8,128)(2,1)}, bf16[544,256]{1,0:T(8,128)(2,1)S(1)}, u32[]{:S(2)}, u32[]{:S(2)}) collective-permute-start(bf16[544,256]{1,0:T(8,128)(2,1)} %get-tuple-element.28), channel_id=1, source_target_pairs={{0,1},{1,0},{2,3},{3,2},{4,5},{5,4},{6,7},{7,6},{8,9},{9,8},{10,11... | collective-permute-start | bytes 835592 | tf_op jit(solution)/shard_map/ppermute | solution.py:437
  12.2 18.1 %collective-permute-start.1 = (bf16[544,256]{1,0:T(8,128)(2,1)}, bf16[544,256]{1,0:T(8,128)(2,1)S(1)}, u32[]{:S(2)}, u32[]{:S(2)}) collective-permute-start(bf16[544,256]{1,0:T(8,128)(2,1)} %get-tuple-element.29), channel_id=1, source_target_pairs={{0,2},{1,3},{2,0},{3,1},{4,6},{5,7},{6,4},{7,5},{8,10},{9,11},{10,... | collective-permute-start | bytes 835592 | tf_op jit(solution)/shard_map/ppermute | solution.py:437
  12.3 22.3 %collective-permute-start.2 = (bf16[544,256]{1,0:T(8,128)(2,1)}, bf16[544,256]{1,0:T(8,128)(2,1)S(1)}, u32[]{:S(2)}, u32[]{:S(2)}) collective-permute-start(bf16[544,256]{1,0:T(8,128)(2,1)} %get-tuple-element.30), channel_id=1, source_target_pairs={{0,3},{1,2},{2,1},{3,0},{4,7},{5,6},{6,5},{7,4},{8,11},{9,10},{10,... | collective-permute-start | bytes 835592 | tf_op jit(solution)/shard_map/ppermute | solution.py:437
  30.3 4.3 copy-start.5
  30.3 4.3 copy-start.6
  34.6 0.7 copy-start.7
  34.6 1.0 copy-start.4
  681.4 39.7 %copy-start.2 = (bf16[192,2048]{1,0:T(8,128)(2,1)S(1)}, bf16[192,2048]{1,0:T(8,128)(2,1)}, u32[]{:S(2)}) copy-start(bf16[192,2048]{1,0:T(8,128)(2,1)} %get-tuple-element.31) | copy-start | bytes 2359300
  681.4 40.6 %copy-start.1 = (f32[192,2048]{1,0:T(8,128)S(1)}, f32[192,2048]{1,0:T(8,128)}, u32[]{:S(2)}) copy-start(f32[192,2048]{1,0:T(8,128)} %get-tuple-element.32) | copy-start | bytes 4718596

commit v8 on v7

--- a/solution.py
+++ b/solution.py
@@ -323,7 +323,7 @@
 F32 = jnp.float32
 QUARTERS = 4
 MESH = pl.DeviceIdType.MESH
-TICKS = (2, 1, 2, 2, 3, 2, 1, 1, 1, 2, 4, 2, 2)
+TICKS = (2, 1, 2, 2, 3, 2, 1, 1, 1, 2, 6, 2, 2)
 LINES = 2
 
 
@@ -1956,38 +1956,77 @@
         a.reshape(tiles_count, n, quarter, wide) for a in (results.owned, results.near)
     )
 
-    def place(me_ref, own_ref, near_ref, gate, up, down, query, out, key, value):
-        for source, e in ((own_ref, 0), (near_ref, 1)):
-
-            @pl.when(pl.program_id(1) == e)
-            def _():
-                for q in range(QUARTERS):
-                    here = slice(q * quarter, (q + 1) * quarter)
-                    down[here, :] = source[3 * q, 0].astype(F32)
-                    gate[:, here] = source[3 * q + 1, 0].T.astype(F32)
-                    up[:, here] = source[3 * q + 2, 0].T.astype(F32)
-                query[...] = source[query_at, 0].T.astype(F32)
-                out[...] = source[output_at, 0].astype(F32)
-
-                @pl.when(me_ref[1] == e)
+    def place(
+        me_ref, own_ref, near_ref, gate, up, down, query, out, key, value, taken, turned, straight, in_sem, out_sem
+    ):
+        chip, side = me_ref[0], me_ref[1]
+        steps = 2 * n
+
+        def take(s, t, source):
+            return pltpu.make_async_copy(source.at[t, s // 2], taken.at[t], in_sem.at[t])
+
+        def start_taking(s, t):
+            for source, e in ((own_ref, 0), (near_ref, 1)):
+
+                @pl.when(s % 2 == e)
                 def _():
-                    key[...] = source[kv_at, 0].T.astype(F32)
-
-                @pl.when(me_ref[1] != e)
+                    take(s, t, source).start()
+
+        def is_straight(t):
+            return t == output_at or (t < query_at and t % 3 == 0)
+
+        def goal(s, t):
+            owner = 2 * (chip ^ (s // 2)) + (side ^ (s % 2))
+            if t == query_at:
+                return query.at[:, column(owner, HD)]
+            if t == output_at:
+                return out.at[column(owner, HD)]
+            here = column(owner * QUARTERS + t // 3, quarter)
+            return (down.at[here], gate.at[:, here], up.at[:, here])[t % 3]
+
+        def put(s, t, use):
+            source = straight.at[t // 3] if is_straight(t) else turned.at[t]
+            if t != kv_at:
+                use(pltpu.make_async_copy(source, goal(s, t), out_sem.at[t]))
+                return
+            for target, e in ((key, 0), (value, 1)):
+
+                @pl.when((side + s) % 2 == e)
                 def _():
-                    value[...] = source[kv_at, 0].T.astype(F32)
-
-    def owner(d, e, me):
-        return 2 * (me[0] ^ d) + (me[1] ^ e)
-
-    by_chip = pl.BlockSpec((tiles_count, 1, quarter, wide), lambda d, e, me: (0, d, 0, 0))
-    placed = run_grid(
+                    there = target.at[:, column(chip ^ (s // 2), HD)]
+                    use(pltpu.make_async_copy(source, there, out_sem.at[t]))
+
+        for t in range(tiles_count):
+            start_taking(0, t)
+
+        def one(s, _):
+            for t in range(tiles_count):
+                take(s, t, own_ref).wait()
+
+                @pl.when(s > 0)
+                def _():
+                    put(s - 1, t, lambda copy: copy.wait())
+
+                if is_straight(t):
+                    straight[t // 3] = taken[t].astype(F32)
+                else:
+                    turned[t] = taken[t].T.astype(F32)
+                put(s, t, lambda copy: copy.start())
+
+                @pl.when(s + 1 < steps)
+                def _():
+                    start_taking(s + 1, t)
+
+            return 0
+
+        lax.fori_loop(0, steps, one, 0)
+        for t in range(tiles_count):
+            put(steps - 1, t, lambda copy: copy.wait())
+
+    in_place = pl.BlockSpec(memory_space=pl.ANY)
+    placed = pl.pallas_call(
         place,
-        me,
-        (n, 2),
-        [owned_tiles, near_tiles],
-        [by_chip, by_chip],
-        [
+        out_shape=[
             shape(a.shape, F32)
             for a in (
                 gate_weight,
@@ -1999,15 +2038,18 @@
                 value_weight,
             )
         ],
-        [pl.BlockSpec((wide, part), lambda d, e, me: (0, owner(d, e, me)))] * 2
-        + [
-            pl.BlockSpec((part, wide), lambda d, e, me: (owner(d, e, me), 0)),
-            pl.BlockSpec((wide, HD), lambda d, e, me: (0, owner(d, e, me))),
-            pl.BlockSpec((HD, wide), lambda d, e, me: (owner(d, e, me), 0)),
-        ]
-        + [pl.BlockSpec((wide, HD), lambda d, e, me: (0, me[0] ^ d))] * 2,
+        in_specs=[pl.BlockSpec(memory_space=pltpu.SMEM), in_place, in_place],
+        out_specs=[in_place] * 7,
+        scratch_shapes=[
+            pltpu.VMEM((tiles_count, quarter, wide), BF16),
+            pltpu.VMEM((tiles_count, wide, quarter), F32),
+            pltpu.VMEM((QUARTERS + 1, quarter, wide), F32),
+            dma((tiles_count,)),
+            dma((tiles_count,)),
+        ],
+        compiler_params=pltpu.CompilerParams(vmem_limit_bytes=VMEM_BYTES),
         name="place",
-    )
+    )(me, owned_tiles, near_tiles)
     gate_grad, up_grad, down_grad, query_grad, output_grad, key_grad, value_grad = placed
 
     return (

time: 725 us -> 713 us (0.983)
  Pallas kernels: 688 us -> 675 us
    pallas_call x2 -> x1, Pallas kernels: 43.1 us -> 3.42 us  [run_grid(): pl.pallas_call(body, out_shape=outs, grid_spec=pltpu.PrefetchScalarGridSp...]
    pallas_call x0 -> x1, Pallas kernels: none -> 32 us  [plane_layer(): pl.pallas_call(place, out_shape=[shape(a.shape, F32) for a in (gate_weigh...]
where the time goes in v8:
time: 713 us; the launch traced here: 711 us
  Pallas kernels  675 us (95%)
  waiting for transfers between devices  12.3 us (2%)
  local copies, waits for them, and re-layouts  10.8 us (2%)
  starting transfers between devices  8.01 us (1%)
    pallas_call x1, Pallas kernels, plane_layer(): pl.pallas_call(backward, out_shape=jax.tree.leaves(out_hbm), in_specs=[pl...  640 us
    pallas_call x1, Pallas kernels, plane_layer(): pl.pallas_call(place, out_shape=[shape(a.shape, F32) for a in (gate_weigh...  32 us
  transfers between devices with their start and end apart: 5, of which 2 were waited for; matrix products, arithmetic and copies ran while one was open for 1% of the time, Pallas kernels for 0%

profile of v8, /device:TPU:0, one launch (start us, length us, event | category | flops | bytes accessed | tf_op | source)
XLA Modules:
  0.0 710.6 jit_solution(17699346759659366991)
XLA Ops:
  0.6 3.0 collective-permute-start.4
  3.7 1.5 collective-permute-start.3
  5.2 1.3 reshape.283.refs_8_
  6.4 1.3 reshape.284.refs_9_
  7.7 0.6 pad_add_fusion.me_ref
  8.3 3.4 cut_weights.1
  11.7 0.5 collective-permute-start
  12.3 2.9 collective-permute-start.2
  15.6 0.6 gather_fusion
  16.5 0.7 gather_fusion.1
  17.2 0.7 reshape.286.refs_14_
  17.9 1.5 reshape.305.refs_15_
  19.5 0.1 multiply_bitcast_fusion
  19.6 1.4 fusion.1
  21.0 1.2 pad_maximum_fusion.refs_16_
  22.3 8.0 %collective-permute-done.refs_4_ = bf16[544,256]{1,0:T(8,128)(2,1)S(1)} collective-permute-done((bf16[544,256]{1,0:T(8,128)(2,1)}, bf16[544,256]{1,0:T(8,128)(2,1)S(1)}, u32[]{:S(2)}, u32[]{:S(2)}) %collective-permute-start) | collective-permute-done | bytes 278560 | tf_op jit(solution)/shard_map/ppermute | solution.py:437
  30.3 4.3 collective-permute-done.2.refs_6_
  34.7 0.7 copy-done.7
  35.3 0.3 copy-done.4
  35.6 639.5 %backward.1 = (bf16[4,2,192,2048]{3,2,1,0:T(8,128)(2,1)}, bf16[2,4,192,2048]{3,2,1,0:T(8,128)(2,1)}, bf16[30,2,256,512]{3,2,1,0:T(8,128)(2,1)}, bf16[30,2,256,51...) custom-call(bf16[192,2048]{1,0:T(8,128)(2,1)} %bitcast.24, ...), custom_call_target="tpu_custom_call" | custom-call | flops 96636764160 | bytes 130381824 | tf_op jit(solution)/shard_map/backward/pallas_call | solution.py:1941
  675.1 1.4 fusion.9
  676.5 32.0 %place.1 = (f32[512,8192]{1,0:T(8,128)}, f32[512,8192]{1,0:T(8,128)}, f32[8192,512]{1,0:T(8,128)}, f32[512,2048]{1,0:T(8,128)}, f32[2048,512]{1,0:T(8,128)}, /*index=5*/f32[512,1024]{1,0:T(8,128)}, f32[512,1024]{1,0:T(8,128)}) custom-call(s32[2]{0:T(128)} %pad_add_fusion.me_ref, bf16[15,4,256,512]{3,2,1,0:T(8,128)(2,1)} %bitcast.18, ...), custom_call_target="tpu_custom_call" | custom-call | tf_op jit(solution)/shard_map/place/pallas_call | solution.py:2027
  708.6 0.9 copy.27
  709.5 1.1 copy.28
  (33 shorter events, 0.8 us)
Async XLA Ops:
  0.6 34.0 %collective-permute-start.4 = (bf16[192,2048]{1,0:T(8,128)(2,1)}, bf16[192,2048]{1,0:T(8,128)(2,1)S(1)}, u32[]{:S(2)}, u32[]{:S(2)}) collective-permute-start(bf16[192,2048]{1,0:T(8,128)(2,1)} %bitcast.25), channel_id=1, source_target_pairs={{0,2},{1,3},{2,0},{3,1},{4,6},{5,7},{6,4},{7,5},{8,10},{9,11},{10,... | collective-permute-start | bytes 2359304 | tf_op jit(solution)/shard_map/ppermute | solution.py:437
  3.7 31.0 %collective-permute-start.3 = (bf16[192,2048]{1,0:T(8,128)(2,1)}, bf16[192,2048]{1,0:T(8,128)(2,1)}, u32[]{:S(2)}, u32[]{:S(2)}) collective-permute-start(bf16[192,2048]{1,0:T(8,128)(2,1)} %bitcast.26), channel_id=1, source_target_pairs={{0,1},{1,0},{2,3},{3,2},{4,5},{5,4},{6,7},{7,6},{8,9},{9,8},{10,11... | collective-permute-start | bytes 2359304 | tf_op jit(solution)/shard_map/ppermute | solution.py:437
  8.3 7.1 copy-start
  8.3 8.2 %copy-start.3 = (s32[4,1536]{1,0:T(4,128)S(1)}, s32[4,1536]{1,0:T(4,128)}, u32[]{:S(2)}) copy-start(s32[4,1536]{1,0:T(4,128)} %param.24) | copy-start | bytes 73732
  11.7 18.6 %collective-permute-start = (bf16[544,256]{1,0:T(8,128)(2,1)}, bf16[544,256]{1,0:T(8,128)(2,1)S(1)}, u32[]{:S(2)}, u32[]{:S(2)}) collective-permute-start(bf16[544,256]{1,0:T(8,128)(2,1)} %get-tuple-element.28), channel_id=1, source_target_pairs={{0,1},{1,0},{2,3},{3,2},{4,5},{5,4},{6,7},{7,6},{8,9},{9,8},{10,11... | collective-permute-start | bytes 835592 | tf_op jit(solution)/shard_map/ppermute | solution.py:437
  12.2 18.1 %collective-permute-start.1 = (bf16[544,256]{1,0:T(8,128)(2,1)}, bf16[544,256]{1,0:T(8,128)(2,1)S(1)}, u32[]{:S(2)}, u32[]{:S(2)}) collective-permute-start(bf16[544,256]{1,0:T(8,128)(2,1)} %get-tuple-element.29), channel_id=1, source_target_pairs={{0,2},{1,3},{2,0},{3,1},{4,6},{5,7},{6,4},{7,5},{8,10},{9,11},{10,... | collective-permute-start | bytes 835592 | tf_op jit(solution)/shard_map/ppermute | solution.py:437
  12.3 22.3 %collective-permute-start.2 = (bf16[544,256]{1,0:T(8,128)(2,1)}, bf16[544,256]{1,0:T(8,128)(2,1)S(1)}, u32[]{:S(2)}, u32[]{:S(2)}) collective-permute-start(bf16[544,256]{1,0:T(8,128)(2,1)} %get-tuple-element.30), channel_id=1, source_target_pairs={{0,3},{1,2},{2,1},{3,0},{4,7},{5,6},{6,5},{7,4},{8,11},{9,10},{10,... | collective-permute-start | bytes 835592 | tf_op jit(solution)/shard_map/ppermute | solution.py:437
  30.3 4.3 copy-start.5
  30.3 4.3 copy-start.6
  34.6 0.7 copy-start.7
  34.6 1.0 copy-start.4
  676.5 32.1 %copy-start.2 = (bf16[192,2048]{1,0:T(8,128)(2,1)S(1)}, bf16[192,2048]{1,0:T(8,128)(2,1)}, u32[]{:S(2)}) copy-start(bf16[192,2048]{1,0:T(8,128)(2,1)} %get-tuple-element.31) | copy-start | bytes 2359300
  676.5 33.0 %copy-start.1 = (f32[192,2048]{1,0:T(8,128)S(1)}, f32[192,2048]{1,0:T(8,128)}, u32[]{:S(2)}) copy-start(f32[192,2048]{1,0:T(8,128)} %get-tuple-element.32) | copy-start | bytes 4718596

commit v9 on v8

--- a/solution.py
+++ b/solution.py
@@ -1528,6 +1528,12 @@
                 def _():
                     rows_of_chip(t, two_far, two_half, two_near)
 
+                    @pl.when(t == 2)
+                    def _():
+                        for d in range(1, n):
+                            every(feed_far(1, d), starts)
+
+
                 now = span(t * pair, pair)
                 cot_now = pl.ds(pl.multiple_of(plane_rows + t * pair, pair), pair)
                 both = jnp.zeros((pair, 2 * quarter), F32)
@@ -1549,11 +1555,6 @@
                 return 0
 
             lax.fori_loop(0, n, forward, 0)
-
-            @pl.when(q == 0)
-            def _():
-                for d in range(1, n):
-                    every(feed_far(1, d), starts)
 
             step(3 * q - 2)
 

time: 713 us -> 706 us (level)
  no operation moved by 1% of the time
where the time goes in v9:
time: 706 us; the launch traced here: 704 us
  Pallas kernels  668 us (95%)
  waiting for transfers between devices  12.3 us (2%)
  local copies, waits for them, and re-layouts  10.8 us (2%)
  starting transfers between devices  8.01 us (1%)
    pallas_call x1, Pallas kernels, plane_layer(): pl.pallas_call(backward, out_shape=jax.tree.leaves(out_hbm), in_specs=[pl...  633 us
    pallas_call x1, Pallas kernels, plane_layer(): pl.pallas_call(place, out_shape=[shape(a.shape, F32) for a in (gate_weigh...  32 us
  transfers between devices with their start and end apart: 5, of which 2 were waited for; matrix products, arithmetic and copies ran while one was open for 1% of the time, Pallas kernels for 0%

profile of v9, /device:TPU:0, one launch (start us, length us, event | category | flops | bytes accessed | tf_op | source)
XLA Modules:
  0.0 704.0 jit_solution(17572553567900235933)
XLA Ops:
  0.6 3.0 collective-permute-start.4
  3.7 1.5 collective-permute-start.3
  5.2 1.3 reshape.283.refs_8_
  6.4 1.3 reshape.284.refs_9_
  7.7 0.6 pad_add_fusion.me_ref
  8.3 3.4 cut_weights.1
  11.7 0.5 collective-permute-start
  12.3 2.9 collective-permute-start.2
  15.6 0.6 gather_fusion
  16.5 0.7 gather_fusion.1
  17.2 0.7 reshape.286.refs_14_
  17.9 1.5 reshape.305.refs_15_
  19.5 0.1 multiply_bitcast_fusion
  19.6 1.4 fusion.1
  21.0 1.2 pad_maximum_fusion.refs_16_
  22.3 8.0 %collective-permute-done.refs_4_ = bf16[544,256]{1,0:T(8,128)(2,1)S(1)} collective-permute-done((bf16[544,256]{1,0:T(8,128)(2,1)}, bf16[544,256]{1,0:T(8,128)(2,1)S(1)}, u32[]{:S(2)}, u32[]{:S(2)}) %collective-permute-start) | collective-permute-done | bytes 278560 | tf_op jit(solution)/shard_map/ppermute | solution.py:437
  30.3 4.3 collective-permute-done.2.refs_6_
  34.7 0.7 copy-done.7
  35.3 0.3 copy-done.4
  35.6 633.0 %backward.1 = (bf16[4,2,192,2048]{3,2,1,0:T(8,128)(2,1)}, bf16[2,4,192,2048]{3,2,1,0:T(8,128)(2,1)}, bf16[30,2,256,512]{3,2,1,0:T(8,128)(2,1)}, bf16[30,2,256,51...) custom-call(bf16[192,2048]{1,0:T(8,128)(2,1)} %bitcast.24, ...), custom_call_target="tpu_custom_call" | custom-call | flops 96636764160 | bytes 130381824 | tf_op jit(solution)/shard_map/backward/pallas_call | solution.py:1942
  668.6 1.4 fusion.9
  669.9 32.0 %place.1 = (f32[512,8192]{1,0:T(8,128)}, f32[512,8192]{1,0:T(8,128)}, f32[8192,512]{1,0:T(8,128)}, f32[512,2048]{1,0:T(8,128)}, f32[2048,512]{1,0:T(8,128)}, /*index=5*/f32[512,1024]{1,0:T(8,128)}, f32[512,1024]{1,0:T(8,128)}) custom-call(s32[2]{0:T(128)} %pad_add_fusion.me_ref, bf16[15,4,256,512]{3,2,1,0:T(8,128)(2,1)} %bitcast.18, ...), custom_call_target="tpu_custom_call" | custom-call | tf_op jit(solution)/shard_map/place/pallas_call | solution.py:2028
  702.0 0.9 copy.27
  702.9 1.1 copy.28
  (33 shorter events, 0.8 us)
Async XLA Ops:
  0.6 34.0 %collective-permute-start.4 = (bf16[192,2048]{1,0:T(8,128)(2,1)}, bf16[192,2048]{1,0:T(8,128)(2,1)S(1)}, u32[]{:S(2)}, u32[]{:S(2)}) collective-permute-start(bf16[192,2048]{1,0:T(8,128)(2,1)} %bitcast.25), channel_id=1, source_target_pairs={{0,2},{1,3},{2,0},{3,1},{4,6},{5,7},{6,4},{7,5},{8,10},{9,11},{10,... | collective-permute-start | bytes 2359304 | tf_op jit(solution)/shard_map/ppermute | solution.py:437
  3.7 31.0 %collective-permute-start.3 = (bf16[192,2048]{1,0:T(8,128)(2,1)}, bf16[192,2048]{1,0:T(8,128)(2,1)}, u32[]{:S(2)}, u32[]{:S(2)}) collective-permute-start(bf16[192,2048]{1,0:T(8,128)(2,1)} %bitcast.26), channel_id=1, source_target_pairs={{0,1},{1,0},{2,3},{3,2},{4,5},{5,4},{6,7},{7,6},{8,9},{9,8},{10,11... | collective-permute-start | bytes 2359304 | tf_op jit(solution)/shard_map/ppermute | solution.py:437
  8.3 7.1 %copy-start = (s32[8]{0:T(128)S(1)}, s32[8]{0:T(128)}, u32[]{:S(2)}) copy-start(s32[8]{0:T(128)} %param.25) | copy-start | bytes 100
  8.3 8.2 %copy-start.3 = (s32[4,1536]{1,0:T(4,128)S(1)}, s32[4,1536]{1,0:T(4,128)}, u32[]{:S(2)}) copy-start(s32[4,1536]{1,0:T(4,128)} %param.24) | copy-start | bytes 73732
  11.7 18.6 %collective-permute-start = (bf16[544,256]{1,0:T(8,128)(2,1)}, bf16[544,256]{1,0:T(8,128)(2,1)S(1)}, u32[]{:S(2)}, u32[]{:S(2)}) collective-permute-start(bf16[544,256]{1,0:T(8,128)(2,1)} %get-tuple-element.28), channel_id=1, source_target_pairs={{0,1},{1,0},{2,3},{3,2},{4,5},{5,4},{6,7},{7,6},{8,9},{9,8},{10,11... | collective-permute-start | bytes 835592 | tf_op jit(solution)/shard_map/ppermute | solution.py:437
  12.2 18.1 %collective-permute-start.1 = (bf16[544,256]{1,0:T(8,128)(2,1)}, bf16[544,256]{1,0:T(8,128)(2,1)S(1)}, u32[]{:S(2)}, u32[]{:S(2)}) collective-permute-start(bf16[544,256]{1,0:T(8,128)(2,1)} %get-tuple-element.29), channel_id=1, source_target_pairs={{0,2},{1,3},{2,0},{3,1},{4,6},{5,7},{6,4},{7,5},{8,10},{9,11},{10,... | collective-permute-start | bytes 835592 | tf_op jit(solution)/shard_map/ppermute | solution.py:437
  12.3 22.3 %collective-permute-start.2 = (bf16[544,256]{1,0:T(8,128)(2,1)}, bf16[544,256]{1,0:T(8,128)(2,1)S(1)}, u32[]{:S(2)}, u32[]{:S(2)}) collective-permute-start(bf16[544,256]{1,0:T(8,128)(2,1)} %get-tuple-element.30), channel_id=1, source_target_pairs={{0,3},{1,2},{2,1},{3,0},{4,7},{5,6},{6,5},{7,4},{8,11},{9,10},{10,... | collective-permute-start | bytes 835592 | tf_op jit(solution)/shard_map/ppermute | solution.py:437
  30.3 4.3 copy-start.5
  30.3 4.3 copy-start.6
  34.6 0.7 copy-start.7
  34.6 1.0 copy-start.4
  669.9 32.1 %copy-start.2 = (bf16[192,2048]{1,0:T(8,128)(2,1)S(1)}, bf16[192,2048]{1,0:T(8,128)(2,1)}, u32[]{:S(2)}) copy-start(bf16[192,2048]{1,0:T(8,128)(2,1)} %get-tuple-element.31) | copy-start | bytes 2359300
  669.9 33.0 %copy-start.1 = (f32[192,2048]{1,0:T(8,128)S(1)}, f32[192,2048]{1,0:T(8,128)}, u32[]{:S(2)}) copy-start(f32[192,2048]{1,0:T(8,128)} %get-tuple-element.32) | copy-start | bytes 4718596

commit v10 on v9

--- a/solution.py
+++ b/solution.py
@@ -698,7 +698,8 @@
         partner = (2 * (z + 1 - 2 * (z % 2)) + side, chip)
         other_middle = (2 * (3 - z) + side, chip)
         other_core = (here + 1 - 2 * side, chip)
-        below, above = (here - 2, chip), (here + 2, chip)
+        below = ((here + ctx_count - 2) % ctx_count, chip)
+        above = ((here + 2) % ctx_count, chip)
         blocks = [pl.ds(pl.multiple_of(c * wide, wide), wide) for c in chips]
         work, feed, heads, turned, stage = r.work, r.feed, r.heads, r.turned, r.stage
 

time: 706 us -> 706 us (level)
  no operation moved by 1% of the time
where the time goes in v10:
time: 706 us; the launch traced here: 704 us
  Pallas kernels  668 us (95%)
  waiting for transfers between devices  12.3 us (2%)
  local copies, waits for them, and re-layouts  10.8 us (2%)
  starting transfers between devices  8.01 us (1%)
    pallas_call x1, Pallas kernels, plane_layer(): pl.pallas_call(backward, out_shape=jax.tree.leaves(out_hbm), in_specs=[pl...  633 us
    pallas_call x1, Pallas kernels, plane_layer(): pl.pallas_call(place, out_shape=[shape(a.shape, F32) for a in (gate_weigh...  32 us
  transfers between devices with their start and end apart: 5, of which 2 were waited for; matrix products, arithmetic and copies ran while one was open for 1% of the time, Pallas kernels for 0%

profile of v10, /device:TPU:0, one launch (start us, length us, event | category | flops | bytes accessed | tf_op | source)
XLA Modules:
  0.0 704.0 jit_solution(3720155841403543286)
XLA Ops:
  0.6 3.0 collective-permute-start.4
  3.7 1.5 collective-permute-start.3
  5.2 1.3 reshape.283.refs_8_
  6.4 1.3 reshape.284.refs_9_
  7.7 0.6 pad_add_fusion.me_ref
  8.3 3.4 cut_weights.1
  11.7 0.5 collective-permute-start
  12.3 2.9 collective-permute-start.2
  15.6 0.6 gather_fusion
  16.5 0.7 gather_fusion.1
  17.2 0.7 reshape.286.refs_14_
  17.9 1.5 reshape.305.refs_15_
  19.5 0.1 multiply_bitcast_fusion
  19.6 1.4 fusion.1
  21.0 1.2 pad_maximum_fusion.refs_16_
  22.3 8.0 %collective-permute-done.refs_4_ = bf16[544,256]{1,0:T(8,128)(2,1)S(1)} collective-permute-done((bf16[544,256]{1,0:T(8,128)(2,1)}, bf16[544,256]{1,0:T(8,128)(2,1)S(1)}, u32[]{:S(2)}, u32[]{:S(2)}) %collective-permute-start) | collective-permute-done | bytes 278560 | tf_op jit(solution)/shard_map/ppermute | solution.py:437
  30.3 4.3 collective-permute-done.2.refs_6_
  34.7 0.7 copy-done.7
  35.3 0.3 copy-done.4
  35.6 633.0 %backward.1 = (bf16[4,2,192,2048]{3,2,1,0:T(8,128)(2,1)}, bf16[2,4,192,2048]{3,2,1,0:T(8,128)(2,1)}, bf16[30,2,256,512]{3,2,1,0:T(8,128)(2,1)}, bf16[30,2,256,51...) custom-call(bf16[192,2048]{1,0:T(8,128)(2,1)} %bitcast.24, ...), custom_call_target="tpu_custom_call" | custom-call | flops 96636764160 | bytes 130381824 | tf_op jit(solution)/shard_map/backward/pallas_call | solution.py:1943
  668.6 1.4 fusion.9
  669.9 32.0 %place.1 = (f32[512,8192]{1,0:T(8,128)}, f32[512,8192]{1,0:T(8,128)}, f32[8192,512]{1,0:T(8,128)}, f32[512,2048]{1,0:T(8,128)}, f32[2048,512]{1,0:T(8,128)}, /*index=5*/f32[512,1024]{1,0:T(8,128)}, f32[512,1024]{1,0:T(8,128)}) custom-call(s32[2]{0:T(128)} %pad_add_fusion.me_ref, bf16[15,4,256,512]{3,2,1,0:T(8,128)(2,1)} %bitcast.18, ...), custom_call_target="tpu_custom_call" | custom-call | tf_op jit(solution)/shard_map/place/pallas_call | solution.py:2029
  702.0 0.9 copy.27
  702.9 1.1 copy.28
  (33 shorter events, 0.8 us)
Async XLA Ops:
  0.6 34.0 %collective-permute-start.4 = (bf16[192,2048]{1,0:T(8,128)(2,1)}, bf16[192,2048]{1,0:T(8,128)(2,1)S(1)}, u32[]{:S(2)}, u32[]{:S(2)}) collective-permute-start(bf16[192,2048]{1,0:T(8,128)(2,1)} %bitcast.25), channel_id=1, source_target_pairs={{0,2},{1,3},{2,0},{3,1},{4,6},{5,7},{6,4},{7,5},{8,10},{9,11},{10,... | collective-permute-start | bytes 2359304 | tf_op jit(solution)/shard_map/ppermute | solution.py:437
  3.7 31.0 %collective-permute-start.3 = (bf16[192,2048]{1,0:T(8,128)(2,1)}, bf16[192,2048]{1,0:T(8,128)(2,1)}, u32[]{:S(2)}, u32[]{:S(2)}) collective-permute-start(bf16[192,2048]{1,0:T(8,128)(2,1)} %bitcast.26), channel_id=1, source_target_pairs={{0,1},{1,0},{2,3},{3,2},{4,5},{5,4},{6,7},{7,6},{8,9},{9,8},{10,11... | collective-permute-start | bytes 2359304 | tf_op jit(solution)/shard_map/ppermute | solution.py:437
  8.3 7.1 %copy-start = (s32[8]{0:T(128)S(1)}, s32[8]{0:T(128)}, u32[]{:S(2)}) copy-start(s32[8]{0:T(128)} %param.25) | copy-start | bytes 100
  8.3 8.2 %copy-start.3 = (s32[4,1536]{1,0:T(4,128)S(1)}, s32[4,1536]{1,0:T(4,128)}, u32[]{:S(2)}) copy-start(s32[4,1536]{1,0:T(4,128)} %param.24) | copy-start | bytes 73732
  11.7 18.6 %collective-permute-start = (bf16[544,256]{1,0:T(8,128)(2,1)}, bf16[544,256]{1,0:T(8,128)(2,1)S(1)}, u32[]{:S(2)}, u32[]{:S(2)}) collective-permute-start(bf16[544,256]{1,0:T(8,128)(2,1)} %get-tuple-element.28), channel_id=1, source_target_pairs={{0,1},{1,0},{2,3},{3,2},{4,5},{5,4},{6,7},{7,6},{8,9},{9,8},{10,11... | collective-permute-start | bytes 835592 | tf_op jit(solution)/shard_map/ppermute | solution.py:437
  12.2 18.1 %collective-permute-start.1 = (bf16[544,256]{1,0:T(8,128)(2,1)}, bf16[544,256]{1,0:T(8,128)(2,1)S(1)}, u32[]{:S(2)}, u32[]{:S(2)}) collective-permute-start(bf16[544,256]{1,0:T(8,128)(2,1)} %get-tuple-element.29), channel_id=1, source_target_pairs={{0,2},{1,3},{2,0},{3,1},{4,6},{5,7},{6,4},{7,5},{8,10},{9,11},{10,... | collective-permute-start | bytes 835592 | tf_op jit(solution)/shard_map/ppermute | solution.py:437
  12.3 22.3 %collective-permute-start.2 = (bf16[544,256]{1,0:T(8,128)(2,1)}, bf16[544,256]{1,0:T(8,128)(2,1)S(1)}, u32[]{:S(2)}, u32[]{:S(2)}) collective-permute-start(bf16[544,256]{1,0:T(8,128)(2,1)} %get-tuple-element.30), channel_id=1, source_target_pairs={{0,3},{1,2},{2,1},{3,0},{4,7},{5,6},{6,5},{7,4},{8,11},{9,10},{10,... | collective-permute-start | bytes 835592 | tf_op jit(solution)/shard_map/ppermute | solution.py:437
  30.3 4.3 copy-start.5
  30.3 4.3 copy-start.6
  34.6 0.7 copy-start.7
  34.6 1.0 copy-start.4
  669.9 32.1 %copy-start.2 = (bf16[192,2048]{1,0:T(8,128)(2,1)S(1)}, bf16[192,2048]{1,0:T(8,128)(2,1)}, u32[]{:S(2)}) copy-start(bf16[192,2048]{1,0:T(8,128)(2,1)} %get-tuple-element.31) | copy-start | bytes 2359300
  669.9 33.0 %copy-start.1 = (f32[192,2048]{1,0:T(8,128)S(1)}, f32[192,2048]{1,0:T(8,128)}, u32[]{:S(2)}) copy-start(f32[192,2048]{1,0:T(8,128)} %get-tuple-element.32) | copy-start | bytes 4718596
